TPU v7x, 32 devices: a whole 2x2x4 slice. The times are simulated.
32 devices in a mesh: dp: 8 (over z, x), mp: 4 (over y, core).
Axes of the slice: x: 2, y: 2, z: 4, core: 2. Of those that a mesh axis runs over, the one named last changes fastest.
Arguments:
- block_input: bfloat16 [12544, 1280], P('dp'), may hold values from -6 to 6
- window_place: int32 [64], P('dp'), may hold values from 0 to 24, as said below
- slot_live: int32 [64], P('dp'), may hold values from 0 to 1, as said below
- norm_one_gain: float32 [1280], replicated, may hold values from 0.25 to 1.75
- norm_one_shift: float32 [1280], replicated, may hold values from -1 to 1
- qkv_weight: bfloat16 [3, 1280, 1280], P(None, 'dp', 'mp'), may hold values from -0.15625 to 0.15625
- qv_bias: float32 [2, 1280], replicated, may hold values from -1.5 to 1.5
- proj_weight: bfloat16 [1280, 1280], P('mp', 'dp'), may hold values from -1.25 to 1.25
- proj_bias: float32 [1280], replicated, may hold values from -1 to 1
- norm_two_gain: float32 [1280], replicated, may hold values from 0.25 to 1.75
- norm_two_shift: float32 [1280], replicated, may hold values from -1 to 1
- up_weight: bfloat16 [1280, 5120], P('dp', 'mp'), may hold values from -0.15625 to 0.15625
- up_bias: float32 [5120], replicated, may hold values from -1.5 to 1.5
- down_weight: bfloat16 [5120, 1280], P('mp', 'dp'), may hold values from -0.078125 to 0.078125
- down_bias: float32 [1280], replicated, may hold values from -1 to 1
- rel_height: float32 [27, 80], replicated, may hold values from -0.9 to 0.9
- rel_width: float32 [27, 80], replicated, may hold values from -0.9 to 0.9
- cotangent: bfloat16 [12544, 1280], P('dp'), may hold values from -6 to 6
Outputs:
- block_output: bfloat16 [12544, 1280], P('dp')
- input_grad: float32 [12544, 1280], P('dp')
- norm_one_gain_grad: float32 [1280], replicated
- norm_one_shift_grad: float32 [1280], replicated
- qkv_grad: float32 [3, 1280, 1280], P(None, 'dp', 'mp')
- qv_bias_grad: float32 [2, 1280], replicated
- proj_grad: float32 [1280, 1280], P('mp', 'dp')
- proj_bias_grad: float32 [1280], replicated
- norm_two_gain_grad: float32 [1280], replicated
- norm_two_shift_grad: float32 [1280], replicated
- up_grad: float32 [1280, 5120], P('dp', 'mp')
- up_bias_grad: float32 [5120], replicated
- down_grad: float32 [5120, 1280], P('mp', 'dp')
- down_bias_grad: float32 [1280], replicated
- rel_height_grad: float32 [27, 80], replicated
- rel_width_grad: float32 [27, 80], replicated
Inputs may be any that keep to these rules, and one draw needn't show every extreme that they name: `window_place`: the first 4 slots of each device belong to the first micro-batch, the next 4 to the second. Over all devices, the live slots of the first micro-batch hold the windows of 1 image, those of the second micro-batch the windows of 1 image, each image's 5 * 5 places once each; a padding slot's place is arbitrary. `slot_live`: exactly 25 of the first micro-batch's slots and 25 of the second's are live, spread over the devices in any way.
All inputs are finite; a program needn't handle non-finite values.
Results may differ from a plain program's by a relative error of at most 0.017.
Values may be sent and summed in bfloat16 or wider, within the bound.
No kernel may reach another device: no remote copies, remote signals or barrier semaphores. Data moves between devices by JAX's collectives and lax.ppermute only.
A program may use at most 256 MiB of HBM per device.

v0:
```python
from functools import partial

import jax
import jax.numpy as jnp
from jax import lax
from jax.sharding import PartitionSpec as P

HD = 80
WIN = 14
SIDE = 64
WIN_DEV_A = 3
GRID = 5
WTOK = 196
RELN = 27


epsilon = 1e-06
highest = lax.Precision.HIGHEST


def layer_norm(values, gain, shift):
    center = jnp.mean(values, axis=-1, keepdims=True)
    centred = values - center
    spread = jnp.mean(centred * centred, axis=-1, keepdims=True)
    return centred * lax.rsqrt(spread + epsilon) * gain + shift


def masked_norm(values, gain, shift, mask):
    return layer_norm(values, gain, shift) * mask[:, None]


def exact_gelu(values):
    return jax.nn.gelu(values, approximate=False)


def token_valid(window_place, slot_live):
    position = jnp.arange(WTOK, dtype=jnp.int32)
    inner_row = position // WIN
    inner_col = position % WIN
    grid_row = (window_place // GRID)[:, None]
    grid_col = (window_place % GRID)[:, None]
    inside = (
        (grid_row * WIN + inner_row[None, :] < SIDE)
        & (grid_col * WIN + inner_col[None, :] < SIDE)
        & (slot_live[:, None] == 1)
    )
    return jnp.where(inside, 1.0, 0.0).astype(jnp.float32)


def offset_table():
    first = jnp.arange(WIN, dtype=jnp.int32)
    target = first[:, None] - first[None, :] + WIN - 1
    return jnp.where(
        target[:, :, None] == jnp.arange(RELN, dtype=jnp.int32)[None, None, :], 1.0, 0.0
    ).astype(jnp.float32)


def contract_rows(left, right):
    return lax.dot_general(
        left, right, (((0,), (0,)), ((), ())), preferred_element_type=jnp.float32
    )


def contract_cols(left, right):
    return lax.dot_general(
        left, right, (((1,), (1,)), ((), ())), preferred_element_type=jnp.float32
    )


def scores_of(queries, keys, table_height, table_width):
    windows, heads, size = (queries.shape[0], queries.shape[2], queries.shape[3])
    scores = jnp.einsum(
        "gqhc,gkhc->ghqk", queries, keys, preferred_element_type=jnp.float32
    ) * size ** (-0.5)
    query_grid = queries.astype(jnp.float32).reshape(windows, WIN, WIN, heads, size)
    bias_height = jnp.einsum("gxyhc,xkc->ghxyk", query_grid, table_height, precision=highest)
    bias_width = jnp.einsum("gxyhc,ykc->ghxyk", query_grid, table_width, precision=highest)
    scores = (
        scores.reshape(windows, heads, WIN, WIN, WIN, WIN)
        + bias_height[:, :, :, :, :, None]
        + bias_width[:, :, :, :, None, :]
    )
    return scores.reshape(windows, heads, WTOK, WTOK)


def attend(queries, keys, values, table_height, table_width):
    scores = scores_of(queries, keys, table_height, table_width)
    top = jnp.max(scores, axis=-1, keepdims=True)
    shifted = jnp.exp(scores - top)
    total = jnp.sum(shifted, axis=-1, keepdims=True)
    shares = (shifted / total).astype(jnp.bfloat16)
    mixed = jnp.einsum("ghqk,gkhc->gqhc", shares, values, preferred_element_type=jnp.float32)
    return (mixed.astype(jnp.bfloat16), top + jnp.log(total))


def attend_back(queries, keys, values, log_total, grad_mixed, table_height, table_width):
    windows, heads, size = (queries.shape[0], queries.shape[2], queries.shape[3])
    scale = size ** (-0.5)
    scores = scores_of(queries, keys, table_height, table_width)
    shares = jnp.exp(scores - log_total)
    grad_shares = jnp.einsum(
        "gqhc,gkhc->ghqk", grad_mixed, values, preferred_element_type=jnp.float32
    )
    grad_values = jnp.einsum(
        "ghqk,gqhc->gkhc",
        shares.astype(jnp.bfloat16),
        grad_mixed,
        preferred_element_type=jnp.float32,
    )
    inner = jnp.sum(shares * grad_shares, axis=-1, keepdims=True)
    grad_scores = (shares * (grad_shares - inner)).astype(jnp.bfloat16)
    grad_queries = (
        jnp.einsum("ghqk,gkhc->gqhc", grad_scores, keys, preferred_element_type=jnp.float32) * scale
    )
    grad_keys = (
        jnp.einsum("ghqk,gqhc->gkhc", grad_scores, queries, preferred_element_type=jnp.float32)
        * scale
    )
    grad_grid = grad_scores.reshape(windows, heads, WIN, WIN, WIN, WIN)
    grad_height = jnp.sum(grad_grid, axis=5, dtype=jnp.float32)
    grad_width = jnp.sum(grad_grid, axis=4, dtype=jnp.float32)
    query_grid = queries.astype(jnp.float32).reshape(windows, WIN, WIN, heads, size)
    extra = jnp.einsum(
        "ghxyk,xkc->gxyhc", grad_height, table_height, precision=highest
    ) + jnp.einsum("ghxyk,ykc->gxyhc", grad_width, table_width, precision=highest)
    grad_queries = grad_queries + extra.reshape(windows, WTOK, heads, size)
    height_part = jnp.einsum("ghxyk,gxyhc->xkc", grad_height, query_grid, precision=highest)
    width_part = jnp.einsum("ghxyk,gxyhc->ykc", grad_width, query_grid, precision=highest)
    return (grad_queries, grad_keys, grad_values, height_part, width_part)


def body(
    block_input,
    window_place,
    slot_live,
    norm_one_gain,
    norm_one_shift,
    qkv_weight,
    qv_bias,
    proj_weight,
    proj_bias,
    norm_two_gain,
    norm_two_shift,
    up_weight,
    up_bias,
    down_weight,
    down_bias,
    rel_height,
    rel_width,
    cotangent,
):
    data_parts = lax.axis_size("dp")
    model_parts = lax.axis_size("mp")
    model_index = lax.axis_index("mp")
    width = block_input.shape[1]
    head_cols = qkv_weight.shape[2]
    local_heads = head_cols // HD
    up_cols = up_weight.shape[1]
    places = GRID * GRID
    images_first = max(1, WIN_DEV_A * data_parts // places)
    slots_first = (images_first * places + data_parts - 1) // data_parts
    slots_all = window_place.shape[0]
    valid = token_valid(window_place, slot_live).reshape(slots_all * WTOK)
    bias_local = lax.dynamic_slice_in_dim(qv_bias, model_index * head_cols, head_cols, 1)
    up_local = lax.dynamic_slice_in_dim(up_bias, model_index * up_cols, up_cols, 0)
    table = offset_table()
    table_height = jnp.einsum("abr,rc->abc", table, rel_height, precision=highest)
    table_width = jnp.einsum("abr,rc->abc", table, rel_width, precision=highest)
    qkv_acc = jnp.zeros((3, width, head_cols), jnp.float32)
    proj_acc = jnp.zeros((head_cols, width), jnp.float32)
    up_acc = jnp.zeros((width, up_cols), jnp.float32)
    down_acc = jnp.zeros((up_cols, width), jnp.float32)
    gain_one_acc = jnp.zeros((width,), jnp.float32)
    shift_one_acc = jnp.zeros((width,), jnp.float32)
    gain_two_acc = jnp.zeros((width,), jnp.float32)
    shift_two_acc = jnp.zeros((width,), jnp.float32)
    proj_bias_acc = jnp.zeros((width,), jnp.float32)
    down_bias_acc = jnp.zeros((width,), jnp.float32)
    up_bias_acc = jnp.zeros((up_cols,), jnp.float32)
    qv_bias_acc = jnp.zeros((2, head_cols), jnp.float32)
    height_acc = jnp.zeros(rel_height.shape, jnp.float32)
    width_acc = jnp.zeros(rel_width.shape, jnp.float32)
    outputs = []
    input_grads = []
    for first, count in ((0, slots_first), (slots_first, slots_all - slots_first)):
        begin = first * WTOK
        finish = (first + count) * WTOK
        row_count = finish - begin
        rows_in = block_input[begin:finish].astype(jnp.float32)
        valid_rows = valid[begin:finish]
        gathered = (
            lax.all_gather(qkv_weight, "dp", axis=1, tiled=True),
            lax.all_gather(proj_weight, "dp", axis=1, tiled=True),
            lax.all_gather(up_weight, "dp", axis=0, tiled=True),
            lax.all_gather(down_weight, "dp", axis=1, tiled=True),
        )
        weight_qkv, weight_proj, weight_up, weight_down = gathered
        normed_full, norm_one_back = jax.vjp(
            partial(masked_norm, mask=valid_rows), rows_in, norm_one_gain, norm_one_shift
        )
        normed = normed_full.astype(jnp.bfloat16)
        projected = jnp.einsum(
            "rd,sdh->srh", normed, weight_qkv, preferred_element_type=jnp.float32
        )
        head_shape = (count, WTOK, local_heads, HD)
        queries = (projected[0] + bias_local[0]).astype(jnp.bfloat16).reshape(head_shape)
        keys = projected[1].astype(jnp.bfloat16).reshape(head_shape)
        values = (projected[2] + bias_local[1]).astype(jnp.bfloat16).reshape(head_shape)
        mixed, log_total = attend(queries, keys, values, table_height, table_width)
        mixed_rows = mixed.reshape(row_count, head_cols)
        attn_partial = jnp.dot(mixed_rows, weight_proj, preferred_element_type=jnp.float32)
        after = rows_in + lax.psum(attn_partial, "mp") + proj_bias
        normed_two_full, norm_two_back = jax.vjp(layer_norm, after, norm_two_gain, norm_two_shift)
        normed_two = normed_two_full.astype(jnp.bfloat16)
        hidden = jnp.dot(normed_two, weight_up, preferred_element_type=jnp.float32) + up_local
        active_full, gelu_back = jax.vjp(exact_gelu, hidden)
        active = active_full.astype(jnp.bfloat16)
        mlp_partial = jnp.dot(active, weight_down, preferred_element_type=jnp.float32)
        branch_two = (
            lax.psum(mlp_partial.astype(jnp.bfloat16), "mp").astype(jnp.float32) + down_bias
        )
        outputs.append((valid_rows[:, None] * (after + branch_two)).astype(jnp.bfloat16))
        weight_qkv, weight_proj, weight_up, weight_down = (
            lax.all_gather(qkv_weight, "dp", axis=1, tiled=True),
            lax.all_gather(proj_weight, "dp", axis=1, tiled=True),
            lax.all_gather(up_weight, "dp", axis=0, tiled=True),
            lax.all_gather(down_weight, "dp", axis=1, tiled=True),
        )
        grad_out = cotangent[begin:finish].astype(jnp.float32) * valid_rows[:, None]
        grad_top = grad_out.astype(jnp.bfloat16)
        down_bias_acc = down_bias_acc + jnp.sum(grad_top, axis=0, dtype=jnp.float32)
        down_acc = down_acc + contract_rows(active, grad_top)
        (grad_hidden_full,) = gelu_back(contract_cols(grad_top, weight_down))
        grad_hidden = grad_hidden_full.astype(jnp.bfloat16)
        up_bias_acc = up_bias_acc + jnp.sum(grad_hidden, axis=0, dtype=jnp.float32)
        up_acc = up_acc + contract_rows(normed_two, grad_hidden)
        norm_two_partial = contract_cols(grad_hidden, weight_up)
        grad_normed_two = lax.psum(norm_two_partial.astype(jnp.bfloat16), "mp").astype(jnp.float32)
        grad_after_norm, gain_two_part, shift_two_part = norm_two_back(grad_normed_two)
        grad_after = grad_out + grad_after_norm
        grad_branch = grad_after.astype(jnp.bfloat16)
        gain_two_acc = gain_two_acc + gain_two_part
        shift_two_acc = shift_two_acc + shift_two_part
        proj_bias_acc = proj_bias_acc + jnp.sum(grad_branch, axis=0, dtype=jnp.float32)
        proj_acc = proj_acc + contract_rows(mixed_rows, grad_branch)
        grad_mixed = (
            contract_cols(grad_branch, weight_proj).astype(jnp.bfloat16).reshape(head_shape)
        )
        grad_queries, grad_keys, grad_values, height_part, width_part = attend_back(
            queries, keys, values, log_total, grad_mixed, table_height, table_width
        )
        height_acc = height_acc + jnp.einsum("abr,abc->rc", table, height_part, precision=highest)
        width_acc = width_acc + jnp.einsum("abr,abc->rc", table, width_part, precision=highest)
        stacked = jnp.stack(
            [
                grad_queries.reshape(row_count, head_cols),
                grad_keys.reshape(row_count, head_cols),
                grad_values.reshape(row_count, head_cols),
            ]
        ).astype(jnp.bfloat16)
        qv_bias_acc = qv_bias_acc + jnp.sum(stacked[0::2], axis=1, dtype=jnp.float32)
        qkv_acc = qkv_acc + jnp.einsum(
            "rd,srh->sdh", normed, stacked, preferred_element_type=jnp.float32
        )
        norm_one_partial = jnp.einsum(
            "srh,sdh->rd", stacked, weight_qkv, preferred_element_type=jnp.float32
        )
        grad_normed = lax.psum(norm_one_partial.astype(jnp.bfloat16), "mp").astype(jnp.float32)
        grad_rows_norm, gain_one_part, shift_one_part = norm_one_back(grad_normed)
        input_grads.append(grad_after + grad_rows_norm)
        gain_one_acc = gain_one_acc + gain_one_part
        shift_one_acc = shift_one_acc + shift_one_part
    qkv_grad, proj_grad, up_grad, down_grad = (
        lax.psum_scatter(
            qkv_acc.astype(jnp.bfloat16), "dp", scatter_dimension=1, tiled=True
        ).astype(jnp.float32),
        lax.psum_scatter(
            proj_acc.astype(jnp.bfloat16), "dp", scatter_dimension=1, tiled=True
        ).astype(jnp.float32),
        lax.psum_scatter(up_acc.astype(jnp.bfloat16), "dp", scatter_dimension=0, tiled=True).astype(
            jnp.float32
        ),
        lax.psum_scatter(
            down_acc.astype(jnp.bfloat16), "dp", scatter_dimension=1, tiled=True
        ).astype(jnp.float32),
    )
    feature_mask = jnp.where(
        jnp.arange(width, dtype=jnp.int32) // (width // model_parts) == model_index, 1.0, 0.0
    ).astype(jnp.float32)
    qv_full = lax.dynamic_update_slice_in_dim(
        jnp.zeros((2, width), jnp.float32), qv_bias_acc, model_index * head_cols, 1
    )
    up_full = lax.dynamic_update_slice_in_dim(
        jnp.zeros(up_bias.shape, jnp.float32), up_bias_acc, model_index * up_cols, 0
    )
    small = lax.psum(
        (
            gain_one_acc * feature_mask,
            shift_one_acc * feature_mask,
            qv_full,
            proj_bias_acc * feature_mask,
            gain_two_acc * feature_mask,
            shift_two_acc * feature_mask,
            up_full,
            down_bias_acc * feature_mask,
            height_acc,
            width_acc,
        ),
        ("dp", "mp"),
    )
    return (
        jnp.concatenate(outputs, axis=0),
        jnp.concatenate(input_grads, axis=0),
        small[0],
        small[1],
        qkv_grad,
        small[2],
        proj_grad,
        small[3],
        small[4],
        small[5],
        up_grad,
        small[6],
        down_grad,
        small[7],
        small[8],
        small[9],
    )


def solution(mesh):
    in_specs = (
        P("dp", None),
        P("dp"),
        P("dp"),
        P(),
        P(),
        P(None, "dp", "mp"),
        P(),
        P("mp", "dp"),
        P(),
        P(),
        P(),
        P("dp", "mp"),
        P(),
        P("mp", "dp"),
        P(),
        P(),
        P(),
        P("dp", None),
    )
    out_specs = (
        P("dp", None),
        P("dp", None),
        P(),
        P(),
        P(None, "dp", "mp"),
        P(),
        P("mp", "dp"),
        P(),
        P(),
        P(),
        P("dp", "mp"),
        P(),
        P("mp", "dp"),
        P(),
        P(),
        P(),
    )
    return jax.shard_map(body, mesh=mesh, in_specs=in_specs, out_specs=out_specs, check_vma=False)
```

profile of v0, /device:TPU:0, one launch (start us, length us, event | category | flops | bytes accessed | tf_op | source)
XLA Modules:
  0.0 1405.7 jit_solution(11544365192905765533)
XLA Ops:
  16.5 38.1 %all_gather.9 = bf16[320,1280]{0,1:T(8,128)(2,1)} all-gather(bf16[320,160]{0,1:T(8,128)(2,1)S(1)} %copy-done.78), channel_id=1, replica_groups=mesh['dp'=8,'mp'=4] {'dp'}, dimensions={1}, use_global_device_ids=true | all-gather | bytes 921600 | tf_op jit(solution)/shard_map/all_gather | solution.py:193
  54.6 23.5 %all-gather.4.cloned.1.call-done = bf16[3,1280,320]{2,1,0:T(8,128)(2,1)} async-done(((bf16[3,160,320]{2,1,0:T(8,128)(2,1)}), bf16[3,1280,320]{2,1,0:T(8,128)(2,1)}) %all-gather.4.cloned.1.call-update) | async-done | bytes 2457616 | tf_op jit(solution)/shard_map/all_gather | solution.py:192
  78.1 5.7 convolution_bitcast_fusion
  88.5 5.7 convolution_bitcast_fusion.1
  104.1 7.7 convolution_bitcast_fusion.2
  111.8 7.7 convolution_bitcast_fusion.3
  119.6 7.7 convolution_bitcast_fusion.4
  127.3 6.5 convolution_bitcast_fusion.5
  159.8 10.2 add.440
  170.0 14.8 %add.441 = f32[4,4,196,196]{3,2,1,0:T(8,128)S(1)} reshape(f32[4,4,14,14,14,14]{5,4,3,2,1,0:T(8,128)} %add.440) | data formatting | bytes 4917248 | tf_op jit(solution)/shard_map/add | solution.py:79
  187.8 9.7 add.443
  197.5 14.8 %add.444 = f32[4,4,196,196]{3,2,1,0:T(8,128)S(1)} reshape(f32[4,4,14,14,14,14]{5,4,3,2,1,0:T(8,128)} %add.443) | data formatting | bytes 4917248 | tf_op jit(solution)/shard_map/add | solution.py:79
  215.5 4.7 fusion.225
  224.6 9.1 add.463
  233.7 14.8 %add.464 = f32[4,4,196,196]{3,2,1,0:T(8,128)S(1)} reshape(f32[4,4,14,14,14,14]{5,4,3,2,1,0:T(8,128)} %add.463) | data formatting | bytes 4917248 | tf_op jit(solution)/shard_map/add | solution.py:79
  251.5 9.7 add.466
  261.2 14.8 %add.467 = f32[4,4,196,196]{3,2,1,0:T(8,128)S(1)} reshape(f32[4,4,14,14,14,14]{5,4,3,2,1,0:T(8,128)} %add.466) | data formatting | bytes 4917248 | tf_op jit(solution)/shard_map/add | solution.py:79
  279.3 4.7 fusion.226
  295.3 145.5 %all-reduce.11.cloned.1.call-done = (f32[784,1280]{1,0:T(8,128)}, f32[784,1280]{1,0:T(8,128)}) async-done(((f32[784,1280]{1,0:T(8,128)}, f32[784,1280]{1,0:T(8,128)}), (f32[784,1280]{1,0:T(8,128)}, f32[784,1280]{1,0:T(8,128)})) %all-reduce.11.cloned.1.call-update) | async-done | bytes 8028176 | tf_op jit(solution)/shard_map/psum | solution.py:212
  440.8 5.6 fusion.217
  449.7 55.3 %all-gather.6.cloned.1.call-done = bf16[1280,1280]{1,0:T(8,128)(2,1)} async-done(((bf16[160,1280]{1,0:T(8,128)(2,1)}), bf16[1280,1280]{1,0:T(8,128)(2,1)}) %all-gather.6.cloned.1.call-update) | async-done | bytes 3276816 | tf_op jit(solution)/shard_map/all_gather | solution.py:194
  505.0 15.9 %multiply_convert_fusion.3 = (bf16[784,1280]{1,0:T(8,128)(2,1)S(1)}, f32[784,1280]{1,0:T(8,128)}, f32[784,1280]{1,0:T(8,128)}) fusion(f32[1280]{0:T(1024)S(1)} %dynamic_slice.7, bf16[1280,1280]{1,0:T(8,128)(2,1)} %all-gather.6.cloned.1.call-done, f32[784,1280]{1,0:T(8,128)} %copy-done.5, f32[1280]{0:T(1024)S(1)} %copy-done.122, f32[1280]{0:T(1024)S(1)} %copy-done.107, ...), kind=kOutput, calls=%fused_computation.102 | convolution fusion | flops 2640261120 | bytes 17347712 | tf_op jit(solution)/shard_map/dot_general | solution.py:215
  520.9 46.6 %all-gather.8.cloned.1.call-done = bf16[1280,1280]{0,1:T(8,128)(2,1)} async-done(((bf16[1280,160]{0,1:T(8,128)(2,1)}), bf16[1280,1280]{0,1:T(8,128)(2,1)}) %all-gather.8.cloned.1.call-update) | async-done | bytes 3276816 | tf_op jit(solution)/shard_map/all_gather | solution.py:195
  567.5 9.4 convert_reduce_fusion.7
  582.2 12.4 multiply_convert_fusion.1
  594.6 4.8 convert_reduce_fusion.6
  605.5 6.3 convolution_convert_fusion.3
  615.8 70.6 %all-reduce.15.cloned.1.call-done = (bf16[784,1280]{1,0:T(8,128)(2,1)}, bf16[784,1280]{1,0:T(8,128)(2,1)}) async-done(((bf16[784,1280]{1,0:T(8,128)(2,1)}, bf16[784,1280]{1,0:T(8,128)(2,1)}), (bf16[784,1280]{1,0:T(8,128)(2,1)}, bf16[784,1280]{1,0:T(8,128)(2,1)})) %all-reduce.15.cloned.1.call-update) | async-done | bytes 4014096 | tf_op jit(solution)/shard_map/psum | solution.py:238
  686.4 6.9 fusion.36
  748.3 16.4 %reshape.327 = f32[4,4,14,14,14,14]{5,4,3,2,1,0:T(8,128)} reshape(f32[4,4,196,196]{3,2,1,0:T(8,128)} %copy.160) | data formatting | bytes 4917248 | tf_op jit(solution)/shard_map/convert_element_type | solution.py:120
  764.7 15.0 %reshape.326 = f32[4,4,14,14,14,14]{5,4,3,2,1,0:T(8,128)} reshape(f32[4,4,196,196]{3,2,1,0:T(8,128)S(1)} %copy-done.42) | data formatting | bytes 4917248 | tf_op jit(solution)/shard_map/convert_element_type | solution.py:120
  779.7 24.3 %fusion.210 = (f32[4,4,14,14,14]{4,3,2,1,0:T(8,128)}, f32[4,4,14,14,14]{4,3,2,1,0:T(8,128)}, f32[4,4,14,14,14]{4,3,2,1,0:T(8,128)}, f32[4,4,14,14,14]{4,3,2,1,0:T(8,128)}) fusion(f32[4,4,14,14,14,14]{5,4,3,2,1,0:T(8,128)} %reshape.326, f32[4,4,14,14,14,14]{5,4,3,2,1,0:T(8,128)} %reshape.327), kind=kLoop, calls=%fused_computation.343 | loop fusion | flops 2283008 | bytes 5619712 | tf_op jit(solution)/shard_map/reduce_sum | solution.py:120
  824.8 4.7 fusion.230
  860.1 6.8 bitcast_convert_fusion
  871.3 6.2 fusion.198
  877.6 5.7 fusion.1
  883.4 6.6 fusion.209
  890.1 5.7 fusion
  896.1 5.3 fusion.134
  906.1 7.9 copy.209
  914.0 8.4 reshape.344
  940.1 79.9 %all-reduce.13.cloned.1.call-done = (bf16[784,1280]{1,0:T(8,128)(2,1)}, bf16[784,1280]{1,0:T(8,128)(2,1)}, bf16[784,1280]{1,0:T(8,128)(2,1)}, bf16[784,1280]{1,0:T(8,128)(2,1)}) async-done(((bf16[784,1280]{1,0:T(8,128)(2,1)}, bf16[784,1280]{1,0:T(8,128)(2,1)}, bf16[784,1280]{1,0:T(8,128)(2,1)}, bf16[784,1280]{1,0:T(8,128)(2,1)}), (bf16[784,1280]{1,0:T(8,128)(2,1)}, bf16[784,1280]{1,0:T(8,128)(2,1)}, ...) | async-done | bytes 8028176 | tf_op jit(solution)/shard_map/psum | solution.py:220
  1020.0 6.7 fusion.29
  1028.0 11.4 multiply_convert_fusion.2
  1055.9 44.2 %reduce-scatter.11.cloned.1.call-done = bf16[1280,160]{0,1:T(8,128)(2,1)} async-done(((bf16[1280,1280]{0,1:T(8,128)(2,1)}), bf16[1280,160]{0,1:T(8,128)(2,1)}) %reduce-scatter.11.cloned.1.call-update) | async-done | bytes 409616 | tf_op jit(solution)/shard_map/reduce_scatter | solution.py:283
  1102.0 76.7 %reduce-scatter.9.cloned.1.call-done = bf16[160,1280]{1,0:T(8,128)(2,1)} async-done(((bf16[1280,1280]{1,0:T(8,128)(2,1)}), bf16[160,1280]{1,0:T(8,128)(2,1)}) %reduce-scatter.9.cloned.1.call-update) | async-done | bytes 409616 | tf_op jit(solution)/shard_map/reduce_scatter | solution.py:280
  1180.7 71.1 %reduce-scatter.13.cloned.1.call-done = bf16[160,960]{1,0:T(8,128)(2,1)} async-done(((bf16[1280,960]{1,0:T(8,128)(2,1)}), bf16[160,960]{1,0:T(8,128)(2,1)}) %reduce-scatter.13.cloned.1.call-update) | async-done | bytes 307216
  1254.8 131.1 %all-reduce.9.cloned.1.call-done = (f32[1280]{0:T(1024)}, f32[1280]{0:T(1024)}, f32[2,1280]{1,0:T(2,128)}, f32[1280]{0:T(1024)}, f32[1280]{0:T(1024)}, /*index=5...) async-done(((f32[1280]{0:T(1024)}, f32[1280]{0:T(1024)}, f32[2,1280]{1,0:T(2,128)}, f32[1280]{0:T(1024)}, f32[1280]{0:T(1024)}, ...) | async-done | bytes 78736 | tf_op jit(solution)/shard_map/psum | solution.py:296
  (449 shorter events, 266.4 us)
Async XLA Ops:
  7.2 70.9 %all-gather.4.cloned.1.call-start = ((), (), s32[]{:S(2)}) async-start(), calls=%async_computation.4 | async-start | bytes 3317760 | tf_op jit(solution)/shard_map/all_gather | solution.py:192
  7.9 432.8 %all-reduce.11.cloned.1.call-start = ((), (), s32[]{:S(2)}) async-start(), calls=%async_computation.12 | async-start | bytes 16056320 | tf_op jit(solution)/shard_map/psum | solution.py:212
  8.9 275.5 %copy-start.112 = (f32[4,80]{1,0:T(4,128)}, f32[4,80]{1,0:T(4,128)S(1)}, u32[]{:S(2)}) copy-start(f32[4,80]{1,0:T(4,128)S(1)} %add.432) | copy-start | bytes 3844
  9.0 270.3 %copy-start.88 = (f32[4,80]{1,0:T(4,128)}, f32[4,80]{1,0:T(4,128)S(1)}, u32[]{:S(2)}) copy-start(f32[4,80]{1,0:T(4,128)S(1)} %add.435) | copy-start | bytes 3844
  10.5 67.5 %copy-start.85 = (f32[784]{0:T(1024)}, f32[784]{0:T(1024)S(1)}, u32[]{:S(2)}) copy-start(f32[784]{0:T(1024)S(1)} %mul.418) | copy-start | bytes 9412
  10.6 77.9 %copy-start.83 = (f32[784]{0:T(1024)}, f32[784]{0:T(1024)S(1)}, u32[]{:S(2)}) copy-start(f32[784]{0:T(1024)S(1)} %mul.398) | copy-start | bytes 9412
  11.0 108.6 %copy-start.63 = (f32[14,14,80,1,1]{2,1,4,3,0:T(8,128)}, f32[14,14,80,1,1]{2,1,4,3,0:T(8,128)S(1)}, u32[]{:S(2)}) copy-start(f32[14,14,80,1,1]{2,1,4,3,0:T(8,128)S(1)} %convolution_bitcast_fusion.10) | copy-start | bytes 188164
  12.2 115.1 %copy-start.60 = (f32[14,14,80,1,1]{2,1,4,3,0:T(8,128)}, f32[14,14,80,1,1]{2,1,4,3,0:T(8,128)S(1)}, u32[]{:S(2)}) copy-start(f32[14,14,80,1,1]{2,1,4,3,0:T(8,128)S(1)} %convolution_bitcast_fusion.11) | copy-start | bytes 188164
  12.3 65.8 %copy-start.76 = (f32[1280]{0:T(1024)S(1)}, f32[1280]{0:T(1024)}, u32[]{:S(2)}) copy-start(f32[1280]{0:T(1024)} %param.21) | copy-start | bytes 15364
  12.3 65.8 %copy-start.124 = (f32[1280]{0:T(1024)S(1)}, f32[1280]{0:T(1024)}, u32[]{:S(2)}) copy-start(f32[1280]{0:T(1024)} %param.22) | copy-start | bytes 15364
  15.1 73.4 %copy-start.79 = (f32[784]{0:T(1024)}, f32[784]{0:T(1024)S(1)}, u32[]{:S(2)}) copy-start(f32[784]{0:T(1024)S(1)} %broadcast_multiply_fusion.3) | copy-start | bytes 9412
  15.2 68.6 %copy-start.81 = (f32[784]{0:T(1024)}, f32[784]{0:T(1024)S(1)}, u32[]{:S(2)}) copy-start(f32[784]{0:T(1024)S(1)} %broadcast_multiply_fusion.1) | copy-start | bytes 9412
  16.4 67.4 %copy-start.95 = (f32[784]{0:T(1024)}, f32[784]{0:T(1024)S(1)}, u32[]{:S(2)}) copy-start(f32[784]{0:T(1024)S(1)} %get-tuple-element.83) | copy-start | bytes 9412
  16.4 67.4 %copy-start.97 = (f32[784]{0:T(1024)}, f32[784]{0:T(1024)S(1)}, u32[]{:S(2)}) copy-start(f32[784]{0:T(1024)S(1)} %get-tuple-element.82) | copy-start | bytes 9412
  16.4 72.1 %copy-start.99 = (f32[784]{0:T(1024)}, f32[784]{0:T(1024)S(1)}, u32[]{:S(2)}) copy-start(f32[784]{0:T(1024)S(1)} %fusion.178) | copy-start | bytes 9412
  16.4 67.4 %copy-start.101 = (f32[784]{0:T(1024)}, f32[784]{0:T(1024)S(1)}, u32[]{:S(2)}) copy-start(f32[784]{0:T(1024)S(1)} %fusion.180) | copy-start | bytes 9412
  104.1 23.2 %copy-start.31 = (bf16[4,14,14,4,80]{4,3,2,1,0:T(4,128)(2,1)}, bf16[4,14,14,4,80]{4,3,2,1,0:T(4,128)(2,1)S(1)}, u32[]{:S(2)}) copy-start(bf16[4,14,14,4,80]{4,3,2,1,0:T(4,128)(2,1)S(1)} %get-tuple-element.150) | copy-start | bytes 1505284
  104.1 23.2 %copy-start.33 = (bf16[4,14,14,4,80]{4,3,2,1,0:T(4,128)(2,1)}, bf16[4,14,14,4,80]{4,3,2,1,0:T(4,128)(2,1)S(1)}, u32[]{:S(2)}) copy-start(bf16[4,14,14,4,80]{4,3,2,1,0:T(4,128)(2,1)S(1)} %get-tuple-element.149) | copy-start | bytes 1505284
  119.6 17.4 %copy-start.55 = (f32[1,784,320]{1,2,0:T(8,128)S(1)}, f32[1,784,320]{1,2,0:T(8,128)}, u32[]{:S(2)}) copy-start(f32[1,784,320]{1,2,0:T(8,128)} %get-tuple-element.132) | copy-start | bytes 3010564
  293.1 147.7 %copy-start.114 = (f32[1280]{0:T(1024)S(1)}, f32[1280]{0:T(1024)}, u32[]{:S(2)}) copy-start(f32[1280]{0:T(1024)} %param.26) | copy-start | bytes 15364
  293.1 211.8 %all-gather.6.cloned.1.call-start = ((), (), s32[]{:S(2)}) async-start(), calls=%async_computation.5 | async-start | bytes 3686400 | tf_op jit(solution)/shard_map/all_gather | solution.py:194
  293.9 273.6 %all-gather.8.cloned.1.call-start = ((), (), s32[]{:S(2)}) async-start(), calls=%async_computation.6 | async-start | bytes 3686400 | tf_op jit(solution)/shard_map/all_gather | solution.py:195
  294.4 392.0 %all-reduce.15.cloned.1.call-start = ((), (), s32[]{:S(2)}) async-start(), calls=%async_computation.14 | async-start | bytes 8028160 | tf_op jit(solution)/shard_map/psum | solution.py:238
  446.4 58.5 %copy-start.107 = (f32[1280]{0:T(1024)S(1)}, f32[1280]{0:T(1024)}, u32[]{:S(2)}) copy-start(f32[1280]{0:T(1024)} %param.27) | copy-start | bytes 15364
  446.5 58.5 %copy-start.122 = (f32[1280]{0:T(1024)S(1)}, f32[1280]{0:T(1024)}, u32[]{:S(2)}) copy-start(f32[1280]{0:T(1024)} %param.28) | copy-start | bytes 15364
  449.7 117.8 %copy-start.84 = (f32[784]{0:T(1024)S(1)}, f32[784]{0:T(1024)}, u32[]{:S(2)}) copy-start(f32[784]{0:T(1024)} %copy-done.83) | copy-start | bytes 9412
  520.9 84.6 %copy-start.127 = (bf16[784,1280]{1,0:T(8,128)(2,1)}, bf16[784,1280]{1,0:T(8,128)(2,1)S(1)}, u32[]{:S(2)}) copy-start(bf16[784,1280]{1,0:T(8,128)(2,1)S(1)} %get-tuple-element.120) | copy-start | bytes 6021124
  567.5 10.7 copy-start.120
  582.2 12.4 copy-start.19
  582.2 12.4 copy-start.86
  582.2 12.4 copy-start.118
  604.8 333.7 %reduce-scatter.7.cloned.1.call-start = ((), (), s32[]{:S(2)}) async-start(), calls=%async_computation.7 | async-start | bytes 1105920 | tf_op jit(solution)/shard_map/reduce_scatter | solution.py:277
  746.4 273.5 %all-reduce.13.cloned.1.call-start = ((), (), s32[]{:S(2)}) async-start(), calls=%async_computation.13 | async-start | bytes 16056320 | tf_op jit(solution)/shard_map/psum | solution.py:220
  748.3 16.5 %copy-start.42 = (f32[4,4,196,196]{3,2,1,0:T(8,128)S(1)}, f32[4,4,196,196]{3,2,1,0:T(8,128)}, u32[]{:S(2)}) copy-start(f32[4,4,196,196]{3,2,1,0:T(8,128)} %copy.145) | copy-start | bytes 7375876
  779.7 27.1 %copy-start.64 = (f32[14,14,80,1,1]{2,1,4,3,0:T(8,128)S(1)}, f32[14,14,80,1,1]{2,1,4,3,0:T(8,128)}, u32[]{:S(2)}) copy-start(f32[14,14,80,1,1]{2,1,4,3,0:T(8,128)} %copy-done.63) | copy-start | bytes 188164
  838.6 12.1 copy-start.66
  871.3 228.8 %reduce-scatter.11.cloned.1.call-start = ((), (), s32[]{:S(2)}) async-start(), calls=%async_computation.9 | async-start | bytes 3686400 | tf_op jit(solution)/shard_map/reduce_scatter | solution.py:283
  883.3 295.5 %reduce-scatter.9.cloned.1.call-start = ((), (), s32[]{:S(2)}) async-start(), calls=%async_computation.8 | async-start | bytes 3686400 | tf_op jit(solution)/shard_map/reduce_scatter | solution.py:280
  895.8 356.0 %reduce-scatter.13.cloned.1.call-start = ((), (), s32[]{:S(2)}) async-start(), calls=%async_computation.10 | async-start | bytes 2949120
  914.0 11.7 copy-start.34
  922.3 9.9 copy-start.32
  925.6 8.6 copy-start.94
  937.7 448.1 %all-reduce.9.cloned.1.call-start = ((), (), s32[]{:S(2)}) async-start(), calls=%async_computation.11 | async-start | bytes 225280 | tf_op jit(solution)/shard_map/psum | solution.py:296
  1028.0 13.2 copy-start.22
  1028.0 13.2 copy-start.26
  1028.0 13.2 copy-start.36
  1028.0 13.2 copy-start.106
  1051.5 347.5 %copy-start.1 = (f32[27,80]{1,0:T(8,128)S(1)}, f32[27,80]{1,0:T(8,128)}, u32[]{:S(2)}) copy-start(f32[27,80]{1,0:T(8,128)} %param.34) | copy-start | bytes 25924
  (95 other events, 447.0 us)
Sparse Core Ops, SparseCore 0:
  10.2 67.7 all-gather.3
  293.3 147.4 all-reduce.10
  443.0 61.9 all-gather.5
  507.0 60.4 all-gather.7
  604.9 81.4 all-reduce.14
  746.5 63.4 reduce-scatter.6
  871.4 148.4 all-reduce.12
  1024.0 76.0 reduce-scatter.10
  1103.7 75.0 reduce-scatter.8
  1182.5 69.2 reduce-scatter.12
  1260.6 125.2 all-reduce.8
where the time goes:
time: 1410 us
  waiting for transfers between devices  747 us (53%)
  local copies, waits for them, and re-layouts  289 us (20%)
  matrix products  219 us (16%)
  other arithmetic  97.7 us (7%)
  blocking collectives  38.1 us (3%)
  between operations  15.8 us (1%)
    psum x1, waiting for transfers between devices, body(): after = rows_in + lax.psum(attn_partial, 'mp') + proj_bias  145 us
    psum x1, waiting for transfers between devices, body(): lax.psum((gain_one_acc * feature_mask, shift_one_acc * feature_mask, qv_f...  131 us
    add x12, local copies, waits for them, and re-layouts, scores_of(): scores.reshape(windows, heads, WIN, WIN, WIN, WIN)  110 us
    psum x1, waiting for transfers between devices, body(): lax.psum(mlp_partial.astype(jnp.bfloat16), 'mp').astype(jnp.float32)  79.9 us
    reduce_scatter x1, waiting for transfers between devices, body(): lax.psum_scatter(up_acc.astype(jnp.bfloat16), 'dp', scatter_dimension=0,...  76.7 us
    unnamed x12, waiting for transfers between devices  73.2 us
    psum x1, waiting for transfers between devices, body(): lax.psum(norm_two_partial.astype(jnp.bfloat16), 'mp').astype(jnp.float32)  70.6 us
    all_gather x1, waiting for transfers between devices, body(): lax.all_gather(up_weight, 'dp', axis=0, tiled=True)  55.3 us
  transfers between devices with their start and end apart: 11, of which 10 were waited for; matrix products, arithmetic and copies ran while one was open for 20% of the time, Pallas kernels for 0%

commit v1 on v0

v1 whole, which is shorter than its diff:
```python
from functools import partial

import jax
import jax.numpy as jnp
import numpy as np
from jax import lax
from jax.experimental import pallas as pl
from jax.experimental.pallas import tpu as pltpu
from jax.sharding import PartitionSpec as P

HD = 80
WIN = 14
SIDE = 64
GRID = 5
WTOK = 196
RELN = 27
ROWS = 208
SCALE = HD ** (-0.5)
EPS = 1e-06
F32 = jnp.float32
BF16 = jnp.bfloat16
ANY = pl.BlockSpec(memory_space=pl.ANY)
highest = lax.Precision.HIGHEST


def dot(left, right):
    return lax.dot_general(left, right, (((1,), (0,)), ((), ())), preferred_element_type=F32)


def dot_nt(left, right):
    return lax.dot_general(left, right, (((1,), (1,)), ((), ())), preferred_element_type=F32)


def dot_tn(left, right):
    return lax.dot_general(left, right, (((0,), (0,)), ((), ())), preferred_element_type=F32)


def whole(array):
    zeros = (0,) * len(array.shape)
    return pl.BlockSpec(array.shape, lambda *_: zeros)


def params(megabytes):
    return pltpu.CompilerParams(vmem_limit_bytes=megabytes * 2**20)


def struct(shape, dtype):
    return jax.ShapeDtypeStruct(shape, dtype)


def assemble(offsets, pieces, target, sems):
    copies = []
    for index, piece in enumerate(pieces):
        count = piece.shape[0]
        start = pl.multiple_of(offsets[index], 16)
        copies.append(
            pltpu.make_async_copy(piece, target.at[pl.ds(start, count)], sems.at[index])
        )
    for copy in copies:
        copy.start()
    for copy in copies:
        copy.wait()


def norm_parts(values):
    center = jnp.mean(values, axis=-1, keepdims=True)
    centred = values - center
    spread = jnp.mean(centred * centred, axis=-1, keepdims=True)
    rstd = lax.rsqrt(spread + EPS)
    return centred * rstd, rstd


def norm_one_kernel(x_ref, valid_ref, gain_ref, shift_ref, out_ref):
    xhat, _ = norm_parts(x_ref[...].astype(F32))
    out_ref[...] = ((xhat * gain_ref[...] + shift_ref[...]) * valid_ref[...]).astype(BF16)


def norm_one(x, valid, gain, shift):
    rows, width = x.shape
    return pl.pallas_call(
        norm_one_kernel,
        grid=(rows // ROWS,),
        in_specs=[
            pl.BlockSpec((ROWS, width), lambda i: (i, 0)),
            pl.BlockSpec((ROWS, 1), lambda i: (i, 0)),
            whole(gain),
            whole(shift),
        ],
        out_specs=pl.BlockSpec((ROWS, width), lambda i: (i, 0)),
        out_shape=struct(x.shape, BF16),
        name="norm_one",
    )(x, valid, gain, shift)


def total(refs, rows):
    value = refs[0][:rows].astype(F32)
    for ref in refs[1:]:
        value = value + ref[:rows].astype(F32)
    return value


def norm_two_kernel(count, *refs):
    parts, (x_ref, bias_ref, gain_ref, shift_ref, after_ref, normed_ref) = (
        refs[:count],
        refs[count:],
    )
    rows = x_ref.shape[0]
    after = x_ref[...].astype(F32) + total(parts, rows) + bias_ref[...]
    xhat, _ = norm_parts(after)
    after_ref[...] = after
    normed_ref[...] = (xhat * gain_ref[...] + shift_ref[...]).astype(BF16)


def norm_two(parts, x, bias, gain, shift):
    return pl.pallas_call(
        partial(norm_two_kernel, len(parts)),
        out_shape=(struct(x.shape, F32), struct(x.shape, BF16)),
        compiler_params=params(32),
        name="norm_two",
    )(*parts, x, bias, gain, shift)


def finish_kernel(count, *refs):
    parts, (after_ref, valid_ref, bias_ref, out_ref) = refs[:count], refs[count:]
    rows = after_ref.shape[0]
    branch = total(parts, rows) + bias_ref[...]
    out_ref[...] = (valid_ref[...] * (after_ref[...] + branch)).astype(BF16)


def finish(parts, after, valid, bias):
    return pl.pallas_call(
        partial(finish_kernel, len(parts)),
        out_shape=struct(after.shape, BF16),
        compiler_params=params(32),
        name="finish",
    )(*parts, after, valid, bias)


def norm_back(upstream, xhat, rstd, gain):
    weighted = upstream * gain
    inner = jnp.mean(weighted * xhat, axis=-1, keepdims=True)
    level = jnp.mean(weighted, axis=-1, keepdims=True)
    return rstd * (weighted - level - xhat * inner)


def norm_two_back_kernel(count, *refs):
    parts = refs[:count]
    after_ref, top_ref, gain_ref, grad_ref, branch_ref, sums_ref = refs[count:]
    rows = after_ref.shape[0]
    upstream = total(parts, rows)
    xhat, rstd = norm_parts(after_ref[...])
    top = top_ref[...].astype(F32)
    grad = top + norm_back(upstream, xhat, rstd, gain_ref[...])
    branch = grad.astype(BF16)
    grad_ref[...] = grad
    branch_ref[...] = branch
    sums_ref[0:1] = jnp.sum(upstream * xhat, axis=0, keepdims=True)
    sums_ref[1:2] = jnp.sum(upstream, axis=0, keepdims=True)
    sums_ref[2:3] = jnp.sum(branch.astype(F32), axis=0, keepdims=True)
    sums_ref[3:4] = jnp.sum(top, axis=0, keepdims=True)


def norm_two_back(parts, after, top, gain):
    return pl.pallas_call(
        partial(norm_two_back_kernel, len(parts)),
        out_shape=(
            struct(after.shape, F32),
            struct(after.shape, BF16),
            struct((4, after.shape[1]), F32),
        ),
        compiler_params=params(40),
        name="norm_two_back",
    )(*parts, after, top, gain)


def norm_one_back_kernel(count, *refs):
    parts = refs[:count]
    x_ref, valid_ref, grad_ref, gain_ref, out_ref, sums_ref = refs[count:]
    rows = x_ref.shape[0]
    upstream = total(parts, rows) * valid_ref[...]
    xhat, rstd = norm_parts(x_ref[...].astype(F32))
    out_ref[...] = (grad_ref[...] + norm_back(upstream, xhat, rstd, gain_ref[...])).astype(BF16)
    sums_ref[0:1] = jnp.sum(upstream * xhat, axis=0, keepdims=True)
    sums_ref[1:2] = jnp.sum(upstream, axis=0, keepdims=True)


def norm_one_back(parts, x, valid, grad, gain):
    return pl.pallas_call(
        partial(norm_one_back_kernel, len(parts)),
        out_shape=(struct(x.shape, BF16), struct((2, x.shape[1]), F32)),
        compiler_params=params(40),
        name="norm_one_back",
    )(*parts, x, valid, grad, gain)


def qkv_kernel(count, cols, offsets, *refs):
    pieces = refs[:count]
    x_ref, bias_ref, q_ref, k_ref, v_ref, w_ref, buffer, sems = refs[count:]
    wide = q_ref.shape[1]

    @pl.when(pl.program_id(0) == 0)
    def _():
        assemble(offsets, pieces, buffer, sems)
        for slot in range(4):
            base = slot * wide
            w_ref[:, base : base + cols] = buffer[:, slot * cols : (slot + 1) * cols]
            if wide > cols:
                w_ref[:, base + cols : base + wide] = jnp.zeros(
                    (w_ref.shape[0], wide - cols), BF16
                )

    x = x_ref[...]
    for slot, ref in enumerate((q_ref, k_ref, v_ref)):
        span = slice(slot * wide, (slot + 1) * wide)
        ref[...] = (dot(x, w_ref[:, span]) + bias_ref[:, span]).astype(BF16)


def project(offsets, pieces, x, bias, cols, wide):
    rows, width = x.shape
    step = 2 * ROWS
    block = pl.BlockSpec((step, wide), lambda i, *_: (i, 0))
    return pl.pallas_call(
        partial(qkv_kernel, len(pieces), cols),
        grid_spec=pltpu.PrefetchScalarGridSpec(
            num_scalar_prefetch=1,
            grid=(rows // step,),
            in_specs=[ANY] * len(pieces)
            + [pl.BlockSpec((step, width), lambda i, *_: (i, 0)), whole(bias)],
            out_specs=[block, block, block, pl.BlockSpec((width, 4 * wide), lambda i, *_: (0, 0))],
            scratch_shapes=[
                pltpu.VMEM((width, 4 * cols), BF16),
                pltpu.SemaphoreType.DMA((len(pieces),)),
            ],
        ),
        out_shape=[struct((rows, wide), BF16)] * 3 + [struct((width, 4 * wide), BF16)],
        compiler_params=params(48),
        name="qkv",
    )(offsets, *pieces, x, bias)


def head_spans(heads, wide):
    spans = []
    for head in range(heads):
        first, last = head * HD, head * HD + HD
        low = first // 128 * 128
        high = min((last + 127) // 128 * 128, wide)
        spans.append((low, high, first, last))
    return spans


def lane_mask(span):
    low, high, first, last = span
    lane = lax.broadcasted_iota(jnp.int32, (1, high - low), 1) + low
    return jnp.where((lane >= first) & (lane < last), 1.0, 0.0).astype(BF16)


def shift_counts():
    token = lax.broadcasted_iota(jnp.int32, (ROWS, 128), 0)
    row = (token * 9363) >> 17
    col = token - row * WIN
    return jnp.maximum(WIN - 1 - row, 0), WIN - 1 - col


def shift_lanes(values, counts, back):
    for step in (1, 2, 4, 8):
        moved = pltpu.roll(values, step if back else 128 - step, 1)
        values = jnp.where((counts & step) != 0, moved, values)
    return values


def lane_kind():
    lane = lax.broadcasted_iota(jnp.int32, (ROWS, 128), 1) & 31
    return lane < WIN, (lane >= 16) & (lane < 16 + WIN), lane == 31


def split_two(values):
    high = values.astype(BF16)
    return high, (values - high.astype(F32)).astype(BF16)


def bias_operand(q, rel_high, rel_low, counts):
    table = dot(q, rel_high) + dot(q, rel_low)
    by_row = shift_lanes(table[:, :128], counts[0], False)
    by_col = shift_lanes(table[:, 128:], counts[1], False)
    is_row, is_col, is_last = lane_kind()
    packed = jnp.where(
        is_row, by_row, jnp.where(is_col, by_col, jnp.where(is_last, 1.0, 0.0))
    )
    high, low = split_two(packed)
    return jnp.concatenate([high, low], axis=1)


def add_lanes(parts, values, span):
    low, high = span[0], span[1]
    for index in range(low // 128, high // 128):
        piece = values[:, index * 128 - low : index * 128 - low + 128]
        parts[index] = piece if parts[index] is None else parts[index] + piece


def attend_kernel(heads, split, q_ref, k_ref, v_ref, rh_ref, rl_ref, mark_ref, w_ref, *outs):
    mixed_ref, log_ref = outs[:2]
    q, k, v = q_ref[...], k_ref[...], v_ref[...]
    wide = q.shape[1]
    bias = bias_operand(q, rh_ref[...], rl_ref[...], shift_counts())
    lane = lax.broadcasted_iota(jnp.int32, (ROWS, 128), 1)
    logs = jnp.zeros((ROWS, 128), F32)
    parts = [None] * (wide // 128)
    for head, span in enumerate(head_spans(heads, wide)):
        mask = lane_mask(span)
        cut = slice(span[0], span[1])
        scores = SCALE * dot_nt(q[:, cut], k[:, cut] * mask) + dot_nt(bias, mark_ref[head])
        top = jnp.max(scores, axis=-1, keepdims=True)
        shifted = jnp.exp(scores - top)
        norm = jnp.sum(shifted, axis=-1, keepdims=True)
        shares = (shifted * (1.0 / norm)).astype(BF16)
        logs = jnp.where(lane == head, top + jnp.log(norm), logs)
        add_lanes(parts, dot(shares, v[:, cut] * mask), span)
    mixed = jnp.concatenate(parts, axis=1).astype(BF16)
    mixed_ref[...] = mixed
    log_ref[...] = logs
    branch = dot_nt(mixed, w_ref[...]).astype(BF16)
    if split:
        keep_ref, send_ref = outs[2:]
        step = pl.program_id(0)

        @pl.when(step < split)
        def _():
            send_ref[...] = branch

        @pl.when(step >= split)
        def _():
            keep_ref[...] = branch
    else:
        outs[2][...] = branch


def split_specs(windows, split, width):
    rows = ROWS * (windows - split)
    if not split:
        return [pl.BlockSpec((ROWS, width), lambda i: (i, 0))], [struct((rows, width), BF16)]
    return (
        [
            pl.BlockSpec((ROWS, width), lambda i: (jnp.maximum(i - split, 0), 0)),
            pl.BlockSpec((ROWS, width), lambda i: (jnp.minimum(i, split - 1), 0)),
        ],
        [struct((rows, width), BF16), struct((ROWS * split, width), BF16)],
    )


def attend(heads, part, windows, split, q, k, v, rel_high, rel_low, marks, weights):
    wide = q.shape[1]
    width = weights.shape[0]

    def place(i):
        return (i + split) % windows if split else i

    block = pl.BlockSpec((ROWS, wide), lambda i: (part * windows + place(i), 0))
    specs, shapes = split_specs(windows, split, width)
    return pl.pallas_call(
        partial(attend_kernel, heads, split),
        grid=(windows,),
        in_specs=[
            block,
            block,
            block,
            whole(rel_high),
            whole(rel_low),
            whole(marks),
            pl.BlockSpec((width, wide), lambda i: (0, 3)),
        ],
        out_specs=[
            pl.BlockSpec((ROWS, wide), lambda i: (place(i), 0)),
            pl.BlockSpec((ROWS, 128), lambda i: (place(i), 0)),
        ]
        + specs,
        out_shape=[
            struct((windows * ROWS, wide), BF16),
            struct((windows * ROWS, 128), F32),
        ]
        + shapes,
        compiler_params=params(40),
        name="attend",
    )(q, k, v, rel_high, rel_low, marks, weights)


def attend_back_kernel(heads, windows, split, count, *refs):
    pieces = refs[:count]
    q_ref, k_ref, v_ref, log_ref, rh_ref, rl_ref, mark_ref, w_ref = refs[count : count + 8]
    grads_ref, branch_ref, rel_ref, sum_ref = refs[count + 8 : count + 12]
    outs = refs[count + 12 :]
    step = pl.program_id(0)

    @pl.when(step == 0)
    def _():
        start = 0
        for piece in pieces:
            branch_ref[start : start + piece.shape[0]] = piece[...]
            start += piece.shape[0]
        rel_ref[...] = jnp.zeros(rel_ref.shape, F32)
        sum_ref[...] = jnp.zeros(sum_ref.shape, F32)

    place = lax.rem(step + split, windows) if split else step
    q, k, v = q_ref[...], k_ref[...], v_ref[...]
    wide = q.shape[1]
    top = branch_ref[pl.ds(pl.multiple_of(place * ROWS, 16), ROWS), :]
    grad_mixed = dot(top, w_ref[:, 3 * wide :]).astype(BF16)
    rel_high, rel_low = rh_ref[...], rl_ref[...]
    counts = shift_counts()
    bias = bias_operand(q, rel_high, rel_low, counts)
    grad_q, grad_k, grad_v = ([None] * (wide // 128) for _ in range(3))
    grad_bias = None
    for head, span in enumerate(head_spans(heads, wide)):
        mask = lane_mask(span)
        cut = slice(span[0], span[1])
        key = k[:, cut] * mask
        query = q[:, cut]
        upper = grad_mixed[:, cut]
        mark = mark_ref[head]
        scores = SCALE * dot_nt(query, key) + dot_nt(bias, mark)
        shares = jnp.exp(scores - log_ref[:, head : head + 1])
        grad_shares = dot_nt(upper, v[:, cut] * mask)
        inner = jnp.sum(shares * grad_shares, axis=-1, keepdims=True)
        grad_scores = (shares * (grad_shares - inner)).astype(BF16)
        add_lanes(grad_v, dot_tn(shares.astype(BF16), upper * mask), span)
        add_lanes(grad_q, dot(grad_scores, key), span)
        add_lanes(grad_k, dot_tn(grad_scores, query * mask), span)
        part = dot(grad_scores, mark[:, :128])
        grad_bias = part if grad_bias is None else grad_bias + part
    is_row, is_col, _ = lane_kind()
    by_row = shift_lanes(jnp.where(is_row, grad_bias, 0.0), counts[0], True)
    by_col = shift_lanes(jnp.where(is_col, grad_bias, 0.0), counts[1], True)
    high, low = split_two(jnp.concatenate([by_row, by_col], axis=1))
    extra = dot_nt(high, rel_high) + dot_nt(low, rel_high) + dot_nt(high, rel_low)
    extra = extra + dot_nt(low, rel_low)
    rel_ref[...] += dot_tn(high, q) + dot_tn(low, q)
    grad_q = (SCALE * jnp.concatenate(grad_q, axis=1) + extra).astype(BF16)
    grad_k = (SCALE * jnp.concatenate(grad_k, axis=1)).astype(BF16)
    grad_v = jnp.concatenate(grad_v, axis=1).astype(BF16)
    partial_sum = None
    for slot, grad in enumerate((grad_q, grad_k, grad_v)):
        cut = slice(slot * wide, (slot + 1) * wide)
        grads_ref[:, cut] = grad
        sum_ref[:, cut] += jnp.sum(grad.astype(F32), axis=0, keepdims=True)
        term = dot_nt(grad, w_ref[:, cut])
        partial_sum = term if partial_sum is None else partial_sum + term
    result = partial_sum.astype(BF16)
    if split:
        keep_ref, send_ref = outs

        @pl.when(step < split)
        def _():
            send_ref[...] = result

        @pl.when(step >= split)
        def _():
            keep_ref[...] = result
    else:
        outs[0][...] = result


def attend_back(
    heads, part, windows, split, pieces, q, k, v, logs, rel_high, rel_low, marks, weights
):
    wide = q.shape[1]
    width = weights.shape[0]

    def place(i):
        return (i + split) % windows if split else i

    block = pl.BlockSpec((ROWS, wide), lambda i: (part * windows + place(i), 0))
    specs, shapes = split_specs(windows, split, width)
    rows = windows * ROWS
    branch = struct((rows, width), BF16)
    rel = struct((256, wide), F32)
    sums = struct((1, 3 * wide), F32)
    return pl.pallas_call(
        partial(attend_back_kernel, heads, windows, split, len(pieces)),
        grid=(windows,),
        in_specs=[whole(piece) for piece in pieces]
        + [
            block,
            block,
            block,
            pl.BlockSpec((ROWS, 128), lambda i: (place(i), 0)),
            whole(rel_high),
            whole(rel_low),
            whole(marks),
            whole(weights),
        ],
        out_specs=[
            pl.BlockSpec((ROWS, 3 * wide), lambda i: (place(i), 0)),
            whole(branch),
            whole(rel),
            whole(sums),
        ]
        + specs,
        out_shape=[struct((rows, 3 * wide), BF16), branch, rel, sums] + shapes,
        compiler_params=params(56),
        name="attend_back",
    )(*pieces, q, k, v, logs, rel_high, rel_low, marks, weights)


def mlp_kernel(count, weights, chunk, offsets, *refs):
    pieces = refs[:count]
    up_pieces = refs[count : count + weights]
    down_pieces = refs[count + weights : count + 2 * weights]
    refs = refs[count + 2 * weights :]
    top_ref, bias_ref, active_ref, hidden_ref, normed_ref, sum_ref = refs[:6]
    back_ref, out_ref, up, down, sems = refs[6:]
    step = pl.program_id(0)
    block = top_ref.shape[0]

    @pl.when(step == 0)
    def _():
        start = 0
        for piece in pieces:
            normed_ref[start : start + piece.shape[0]] = piece[...]
            start += piece.shape[0]
        sum_ref[...] = jnp.zeros(sum_ref.shape, F32)
        assemble(offsets, up_pieces, up, sems.at[0])
        assemble(offsets, down_pieces, down, sems.at[1])

    normed = normed_ref[pl.ds(pl.multiple_of(step * block, 16), block), :]
    top = top_ref[...]
    units = up.shape[1]
    width = up.shape[0]

    def first(index, carry):
        cut = pl.ds(pl.multiple_of(index * chunk, 128), chunk)
        hidden = dot(normed, up[:, cut]) + bias_ref[:, cut]
        half = 0.5 * (1.0 + lax.erf(hidden * (0.5**0.5)))
        slope = half + hidden * jnp.exp(-0.5 * hidden * hidden) * float((2.0 * np.pi) ** -0.5)
        active_ref[:, cut] = (hidden * half).astype(BF16)
        grad = (dot(top, down[:, cut]) * slope).astype(BF16)
        hidden_ref[:, cut] = grad
        sum_ref[:, cut] += jnp.sum(grad.astype(F32), axis=0, keepdims=True)
        return carry

    lax.fori_loop(0, units // chunk, first, 0)
    grad_hidden = hidden_ref[...]
    active = active_ref[...]

    def second(index, carry):
        cut = pl.ds(pl.multiple_of(index * 256, 128), 256)
        back_ref[:, cut] = dot_nt(grad_hidden, up[cut, :]).astype(BF16)
        out_ref[:, cut] = dot_nt(active, down[cut, :]).astype(BF16)
        return carry

    lax.fori_loop(0, width // 256, second, 0)


def mlp(offsets, pieces, up_pieces, down_pieces, top, part, bias):
    rows = sum(piece.shape[0] for piece in pieces)
    width = pieces[0].shape[1]
    units = up_pieces[0].shape[1]
    block = 2 * ROWS
    blocks = rows // block
    chunk = 256 if units % 256 == 0 else 128
    normed = struct((rows, width), BF16)
    sums = struct((1, units), F32)
    wide = pl.BlockSpec((block, units), lambda i, *_: (i, 0))
    narrow = pl.BlockSpec((block, width), lambda i, *_: (i, 0))
    return pl.pallas_call(
        partial(mlp_kernel, len(pieces), len(up_pieces), chunk),
        grid_spec=pltpu.PrefetchScalarGridSpec(
            num_scalar_prefetch=1,
            grid=(blocks,),
            in_specs=[whole(piece) for piece in pieces]
            + [ANY] * (2 * len(up_pieces))
            + [pl.BlockSpec((block, width), lambda i, *_: (part * blocks + i, 0)), whole(bias)],
            out_specs=[wide, wide, whole(normed), whole(sums), narrow, narrow],
            scratch_shapes=[
                pltpu.VMEM((width, units), BF16),
                pltpu.VMEM((width, units), BF16),
                pltpu.SemaphoreType.DMA((2, len(up_pieces))),
            ],
        ),
        out_shape=[struct((rows, units), BF16)] * 2
        + [normed, sums]
        + [struct((rows, width), BF16)] * 2,
        compiler_params=params(56),
        name="mlp",
    )(offsets, *pieces, *up_pieces, *down_pieces, top, bias)


def weight_grad_kernel(groups, cols, chunk, starts, *refs):
    count = sum(2 * len(group) for group in groups)
    operands = refs[:count]
    outs = refs[count:-2]
    result, sems = refs[-2:]
    width = result.shape[0]

    def loop(index, carry):
        rows = pl.ds(pl.multiple_of(index * chunk, 128), chunk)
        at = 0
        for slot, group in enumerate(groups):
            for member, (low, high) in enumerate(group):
                left, right = operands[at], operands[at + 1]
                at += 2
                term = dot_tn(left[:, rows], right[:, low:high])
                value = term if member == 0 else value + term
            result[rows, slot * cols : (slot + 1) * cols] = value[:, :cols].astype(BF16)
        return carry

    lax.fori_loop(0, width // chunk, loop, 0)
    copies = []
    for out in outs:
        for index in range(out.shape[0]):
            size = out.shape[1]
            start = pl.multiple_of(starts[len(copies)], 16)
            copies.append(
                pltpu.make_async_copy(
                    result.at[pl.ds(start, size)], out.at[index], sems.at[len(copies)]
                )
            )
    for copy in copies:
        copy.start()
    for copy in copies:
        copy.wait()


def weight_grad(starts, groups, cols, shapes):
    operands = []
    for group in groups:
        for left, right, _, _ in group:
            operands += [left, right]
    spans = [[(low, high) for _, _, low, high in group] for group in groups]
    width = operands[0].shape[1]
    count = sum(shape[0] for shape in shapes)
    return pl.pallas_call(
        partial(weight_grad_kernel, spans, cols, 256),
        grid_spec=pltpu.PrefetchScalarGridSpec(
            num_scalar_prefetch=1,
            grid=(1,),
            in_specs=[whole(operand) for operand in operands],
            out_specs=[ANY] * len(shapes),
            scratch_shapes=[
                pltpu.VMEM((width, cols * len(groups)), BF16),
                pltpu.SemaphoreType.DMA((count,)),
            ],
        ),
        out_shape=[struct(shape, BF16) for shape in shapes],
        compiler_params=params(56),
        name="weight_grad",
    )(starts, *operands)


def place_kernel(count, order, *refs):
    pieces, out_ref, buffer = refs[:count], refs[count], refs[count + 1]
    for me in range(4):

        @pl.when(order[0] == me)
        def _(me=me):
            for index in range(count):
                step = (0, 2, 1, 3)[index % 4]
                start = (index // 4 * 4 + (me ^ step)) * WTOK
                buffer[start : start + WTOK] = pieces[index][:WTOK].astype(F32)

    out_ref[...] = buffer[...].astype(out_ref.dtype)


def place_windows(order, pieces, dtype):
    width = pieces[0].shape[1]
    shape = (len(pieces) * WTOK, width)
    return pl.pallas_call(
        partial(place_kernel, len(pieces)),
        grid_spec=pltpu.PrefetchScalarGridSpec(
            num_scalar_prefetch=1,
            grid=(1,),
            in_specs=[whole(piece) for piece in pieces],
            out_specs=pl.BlockSpec(shape, lambda *_: (0, 0)),
            scratch_shapes=[pltpu.VMEM(shape, F32)],
        ),
        out_shape=struct(shape, dtype),
        compiler_params=params(56),
        name="place_windows",
    )(order, *pieces)


def token_valid(window_place, slot_live):
    position = jnp.arange(WTOK, dtype=jnp.int32)
    inner_row = position // WIN
    inner_col = position % WIN
    grid_row = (window_place // GRID)[:, None]
    grid_col = (window_place % GRID)[:, None]
    inside = (
        (grid_row * WIN + inner_row[None, :] < SIDE)
        & (grid_col * WIN + inner_col[None, :] < SIDE)
        & (slot_live[:, None] == 1)
    )
    return jnp.where(inside, 1.0, 0.0).astype(F32)


def key_marks(heads):
    marks = np.zeros((heads, ROWS, 256), np.float32)
    for head in range(heads):
        for token in range(WTOK):
            for half in (0, 128):
                marks[head, token, half + head * 32 + token // WIN] = 1.0
                marks[head, token, half + head * 32 + 16 + token % WIN] = 1.0
        marks[head, WTOK:, head * 32 + 31] = -1e30
    return marks.astype(BF16)


def rel_operand(rel_height, rel_width, heads, wide):
    lanes = jnp.zeros((wide, 256), F32)
    high = rel_height[::-1].T
    flat = rel_width[::-1].T
    for head in range(heads):
        rows = slice(head * HD, head * HD + HD)
        lanes = lanes.at[rows, head * 32 : head * 32 + RELN].set(high)
        first = head * 32 + 16
        fit = min(RELN, 128 - first)
        lanes = lanes.at[rows, 128 + first : 128 + first + fit].set(flat[:, :fit])
        if fit < RELN:
            lanes = lanes.at[rows, 128 : 128 + RELN - fit].set(flat[:, fit:])
    return split_two(lanes)


def rel_result(sums, heads):
    high = jnp.zeros((RELN, HD), F32)
    flat = jnp.zeros((RELN, HD), F32)
    for head in range(heads):
        cols = sums[:, head * HD : head * HD + HD]
        high = high + cols[head * 32 : head * 32 + RELN]
        rolled = jnp.concatenate([cols[128:], cols[128:]], axis=0)
        flat = flat + rolled[head * 32 + 16 : head * 32 + 16 + RELN]
    return high[::-1], flat[::-1]


def add_all(values):
    out = values[0]
    for value in values[1:]:
        out = out + value
    return out


def body(
    block_input,
    window_place,
    slot_live,
    norm_one_gain,
    norm_one_shift,
    qkv_weight,
    qv_bias,
    proj_weight,
    proj_bias,
    norm_two_gain,
    norm_two_shift,
    up_weight,
    up_bias,
    down_weight,
    down_bias,
    rel_height,
    rel_width,
    cotangent,
):
    data_parts = lax.axis_size("dp")
    model_parts = lax.axis_size("mp")
    data_index = lax.axis_index("dp")
    model_index = lax.axis_index("mp")
    width = block_input.shape[1]
    share = qkv_weight.shape[1]
    cols = qkv_weight.shape[2]
    heads = cols // HD
    wide = (cols + 127) // 128 * 128
    units = up_weight.shape[1]
    slots = window_place.shape[0]
    rings = data_parts == 8 and model_parts == 4 and slots % 4 == 0
    padded = (slots + model_parts - 1) // model_parts * model_parts
    halves = padded // 4 if rings else 1
    windows = padded // halves
    split = 2 if rings else 0
    part_rows = windows * ROWS
    own_rows = part_rows // model_parts

    if rings:
        depth, side = data_index // 2, data_index % 2
        y_bit, core_bit = model_index // 2, model_index % 2
        over_x = partial(lax.ppermute, axis_name="dp", perm=[(d, d ^ 1) for d in range(8)])
        over_z = partial(lax.ppermute, axis_name="dp", perm=[(d, (d + 2) % 8) for d in range(8)])
        over_y = partial(lax.ppermute, axis_name="mp", perm=[(m, m ^ 2) for m in range(4)])
        over_core = partial(lax.ppermute, axis_name="mp", perm=[(m, m ^ 1) for m in range(4)])

    def gather(piece):
        if not rings:
            return [lax.all_gather(piece, "dp", axis=0, tiled=True)]
        line = [piece]
        for _ in range(3):
            line.append(over_z(line[-1]))
        return [item for held in line for item in (held, over_x(held))]

    if rings:
        offsets = []
        starts = []
        for back in range(4):
            behind = (depth - back) % 4
            offsets += [share * (2 * behind + side), share * (2 * behind + 1 - side)]
        for other in (0, 1):
            for ahead in range(4):
                target = 2 * ((depth + ahead) % 4) + (1 - side if other == 0 else side)
                starts.append(share * target)
        offsets = jnp.stack(offsets).astype(jnp.int32)
        starts = jnp.stack(starts).astype(jnp.int32)
        grad_shapes = [(4, share), (4, share)]
    else:
        offsets = jnp.zeros((1,), jnp.int32)
        starts = jnp.zeros((1,), jnp.int32)
        grad_shapes = [(1, width)]

    def scatter(parts):
        if not rings:
            return lax.psum_scatter(
                parts[0][0], "dp", scatter_dimension=0, tiled=True
            ).astype(F32)
        send, keep = parts
        came = over_x(send)
        sums = [keep[k].astype(F32) + came[k].astype(F32) for k in range(4)]
        moving = over_z(sums[3].astype(BF16))
        moving = over_z((sums[2] + moving.astype(F32)).astype(BF16))
        moving = over_z((sums[1] + moving.astype(F32)).astype(BF16))
        return sums[0] + moving.astype(F32)

    def rows_scatter(parts):
        if not rings:
            return [lax.psum_scatter(parts[0], "mp", scatter_dimension=0, tiled=True)]
        keep, send = parts
        came = over_core(send)
        passed = (keep[ROWS:].astype(F32) + came[ROWS:].astype(F32)).astype(BF16)
        return [keep, came, over_y(passed)]

    def rows_gather(own):
        if not rings:
            return [lax.all_gather(own, "mp", axis=0, tiled=True)]
        across = over_y(own)
        return [own, across, over_core(own), over_core(across)]

    def sum_all(vector):
        if not rings:
            return lax.psum(vector, ("dp", "mp"))
        for step in (1, 2):
            vector = vector + lax.ppermute(
                vector, "mp", [(m, m ^ step) for m in range(4)]
            )
        for step in (1, 2, 4):
            vector = vector + lax.ppermute(
                vector, "dp", [(d, d ^ step) for d in range(8)]
            )
        return vector

    def to_local(array):
        array = array.reshape((slots, WTOK) + array.shape[1:])
        tail = [(0, 0)] * (array.ndim - 2)
        if rings:
            shape = array.shape
            array = array.reshape((halves, 2, 2) + shape[1:])
            array = jnp.where(y_bit == 1, jnp.flip(array, 1), array)
            array = jnp.where(core_bit == 1, jnp.flip(array, 2), array)
            array = jnp.swapaxes(array, 1, 2).reshape(shape)
        array = jnp.pad(array, [(0, padded - slots), (0, ROWS - WTOK)] + tail)
        return array.reshape((padded * ROWS,) + array.shape[2:])

    def own_slice(array, part):
        if rings:
            return array[part * part_rows : part * part_rows + own_rows]
        return lax.dynamic_slice_in_dim(array, model_index * own_rows, own_rows, 0)

    def to_global(pieces, dtype):
        if rings:
            return place_windows(model_index.astype(jnp.int32).reshape(1), pieces, dtype)
        whole_rows = pieces[0].reshape(padded, ROWS, width)
        return whole_rows[:slots, :WTOK].reshape(slots * WTOK, width).astype(dtype)

    first_piece = jnp.concatenate([qkv_weight[0], qkv_weight[1], qkv_weight[2], proj_weight.T], 1)
    first_weights = gather(first_piece)
    down_pieces = gather(down_weight.T)
    up_pieces = gather(up_weight)

    row = lambda v: v.reshape(1, -1)
    gain_one, shift_one = row(norm_one_gain), row(norm_one_shift)
    gain_two, shift_two = row(norm_two_gain), row(norm_two_shift)
    bias_local = lax.dynamic_slice_in_dim(qv_bias, model_index * cols, cols, 1)
    bias_local = jnp.pad(bias_local, [(0, 0), (0, wide - cols)])
    bias_qkv = row(jnp.stack([bias_local[0], jnp.zeros_like(bias_local[0]), bias_local[1]]))
    up_local = row(lax.dynamic_slice_in_dim(up_bias, model_index * units, units, 0))
    rel_high, rel_low = rel_operand(rel_height, rel_width, heads, wide)
    marks = jnp.asarray(key_marks(heads))

    valid = to_local(token_valid(window_place, slot_live).reshape(slots * WTOK, 1))
    rows_in = to_local(block_input)
    grad_top = (to_local(cotangent) * valid.astype(BF16)).astype(BF16)
    normed = norm_one(rows_in, valid, gain_one, shift_one)

    q, k, v, weights = project(offsets, first_weights, normed, bias_qkv, cols, wide)
    attended = [
        attend(heads, part, windows, split, q, k, v, rel_high, rel_low, marks, weights)
        for part in range(halves)
    ]
    afters, normed_twos = [], []
    for part in range(halves):
        parts = rows_scatter(attended[part][2:])
        after, normed_two = norm_two(
            parts, own_slice(rows_in, part), row(proj_bias), gain_two, shift_two
        )
        afters.append(after)
        normed_twos.append(rows_gather(normed_two))

    mlps = [
        mlp(offsets, normed_twos[part], up_pieces, down_pieces, grad_top, part, up_local)
        for part in range(halves)
    ]

    def split_rows(array):
        return [array[: 2 * ROWS], array[2 * ROWS :]] if rings else [array]

    grad_afters, branches, sums_two = [], [], []
    for part in range(halves):
        parts = rows_scatter(split_rows(mlps[part][4]))
        grad_after, branch, sums = norm_two_back(
            parts, afters[part], own_slice(grad_top, part), gain_two
        )
        grad_afters.append(grad_after)
        branches.append(rows_gather(branch))
        sums_two.append(sums)
    out_pieces = []
    for part in range(halves):
        parts = rows_scatter(split_rows(mlps[part][5]))
        own = finish(parts, afters[part], own_slice(valid, part), row(down_bias))
        out_pieces += rows_gather(own)
    block_output = to_global(out_pieces, BF16)

    top_parts = [
        grad_top[part * part_rows : (part + 1) * part_rows] for part in range(halves)
    ]
    normed_parts = [
        normed[part * part_rows : (part + 1) * part_rows] for part in range(halves)
    ]
    shapes = [shape + (units,) for shape in grad_shapes]
    down_grad = scatter(
        weight_grad(
            starts, [[(top_parts[i], mlps[i][0], 0, units) for i in range(halves)]], units, shapes
        )
    )
    up_grad = scatter(
        weight_grad(
            starts, [[(mlps[i][2], mlps[i][1], 0, units) for i in range(halves)]], units, shapes
        )
    )

    backs = [
        attend_back(
            heads,
            part,
            windows,
            split,
            branches[part],
            q,
            k,
            v,
            attended[part][1],
            rel_high,
            rel_low,
            marks,
            weights,
        )
        for part in range(halves)
    ]
    in_pieces, sums_one = [], []
    for part in range(halves):
        parts = rows_scatter(backs[part][4:])
        own, sums = norm_one_back(
            parts, own_slice(rows_in, part), own_slice(valid, part), grad_afters[part], gain_one
        )
        sums_one.append(sums)
        in_pieces += rows_gather(own)
    input_grad = to_global(in_pieces, F32)
    groups = [
        [
            (normed_parts[i], backs[i][0], slot * wide, (slot + 1) * wide)
            for i in range(halves)
        ]
        for slot in range(3)
    ]
    groups.append([(backs[i][1], attended[i][0], 0, wide) for i in range(halves)])
    first_grad = scatter(
        weight_grad(starts, groups, cols, [shape + (4 * cols,) for shape in grad_shapes])
    )

    two = add_all(sums_two)
    one = add_all(sums_one)
    qv_sums = add_all([item[3] for item in backs]).reshape(3, wide)[0::2, :cols]
    rel_sums = rel_result(add_all([item[2] for item in backs]), heads)
    up_sums = add_all([item[3] for item in mlps]).reshape(units)
    qv_full = lax.dynamic_update_slice_in_dim(
        jnp.zeros((2, width), F32), qv_sums, model_index * cols, 1
    )
    up_full = lax.dynamic_update_slice_in_dim(
        jnp.zeros(up_bias.shape, F32), up_sums, model_index * units, 0
    )

    def sum_bundle(arrays):
        sizes = [array.size for array in arrays]
        flat = jnp.concatenate([array.reshape(-1) for array in arrays])
        count = (flat.size + 1023) // 1024 * 1024
        flat = jnp.pad(flat, (0, count - flat.size)).reshape(-1, 128)
        flat = sum_all(flat).reshape(-1)
        outs, at = [], 0
        for array, size in zip(arrays, sizes):
            outs.append(flat[at : at + size].reshape(array.shape))
            at += size
        return outs

    two_sums, up_bias_grad = sum_bundle([two, up_full])
    one_sums, qv_bias_grad, height_grad, width_grad = sum_bundle(
        [one, qv_full, rel_sums[0], rel_sums[1]]
    )
    qkv_grad = jnp.stack([first_grad[:, slot * cols : (slot + 1) * cols] for slot in range(3)])
    proj_grad = first_grad[:, 3 * cols :].T
    return (
        block_output,
        input_grad,
        one_sums[0],
        one_sums[1],
        qkv_grad,
        qv_bias_grad,
        proj_grad,
        two_sums[2],
        two_sums[0],
        two_sums[1],
        up_grad,
        up_bias_grad,
        down_grad.T,
        two_sums[3],
        height_grad,
        width_grad,
    )


def solution(mesh):
    in_specs = (
        P("dp", None),
        P("dp"),
        P("dp"),
        P(),
        P(),
        P(None, "dp", "mp"),
        P(),
        P("mp", "dp"),
        P(),
        P(),
        P(),
        P("dp", "mp"),
        P(),
        P("mp", "dp"),
        P(),
        P(),
        P(),
        P("dp", None),
    )
    out_specs = (
        P("dp", None),
        P("dp", None),
        P(),
        P(),
        P(None, "dp", "mp"),
        P(),
        P("mp", "dp"),
        P(),
        P(),
        P(),
        P("dp", "mp"),
        P(),
        P("mp", "dp"),
        P(),
        P(),
        P(),
    )
    return jax.shard_map(body, mesh=mesh, in_specs=in_specs, out_specs=out_specs, check_vma=False)
```

time: 1410 us -> 567 us (0.40)
  waiting for transfers between devices: 747 us -> 111 us
  Pallas kernels: 0 us -> 225 us
  matrix products: 219 us -> 0 us
  local copies, waits for them, and re-layouts: 289 us -> 107 us
  starting transfers between devices: 0.44 us -> 66.8 us
  other arithmetic: 97.7 us -> 49.9 us
  blocking collectives: 38.1 us -> 0 us
    psum x4 -> x0, waiting for transfers between devices: 427 us -> none  [the longest x1 145 us: body(): after = rows_in + lax.psum(attn_partial, 'mp') + proj_bias]
    pallas_call x0 -> x21, Pallas kernels: none -> 225 us  [the longest x3 52.8 us: weight_grad(): pl.pallas_call(partial(weight_grad_kernel, spans, cols, 256), grid_spec=p...]
    dot_general x54 -> x0, matrix products: 219 us -> none  [the longest x6 31.1 us: contract_rows(): lax.dot_general(left, right, (((0,), (0,)), ((), ())), preferred_element_...]
    all_gather x3 -> x0, waiting for transfers between devices: 125 us -> none  [the longest x1 55.3 us: body(): lax.all_gather(up_weight, 'dp', axis=0, tiled=True)]
    reduce_scatter x3 -> x0, waiting for transfers between devices: 121 us -> none  [the longest x1 76.7 us: body(): lax.psum_scatter(up_acc.astype(jnp.bfloat16), 'dp', scatter_dimension=0,...]
    add x16 -> x4, local copies, waits for them, and re-layouts: 114 us -> 0.37 us  [the longest x2 0.19 us: token_valid(): grid_row * WIN + inner_row[None, :] < SIDE]
    ppermute x0 -> x83, waiting for transfers between devices: none -> 111 us  [the longest x6 31.7 us: sum_all(): lax.ppermute(vector, 'dp', [(d, d ^ step) for d in range(8)])]
    unnamed x12 -> x0, waiting for transfers between devices: 73.2 us -> none
  transfers between devices with their start and end apart: 11 -> 83, of which waited for: 10 -> 21; matrix products, arithmetic and copies ran while one was open for 20% -> 20% of each run, Pallas kernels for 0% -> 36%
where the time goes in v1:
time: 567 us; the launch traced here: 562 us
  Pallas kernels  225 us (40%)
  waiting for transfers between devices  111 us (20%)
  local copies, waits for them, and re-layouts  107 us (19%)
  starting transfers between devices  66.8 us (12%)
  other arithmetic  49.9 us (9%)
    pallas_call x3, Pallas kernels, weight_grad(): pl.pallas_call(partial(weight_grad_kernel, spans, cols, 256), grid_spec=p...  52.8 us
    pallas_call x2, Pallas kernels, mlp(): pl.pallas_call(partial(mlp_kernel, len(pieces), len(up_pieces), chunk), g...  52.6 us
    pallas_call x2, Pallas kernels, attend_back(): pl.pallas_call(partial(attend_back_kernel, heads, windows, split, len(pie...  47.3 us
    unnamed x225, local copies, waits for them, and re-layouts  39.7 us
    ppermute x6, waiting for transfers between devices, sum_all(): lax.ppermute(vector, 'dp', [(d, d ^ step) for d in range(8)])  31.7 us
    ppermute x9, waiting for transfers between devices, gather(): line.append(over_z(line[-1]))  31 us
    pallas_call x2, Pallas kernels, attend(): pl.pallas_call(partial(attend_kernel, heads, split), grid=(windows,), in_...  20 us
    ppermute x8, waiting for transfers between devices, rows_gather(): across = over_y(own)  15 us
  transfers between devices with their start and end apart: 83, of which 21 were waited for; matrix products, arithmetic and copies ran while one was open for 20% of the time, Pallas kernels for 36%

profile of v1, /device:TPU:0, one launch (start us, length us, event | category | flops | bytes accessed | tf_op | source)
XLA Modules:
  0.0 562.1 jit_solution(9321244326964660076)
XLA Ops:
  2.9 3.1 collective-permute-start.1
  8.1 4.9 reshape_reshape.6
  13.0 4.9 reshape_reshape.7
  17.9 8.9 %reverse_select_fusion.1 = (bf16[2,2,2,196,1280]{4,3,2,1,0:T(8,128)(2,1)}, bf16[2,2,2,196,1280]{4,3,2,1,0:T(8,128)(2,1)S(1)}) fusion(bf16[2,2,2,196,1280]{4,3,2,1,0:T(8,128)(2,1)} %reshape_reshape.7, pred[]{:T(512)S(6)} %eq.34, bf16[2,2,2,196,1280]{4,3,2,1,0:T(8,128)(2,1)} %reshape_reshape.6), kind=kLoop, calls=%fused_computation.1 | loop fusion | flops 4014080 | bytes 16056321 | tf_op jit(solution)/shard_map/jit(_where)/select_n | solution.py:857
  26.8 2.8 fusion
  31.5 10.8 %collective-permute-done.3.refs_4_ = bf16[160,1280]{1,0:T(8,128)(2,1)S(1)} collective-permute-done((bf16[160,1280]{1,0:T(8,128)(2,1)S(1)}, bf16[160,1280]{1,0:T(8,128)(2,1)S(1)}, u32[]{:S(2)}, u32[]{:S(2)}) %collective-permute-start.3) | collective-permute-done | bytes 409632 | tf_op jit(solution)/shard_map/ppermute | solution.py:790
  44.2 4.5 copy.55
  50.4 4.5 pad.58
  60.6 2.6 scatter.31
  72.8 8.2 %norm_one.1.refs_8_ = bf16[1664,1280]{1,0:T(8,128)(2,1)} custom-call(bf16[1664,1280]{1,0:T(8,128)(2,1)} %bitcast.127, f32[1664,1]{1,0:T(8,128)} %reshape.555.valid_ref, f32[1,1280]{1,0:T(1,128)} %reshape.535.gain_ref.refs_6_, f32[1,1280]{1,0:T(1,128)} %reshape.536.shift_ref), custom_call_target="tpu_custom_call" | custom-call | tf_op jit(solution)/shard_map/norm_one/pallas_call | solution.py:80
  90.5 14.4 %qkv.1 = (bf16[1664,384]{1,0:T(8,128)(2,1)S(1)}, bf16[1664,384]{1,0:T(8,128)(2,1)S(1)}, bf16[1664,384]{1,0:T(8,128)(2,1)}, bf16[1280,1536]{1,0:T(8,128)(2,1)}) custom-call(s32[8]{0:T(128)S(1)} %stack.75.offsets, bf16[160,1280]{1,0:T(8,128)(2,1)S(1)} %copy-done.33, bf16[160,1280]{1,0:T(8,128)(2,1)S(1)} %copy-done.55, bf16[160,1280]{1,0:T(8,128)(2,1)S(1)} %copy-done.53, ...), custom_call_target="tpu_custom_call" | custom-call | tf_op jit(solution)/shard_map/qkv/pallas_call | solution.py:222
  105.0 3.0 copy-done.2
  109.3 10.0 %attend.3 = (bf16[832,384]{1,0:T(8,128)(2,1)S(1)}, f32[832,128]{1,0:T(8,128)S(1)}, bf16[416,1280]{1,0:T(8,128)(2,1)S(1)}, bf16[416,1280]{1,0:T(8,128)(2,1)S(1)}) custom-call(bf16[1664,384]{1,0:T(8,128)(2,1)S(1)} %get-tuple-element.180.q_ref.refs_4_, bf16[1664,384]{1,0:T(8,128)(2,1)S(1)} %get-tuple-element.181.k_ref.refs_5_, bf16[1664,384]{1,0:T(8,128)(2,1)S(1)} %copy-done.5, ...), custom_call_target="tpu_custom_call" | custom-call | tf_op jit(solution)/shard_map/attend/pallas_call | solution.py:359
  121.0 10.0 %attend.2 = (bf16[832,384]{1,0:T(8,128)(2,1)S(1)}, f32[832,128]{1,0:T(8,128)S(1)}, bf16[416,1280]{1,0:T(8,128)(2,1)S(1)}, bf16[416,1280]{1,0:T(8,128)(2,1)S(1)}) custom-call(bf16[1664,384]{1,0:T(8,128)(2,1)S(1)} %get-tuple-element.180.q_ref.refs_4_, bf16[1664,384]{1,0:T(8,128)(2,1)S(1)} %get-tuple-element.181.k_ref.refs_5_, bf16[1664,384]{1,0:T(8,128)(2,1)S(1)} %copy-done.5, ...), custom_call_target="tpu_custom_call" | custom-call | tf_op jit(solution)/shard_map/attend/pallas_call | solution.py:359
  136.7 9.3 %collective-permute-done.20.refs_14_ = bf16[160,1280]{1,0:T(8,128)(2,1)} collective-permute-done((bf16[160,1280]{1,0:T(8,128)(2,1)S(1)}, bf16[160,1280]{1,0:T(8,128)(2,1)}, u32[]{:S(2)}, u32[]{:S(2)}) %collective-permute-start.20) | collective-permute-done | bytes 409632 | tf_op jit(solution)/shard_map/ppermute | solution.py:790
  149.4 5.4 collective-permute-done.13.refs_6_
  159.3 2.8 fusion.1
  177.2 2.8 bitcast_multiply_fusion.refs_20_
  186.1 3.6 collective-permute-done.17.refs_10_
  190.8 2.4 collective-permute-done.16.refs_9_
  195.4 4.5 fusion.20
  201.9 3.4 collective-permute-done.9.refs_1_
  205.4 3.8 collective-permute-done.18.refs_11_
  211.0 26.3 %mlp.3 = (bf16[832,1280]{1,0:T(8,128)(2,1)}, bf16[832,1280]{1,0:T(8,128)(2,1)}, bf16[832,1280]{1,0:T(8,128)(2,1)}, f32[1,1280]{1,0:T(1,128)}, bf16[832,1280]{1,0:T(8,128)(2,1)}, /*index=5*/bf16[832,1280]{1,0:T(8,128)(2,1)}) custom-call(s32[8]{0:T(128)} %copy-done.65, bf16[208,1280]{1,0:T(8,128)(2,1)} %get-tuple-element.191.refs_0_, ...), custom_call_target="tpu_custom_call" | custom-call | tf_op jit(solution)/shard_map/mlp/pallas_call | solution.py:563
  237.3 2.7 fusion.23
  240.0 26.3 %mlp.2 = (bf16[832,1280]{1,0:T(8,128)(2,1)}, bf16[832,1280]{1,0:T(8,128)(2,1)}, bf16[832,1280]{1,0:T(8,128)(2,1)}, f32[1,1280]{1,0:T(1,128)}, bf16[832,1280]{1,0:T(8,128)(2,1)}, /*index=5*/bf16[832,1280]{1,0:T(8,128)(2,1)}) custom-call(s32[8]{0:T(128)} %copy-done.65, bf16[208,1280]{1,0:T(8,128)(2,1)} %copy-done.40, bf16[208,1280]{1,0:T(8,128)(2,1)} %copy-done.80, ...), custom_call_target="tpu_custom_call" | custom-call | tf_op jit(solution)/shard_map/mlp/pallas_call | solution.py:563
  266.2 2.8 fusion.24
  284.4 13.9 %weight_grad.5 = (bf16[4,160,1280]{2,1,0:T(8,128)(2,1)}, bf16[4,160,1280]{2,1,0:T(8,128)(2,1)}) custom-call(s32[8]{0:T(128)} %stack.84.starts, bf16[832,1280]{1,0:T(8,128)(2,1)} %get-tuple-element.239.refs_0_, bf16[832,1280]{1,0:T(8,128)(2,1)} %get-tuple-element.232.refs_1_, bf16[832,1280]{1,0:T(8,128)(2,1)} %get-tuple-element.238.refs_2_, ...), custom_call_target="tpu_custom_call" | custom-call | tf_op jit(solution)/shard_map/weight_grad/pallas_call | solution.py:630
  300.3 14.3 %weight_grad.4 = (bf16[4,160,1280]{2,1,0:T(8,128)(2,1)}, bf16[4,160,1280]{2,1,0:T(8,128)(2,1)}) custom-call(s32[8]{0:T(128)} %stack.84.starts, bf16[832,1280]{1,0:T(8,128)(2,1)} %get-tuple-element.226.refs_0_, bf16[832,1280]{1,0:T(8,128)(2,1)} %get-tuple-element.227.refs_1_, bf16[832,1280]{1,0:T(8,128)(2,1)} %get-tuple-element.228.refs_2_, ...), custom_call_target="tpu_custom_call" | custom-call | tf_op jit(solution)/shard_map/weight_grad/pallas_call | solution.py:630
  315.2 3.2 norm_two_back.3
  319.4 3.0 norm_two_back.2
  330.0 10.8 %collective-permute-done.71 = f32[80,128]{1,0:T(8,128)S(1)} collective-permute-done((f32[80,128]{1,0:T(8,128)S(1)}, f32[80,128]{1,0:T(8,128)S(1)}, u32[]{:S(2)}, u32[]{:S(2)}) %collective-permute-start.71) | collective-permute-done | bytes 40992 | tf_op jit(solution)/shard_map/ppermute | solution.py:842
  344.6 4.6 fusion.21
  349.2 3.0 collective-permute-done.27.refs_2_
  353.0 19.2 %collective-permute-done.72 = f32[80,128]{1,0:T(8,128)S(1)} collective-permute-done((f32[80,128]{1,0:T(8,128)S(1)}, f32[80,128]{1,0:T(8,128)S(1)}, u32[]{:S(2)}, u32[]{:S(2)}) %collective-permute-start.72) | collective-permute-done | bytes 40992 | tf_op jit(solution)/shard_map/ppermute | solution.py:846
  376.3 2.5 finish.3.refs_4_
  378.8 2.5 finish.2.refs_0_
  382.5 2.9 collective-permute-done.73
  387.0 23.6 %attend_back.3 = (bf16[832,1152]{1,0:T(8,128)(2,1)}, bf16[832,1280]{1,0:T(8,128)(2,1)}, f32[256,384]{1,0:T(8,128)}, f32[1,1152]{1,0:T(1,128)}, bf16[416,1280]{1,0:T(8,128)(2,1)}, /*index=5*/bf16[416,1280]{1,0:T(8,128)(2,1)}) custom-call(bf16[208,1280]{1,0:T(8,128)(2,1)} %get-tuple-element.202.refs_0_, bf16[208,1280]{1,0:T(8,128)(2,1)} %collective-permute-done.53.refs_1_, ...), custom_call_target="tpu_custom_call" | custom-call | tf_op jit(solution)/shard_map/attend_back/pallas_call | solution.py:476
  416.3 23.7 %attend_back.2 = (bf16[832,1152]{1,0:T(8,128)(2,1)}, bf16[832,1280]{1,0:T(8,128)(2,1)}, f32[256,384]{1,0:T(8,128)}, f32[1,1152]{1,0:T(1,128)}, bf16[416,1280]{1,0:T(8,128)(2,1)}, /*index=5*/bf16[416,1280]{1,0:T(8,128)(2,1)}) custom-call(bf16[208,1280]{1,0:T(8,128)(2,1)} %get-tuple-element.195.refs_0_, bf16[208,1280]{1,0:T(8,128)(2,1)} %collective-permute-done.43.refs_1_, ...), custom_call_target="tpu_custom_call" | custom-call | tf_op jit(solution)/shard_map/attend_back/pallas_call | solution.py:476
  449.1 24.6 %weight_grad.3 = (bf16[4,160,1280]{2,1,0:T(8,128)(2,1)}, bf16[4,160,1280]{2,1,0:T(8,128)(2,1)}) custom-call(s32[8]{0:T(128)} %stack.84.starts, bf16[832,1280]{1,0:T(8,128)(2,1)} %get-tuple-element.241.refs_0_.refs_4_.refs_8_, bf16[832,1152]{1,0:T(8,128)(2,1)} %get-tuple-element.214.refs_1_.refs_5_.refs_9_, ...), custom_call_target="tpu_custom_call" | custom-call | tf_op jit(solution)/shard_map/weight_grad/pallas_call | solution.py:630
  487.7 7.5 %collective-permute-done.28.refs_1_ = bf16[208,1280]{1,0:T(8,128)(2,1)} collective-permute-done((bf16[208,1280]{1,0:T(8,128)(2,1)}, bf16[208,1280]{1,0:T(8,128)(2,1)}, u32[]{:S(2)}, u32[]{:S(2)}) %collective-permute-start.28) | collective-permute-done | bytes 532512 | tf_op jit(solution)/shard_map/ppermute | solution.py:835
  502.5 5.5 place_windows.2
  508.6 3.2 collective-permute-done.66
  520.5 9.6 %collective-permute-done.64 = f32[80,128]{1,0:T(8,128)S(1)} collective-permute-done((f32[80,128]{1,0:T(8,128)S(1)}, f32[80,128]{1,0:T(8,128)S(1)}, u32[]{:S(2)}, u32[]{:S(2)}) %collective-permute-start.64) | collective-permute-done | bytes 40992 | tf_op jit(solution)/shard_map/ppermute | solution.py:846
  537.6 4.1 collective-permute-done.48.refs_1_
  541.7 3.9 collective-permute-done.68
  550.3 6.6 %place_windows.3 = f32[1568,1280]{1,0:T(8,128)} custom-call(s32[1]{0:T(128)} %bitcast.order, bf16[208,1280]{1,0:T(8,128)(2,1)} %copy-done.43, bf16[208,1280]{1,0:T(8,128)(2,1)} %collective-permute-done.48.refs_1_, bf16[208,1280]{1,0:T(8,128)(2,1)} %copy-done.87, bf16[208,1280]{1,0:T(8,128)(2,1)} %copy-done.91, bf16[208,1280]{1,0:T(8,128)(2,1)} %copy-done.41, ...), custom_call_target="tpu_custom_call" | custom-call | tf_op jit(solution)/shard_map/place_windows/pallas_call | solution.py:665
  (496 shorter events, 179.3 us)
Async XLA Ops:
  2.9 26.9 %collective-permute-start.1 = (bf16[160,1280]{1,0:T(8,128)(2,1)S(1)}, bf16[160,1280]{1,0:T(8,128)(2,1)S(1)}, u32[]{:S(2)}, u32[]{:S(2)}) collective-permute-start(bf16[160,1280]{1,0:T(8,128)(2,1)S(1)} %concatenate.35.refs_0_), channel_id=1, source_target_pairs={{0,8},{4,12},{8,16},{12,20},{16,24},{20,28},{24,0},{28,4},{1,9},{5... | collective-permute-start | bytes 1228808 | tf_op jit(solution)/shard_map/ppermute | solution.py:790
  6.0 75.2 %collective-permute-start = (bf16[160,1280]{1,0:T(8,128)(2,1)S(1)}, bf16[160,1280]{1,0:T(8,128)(2,1)S(1)}, u32[]{:S(2)}, u32[]{:S(2)}) collective-permute-start(bf16[160,1280]{1,0:T(8,128)(2,1)S(1)} %concatenate.35.refs_0_), channel_id=1, source_target_pairs={{0,4},{4,0},{8,12},{12,8},{16,20},{20,16},{24,28},{28,24},{1,5},{5... | collective-permute-start | bytes 1228808 | tf_op jit(solution)/shard_map/ppermute | solution.py:791
  56.1 25.9 %collective-permute-start.2 = (bf16[160,1280]{1,0:T(8,128)(2,1)S(1)}, bf16[160,1280]{1,0:T(8,128)(2,1)S(1)}, u32[]{:S(2)}, u32[]{:S(2)}) collective-permute-start(bf16[160,1280]{1,0:T(8,128)(2,1)S(1)} %collective-permute-done.1.refs_2_), channel_id=1, source_target_pairs={{0,4},{4,0},{8,12},{12,8},{16,20},{20,16},{24,28},{28,24},{1,5},{5... | collective-permute-start | bytes 1228808 | tf_op jit(solution)/shard_map/ppermute | solution.py:791
  56.6 26.2 %collective-permute-start.4 = (bf16[160,1280]{1,0:T(8,128)(2,1)S(1)}, bf16[160,1280]{1,0:T(8,128)(2,1)S(1)}, u32[]{:S(2)}, u32[]{:S(2)}) collective-permute-start(bf16[160,1280]{1,0:T(8,128)(2,1)S(1)} %collective-permute-done.3.refs_4_), channel_id=1, source_target_pairs={{0,4},{4,0},{8,12},{12,8},{16,20},{20,16},{24,28},{28,24},{1,5},{5... | collective-permute-start | bytes 1228808 | tf_op jit(solution)/shard_map/ppermute | solution.py:791
  58.1 25.4 %collective-permute-start.6 = (bf16[160,1280]{1,0:T(8,128)(2,1)S(1)}, bf16[160,1280]{1,0:T(8,128)(2,1)}, u32[]{:S(2)}, u32[]{:S(2)}) collective-permute-start(bf16[160,1280]{1,0:T(8,128)(2,1)S(1)} %collective-permute-done.5.refs_6_), channel_id=1, source_target_pairs={{0,4},{4,0},{8,12},{12,8},{16,20},{20,16},{24,28},{28,24},{1,5},{5... | collective-permute-start | bytes 1228808 | tf_op jit(solution)/shard_map/ppermute | solution.py:791
  133.3 24.5 %collective-permute-start.32 = (bf16[208,1280]{1,0:T(8,128)(2,1)S(1)}, bf16[208,1280]{1,0:T(8,128)(2,1)S(1)}, u32[]{:S(2)}, u32[]{:S(2)}) collective-permute-start(bf16[208,1280]{1,0:T(8,128)(2,1)S(1)} %add_convert_fusion.5), channel_id=1, source_target_pairs={{0,2},{1,3},{2,0},{3,1},{4,6},{5,7},{6,4},{7,5},{8,10},{9,11},{10,... | collective-permute-start | bytes 1597448 | tf_op jit(solution)/shard_map/ppermute | solution.py:830
  134.9 21.4 %collective-permute-start.19 = (bf16[160,1280]{1,0:T(8,128)(2,1)S(1)}, bf16[160,1280]{1,0:T(8,128)(2,1)S(1)}, u32[]{:S(2)}, u32[]{:S(2)}) collective-permute-start(bf16[160,1280]{1,0:T(8,128)(2,1)S(1)} %bitcast.132), channel_id=1, source_target_pairs={{0,4},{4,0},{8,12},{12,8},{16,20},{20,16},{24,28},{28,24},{1,5},{5... | collective-permute-start | bytes 1228808 | tf_op jit(solution)/shard_map/ppermute | solution.py:791
  136.4 18.4 %collective-permute-start.13 = (bf16[160,1280]{1,0:T(8,128)(2,1)S(1)}, bf16[160,1280]{1,0:T(8,128)(2,1)}, u32[]{:S(2)}, u32[]{:S(2)}) collective-permute-start(bf16[160,1280]{1,0:T(8,128)(2,1)S(1)} %copy-done.74), channel_id=1, source_target_pairs={{0,8},{4,12},{8,16},{12,20},{16,24},{20,28},{24,0},{28,4},{1,9},{5... | collective-permute-start | bytes 1228808 | tf_op jit(solution)/shard_map/ppermute | solution.py:790
  147.5 22.3 %collective-permute-start.22 = (bf16[160,1280]{1,0:T(8,128)(2,1)}, bf16[160,1280]{1,0:T(8,128)(2,1)}, u32[]{:S(2)}, u32[]{:S(2)}) collective-permute-start(bf16[160,1280]{1,0:T(8,128)(2,1)} %collective-permute-done.20.refs_14_), channel_id=1, source_target_pairs={{0,8},{4,12},{8,16},{12,20},{16,24},{20,28},{24,0},{28,4},{1,9},{5... | collective-permute-start | bytes 1228808 | tf_op jit(solution)/shard_map/ppermute | solution.py:790
  154.8 18.4 %collective-permute-start.21 = (bf16[160,1280]{1,0:T(8,128)(2,1)}, bf16[160,1280]{1,0:T(8,128)(2,1)}, u32[]{:S(2)}, u32[]{:S(2)}) collective-permute-start(bf16[160,1280]{1,0:T(8,128)(2,1)} %collective-permute-done.20.refs_14_), channel_id=1, source_target_pairs={{0,4},{4,0},{8,12},{12,8},{16,20},{20,16},{24,28},{28,24},{1,5},{5... | collective-permute-start | bytes 1228808 | tf_op jit(solution)/shard_map/ppermute | solution.py:791
  156.3 17.9 %collective-permute-start.14 = (bf16[160,1280]{1,0:T(8,128)(2,1)}, bf16[160,1280]{1,0:T(8,128)(2,1)}, u32[]{:S(2)}, u32[]{:S(2)}) collective-permute-start(bf16[160,1280]{1,0:T(8,128)(2,1)} %collective-permute-done.13.refs_6_), channel_id=1, source_target_pairs={{0,4},{4,0},{8,12},{12,8},{16,20},{20,16},{24,28},{28,24},{1,5},{5... | collective-permute-start | bytes 1228808 | tf_op jit(solution)/shard_map/ppermute | solution.py:791
  157.8 17.9 %collective-permute-start.8 = (bf16[208,1280]{1,0:T(8,128)(2,1)}, bf16[208,1280]{1,0:T(8,128)(2,1)S(1)}, u32[]{:S(2)}, u32[]{:S(2)}) collective-permute-start(bf16[208,1280]{1,0:T(8,128)(2,1)} %add_convert_fusion.7), channel_id=1, source_target_pairs={{0,2},{1,3},{2,0},{3,1},{4,6},{5,7},{6,4},{7,5},{8,10},{9,11},{10,... | collective-permute-start | bytes 1597448 | tf_op jit(solution)/shard_map/ppermute | solution.py:830
  171.8 19.1 %collective-permute-start.23 = (bf16[160,1280]{1,0:T(8,128)(2,1)}, bf16[160,1280]{1,0:T(8,128)(2,1)}, u32[]{:S(2)}, u32[]{:S(2)}) collective-permute-start(bf16[160,1280]{1,0:T(8,128)(2,1)} %collective-permute-done.22.refs_16_), channel_id=1, source_target_pairs={{0,4},{4,0},{8,12},{12,8},{16,20},{20,16},{24,28},{28,24},{1,5},{5... | collective-permute-start | bytes 1228808 | tf_op jit(solution)/shard_map/ppermute | solution.py:791
  174.2 19.1 %collective-permute-start.16 = (bf16[160,1280]{1,0:T(8,128)(2,1)}, bf16[160,1280]{1,0:T(8,128)(2,1)}, u32[]{:S(2)}, u32[]{:S(2)}) collective-permute-start(bf16[160,1280]{1,0:T(8,128)(2,1)} %collective-permute-done.15.refs_8_), channel_id=1, source_target_pairs={{0,4},{4,0},{8,12},{12,8},{16,20},{20,16},{24,28},{28,24},{1,5},{5... | collective-permute-start | bytes 1228808 | tf_op jit(solution)/shard_map/ppermute | solution.py:791
  175.7 19.7 %collective-permute-start.33 = (bf16[208,1280]{1,0:T(8,128)(2,1)}, bf16[208,1280]{1,0:T(8,128)(2,1)}, u32[]{:S(2)}, u32[]{:S(2)}) collective-permute-start(bf16[208,1280]{1,0:T(8,128)(2,1)} %get-tuple-element.191.refs_0_), channel_id=1, source_target_pairs={{0,2},{1,3},{2,0},{3,1},{4,6},{5,7},{6,4},{7,5},{8,10},{9,11},{10,... | collective-permute-start | bytes 1597448 | tf_op jit(solution)/shard_map/ppermute | solution.py:835
  185.5 16.4 %collective-permute-start.25 = (bf16[160,1280]{1,0:T(8,128)(2,1)}, bf16[160,1280]{1,0:T(8,128)(2,1)S(1)}, u32[]{:S(2)}, u32[]{:S(2)}) collective-permute-start(bf16[160,1280]{1,0:T(8,128)(2,1)} %collective-permute-done.24.refs_18_), channel_id=1, source_target_pairs={{0,4},{4,0},{8,12},{12,8},{16,20},{20,16},{24,28},{28,24},{1,5},{5... | collective-permute-start | bytes 1228808 | tf_op jit(solution)/shard_map/ppermute | solution.py:791
  189.7 19.5 %collective-permute-start.18 = (bf16[160,1280]{1,0:T(8,128)(2,1)}, bf16[160,1280]{1,0:T(8,128)(2,1)S(1)}, u32[]{:S(2)}, u32[]{:S(2)}) collective-permute-start(bf16[160,1280]{1,0:T(8,128)(2,1)} %collective-permute-done.17.refs_10_), channel_id=1, source_target_pairs={{0,4},{4,0},{8,12},{12,8},{16,20},{20,16},{24,28},{28,24},{1,5},{5... | collective-permute-start | bytes 1228808 | tf_op jit(solution)/shard_map/ppermute | solution.py:791
  190.8 18.4 %collective-permute-start.34 = (bf16[208,1280]{1,0:T(8,128)(2,1)}, bf16[208,1280]{1,0:T(8,128)(2,1)S(1)}, u32[]{:S(2)}, u32[]{:S(2)}) collective-permute-start(bf16[208,1280]{1,0:T(8,128)(2,1)} %get-tuple-element.191.refs_0_), channel_id=1, source_target_pairs={{0,1},{1,0},{2,3},{3,2},{4,5},{5,4},{6,7},{7,6},{8,9},{9,8},{10,11... | collective-permute-start | bytes 1597448 | tf_op jit(solution)/shard_map/ppermute | solution.py:836
  201.9 38.0 %collective-permute-start.10 = (bf16[208,1280]{1,0:T(8,128)(2,1)S(1)}, bf16[208,1280]{1,0:T(8,128)(2,1)}, u32[]{:S(2)}, u32[]{:S(2)}) collective-permute-start(bf16[208,1280]{1,0:T(8,128)(2,1)S(1)} %get-tuple-element.186.refs_0_), channel_id=1, source_target_pairs={{0,1},{1,0},{2,3},{3,2},{4,5},{5,4},{6,7},{7,6},{8,9},{9,8},{10,11... | collective-permute-start | bytes 1597448 | tf_op jit(solution)/shard_map/ppermute | solution.py:836
  205.3 34.6 %collective-permute-start.11 = (bf16[208,1280]{1,0:T(8,128)(2,1)S(1)}, bf16[208,1280]{1,0:T(8,128)(2,1)}, u32[]{:S(2)}, u32[]{:S(2)}) collective-permute-start(bf16[208,1280]{1,0:T(8,128)(2,1)S(1)} %collective-permute-done.9.refs_1_), channel_id=1, source_target_pairs={{0,1},{1,0},{2,3},{3,2},{4,5},{5,4},{6,7},{7,6},{8,9},{9,8},{10,11... | collective-permute-start | bytes 1597448 | tf_op jit(solution)/shard_map/ppermute | solution.py:836
  239.9 33.5 %collective-permute-start.51 = (bf16[416,1280]{1,0:T(8,128)(2,1)S(1)}, bf16[416,1280]{1,0:T(8,128)(2,1)S(1)}, u32[]{:S(2)}, u32[]{:S(2)}) collective-permute-start(bf16[416,1280]{1,0:T(8,128)(2,1)S(1)} %get-tuple-element.246), channel_id=1, source_target_pairs={{0,1},{1,0},{2,3},{3,2},{4,5},{5,4},{6,7},{7,6},{8,9},{9,8},{10,11... | collective-permute-start | bytes 3194888 | tf_op jit(solution)/shard_map/ppermute | solution.py:828
  271.0 52.6 %collective-permute-start.36 = (bf16[416,1280]{1,0:T(8,128)(2,1)}, bf16[416,1280]{1,0:T(8,128)(2,1)}, u32[]{:S(2)}, u32[]{:S(2)}) collective-permute-start(bf16[416,1280]{1,0:T(8,128)(2,1)} %get-tuple-element.250), channel_id=1, source_target_pairs={{0,1},{1,0},{2,3},{3,2},{4,5},{5,4},{6,7},{7,6},{8,9},{9,8},{10,11... | collective-permute-start | bytes 3194888 | tf_op jit(solution)/shard_map/ppermute | solution.py:828
  273.4 53.7 %collective-permute-start.26 = (bf16[416,1280]{1,0:T(8,128)(2,1)}, bf16[416,1280]{1,0:T(8,128)(2,1)}, u32[]{:S(2)}, u32[]{:S(2)}) collective-permute-start(bf16[416,1280]{1,0:T(8,128)(2,1)} %get-tuple-element.252), channel_id=1, source_target_pairs={{0,1},{1,0},{2,3},{3,2},{4,5},{5,4},{6,7},{7,6},{8,9},{9,8},{10,11... | collective-permute-start | bytes 3194888 | tf_op jit(solution)/shard_map/ppermute | solution.py:828
  276.5 38.1 %collective-permute-start.52 = (bf16[208,1280]{1,0:T(8,128)(2,1)}, bf16[208,1280]{1,0:T(8,128)(2,1)}, u32[]{:S(2)}, u32[]{:S(2)}) collective-permute-start(bf16[208,1280]{1,0:T(8,128)(2,1)} %add_convert_fusion.1), channel_id=1, source_target_pairs={{0,2},{1,3},{2,0},{3,1},{4,6},{5,7},{6,4},{7,5},{8,10},{9,11},{10,... | collective-permute-start | bytes 1597448 | tf_op jit(solution)/shard_map/ppermute | solution.py:830
  280.9 38.5 %collective-permute-start.42 = (bf16[208,1280]{1,0:T(8,128)(2,1)}, bf16[208,1280]{1,0:T(8,128)(2,1)}, u32[]{:S(2)}, u32[]{:S(2)}) collective-permute-start(bf16[208,1280]{1,0:T(8,128)(2,1)} %add_convert_fusion.3), channel_id=1, source_target_pairs={{0,2},{1,3},{2,0},{3,1},{4,6},{5,7},{6,4},{7,5},{8,10},{9,11},{10,... | collective-permute-start | bytes 1597448 | tf_op jit(solution)/shard_map/ppermute | solution.py:830
  298.3 82.9 %collective-permute-start.79 = (bf16[4,160,1280]{2,1,0:T(8,128)(2,1)}, bf16[4,160,1280]{2,1,0:T(8,128)(2,1)}, u32[]{:S(2)}, u32[]{:S(2)}) collective-permute-start(bf16[4,160,1280]{2,1,0:T(8,128)(2,1)} %get-tuple-element.235), channel_id=1, source_target_pairs={{0,4},{4,0},{8,12},{12,8},{16,20},{20,16},{24,28},{28,24},{1,5},{5... | collective-permute-start | bytes 4915208 | tf_op jit(solution)/shard_map/ppermute | solution.py:817
  314.6 96.1 %collective-permute-start.75 = (bf16[4,160,1280]{2,1,0:T(8,128)(2,1)}, bf16[4,160,1280]{2,1,0:T(8,128)(2,1)}, u32[]{:S(2)}, u32[]{:S(2)}) collective-permute-start(bf16[4,160,1280]{2,1,0:T(8,128)(2,1)} %get-tuple-element.231), channel_id=1, source_target_pairs={{0,4},{4,0},{8,12},{12,8},{16,20},{20,16},{24,28},{28,24},{1,5},{5... | collective-permute-start | bytes 4915208 | tf_op jit(solution)/shard_map/ppermute | solution.py:817
  325.0 17.3 %collective-permute-start.37 = (bf16[208,1280]{1,0:T(8,128)(2,1)S(1)}, bf16[208,1280]{1,0:T(8,128)(2,1)S(1)}, u32[]{:S(2)}, u32[]{:S(2)}) collective-permute-start(bf16[208,1280]{1,0:T(8,128)(2,1)S(1)} %add_convert_fusion.4), channel_id=1, source_target_pairs={{0,2},{1,3},{2,0},{3,1},{4,6},{5,7},{6,4},{7,5},{8,10},{9,11},{10,... | collective-permute-start | bytes 1597448 | tf_op jit(solution)/shard_map/ppermute | solution.py:830
  328.5 23.7 %collective-permute-start.27 = (bf16[208,1280]{1,0:T(8,128)(2,1)S(1)}, bf16[208,1280]{1,0:T(8,128)(2,1)S(1)}, u32[]{:S(2)}, u32[]{:S(2)}) collective-permute-start(bf16[208,1280]{1,0:T(8,128)(2,1)S(1)} %add_convert_fusion.6), channel_id=1, source_target_pairs={{0,2},{1,3},{2,0},{3,1},{4,6},{5,7},{6,4},{7,5},{8,10},{9,11},{10,... | collective-permute-start | bytes 1597448 | tf_op jit(solution)/shard_map/ppermute | solution.py:830
  340.8 32.9 %collective-permute-start.53 = (bf16[208,1280]{1,0:T(8,128)(2,1)}, bf16[208,1280]{1,0:T(8,128)(2,1)}, u32[]{:S(2)}, u32[]{:S(2)}) collective-permute-start(bf16[208,1280]{1,0:T(8,128)(2,1)} %get-tuple-element.202.refs_0_), channel_id=1, source_target_pairs={{0,2},{1,3},{2,0},{3,1},{4,6},{5,7},{6,4},{7,5},{8,10},{9,11},{10,... | collective-permute-start | bytes 1597448 | tf_op jit(solution)/shard_map/ppermute | solution.py:835
  343.1 29.1 %collective-permute-start.72 = (f32[80,128]{1,0:T(8,128)S(1)}, f32[80,128]{1,0:T(8,128)S(1)}, u32[]{:S(2)}, u32[]{:S(2)}) collective-permute-start(f32[80,128]{1,0:T(8,128)S(1)} %add.454), channel_id=1, source_target_pairs={{0,4},{4,0},{8,12},{12,8},{16,20},{20,16},{24,28},{28,24},{1,5},{5... | collective-permute-start | bytes 122888 | tf_op jit(solution)/shard_map/ppermute | solution.py:846
  353.0 32.4 %collective-permute-start.54 = (bf16[208,1280]{1,0:T(8,128)(2,1)}, bf16[208,1280]{1,0:T(8,128)(2,1)}, u32[]{:S(2)}, u32[]{:S(2)}) collective-permute-start(bf16[208,1280]{1,0:T(8,128)(2,1)} %get-tuple-element.202.refs_0_), channel_id=1, source_target_pairs={{0,1},{1,0},{2,3},{3,2},{4,5},{5,4},{6,7},{7,6},{8,9},{9,8},{10,11... | collective-permute-start | bytes 1597448 | tf_op jit(solution)/shard_map/ppermute | solution.py:836
  385.3 28.6 %collective-permute-start.44 = (bf16[208,1280]{1,0:T(8,128)(2,1)}, bf16[208,1280]{1,0:T(8,128)(2,1)S(1)}, u32[]{:S(2)}, u32[]{:S(2)}) collective-permute-start(bf16[208,1280]{1,0:T(8,128)(2,1)} %get-tuple-element.195.refs_0_), channel_id=1, source_target_pairs={{0,1},{1,0},{2,3},{3,2},{4,5},{5,4},{6,7},{7,6},{8,9},{9,8},{10,11... | collective-permute-start | bytes 1597448 | tf_op jit(solution)/shard_map/ppermute | solution.py:836
  385.4 98.8 %collective-permute-start.38 = (bf16[208,1280]{1,0:T(8,128)(2,1)}, bf16[208,1280]{1,0:T(8,128)(2,1)}, u32[]{:S(2)}, u32[]{:S(2)}) collective-permute-start(bf16[208,1280]{1,0:T(8,128)(2,1)} %finish.3.refs_4_), channel_id=1, source_target_pairs={{0,2},{1,3},{2,0},{3,1},{4,6},{5,7},{6,4},{7,5},{8,10},{9,11},{10,... | collective-permute-start | bytes 1597448 | tf_op jit(solution)/shard_map/ppermute | solution.py:835
  386.0 26.3 %collective-permute-start.74 = (f32[80,128]{1,0:T(8,128)S(1)}, f32[80,128]{1,0:T(8,128)S(1)}, u32[]{:S(2)}, u32[]{:S(2)}) collective-permute-start(f32[80,128]{1,0:T(8,128)S(1)} %add.456), channel_id=1, source_target_pairs={{0,16},{4,20},{8,24},{12,28},{16,0},{20,4},{24,8},{28,12},{1,17},{... | collective-permute-start | bytes 122888 | tf_op jit(solution)/shard_map/ppermute | solution.py:846
  387.0 28.5 %collective-permute-start.45 = (bf16[208,1280]{1,0:T(8,128)(2,1)}, bf16[208,1280]{1,0:T(8,128)(2,1)S(1)}, u32[]{:S(2)}, u32[]{:S(2)}) collective-permute-start(bf16[208,1280]{1,0:T(8,128)(2,1)} %collective-permute-done.43.refs_1_), channel_id=1, source_target_pairs={{0,1},{1,0},{2,3},{3,2},{4,5},{5,4},{6,7},{7,6},{8,9},{9,8},{10,11... | collective-permute-start | bytes 1597448 | tf_op jit(solution)/shard_map/ppermute | solution.py:836
  410.6 32.4 %collective-permute-start.56 = (bf16[416,1280]{1,0:T(8,128)(2,1)}, bf16[416,1280]{1,0:T(8,128)(2,1)S(1)}, u32[]{:S(2)}, u32[]{:S(2)}) collective-permute-start(bf16[416,1280]{1,0:T(8,128)(2,1)} %get-tuple-element.205), channel_id=1, source_target_pairs={{0,1},{1,0},{2,3},{3,2},{4,5},{5,4},{6,7},{7,6},{8,9},{9,8},{10,11... | collective-permute-start | bytes 3194888 | tf_op jit(solution)/shard_map/ppermute | solution.py:828
  412.3 28.4 %collective-permute-start.80 = (bf16[160,1280]{1,0:T(8,128)(2,1)S(1)}, bf16[160,1280]{1,0:T(8,128)(2,1)}, u32[]{:S(2)}, u32[]{:S(2)}) collective-permute-start(bf16[160,1280]{1,0:T(8,128)(2,1)S(1)} %fusion.11), channel_id=1, source_target_pairs={{0,8},{4,12},{8,16},{12,20},{16,24},{20,28},{24,0},{28,4},{1,9},{5... | collective-permute-start | bytes 1228808 | tf_op jit(solution)/shard_map/ppermute | solution.py:819
  414.0 33.2 %collective-permute-start.76 = (bf16[160,1280]{1,0:T(8,128)(2,1)S(1)}, bf16[160,1280]{1,0:T(8,128)(2,1)S(1)}, u32[]{:S(2)}, u32[]{:S(2)}) collective-permute-start(bf16[160,1280]{1,0:T(8,128)(2,1)S(1)} %fusion.10), channel_id=1, source_target_pairs={{0,8},{4,12},{8,16},{12,20},{16,24},{20,28},{24,0},{28,4},{1,9},{5... | collective-permute-start | bytes 1228808 | tf_op jit(solution)/shard_map/ppermute | solution.py:819
  442.8 43.0 %collective-permute-start.81 = (bf16[160,1280]{1,0:T(8,128)(2,1)}, bf16[160,1280]{1,0:T(8,128)(2,1)}, u32[]{:S(2)}, u32[]{:S(2)}) collective-permute-start(bf16[160,1280]{1,0:T(8,128)(2,1)} %fusion.2), channel_id=1, source_target_pairs={{0,8},{4,12},{8,16},{12,20},{16,24},{20,28},{24,0},{28,4},{1,9},{5... | collective-permute-start | bytes 1228808 | tf_op jit(solution)/shard_map/ppermute | solution.py:820
  444.0 32.0 %collective-permute-start.57 = (bf16[208,1280]{1,0:T(8,128)(2,1)}, bf16[208,1280]{1,0:T(8,128)(2,1)}, u32[]{:S(2)}, u32[]{:S(2)}) collective-permute-start(bf16[208,1280]{1,0:T(8,128)(2,1)} %add_convert_fusion), channel_id=1, source_target_pairs={{0,2},{1,3},{2,0},{3,1},{4,6},{5,7},{6,4},{7,5},{8,10},{9,11},{10,... | collective-permute-start | bytes 1597448 | tf_op jit(solution)/shard_map/ppermute | solution.py:830
  446.6 33.8 %collective-permute-start.47 = (bf16[208,1280]{1,0:T(8,128)(2,1)}, bf16[208,1280]{1,0:T(8,128)(2,1)}, u32[]{:S(2)}, u32[]{:S(2)}) collective-permute-start(bf16[208,1280]{1,0:T(8,128)(2,1)} %add_convert_fusion.2), channel_id=1, source_target_pairs={{0,2},{1,3},{2,0},{3,1},{4,6},{5,7},{6,4},{7,5},{8,10},{9,11},{10,... | collective-permute-start | bytes 1597448 | tf_op jit(solution)/shard_map/ppermute | solution.py:830
  473.7 38.1 %collective-permute-start.66 = (bf16[4,160,1280]{2,1,0:T(8,128)(2,1)}, bf16[4,160,1280]{2,1,0:T(8,128)(2,1)}, u32[]{:S(2)}, u32[]{:S(2)}) collective-permute-start(bf16[4,160,1280]{2,1,0:T(8,128)(2,1)} %get-tuple-element.221), channel_id=1, source_target_pairs={{0,4},{4,0},{8,12},{12,8},{16,20},{20,16},{24,28},{28,24},{1,5},{5... | collective-permute-start | bytes 4915208 | tf_op jit(solution)/shard_map/ppermute | solution.py:817
  499.4 16.9 %collective-permute-start.82 = (bf16[160,1280]{1,0:T(8,128)(2,1)S(1)}, bf16[160,1280]{1,0:T(8,128)(2,1)S(1)}, u32[]{:S(2)}, u32[]{:S(2)}) collective-permute-start(bf16[160,1280]{1,0:T(8,128)(2,1)S(1)} %fusion.3), channel_id=1, source_target_pairs={{0,8},{4,12},{8,16},{12,20},{16,24},{20,28},{24,0},{28,4},{1,9},{5... | collective-permute-start | bytes 1228808 | tf_op jit(solution)/shard_map/ppermute | solution.py:821
  500.0 34.1 %collective-permute-start.78 = (bf16[160,1280]{1,0:T(8,128)(2,1)S(1)}, bf16[160,1280]{1,0:T(8,128)(2,1)}, u32[]{:S(2)}, u32[]{:S(2)}) collective-permute-start(bf16[160,1280]{1,0:T(8,128)(2,1)S(1)} %fusion.6), channel_id=1, source_target_pairs={{0,8},{4,12},{8,16},{12,20},{16,24},{20,28},{24,0},{28,4},{1,9},{5... | collective-permute-start | bytes 1228808 | tf_op jit(solution)/shard_map/ppermute | solution.py:821
  513.0 17.7 %collective-permute-start.67 = (bf16[160,1280]{1,0:T(8,128)(2,1)S(1)}, bf16[160,1280]{1,0:T(8,128)(2,1)S(1)}, u32[]{:S(2)}, u32[]{:S(2)}) collective-permute-start(bf16[160,1280]{1,0:T(8,128)(2,1)S(1)} %fusion.9), channel_id=1, source_target_pairs={{0,8},{4,12},{8,16},{12,20},{16,24},{20,28},{24,0},{28,4},{1,9},{5... | collective-permute-start | bytes 1228808 | tf_op jit(solution)/shard_map/ppermute | solution.py:819
  518.5 19.0 %collective-permute-start.58 = (bf16[208,1280]{1,0:T(8,128)(2,1)S(1)}, bf16[208,1280]{1,0:T(8,128)(2,1)S(1)}, u32[]{:S(2)}, u32[]{:S(2)}) collective-permute-start(bf16[208,1280]{1,0:T(8,128)(2,1)S(1)} %copy-done.42), channel_id=1, source_target_pairs={{0,2},{1,3},{2,0},{3,1},{4,6},{5,7},{6,4},{7,5},{8,10},{9,11},{10,... | collective-permute-start | bytes 1597448 | tf_op jit(solution)/shard_map/ppermute | solution.py:835
  520.0 21.7 %collective-permute-start.48 = (bf16[208,1280]{1,0:T(8,128)(2,1)S(1)}, bf16[208,1280]{1,0:T(8,128)(2,1)}, u32[]{:S(2)}, u32[]{:S(2)}) collective-permute-start(bf16[208,1280]{1,0:T(8,128)(2,1)S(1)} %get-tuple-element.200.refs_0_), channel_id=1, source_target_pairs={{0,2},{1,3},{2,0},{3,1},{4,6},{5,7},{6,4},{7,5},{8,10},{9,11},{10,... | collective-permute-start | bytes 1597448 | tf_op jit(solution)/shard_map/ppermute | solution.py:835
  (146 other events, 1401.4 us)

commit v2 on v1

--- a/solution.py
+++ b/solution.py
@@ -19,7 +19,7 @@
 EPS = 1e-06
 F32 = jnp.float32
 BF16 = jnp.bfloat16
-ANY = pl.BlockSpec(memory_space=pl.ANY)
+ANY = pl.BlockSpec(memory_space=pltpu.HBM)
 highest = lax.Precision.HIGHEST
 
 
@@ -70,26 +70,53 @@
     return centred * rstd, rstd
 
 
-def norm_one_kernel(x_ref, valid_ref, gain_ref, shift_ref, out_ref):
-    xhat, _ = norm_parts(x_ref[...].astype(F32))
-    out_ref[...] = ((xhat * gain_ref[...] + shift_ref[...]) * valid_ref[...]).astype(BF16)
-
-
-def norm_one(x, valid, gain, shift):
-    rows, width = x.shape
+def prepare_kernel(order, places, lives, x_ref, top_ref, gain_ref, shift_ref, *outs):
+    rows_ref, normed_ref, grad_ref, valid_ref = outs
+    slot = order[pl.program_id(0)]
+    token = lax.broadcasted_iota(jnp.int32, (WTOK, 1), 0)
+    row = (token * 9363) >> 17
+    col = token - row * WIN
+    spot = places[slot]
+    high = spot // GRID * WIN
+    wide = spot % GRID * WIN
+    inside = (high + row < SIDE) & (wide + col < SIDE) & (lives[slot] == 1)
+    valid = jnp.where(inside, 1.0, 0.0).astype(F32)
+    x = x_ref[0]
+    xhat, _ = norm_parts(x.astype(F32))
+    normed = (xhat * gain_ref[...] + shift_ref[...]) * valid
+    empty = jnp.zeros((ROWS - WTOK, x.shape[1]), F32)
+    normed_ref[...] = jnp.concatenate([normed, empty], axis=0).astype(BF16)
+    grad = top_ref[0].astype(F32) * valid
+    grad_ref[...] = jnp.concatenate([grad, empty], axis=0).astype(BF16)
+    rows_ref[...] = jnp.concatenate([x.astype(F32), empty], axis=0).astype(BF16)
+    valid_ref[...] = jnp.concatenate([valid, empty[:, :1]], axis=0)
+
+
+def prepare(order, places, lives, x, top, gain, shift):
+    count = order.shape[0]
+    width = x.shape[2]
+    window = pl.BlockSpec((1, WTOK, width), lambda i, order, *_: (order[i], 0, 0))
+    block = pl.BlockSpec((ROWS, width), lambda i, *_: (i, 0))
     return pl.pallas_call(
-        norm_one_kernel,
-        grid=(rows // ROWS,),
-        in_specs=[
-            pl.BlockSpec((ROWS, width), lambda i: (i, 0)),
-            pl.BlockSpec((ROWS, 1), lambda i: (i, 0)),
-            whole(gain),
-            whole(shift),
-        ],
-        out_specs=pl.BlockSpec((ROWS, width), lambda i: (i, 0)),
-        out_shape=struct(x.shape, BF16),
-        name="norm_one",
-    )(x, valid, gain, shift)
+        prepare_kernel,
+        grid_spec=pltpu.PrefetchScalarGridSpec(
+            num_scalar_prefetch=3,
+            grid=(count,),
+            in_specs=[window, window, whole(gain), whole(shift)],
+            out_specs=[block] * 3 + [pl.BlockSpec((ROWS, 1), lambda i, *_: (i, 0))],
+        ),
+        out_shape=[struct((count * ROWS, width), BF16)] * 3 + [struct((count * ROWS, 1), F32)],
+        compiler_params=params(60),
+        name="prepare",
+    )(order, places, lives, x, top, gain, shift)
+
+
+def top_rows(shape):
+    return pl.BlockSpec(shape, lambda i: (0, 0))
+
+
+def row_block(shape, at):
+    return pl.BlockSpec(shape, lambda i: (at, 0))
 
 
 def total(refs, rows):
@@ -111,11 +138,16 @@
     normed_ref[...] = (xhat * gain_ref[...] + shift_ref[...]).astype(BF16)
 
 
-def norm_two(parts, x, bias, gain, shift):
+def norm_two(parts, x, at, bias, gain, shift):
+    shape = (parts[-1].shape[0], x.shape[1])
     return pl.pallas_call(
         partial(norm_two_kernel, len(parts)),
-        out_shape=(struct(x.shape, F32), struct(x.shape, BF16)),
-        compiler_params=params(32),
+        grid=(1,),
+        in_specs=[top_rows(shape)] * len(parts)
+        + [row_block(shape, at), whole(bias), whole(gain), whole(shift)],
+        out_specs=[top_rows(shape)] * 2,
+        out_shape=[struct(shape, F32), struct(shape, BF16)],
+        compiler_params=params(60),
         name="norm_two",
     )(*parts, x, bias, gain, shift)
 
@@ -127,11 +159,15 @@
     out_ref[...] = (valid_ref[...] * (after_ref[...] + branch)).astype(BF16)
 
 
-def finish(parts, after, valid, bias):
+def finish(parts, after, valid, at, bias):
     return pl.pallas_call(
         partial(finish_kernel, len(parts)),
+        grid=(1,),
+        in_specs=[top_rows(after.shape)] * (len(parts) + 1)
+        + [row_block((after.shape[0], 1), at), whole(bias)],
+        out_specs=top_rows(after.shape),
         out_shape=struct(after.shape, BF16),
-        compiler_params=params(32),
+        compiler_params=params(60),
         name="finish",
     )(*parts, after, valid, bias)
 
@@ -160,15 +196,16 @@
     sums_ref[3:4] = jnp.sum(top, axis=0, keepdims=True)
 
 
-def norm_two_back(parts, after, top, gain):
+def norm_two_back(parts, after, top, at, gain):
+    sums = struct((4, after.shape[1]), F32)
     return pl.pallas_call(
         partial(norm_two_back_kernel, len(parts)),
-        out_shape=(
-            struct(after.shape, F32),
-            struct(after.shape, BF16),
-            struct((4, after.shape[1]), F32),
-        ),
-        compiler_params=params(40),
+        grid=(1,),
+        in_specs=[top_rows(after.shape)] * (len(parts) + 1)
+        + [row_block(after.shape, at), whole(gain)],
+        out_specs=[top_rows(after.shape)] * 2 + [whole(sums)],
+        out_shape=[struct(after.shape, F32), struct(after.shape, BF16), sums],
+        compiler_params=params(60),
         name="norm_two_back",
     )(*parts, after, top, gain)
 
@@ -184,11 +221,17 @@
     sums_ref[1:2] = jnp.sum(upstream, axis=0, keepdims=True)
 
 
-def norm_one_back(parts, x, valid, grad, gain):
+def norm_one_back(parts, x, valid, at, grad, gain):
+    shape = grad.shape
+    sums = struct((2, shape[1]), F32)
     return pl.pallas_call(
         partial(norm_one_back_kernel, len(parts)),
-        out_shape=(struct(x.shape, BF16), struct((2, x.shape[1]), F32)),
-        compiler_params=params(40),
+        grid=(1,),
+        in_specs=[top_rows(shape)] * len(parts)
+        + [row_block(shape, at), row_block((shape[0], 1), at), top_rows(shape), whole(gain)],
+        out_specs=[top_rows(shape), whole(sums)],
+        out_shape=[struct(shape, BF16), sums],
+        compiler_params=params(60),
         name="norm_one_back",
     )(*parts, x, valid, grad, gain)
 
@@ -233,7 +276,7 @@
             ],
         ),
         out_shape=[struct((rows, wide), BF16)] * 3 + [struct((width, 4 * wide), BF16)],
-        compiler_params=params(48),
+        compiler_params=params(60),
         name="qkv",
     )(offsets, *pieces, x, bias)
 
@@ -279,7 +322,7 @@
 
 
 def bias_operand(q, rel_high, rel_low, counts):
-    table = dot(q, rel_high) + dot(q, rel_low)
+    table = (dot(q, rel_high) + dot(q, rel_low)) * (1.0 / SCALE)
     by_row = shift_lanes(table[:, :128], counts[0], False)
     by_col = shift_lanes(table[:, 128:], counts[1], False)
     is_row, is_col, is_last = lane_kind()
@@ -298,26 +341,27 @@
 
 
 def attend_kernel(heads, split, q_ref, k_ref, v_ref, rh_ref, rl_ref, mark_ref, w_ref, *outs):
-    mixed_ref, log_ref = outs[:2]
+    mixed_ref, shares_ref = outs[:2]
     q, k, v = q_ref[...], k_ref[...], v_ref[...]
     wide = q.shape[1]
     bias = bias_operand(q, rh_ref[...], rl_ref[...], shift_counts())
-    lane = lax.broadcasted_iota(jnp.int32, (ROWS, 128), 1)
-    logs = jnp.zeros((ROWS, 128), F32)
     parts = [None] * (wide // 128)
     for head, span in enumerate(head_spans(heads, wide)):
         mask = lane_mask(span)
         cut = slice(span[0], span[1])
-        scores = SCALE * dot_nt(q[:, cut], k[:, cut] * mask) + dot_nt(bias, mark_ref[head])
+        scores = dot_nt(
+            jnp.concatenate([q[:, cut], bias], axis=1),
+            jnp.concatenate([k[:, cut] * mask, mark_ref[head]], axis=1),
+        )
         top = jnp.max(scores, axis=-1, keepdims=True)
-        shifted = jnp.exp(scores - top)
+        shifted = jnp.exp(SCALE * (scores - top))
         norm = jnp.sum(shifted, axis=-1, keepdims=True)
         shares = (shifted * (1.0 / norm)).astype(BF16)
-        logs = jnp.where(lane == head, top + jnp.log(norm), logs)
+        shares_ref[:, head * 256 : head * 256 + ROWS] = shares
         add_lanes(parts, dot(shares, v[:, cut] * mask), span)
     mixed = jnp.concatenate(parts, axis=1).astype(BF16)
-    mixed_ref[...] = mixed
-    log_ref[...] = logs
+    cols = heads * HD
+    mixed_ref[...] = mixed[:, :cols]
     branch = dot_nt(mixed, w_ref[...]).astype(BF16)
     if split:
         keep_ref, send_ref = outs[2:]
@@ -369,25 +413,25 @@
             pl.BlockSpec((width, wide), lambda i: (0, 3)),
         ],
         out_specs=[
-            pl.BlockSpec((ROWS, wide), lambda i: (place(i), 0)),
-            pl.BlockSpec((ROWS, 128), lambda i: (place(i), 0)),
+            pl.BlockSpec((ROWS, heads * HD), lambda i: (place(i), 0)),
+            pl.BlockSpec((ROWS, heads * 256), lambda i: (place(i), 0)),
         ]
         + specs,
         out_shape=[
-            struct((windows * ROWS, wide), BF16),
-            struct((windows * ROWS, 128), F32),
+            struct((windows * ROWS, heads * HD), BF16),
+            struct((windows * ROWS, heads * 256), BF16),
         ]
         + shapes,
-        compiler_params=params(40),
+        compiler_params=params(60),
         name="attend",
     )(q, k, v, rel_high, rel_low, marks, weights)
 
 
 def attend_back_kernel(heads, windows, split, count, *refs):
     pieces = refs[:count]
-    q_ref, k_ref, v_ref, log_ref, rh_ref, rl_ref, mark_ref, w_ref = refs[count : count + 8]
-    grads_ref, branch_ref, rel_ref, sum_ref = refs[count + 8 : count + 12]
-    outs = refs[count + 12 :]
+    q_ref, k_ref, v_ref, shares_ref, rh_ref, mark_ref, w_ref = refs[count : count + 7]
+    grads_ref, branch_ref, rel_ref, sum_ref = refs[count + 7 : count + 11]
+    outs = refs[count + 11 :]
     step = pl.program_id(0)
 
     @pl.when(step == 0)
@@ -404,45 +448,45 @@
     wide = q.shape[1]
     top = branch_ref[pl.ds(pl.multiple_of(place * ROWS, 16), ROWS), :]
     grad_mixed = dot(top, w_ref[:, 3 * wide :]).astype(BF16)
-    rel_high, rel_low = rh_ref[...], rl_ref[...]
-    counts = shift_counts()
-    bias = bias_operand(q, rel_high, rel_low, counts)
     grad_q, grad_k, grad_v = ([None] * (wide // 128) for _ in range(3))
     grad_bias = None
     for head, span in enumerate(head_spans(heads, wide)):
         mask = lane_mask(span)
         cut = slice(span[0], span[1])
-        key = k[:, cut] * mask
-        query = q[:, cut]
+        size = span[1] - span[0]
         upper = grad_mixed[:, cut]
-        mark = mark_ref[head]
-        scores = SCALE * dot_nt(query, key) + dot_nt(bias, mark)
-        shares = jnp.exp(scores - log_ref[:, head : head + 1])
-        grad_shares = dot_nt(upper, v[:, cut] * mask)
-        inner = jnp.sum(shares * grad_shares, axis=-1, keepdims=True)
-        grad_scores = (shares * (grad_shares - inner)).astype(BF16)
-        add_lanes(grad_v, dot_tn(shares.astype(BF16), upper * mask), span)
-        add_lanes(grad_q, dot(grad_scores, key), span)
-        add_lanes(grad_k, dot_tn(grad_scores, query * mask), span)
-        part = dot(grad_scores, mark[:, :128])
+        rounded = shares_ref[:, head * 256 : head * 256 + ROWS]
+        shares = rounded.astype(F32)
+        weighted = shares * dot_nt(upper, v[:, cut] * mask)
+        inner = jnp.sum(weighted, axis=-1, keepdims=True)
+        grad_scores = (weighted - shares * inner).astype(BF16)
+        add_lanes(grad_v, dot_tn(rounded, upper * mask), span)
+        both = dot(
+            grad_scores,
+            jnp.concatenate([k[:, cut] * mask, mark_ref[head][:, :128]], axis=1),
+        )
+        add_lanes(grad_q, both[:, :size], span)
+        part = both[:, size:]
         grad_bias = part if grad_bias is None else grad_bias + part
+        add_lanes(grad_k, dot_tn(grad_scores, q[:, cut] * mask), span)
+    counts = shift_counts()
     is_row, is_col, _ = lane_kind()
     by_row = shift_lanes(jnp.where(is_row, grad_bias, 0.0), counts[0], True)
     by_col = shift_lanes(jnp.where(is_col, grad_bias, 0.0), counts[1], True)
-    high, low = split_two(jnp.concatenate([by_row, by_col], axis=1))
-    extra = dot_nt(high, rel_high) + dot_nt(low, rel_high) + dot_nt(high, rel_low)
-    extra = extra + dot_nt(low, rel_low)
-    rel_ref[...] += dot_tn(high, q) + dot_tn(low, q)
+    packed = jnp.concatenate([by_row, by_col], axis=1).astype(BF16)
+    extra = dot_nt(packed, rh_ref[...])
+    rel_ref[...] += dot_tn(packed, q)
     grad_q = (SCALE * jnp.concatenate(grad_q, axis=1) + extra).astype(BF16)
     grad_k = (SCALE * jnp.concatenate(grad_k, axis=1)).astype(BF16)
     grad_v = jnp.concatenate(grad_v, axis=1).astype(BF16)
-    partial_sum = None
+    cols = heads * HD
     for slot, grad in enumerate((grad_q, grad_k, grad_v)):
         cut = slice(slot * wide, (slot + 1) * wide)
-        grads_ref[:, cut] = grad
+        grads_ref[:, slot * cols : (slot + 1) * cols] = grad[:, :cols]
         sum_ref[:, cut] += jnp.sum(grad.astype(F32), axis=0, keepdims=True)
-        term = dot_nt(grad, w_ref[:, cut])
-        partial_sum = term if partial_sum is None else partial_sum + term
+    partial_sum = dot_nt(
+        jnp.concatenate([grad_q, grad_k, grad_v], axis=1), w_ref[:, : 3 * wide]
+    )
     result = partial_sum.astype(BF16)
     if split:
         keep_ref, send_ref = outs
@@ -459,7 +503,7 @@
 
 
 def attend_back(
-    heads, part, windows, split, pieces, q, k, v, logs, rel_high, rel_low, marks, weights
+    heads, part, windows, split, pieces, q, k, v, shares, rel_high, marks, weights
 ):
     wide = q.shape[1]
     width = weights.shape[0]
@@ -481,214 +525,274 @@
             block,
             block,
             block,
-            pl.BlockSpec((ROWS, 128), lambda i: (place(i), 0)),
+            pl.BlockSpec((ROWS, heads * 256), lambda i: (place(i), 0)),
             whole(rel_high),
-            whole(rel_low),
             whole(marks),
             whole(weights),
         ],
         out_specs=[
-            pl.BlockSpec((ROWS, 3 * wide), lambda i: (place(i), 0)),
+            pl.BlockSpec((ROWS, 3 * heads * HD), lambda i: (place(i), 0)),
             whole(branch),
             whole(rel),
             whole(sums),
         ]
         + specs,
-        out_shape=[struct((rows, 3 * wide), BF16), branch, rel, sums] + shapes,
-        compiler_params=params(56),
+        out_shape=[struct((rows, 3 * heads * HD), BF16), branch, rel, sums] + shapes,
+        compiler_params=params(60),
         name="attend_back",
-    )(*pieces, q, k, v, logs, rel_high, rel_low, marks, weights)
-
-
-def mlp_kernel(count, weights, chunk, offsets, *refs):
+    )(*pieces, q, k, v, shares, rel_high, marks, weights)
+
+
+def mlp_kernel(count, weights, split, offsets, order, *refs):
     pieces = refs[:count]
-    up_pieces = refs[count : count + weights]
-    down_pieces = refs[count + weights : count + 2 * weights]
-    refs = refs[count + 2 * weights :]
-    top_ref, bias_ref, active_ref, hidden_ref, normed_ref, sum_ref = refs[:6]
-    back_ref, out_ref, up, down, sems = refs[6:]
+    weight_pieces = refs[count : count + weights]
+    refs = refs[count + weights :]
+    top_ref, bias_ref, active_ref, hidden_ref, normed_ref, sum_ref, out_ref = refs[:7]
+    backs = refs[7:-3]
+    up, down, sems = refs[-3:]
     step = pl.program_id(0)
     block = top_ref.shape[0]
+    units = up.shape[1]
+    copies = []
+    for half, target in enumerate((down, up)):
+        copies.append([])
+        for index, piece in enumerate(weight_pieces):
+            rows = piece.shape[0]
+            start = pl.multiple_of(offsets[index], 16)
+            copies[half].append(
+                pltpu.make_async_copy(
+                    piece.at[:, half * units : (half + 1) * units],
+                    target.at[pl.ds(start, rows)],
+                    sems.at[half, index],
+                )
+            )
 
     @pl.when(step == 0)
     def _():
+        for copy in copies[1] + copies[0]:
+            copy.start()
         start = 0
         for piece in pieces:
             normed_ref[start : start + piece.shape[0]] = piece[...]
             start += piece.shape[0]
         sum_ref[...] = jnp.zeros(sum_ref.shape, F32)
-        assemble(offsets, up_pieces, up, sems.at[0])
-        assemble(offsets, down_pieces, down, sems.at[1])
-
-    normed = normed_ref[pl.ds(pl.multiple_of(step * block, 16), block), :]
-    top = top_ref[...]
-    units = up.shape[1]
-    width = up.shape[0]
-
-    def first(index, carry):
-        cut = pl.ds(pl.multiple_of(index * chunk, 128), chunk)
-        hidden = dot(normed, up[:, cut]) + bias_ref[:, cut]
-        half = 0.5 * (1.0 + lax.erf(hidden * (0.5**0.5)))
-        slope = half + hidden * jnp.exp(-0.5 * hidden * hidden) * float((2.0 * np.pi) ** -0.5)
-        active_ref[:, cut] = (hidden * half).astype(BF16)
-        grad = (dot(top, down[:, cut]) * slope).astype(BF16)
-        hidden_ref[:, cut] = grad
-        sum_ref[:, cut] += jnp.sum(grad.astype(F32), axis=0, keepdims=True)
-        return carry
-
-    lax.fori_loop(0, units // chunk, first, 0)
-    grad_hidden = hidden_ref[...]
-    active = active_ref[...]
-
-    def second(index, carry):
-        cut = pl.ds(pl.multiple_of(index * 256, 128), 256)
-        back_ref[:, cut] = dot_nt(grad_hidden, up[cut, :]).astype(BF16)
-        out_ref[:, cut] = dot_nt(active, down[cut, :]).astype(BF16)
-        return carry
-
-    lax.fori_loop(0, width // 256, second, 0)
-
-
-def mlp(offsets, pieces, up_pieces, down_pieces, top, part, bias):
+        for copy in copies[1]:
+            copy.wait()
+
+    place = 1 - step if split else step
+    normed = normed_ref[pl.ds(pl.multiple_of(place * block, 16), block), :]
+    hidden = dot(normed, up[...]) + bias_ref[...]
+
+    @pl.when(step == 0)
+    def _():
+        for copy in copies[0]:
+            copy.wait()
+
+    half = 0.5 * (1.0 + lax.erf(hidden * (0.5**0.5)))
+    slope = half + hidden * jnp.exp(-0.5 * hidden * hidden) * float((2.0 * np.pi) ** -0.5)
+    active = (hidden * half).astype(BF16)
+    active_ref[...] = active
+    grad = (dot(top_ref[...], down[...]) * slope).astype(BF16)
+    hidden_ref[...] = grad
+    sum_ref[...] += jnp.sum(grad.astype(F32), axis=0, keepdims=True)
+    back = dot_nt(grad, up[...]).astype(BF16)
+    if split:
+
+        @pl.when(step == 0)
+        def _():
+            backs[1][...] = back
+
+        @pl.when(step == 1)
+        def _():
+            backs[0][...] = back
+    else:
+        backs[0][...] = back
+    result = dot_nt(active, down[...]).astype(BF16)
+    for index in range(block // ROWS):
+        target = order[place * (block // ROWS) + index]
+        out_ref[pl.ds(pl.multiple_of(target * ROWS, 16), ROWS), :] = result[
+            index * ROWS : (index + 1) * ROWS
+        ]
+
+
+def mlp(offsets, order, pieces, weight_pieces, top, part, bias, split):
     rows = sum(piece.shape[0] for piece in pieces)
     width = pieces[0].shape[1]
-    units = up_pieces[0].shape[1]
+    units = weight_pieces[0].shape[1] // 2
     block = 2 * ROWS
     blocks = rows // block
-    chunk = 256 if units % 256 == 0 else 128
     normed = struct((rows, width), BF16)
     sums = struct((1, units), F32)
-    wide = pl.BlockSpec((block, units), lambda i, *_: (i, 0))
-    narrow = pl.BlockSpec((block, width), lambda i, *_: (i, 0))
+
+    def place(i):
+        return 1 - i if split else i
+
+    wide = pl.BlockSpec((block, units), lambda i, *_: (place(i), 0))
+    back = struct((block, width), BF16)
+    if split:
+        back_specs, back_shapes = [whole(back)] * 2, [back] * 2
+    else:
+        back_specs = [pl.BlockSpec((block, width), lambda i, *_: (i, 0))]
+        back_shapes = [normed]
     return pl.pallas_call(
-        partial(mlp_kernel, len(pieces), len(up_pieces), chunk),
+        partial(mlp_kernel, len(pieces), len(weight_pieces), split),
         grid_spec=pltpu.PrefetchScalarGridSpec(
-            num_scalar_prefetch=1,
+            num_scalar_prefetch=2,
             grid=(blocks,),
             in_specs=[whole(piece) for piece in pieces]
-            + [ANY] * (2 * len(up_pieces))
-            + [pl.BlockSpec((block, width), lambda i, *_: (part * blocks + i, 0)), whole(bias)],
-            out_specs=[wide, wide, whole(normed), whole(sums), narrow, narrow],
+            + [ANY] * len(weight_pieces)
+            + [
+                pl.BlockSpec((block, width), lambda i, *_: (part * blocks + place(i), 0)),
+                whole(bias),
+            ],
+            out_specs=[wide, wide, whole(normed), whole(sums), whole(normed)] + back_specs,
             scratch_shapes=[
                 pltpu.VMEM((width, units), BF16),
                 pltpu.VMEM((width, units), BF16),
-                pltpu.SemaphoreType.DMA((2, len(up_pieces))),
+                pltpu.SemaphoreType.DMA((2, len(weight_pieces))),
             ],
         ),
-        out_shape=[struct((rows, units), BF16)] * 2
-        + [normed, sums]
-        + [struct((rows, width), BF16)] * 2,
-        compiler_params=params(56),
+        out_shape=[struct((rows, units), BF16)] * 2 + [normed, sums, normed] + back_shapes,
+        compiler_params=params(60),
         name="mlp",
-    )(offsets, *pieces, *up_pieces, *down_pieces, top, bias)
-
-
-def weight_grad_kernel(groups, cols, chunk, starts, *refs):
-    count = sum(2 * len(group) for group in groups)
+    )(offsets, order, *pieces, *weight_pieces, top, bias)
+
+
+def weight_grad_kernel(sizes, share, targets, *refs):
+    count = 2 * sum(sizes)
     operands = refs[:count]
-    outs = refs[count:-2]
-    result, sems = refs[-2:]
-    width = result.shape[0]
-
-    def loop(index, carry):
-        rows = pl.ds(pl.multiple_of(index * chunk, 128), chunk)
-        at = 0
-        for slot, group in enumerate(groups):
-            for member, (low, high) in enumerate(group):
-                left, right = operands[at], operands[at + 1]
-                at += 2
-                term = dot_tn(left[:, rows], right[:, low:high])
-                value = term if member == 0 else value + term
-            result[rows, slot * cols : (slot + 1) * cols] = value[:, :cols].astype(BF16)
-        return carry
-
-    lax.fori_loop(0, width // chunk, loop, 0)
-    copies = []
-    for out in outs:
-        for index in range(out.shape[0]):
-            size = out.shape[1]
-            start = pl.multiple_of(starts[len(copies)], 16)
-            copies.append(
-                pltpu.make_async_copy(
-                    result.at[pl.ds(start, size)], out.at[index], sems.at[len(copies)]
-                )
-            )
-    for copy in copies:
-        copy.start()
-    for copy in copies:
-        copy.wait()
-
-
-def weight_grad(starts, groups, cols, shapes):
-    operands = []
+    send_ref, keep_ref, result, sems = refs[count:]
+    step = pl.program_id(0)
+    steps = pl.num_programs(0)
+    chunk = operands[0].shape[1]
+    pieces = chunk // share
+    base = pl.multiple_of(step * chunk, 16)
+    at, first = 0, 0
+    for size in sizes:
+        value = None
+        for _ in range(size):
+            left, right = operands[at], operands[at + 1]
+            at += 2
+            term = dot_tn(left[...], right[...])
+            value = term if value is None else value + term
+        span = value.shape[1]
+        result[pl.ds(base, chunk), first : first + span] = value.astype(BF16)
+        first += span
+
+    def copy(index, out, slot):
+        return pltpu.make_async_copy(
+            result.at[pl.ds(pl.multiple_of(index * share, 16), share)], out.at[slot], sems.at[index]
+        )
+
+    for piece in range(pieces):
+        index = step * pieces + piece
+        slot = targets[index]
+
+        @pl.when(slot < 4)
+        def _():
+            copy(index, send_ref, slot).start()
+
+        @pl.when(slot >= 4)
+        def _():
+            copy(index, keep_ref, slot - 4).start()
+
+    @pl.when(step == steps - 1)
+    def _():
+        for index in range(8):
+            copy(index, send_ref, 0).wait()
+
+
+def plain_grad_kernel(sizes, *refs):
+    count = 2 * sum(sizes)
+    operands, out_ref = refs[:count], refs[count]
+    at, first = 0, 0
+    for size in sizes:
+        value = None
+        for _ in range(size):
+            left, right = operands[at], operands[at + 1]
+            at += 2
+            term = dot_tn(left[...], right[...])
+            value = term if value is None else value + term
+        span = value.shape[1]
+        out_ref[:, first : first + span] = value.astype(BF16)
+        first += span
+
+
+def weight_grad(targets, groups, share):
+    operands, specs = [], []
+    chunk = 640 if targets is not None else 256
+    total_cols = 0
     for group in groups:
-        for left, right, _, _ in group:
+        for left, at, rows, right in group:
             operands += [left, right]
-    spans = [[(low, high) for _, _, low, high in group] for group in groups]
+            specs.append(pl.BlockSpec((rows, chunk), lambda i, *_, at=at: (at, i)))
+            specs.append(whole(right))
+        total_cols += group[0][3].shape[1]
     width = operands[0].shape[1]
-    count = sum(shape[0] for shape in shapes)
+    sizes = [len(group) for group in groups]
+    if targets is None:
+        return [
+            pl.pallas_call(
+                partial(plain_grad_kernel, sizes),
+                grid=(width // chunk,),
+                in_specs=specs,
+                out_specs=pl.BlockSpec((chunk, total_cols), lambda i: (i, 0)),
+                out_shape=struct((width, total_cols), BF16),
+                compiler_params=params(60),
+                name="weight_grad",
+            )(*operands)
+        ]
     return pl.pallas_call(
-        partial(weight_grad_kernel, spans, cols, 256),
+        partial(weight_grad_kernel, sizes, share),
+        grid_spec=pltpu.PrefetchScalarGridSpec(
+            num_scalar_prefetch=1,
+            grid=(width // chunk,),
+            in_specs=specs,
+            out_specs=[ANY] * 2,
+            scratch_shapes=[
+                pltpu.VMEM((width, total_cols), BF16),
+                pltpu.SemaphoreType.DMA((8,)),
+            ],
+        ),
+        out_shape=[struct((4, share, total_cols), BF16)] * 2,
+        compiler_params=params(60),
+        name="weight_grad",
+    )(targets, *operands)
+
+
+def place_kernel(part, order, *refs):
+    pieces, out_ref, buffer, sem = refs[:4], refs[-3], refs[-2], refs[-1]
+    rows = buffer.shape[0]
+    for me in range(4):
+
+        @pl.when(order[0] == me)
+        def _(me=me):
+            for index, step in enumerate((0, 2, 1, 3)):
+                start = (me ^ step) * WTOK
+                buffer[start : start + WTOK] = pieces[index][:WTOK].astype(F32)
+
+    copy = pltpu.make_async_copy(buffer, out_ref.at[pl.ds(part * rows, rows)], sem)
+    copy.start()
+    copy.wait()
+
+
+def place_windows(part, order, pieces, rows, held):
+    width = pieces[0].shape[1]
+    operands = list(pieces) + ([] if held is None else [held])
+    return pl.pallas_call(
+        partial(place_kernel, part),
         grid_spec=pltpu.PrefetchScalarGridSpec(
             num_scalar_prefetch=1,
             grid=(1,),
-            in_specs=[whole(operand) for operand in operands],
-            out_specs=[ANY] * len(shapes),
-            scratch_shapes=[
-                pltpu.VMEM((width, cols * len(groups)), BF16),
-                pltpu.SemaphoreType.DMA((count,)),
-            ],
+            in_specs=[whole(piece) for piece in pieces] + [ANY] * (len(operands) - 4),
+            out_specs=ANY,
+            scratch_shapes=[pltpu.VMEM((4 * WTOK, width), F32), pltpu.SemaphoreType.DMA(())],
         ),
-        out_shape=[struct(shape, BF16) for shape in shapes],
-        compiler_params=params(56),
-        name="weight_grad",
-    )(starts, *operands)
-
-
-def place_kernel(count, order, *refs):
-    pieces, out_ref, buffer = refs[:count], refs[count], refs[count + 1]
-    for me in range(4):
-
-        @pl.when(order[0] == me)
-        def _(me=me):
-            for index in range(count):
-                step = (0, 2, 1, 3)[index % 4]
-                start = (index // 4 * 4 + (me ^ step)) * WTOK
-                buffer[start : start + WTOK] = pieces[index][:WTOK].astype(F32)
-
-    out_ref[...] = buffer[...].astype(out_ref.dtype)
-
-
-def place_windows(order, pieces, dtype):
-    width = pieces[0].shape[1]
-    shape = (len(pieces) * WTOK, width)
-    return pl.pallas_call(
-        partial(place_kernel, len(pieces)),
-        grid_spec=pltpu.PrefetchScalarGridSpec(
-            num_scalar_prefetch=1,
-            grid=(1,),
-            in_specs=[whole(piece) for piece in pieces],
-            out_specs=pl.BlockSpec(shape, lambda *_: (0, 0)),
-            scratch_shapes=[pltpu.VMEM(shape, F32)],
-        ),
-        out_shape=struct(shape, dtype),
-        compiler_params=params(56),
+        out_shape=struct((rows, width), F32),
+        input_output_aliases={} if held is None else {5: 0},
+        compiler_params=params(60),
         name="place_windows",
-    )(order, *pieces)
-
-
-def token_valid(window_place, slot_live):
-    position = jnp.arange(WTOK, dtype=jnp.int32)
-    inner_row = position // WIN
-    inner_col = position % WIN
-    grid_row = (window_place // GRID)[:, None]
-    grid_col = (window_place % GRID)[:, None]
-    inside = (
-        (grid_row * WIN + inner_row[None, :] < SIDE)
-        & (grid_col * WIN + inner_col[None, :] < SIDE)
-        & (slot_live[:, None] == 1)
-    )
-    return jnp.where(inside, 1.0, 0.0).astype(F32)
+    )(order, *operands)
 
 
 def key_marks(heads):
@@ -703,17 +807,21 @@
 
 
 def rel_operand(rel_height, rel_width, heads, wide):
-    lanes = jnp.zeros((wide, 256), F32)
     high = rel_height[::-1].T
     flat = rel_width[::-1].T
+    lanes = jnp.zeros((wide, 256), F32)
+
+    def spread(block, row, lane):
+        below = wide - row - HD
+        return jnp.pad(block, ((row, below), (lane, 256 - lane - block.shape[1])))
+
     for head in range(heads):
-        rows = slice(head * HD, head * HD + HD)
-        lanes = lanes.at[rows, head * 32 : head * 32 + RELN].set(high)
         first = head * 32 + 16
         fit = min(RELN, 128 - first)
-        lanes = lanes.at[rows, 128 + first : 128 + first + fit].set(flat[:, :fit])
+        lanes = lanes + spread(high, head * HD, head * 32)
+        lanes = lanes + spread(flat[:, :fit], head * HD, 128 + first)
         if fit < RELN:
-            lanes = lanes.at[rows, 128 : 128 + RELN - fit].set(flat[:, fit:])
+            lanes = lanes + spread(flat[:, fit:], head * HD, 128)
     return split_two(lanes)
 
 
@@ -792,26 +900,17 @@
 
     if rings:
         offsets = []
-        starts = []
         for back in range(4):
             behind = (depth - back) % 4
             offsets += [share * (2 * behind + side), share * (2 * behind + 1 - side)]
-        for other in (0, 1):
-            for ahead in range(4):
-                target = 2 * ((depth + ahead) % 4) + (1 - side if other == 0 else side)
-                starts.append(share * target)
         offsets = jnp.stack(offsets).astype(jnp.int32)
-        starts = jnp.stack(starts).astype(jnp.int32)
-        grad_shapes = [(4, share), (4, share)]
     else:
         offsets = jnp.zeros((1,), jnp.int32)
-        starts = jnp.zeros((1,), jnp.int32)
-        grad_shapes = [(1, width)]
 
     def scatter(parts):
         if not rings:
             return lax.psum_scatter(
-                parts[0][0], "dp", scatter_dimension=0, tiled=True
+                parts[0], "dp", scatter_dimension=0, tiled=True
             ).astype(F32)
         send, keep = parts
         came = over_x(send)
@@ -848,33 +947,13 @@
             )
         return vector
 
-    def to_local(array):
-        array = array.reshape((slots, WTOK) + array.shape[1:])
-        tail = [(0, 0)] * (array.ndim - 2)
-        if rings:
-            shape = array.shape
-            array = array.reshape((halves, 2, 2) + shape[1:])
-            array = jnp.where(y_bit == 1, jnp.flip(array, 1), array)
-            array = jnp.where(core_bit == 1, jnp.flip(array, 2), array)
-            array = jnp.swapaxes(array, 1, 2).reshape(shape)
-        array = jnp.pad(array, [(0, padded - slots), (0, ROWS - WTOK)] + tail)
-        return array.reshape((padded * ROWS,) + array.shape[2:])
-
-    def own_slice(array, part):
-        if rings:
-            return array[part * part_rows : part * part_rows + own_rows]
-        return lax.dynamic_slice_in_dim(array, model_index * own_rows, own_rows, 0)
-
-    def to_global(pieces, dtype):
-        if rings:
-            return place_windows(model_index.astype(jnp.int32).reshape(1), pieces, dtype)
-        whole_rows = pieces[0].reshape(padded, ROWS, width)
-        return whole_rows[:slots, :WTOK].reshape(slots * WTOK, width).astype(dtype)
+    def own_slice(array):
+        rows = array.shape[0] // model_parts
+        return lax.dynamic_slice_in_dim(array, model_index * rows, rows, 0)
 
     first_piece = jnp.concatenate([qkv_weight[0], qkv_weight[1], qkv_weight[2], proj_weight.T], 1)
     first_weights = gather(first_piece)
-    down_pieces = gather(down_weight.T)
-    up_pieces = gather(up_weight)
+    other_weights = gather(jnp.concatenate([down_weight.T, up_weight], 1))
 
     row = lambda v: v.reshape(1, -1)
     gain_one, shift_one = row(norm_one_gain), row(norm_one_shift)
@@ -886,10 +965,43 @@
     rel_high, rel_low = rel_operand(rel_height, rel_width, heads, wide)
     marks = jnp.asarray(key_marks(heads))
 
-    valid = to_local(token_valid(window_place, slot_live).reshape(slots * WTOK, 1))
-    rows_in = to_local(block_input)
-    grad_top = (to_local(cotangent) * valid.astype(BF16)).astype(BF16)
-    normed = norm_one(rows_in, valid, gain_one, shift_one)
+    steps = (0, 2, 1, 3)
+    if rings:
+        local = [model_index ^ step for step in steps]
+        places = [4 * part + spot for part in range(halves) for spot in local]
+    else:
+        local = [jnp.int32(spot) for spot in range(windows)]
+        places = local
+    local = jnp.stack(local).astype(jnp.int32)
+    places = jnp.stack(places).astype(jnp.int32)
+    if rings:
+        targets = []
+        for d in range(8):
+            ahead = (d // 2 - depth) % 4
+            targets.append(ahead + jnp.where(d % 2 == side, 4, 0))
+        targets = jnp.stack(targets).astype(jnp.int32)
+    else:
+        targets = None
+
+    def by_window(array):
+        array = array.reshape((slots, WTOK) + array.shape[1:])
+        return jnp.pad(array, [(0, padded - slots)] + [(0, 0)] * (array.ndim - 1))
+
+    rows_in, normed, grad_top, valid = prepare(
+        places,
+        jnp.pad(window_place, (0, padded - slots)),
+        jnp.pad(slot_live, (0, padded - slots)),
+        by_window(block_input),
+        by_window(cotangent),
+        gain_one,
+        shift_one,
+    )
+    if rings:
+        own_in, own_top, own_valid = rows_in, grad_top, valid
+        at = [4 * part for part in range(halves)]
+    else:
+        own_in, own_top, own_valid = own_slice(rows_in), own_slice(grad_top), own_slice(valid)
+        at = [0]
 
     q, k, v, weights = project(offsets, first_weights, normed, bias_qkv, cols, wide)
     attended = [
@@ -900,50 +1012,53 @@
     for part in range(halves):
         parts = rows_scatter(attended[part][2:])
         after, normed_two = norm_two(
-            parts, own_slice(rows_in, part), row(proj_bias), gain_two, shift_two
+            parts, own_in, at[part], row(proj_bias), gain_two, shift_two
         )
         afters.append(after)
         normed_twos.append(rows_gather(normed_two))
 
     mlps = [
-        mlp(offsets, normed_twos[part], up_pieces, down_pieces, grad_top, part, up_local)
+        mlp(
+            offsets,
+            local,
+            normed_twos[part],
+            other_weights,
+            grad_top,
+            part,
+            up_local,
+            bool(split),
+        )
         for part in range(halves)
     ]
-
-    def split_rows(array):
-        return [array[: 2 * ROWS], array[2 * ROWS :]] if rings else [array]
-
     grad_afters, branches, sums_two = [], [], []
     for part in range(halves):
-        parts = rows_scatter(split_rows(mlps[part][4]))
+        parts = rows_scatter(mlps[part][5:])
         grad_after, branch, sums = norm_two_back(
-            parts, afters[part], own_slice(grad_top, part), gain_two
+            parts, afters[part], own_top, at[part], gain_two
         )
         grad_afters.append(grad_after)
         branches.append(rows_gather(branch))
         sums_two.append(sums)
     out_pieces = []
     for part in range(halves):
-        parts = rows_scatter(split_rows(mlps[part][5]))
-        own = finish(parts, afters[part], own_slice(valid, part), row(down_bias))
-        out_pieces += rows_gather(own)
-    block_output = to_global(out_pieces, BF16)
-
-    top_parts = [
-        grad_top[part * part_rows : (part + 1) * part_rows] for part in range(halves)
-    ]
-    normed_parts = [
-        normed[part * part_rows : (part + 1) * part_rows] for part in range(halves)
-    ]
-    shapes = [shape + (units,) for shape in grad_shapes]
+        result = lax.psum_scatter(mlps[part][4], "mp", scatter_dimension=0, tiled=True)
+        own = finish([result], afters[part], own_valid, at[part], row(down_bias))
+        out_pieces.append(own)
+    full = lax.all_gather(jnp.concatenate(out_pieces, 0), "mp", axis=0, tiled=True)
+    if rings:
+        full = full.reshape(4, halves, ROWS, width).swapaxes(0, 1)
+    full = full.reshape(padded, ROWS, width)
+    block_output = full[:slots, :WTOK].reshape(slots * WTOK, width)
+
+    blocks = [(part, part_rows) for part in range(halves)]
     down_grad = scatter(
         weight_grad(
-            starts, [[(top_parts[i], mlps[i][0], 0, units) for i in range(halves)]], units, shapes
+            targets, [[(grad_top, *blocks[i], mlps[i][0]) for i in range(halves)]], share
         )
     )
     up_grad = scatter(
         weight_grad(
-            starts, [[(mlps[i][2], mlps[i][1], 0, units) for i in range(halves)]], units, shapes
+            targets, [[(mlps[i][2], 0, part_rows, mlps[i][1]) for i in range(halves)]], share
         )
     )
 
@@ -959,32 +1074,30 @@
             v,
             attended[part][1],
             rel_high,
-            rel_low,
             marks,
             weights,
         )
         for part in range(halves)
     ]
-    in_pieces, sums_one = [], []
+    sums_one = []
+    input_grad = None
     for part in range(halves):
         parts = rows_scatter(backs[part][4:])
         own, sums = norm_one_back(
-            parts, own_slice(rows_in, part), own_slice(valid, part), grad_afters[part], gain_one
+            parts, own_in, own_valid, at[part], grad_afters[part], gain_one
         )
         sums_one.append(sums)
-        in_pieces += rows_gather(own)
-    input_grad = to_global(in_pieces, F32)
+        gathered = rows_gather(own)
+        if rings:
+            input_grad = place_windows(part, local, gathered, slots * WTOK, input_grad)
+        else:
+            full = gathered[0].reshape(padded, ROWS, width)[:slots, :WTOK]
+            input_grad = full.reshape(slots * WTOK, width).astype(F32)
     groups = [
-        [
-            (normed_parts[i], backs[i][0], slot * wide, (slot + 1) * wide)
-            for i in range(halves)
-        ]
-        for slot in range(3)
+        [(normed, *blocks[i], backs[i][0]) for i in range(halves)],
+        [(backs[i][1], 0, part_rows, attended[i][0]) for i in range(halves)],
     ]
-    groups.append([(backs[i][1], attended[i][0], 0, wide) for i in range(halves)])
-    first_grad = scatter(
-        weight_grad(starts, groups, cols, [shape + (4 * cols,) for shape in grad_shapes])
-    )
+    first_grad = scatter(weight_grad(targets, groups, share))
 
     two = add_all(sums_two)
     one = add_all(sums_one)
@@ -1010,9 +1123,8 @@
             at += size
         return outs
 
-    two_sums, up_bias_grad = sum_bundle([two, up_full])
-    one_sums, qv_bias_grad, height_grad, width_grad = sum_bundle(
-        [one, qv_full, rel_sums[0], rel_sums[1]]
+    two_sums, up_bias_grad, one_sums, qv_bias_grad, height_grad, width_grad = sum_bundle(
+        [two, up_full, one, qv_full, rel_sums[0], rel_sums[1]]
     )
     qkv_grad = jnp.stack([first_grad[:, slot * cols : (slot + 1) * cols] for slot in range(3)])
     proj_grad = first_grad[:, 3 * cols :].T

time: 567 us -> 575 us (1.014)
  waiting for transfers between devices: 111 us -> 218 us
  local copies, waits for them, and re-layouts: 107 us -> 44 us
  starting transfers between devices: 66.8 us -> 47.7 us
  Pallas kernels: 225 us -> 209 us
  other arithmetic: 49.9 us -> 35.1 us
  between operations: 2.17 us -> 14.9 us
    ppermute x8 -> x6, waiting for transfers between devices: 3.01 us -> 47.9 us  [rows_scatter(): return [keep, came, over_y(passed)]]
    ppermute x12 -> x8, waiting for transfers between devices: 8.95 us -> 41.6 us  [gather(): return [item for held in line for item in (held, over_x(held))]]
    unnamed x225 -> x119, local copies, waits for them, and re-layouts: 39.7 us -> 10.7 us
    ppermute x6 -> x3, waiting for transfers between devices: 31.7 us -> 3.34 us  [sum_all(): lax.ppermute(vector, 'dp', [(d, d ^ step) for d in range(8)])]
    ppermute x8 -> x6, waiting for transfers between devices: 15 us -> 43 us  [rows_gather(): across = over_y(own)]
    ppermute x9 -> x6, waiting for transfers between devices: 31 us -> 56.7 us  [gather(): line.append(over_z(line[-1]))]
    slice x12 -> x2, local copies, waits for them, and re-layouts: 20.2 us -> 2.35 us  [the longest x1 2.27 us: body(): block_output = full[:slots, :WTOK].reshape(slots * WTOK, width)]
    reshape x1 -> x4, local copies, waits for them, and re-layouts: 1.21 us -> 17.2 us  [the longest x2 9.84 us: by_window(): array = array.reshape((slots, WTOK) + array.shape[1:])]
  transfers between devices with their start and end apart: 83 -> 64, of which waited for: 21 -> 22; matrix products, arithmetic and copies ran while one was open for 20% -> 10% of each run, Pallas kernels for 36% -> 33%
where the time goes in v2:
time: 575 us; the launch traced here: 568 us
  waiting for transfers between devices  218 us (38%)
  Pallas kernels  209 us (36%)
  starting transfers between devices  47.7 us (8%)
  local copies, waits for them, and re-layouts  44 us (8%)
  other arithmetic  35.1 us (6%)
  between operations  14.9 us (3%)
    ppermute x6, waiting for transfers between devices, gather(): line.append(over_z(line[-1]))  56.7 us
    ppermute x6, waiting for transfers between devices, rows_scatter(): return [keep, came, over_y(passed)]  47.9 us
    ppermute x6, waiting for transfers between devices, rows_gather(): across = over_y(own)  43 us
    pallas_call x2, Pallas kernels, mlp(): pl.pallas_call(partial(mlp_kernel, len(pieces), len(weight_pieces), split...  41.8 us
    ppermute x8, waiting for transfers between devices, gather(): return [item for held in line for item in (held, over_x(held))]  41.6 us
    pallas_call x3, Pallas kernels, weight_grad(): pl.pallas_call(partial(weight_grad_kernel, sizes, share), grid_spec=pltpu...  40.6 us
    pallas_call x2, Pallas kernels, attend_back(): pl.pallas_call(partial(attend_back_kernel, heads, windows, split, len(pie...  37.1 us
    pallas_call x2, Pallas kernels, attend(): pl.pallas_call(partial(attend_kernel, heads, split), grid=(windows,), in_...  27.4 us
  transfers between devices with their start and end apart: 64, of which 22 were waited for; matrix products, arithmetic and copies ran while one was open for 10% of the time, Pallas kernels for 33%

profile of v2, /device:TPU:0, one launch (start us, length us, event | category | flops | bytes accessed | tf_op | source)
XLA Modules:
  0.0 567.9 jit_solution(16852811285334964269)
XLA Ops:
  9.6 3.1 collective-permute-start.1
  12.7 11.5 %collective-permute-done.1.refs_2_ = bf16[160,1280]{1,0:T(8,128)(2,1)S(1)} collective-permute-done((bf16[160,1280]{1,0:T(8,128)(2,1)S(1)}, bf16[160,1280]{1,0:T(8,128)(2,1)S(1)}, u32[]{:S(2)}, u32[]{:S(2)}) %collective-permute-start.1) | collective-permute-done | bytes 409632 | tf_op jit(solution)/shard_map/ppermute | solution.py:898
  25.6 11.0 %collective-permute-done.3.refs_4_ = bf16[160,1280]{1,0:T(8,128)(2,1)S(1)} collective-permute-done((bf16[160,1280]{1,0:T(8,128)(2,1)S(1)}, bf16[160,1280]{1,0:T(8,128)(2,1)S(1)}, u32[]{:S(2)}, u32[]{:S(2)}) %collective-permute-start.3) | collective-permute-done | bytes 409632 | tf_op jit(solution)/shard_map/ppermute | solution.py:898
  39.0 11.9 %collective-permute-done.5.refs_6_ = bf16[160,1280]{1,0:T(8,128)(2,1)} collective-permute-done((bf16[160,1280]{1,0:T(8,128)(2,1)S(1)}, bf16[160,1280]{1,0:T(8,128)(2,1)}, u32[]{:S(2)}, u32[]{:S(2)}) %collective-permute-start.5) | collective-permute-done | bytes 409632 | tf_op jit(solution)/shard_map/ppermute | solution.py:898
  54.5 4.9 reshape.167.x_ref
  59.4 4.9 reshape.168.top_ref
  65.0 12.1 %prepare.1 = (bf16[1664,1280]{1,0:T(8,128)(2,1)}, bf16[1664,1280]{1,0:T(8,128)(2,1)}, bf16[1664,1280]{1,0:T(8,128)(2,1)}, f32[1664,1]{1,0:T(8,128)}) custom-call(s32[8]{0:T(128)} %stack.121.order, s32[8]{0:T(128)} %places.1, s32[8]{0:T(128)} %lives.1, bf16[8,196,1280]{2,1,0:T(8,128)(2,1)} %reshape.167.x_ref, bf16[8,196,1280]{2,1,0:T(8,128)(2,1)} %reshape.168.top_ref, ...), custom_call_target="tpu_custom_call" | custom-call | tf_op jit(solution)/shard_map/prepare/pallas_call | solution.py:100
  78.6 14.0 %qkv.1 = (bf16[1664,384]{1,0:T(8,128)(2,1)}, bf16[1664,384]{1,0:T(8,128)(2,1)}, bf16[1664,384]{1,0:T(8,128)(2,1)}, bf16[1280,1536]{1,0:T(8,128)(2,1)}) custom-call(s32[8]{0:T(128)} %stack.111.offsets, bf16[160,1280]{1,0:T(8,128)(2,1)} %copy-done.18, bf16[160,1280]{1,0:T(8,128)(2,1)} %collective-permute-done.refs_1_, bf16[160,1280]{1,0:T(8,128)(2,1)} %copy-done.41, ...), custom_call_target="tpu_custom_call" | custom-call | tf_op jit(solution)/shard_map/qkv/pallas_call | solution.py:265
  92.7 13.6 %attend.2 = (bf16[832,320]{1,0:T(8,128)(2,1)}, bf16[832,1024]{1,0:T(8,128)(2,1)}, bf16[416,1280]{1,0:T(8,128)(2,1)}, bf16[416,1280]{1,0:T(8,128)(2,1)}) custom-call(bf16[1664,384]{1,0:T(8,128)(2,1)} %get-tuple-element.79.q_ref.refs_4_, bf16[1664,384]{1,0:T(8,128)(2,1)} %get-tuple-element.80.k_ref.refs_5_, bf16[1664,384]{1,0:T(8,128)(2,1)} %get-tuple-element.81.v_ref.refs_6_, ...), custom_call_target="tpu_custom_call" | custom-call | tf_op jit(solution)/shard_map/attend/pallas_call | solution.py:403
  106.5 22.4 %collective-permute-done.15.refs_8_ = bf16[160,2560]{1,0:T(8,128)(2,1)S(1)} collective-permute-done((bf16[160,2560]{1,0:T(8,128)(2,1)S(1)}, bf16[160,2560]{1,0:T(8,128)(2,1)S(1)}, u32[]{:S(2)}, u32[]{:S(2)}) %collective-permute-start.15) | collective-permute-done | bytes 819232 | tf_op jit(solution)/shard_map/ppermute | solution.py:898
  134.7 9.8 %collective-permute-done.8.refs_2_ = bf16[208,1280]{1,0:T(8,128)(2,1)S(1)} collective-permute-done((bf16[208,1280]{1,0:T(8,128)(2,1)S(1)}, bf16[208,1280]{1,0:T(8,128)(2,1)S(1)}, u32[]{:S(2)}, u32[]{:S(2)}) %collective-permute-start.8) | collective-permute-done | bytes 532512 | tf_op jit(solution)/shard_map/ppermute | solution.py:929
  145.2 3.0 norm_two.2
  152.8 8.6 %collective-permute-done.9.refs_1_ = bf16[208,1280]{1,0:T(8,128)(2,1)} collective-permute-done((bf16[208,1280]{1,0:T(8,128)(2,1)}, bf16[208,1280]{1,0:T(8,128)(2,1)}, u32[]{:S(2)}, u32[]{:S(2)}) %collective-permute-start.9) | collective-permute-done | bytes 532512 | tf_op jit(solution)/shard_map/ppermute | solution.py:934
  163.5 7.6 %collective-permute-done.14.refs_7_ = bf16[160,2560]{1,0:T(8,128)(2,1)} collective-permute-done((bf16[160,2560]{1,0:T(8,128)(2,1)S(1)}, bf16[160,2560]{1,0:T(8,128)(2,1)}, u32[]{:S(2)}, u32[]{:S(2)}) %collective-permute-start.14) | collective-permute-done | bytes 819232 | tf_op jit(solution)/shard_map/ppermute | solution.py:899
  171.1 17.6 %collective-permute-done.16.refs_9_ = bf16[160,2560]{1,0:T(8,128)(2,1)} collective-permute-done((bf16[160,2560]{1,0:T(8,128)(2,1)S(1)}, bf16[160,2560]{1,0:T(8,128)(2,1)}, u32[]{:S(2)}, u32[]{:S(2)}) %collective-permute-start.16) | collective-permute-done | bytes 819232 | tf_op jit(solution)/shard_map/ppermute | solution.py:899
  188.6 16.0 %collective-permute-done.18.refs_11_ = bf16[160,2560]{1,0:T(8,128)(2,1)} collective-permute-done((bf16[160,2560]{1,0:T(8,128)(2,1)S(1)}, bf16[160,2560]{1,0:T(8,128)(2,1)}, u32[]{:S(2)}, u32[]{:S(2)}) %collective-permute-start.18) | collective-permute-done | bytes 819232 | tf_op jit(solution)/shard_map/ppermute | solution.py:899
  205.4 20.9 %mlp.2 = (bf16[832,1280]{1,0:T(8,128)(2,1)}, bf16[832,1280]{1,0:T(8,128)(2,1)}, bf16[832,1280]{1,0:T(8,128)(2,1)}, f32[1,1280]{1,0:T(1,128)}, bf16[832,1280]{1,0...) custom-call(s32[8]{0:T(128)} %stack.111.offsets, s32[4]{0:T(128)} %pad_add_fusion.1.order, ...), custom_call_target="tpu_custom_call" | custom-call | tf_op jit(solution)/shard_map/mlp/pallas_call | solution.py:637
  226.9 13.8 %attend.3 = (bf16[832,320]{1,0:T(8,128)(2,1)}, bf16[832,1024]{1,0:T(8,128)(2,1)}, bf16[416,1280]{1,0:T(8,128)(2,1)}, bf16[416,1280]{1,0:T(8,128)(2,1)}) custom-call(bf16[1664,384]{1,0:T(8,128)(2,1)} %get-tuple-element.79.q_ref.refs_4_, bf16[1664,384]{1,0:T(8,128)(2,1)} %get-tuple-element.80.k_ref.refs_5_, bf16[1664,384]{1,0:T(8,128)(2,1)} %get-tuple-element.81.v_ref.refs_6_, ...), custom_call_target="tpu_custom_call" | custom-call | tf_op jit(solution)/shard_map/attend/pallas_call | solution.py:403
  240.7 2.9 collective-permute-done.19.refs_1_
  245.7 22.2 %collective-permute-done.20.refs_2_ = bf16[208,1280]{1,0:T(8,128)(2,1)S(1)} collective-permute-done((bf16[208,1280]{1,0:T(8,128)(2,1)S(1)}, bf16[208,1280]{1,0:T(8,128)(2,1)S(1)}, u32[]{:S(2)}, u32[]{:S(2)}) %collective-permute-start.20) | collective-permute-done | bytes 532512 | tf_op jit(solution)/shard_map/ppermute | solution.py:929
  268.7 3.0 norm_two.3
  272.1 13.7 %collective-permute-done.21.refs_1_ = bf16[208,1280]{1,0:T(8,128)(2,1)S(1)} collective-permute-done((bf16[208,1280]{1,0:T(8,128)(2,1)}, bf16[208,1280]{1,0:T(8,128)(2,1)S(1)}, u32[]{:S(2)}, u32[]{:S(2)}) %collective-permute-start.21) | collective-permute-done | bytes 532512 | tf_op jit(solution)/shard_map/ppermute | solution.py:934
  288.6 20.9 %mlp.3 = (bf16[832,1280]{1,0:T(8,128)(2,1)}, bf16[832,1280]{1,0:T(8,128)(2,1)}, bf16[832,1280]{1,0:T(8,128)(2,1)}, f32[1,1280]{1,0:T(1,128)}, bf16[832,1280]{1,0...) custom-call(s32[8]{0:T(128)} %stack.111.offsets, s32[4]{0:T(128)} %pad_add_fusion.1.order, ...), custom_call_target="tpu_custom_call" | custom-call | tf_op jit(solution)/shard_map/mlp/pallas_call | solution.py:637
  310.7 12.1 %weight_grad.5 = (bf16[4,160,1280]{2,1,0:T(8,128)(2,1)}, bf16[4,160,1280]{2,1,0:T(8,128)(2,1)}) custom-call(s32[8]{0:T(128)} %stack.131.targets, bf16[1664,1280]{1,0:T(8,128)(2,1)} %get-tuple-element.87.refs_12_.refs_4_.refs_0_.refs_2_, bf16[832,1280]{1,0:T(8,128)(2,1)} %get-tuple-element.136.refs_1_, ...), custom_call_target="tpu_custom_call" | custom-call | tf_op jit(solution)/shard_map/weight_grad/pallas_call | solution.py:745
  328.9 12.6 %weight_grad.4 = (bf16[4,160,1280]{2,1,0:T(8,128)(2,1)}, bf16[4,160,1280]{2,1,0:T(8,128)(2,1)}) custom-call(s32[8]{0:T(128)} %stack.131.targets, bf16[832,1280]{1,0:T(8,128)(2,1)} %get-tuple-element.130.refs_0_, bf16[832,1280]{1,0:T(8,128)(2,1)} %get-tuple-element.131.refs_1_, bf16[832,1280]{1,0:T(8,128)(2,1)} %get-tuple-element.132.refs_2_, ...), custom_call_target="tpu_custom_call" | custom-call | tf_op jit(solution)/shard_map/weight_grad/pallas_call | solution.py:745
  343.0 4.1 norm_two_back.2
  347.6 15.9 %collective-permute-done.35.refs_2_ = bf16[208,1280]{1,0:T(8,128)(2,1)S(1)} collective-permute-done((bf16[208,1280]{1,0:T(8,128)(2,1)S(1)}, bf16[208,1280]{1,0:T(8,128)(2,1)S(1)}, u32[]{:S(2)}, u32[]{:S(2)}) %collective-permute-start.35) | collective-permute-done | bytes 532512 | tf_op jit(solution)/shard_map/ppermute | solution.py:929
  364.4 4.2 norm_two_back.3
  369.4 6.6 %collective-permute-done.26.refs_1_ = bf16[208,1280]{1,0:T(8,128)(2,1)S(1)} collective-permute-done((bf16[208,1280]{1,0:T(8,128)(2,1)}, bf16[208,1280]{1,0:T(8,128)(2,1)S(1)}, u32[]{:S(2)}, u32[]{:S(2)}) %collective-permute-start.26) | collective-permute-done | bytes 532512 | tf_op jit(solution)/shard_map/ppermute | solution.py:934
  376.7 9.6 %collective-permute-done.36.refs_1_ = bf16[208,1280]{1,0:T(8,128)(2,1)S(1)} collective-permute-done((bf16[208,1280]{1,0:T(8,128)(2,1)}, bf16[208,1280]{1,0:T(8,128)(2,1)S(1)}, u32[]{:S(2)}, u32[]{:S(2)}) %collective-permute-start.36) | collective-permute-done | bytes 532512 | tf_op jit(solution)/shard_map/ppermute | solution.py:934
  388.0 18.5 %attend_back.2 = (bf16[832,960]{1,0:T(8,128)(2,1)}, bf16[832,1280]{1,0:T(8,128)(2,1)}, f32[256,384]{1,0:T(8,128)}, f32[1,1152]{1,0:T(1,128)}, bf16[416,1280]{1,0:T(8,128)(2,1)}, /*index=5*/bf16[416,1280]{1,0:T(8,128)(2,1)}) custom-call(bf16[208,1280]{1,0:T(8,128)(2,1)} %get-tuple-element.98.refs_0_, bf16[208,1280]{1,0:T(8,128)(2,1)} %copy-done.31, ...), custom_call_target="tpu_custom_call" | custom-call | tf_op jit(solution)/shard_map/attend_back/pallas_call | solution.py:520
  411.5 18.6 %attend_back.3 = (bf16[832,960]{1,0:T(8,128)(2,1)}, bf16[832,1280]{1,0:T(8,128)(2,1)}, f32[256,384]{1,0:T(8,128)}, f32[1,1152]{1,0:T(1,128)}, bf16[416,1280]{1,0:T(8,128)(2,1)}, /*index=5*/bf16[416,1280]{1,0:T(8,128)(2,1)}) custom-call(bf16[208,1280]{1,0:T(8,128)(2,1)} %get-tuple-element.106.refs_0_, bf16[208,1280]{1,0:T(8,128)(2,1)} %copy-done.27, ...), custom_call_target="tpu_custom_call" | custom-call | tf_op jit(solution)/shard_map/attend_back/pallas_call | solution.py:520
  442.0 2.3 finish.2
  444.4 2.4 finish.3
  452.0 15.9 %weight_grad.3 = (bf16[4,160,1280]{2,1,0:T(8,128)(2,1)}, bf16[4,160,1280]{2,1,0:T(8,128)(2,1)}) custom-call(s32[8]{0:T(128)} %stack.131.targets, bf16[1664,1280]{1,0:T(8,128)(2,1)} %get-tuple-element.78.refs_8_.refs_0_.refs_2_, bf16[832,960]{1,0:T(8,128)(2,1)} %get-tuple-element.122.refs_1_, bf16[1664,1280]{1,0:T(8,128)(2,1)} %get-tuple-element.78.refs_8_.refs_0_.refs_2_, ...), custom_call_target="tpu_custom_call" | custom-call | tf_op jit(solution)/shard_map/weight_grad/pallas_call | solution.py:745
  469.5 3.7 norm_one_back.2
  473.1 3.7 norm_one_back.3
  483.5 3.4 collective-permute-done.45
  488.3 16.9 %collective-permute-done.49 = bf16[4,160,1280]{2,1,0:T(8,128)(2,1)} collective-permute-done((bf16[4,160,1280]{2,1,0:T(8,128)(2,1)}, bf16[4,160,1280]{2,1,0:T(8,128)(2,1)}, u32[]{:S(2)}, u32[]{:S(2)}) %collective-permute-start.49) | collective-permute-done | bytes 1638432 | tf_op jit(solution)/shard_map/ppermute | solution.py:916
  509.1 2.2 fusion.2
  514.4 5.1 collective-permute-start.48
  524.3 2.3 collective-permute-done.48
  528.5 4.3 collective-permute-done.41.refs_1_
  537.7 4.5 place_windows.2.refs_4_
  543.8 4.5 place_windows.3
  551.5 2.5 copy.40
  554.0 2.3 slice.321
  556.2 4.9 reshape.179
  (305 shorter events, 100.4 us)
Async XLA Ops:
  7.2 434.8 %reduce-scatter.3.cloned.1.call-start = ((), (), s32[]{:S(2)}) async-start(), calls=%async_computation.2 | async-start | bytes 2662400 | tf_op jit(solution)/shard_map/reduce_scatter | solution.py:1044
  9.6 14.6 %collective-permute-start.1 = (bf16[160,1280]{1,0:T(8,128)(2,1)S(1)}, bf16[160,1280]{1,0:T(8,128)(2,1)S(1)}, u32[]{:S(2)}, u32[]{:S(2)}) collective-permute-start(bf16[160,1280]{1,0:T(8,128)(2,1)S(1)} %concatenate.15.refs_0_), channel_id=1, source_target_pairs={{0,8},{4,12},{8,16},{12,20},{16,24},{20,28},{24,0},{28,4},{1,9},{5... | collective-permute-start | bytes 1228808 | tf_op jit(solution)/shard_map/ppermute | solution.py:898
  24.1 54.5 %collective-permute-start = (bf16[160,1280]{1,0:T(8,128)(2,1)S(1)}, bf16[160,1280]{1,0:T(8,128)(2,1)}, u32[]{:S(2)}, u32[]{:S(2)}) collective-permute-start(bf16[160,1280]{1,0:T(8,128)(2,1)S(1)} %concatenate.15.refs_0_), channel_id=1, source_target_pairs={{0,4},{4,0},{8,12},{12,8},{16,20},{20,16},{24,28},{28,24},{1,5},{5... | collective-permute-start | bytes 1228808 | tf_op jit(solution)/shard_map/ppermute | solution.py:899
  36.6 14.3 %collective-permute-start.5 = (bf16[160,1280]{1,0:T(8,128)(2,1)S(1)}, bf16[160,1280]{1,0:T(8,128)(2,1)}, u32[]{:S(2)}, u32[]{:S(2)}) collective-permute-start(bf16[160,1280]{1,0:T(8,128)(2,1)S(1)} %collective-permute-done.3.refs_4_), channel_id=1, source_target_pairs={{0,8},{4,12},{8,16},{12,20},{16,24},{20,28},{24,0},{28,4},{1,9},{5... | collective-permute-start | bytes 1228808 | tf_op jit(solution)/shard_map/ppermute | solution.py:898
  36.7 69.7 %collective-permute-start.13 = (bf16[160,2560]{1,0:T(8,128)(2,1)S(1)}, bf16[160,2560]{1,0:T(8,128)(2,1)S(1)}, u32[]{:S(2)}, u32[]{:S(2)}) collective-permute-start(bf16[160,2560]{1,0:T(8,128)(2,1)S(1)} %pad_maximum_fusion.1.refs_4_), channel_id=1, source_target_pairs={{0,8},{4,12},{8,16},{12,20},{16,24},{20,28},{24,0},{28,4},{1,9},{5... | collective-permute-start | bytes 2457608 | tf_op jit(solution)/shard_map/ppermute | solution.py:898
  37.0 41.6 %collective-permute-start.2 = (bf16[160,1280]{1,0:T(8,128)(2,1)S(1)}, bf16[160,1280]{1,0:T(8,128)(2,1)}, u32[]{:S(2)}, u32[]{:S(2)}) collective-permute-start(bf16[160,1280]{1,0:T(8,128)(2,1)S(1)} %collective-permute-done.1.refs_2_), channel_id=1, source_target_pairs={{0,4},{4,0},{8,12},{12,8},{16,20},{20,16},{24,28},{28,24},{1,5},{5... | collective-permute-start | bytes 1228808 | tf_op jit(solution)/shard_map/ppermute | solution.py:899
  38.3 40.4 %collective-permute-start.4 = (bf16[160,1280]{1,0:T(8,128)(2,1)S(1)}, bf16[160,1280]{1,0:T(8,128)(2,1)}, u32[]{:S(2)}, u32[]{:S(2)}) collective-permute-start(bf16[160,1280]{1,0:T(8,128)(2,1)S(1)} %collective-permute-done.3.refs_4_), channel_id=1, source_target_pairs={{0,4},{4,0},{8,12},{12,8},{16,20},{20,16},{24,28},{28,24},{1,5},{5... | collective-permute-start | bytes 1228808 | tf_op jit(solution)/shard_map/ppermute | solution.py:899
  50.9 27.7 %collective-permute-start.6 = (bf16[160,1280]{1,0:T(8,128)(2,1)}, bf16[160,1280]{1,0:T(8,128)(2,1)}, u32[]{:S(2)}, u32[]{:S(2)}) collective-permute-start(bf16[160,1280]{1,0:T(8,128)(2,1)} %collective-permute-done.5.refs_6_), channel_id=1, source_target_pairs={{0,4},{4,0},{8,12},{12,8},{16,20},{20,16},{24,28},{28,24},{1,5},{5... | collective-permute-start | bytes 1228808 | tf_op jit(solution)/shard_map/ppermute | solution.py:899
  106.4 22.8 %collective-permute-start.7 = (bf16[416,1280]{1,0:T(8,128)(2,1)}, bf16[416,1280]{1,0:T(8,128)(2,1)S(1)}, u32[]{:S(2)}, u32[]{:S(2)}) collective-permute-start(bf16[416,1280]{1,0:T(8,128)(2,1)} %get-tuple-element.84), channel_id=1, source_target_pairs={{0,1},{1,0},{2,3},{3,2},{4,5},{5,4},{6,7},{7,6},{8,9},{9,8},{10,11... | collective-permute-start | bytes 3194888 | tf_op jit(solution)/shard_map/ppermute | solution.py:927
  106.4 22.4 %collective-permute-start.15 = (bf16[160,2560]{1,0:T(8,128)(2,1)S(1)}, bf16[160,2560]{1,0:T(8,128)(2,1)S(1)}, u32[]{:S(2)}, u32[]{:S(2)}) collective-permute-start(bf16[160,2560]{1,0:T(8,128)(2,1)S(1)} %collective-permute-done.13.refs_6_), channel_id=1, source_target_pairs={{0,8},{4,12},{8,16},{12,20},{16,24},{20,28},{24,0},{28,4},{1,9},{5... | collective-permute-start | bytes 2457608 | tf_op jit(solution)/shard_map/ppermute | solution.py:898
  128.9 23.0 %collective-permute-start.17 = (bf16[160,2560]{1,0:T(8,128)(2,1)S(1)}, bf16[160,2560]{1,0:T(8,128)(2,1)S(1)}, u32[]{:S(2)}, u32[]{:S(2)}) collective-permute-start(bf16[160,2560]{1,0:T(8,128)(2,1)S(1)} %collective-permute-done.15.refs_8_), channel_id=1, source_target_pairs={{0,8},{4,12},{8,16},{12,20},{16,24},{20,28},{24,0},{28,4},{1,9},{5... | collective-permute-start | bytes 2457608 | tf_op jit(solution)/shard_map/ppermute | solution.py:898
  132.3 20.5 %collective-permute-start.12 = (bf16[160,2560]{1,0:T(8,128)(2,1)S(1)}, bf16[160,2560]{1,0:T(8,128)(2,1)}, u32[]{:S(2)}, u32[]{:S(2)}) collective-permute-start(bf16[160,2560]{1,0:T(8,128)(2,1)S(1)} %pad_maximum_fusion.1.refs_4_), channel_id=1, source_target_pairs={{0,4},{4,0},{8,12},{12,8},{16,20},{20,16},{24,28},{28,24},{1,5},{5... | collective-permute-start | bytes 2457608 | tf_op jit(solution)/shard_map/ppermute | solution.py:899
  149.8 21.3 %collective-permute-start.14 = (bf16[160,2560]{1,0:T(8,128)(2,1)S(1)}, bf16[160,2560]{1,0:T(8,128)(2,1)}, u32[]{:S(2)}, u32[]{:S(2)}) collective-permute-start(bf16[160,2560]{1,0:T(8,128)(2,1)S(1)} %collective-permute-done.13.refs_6_), channel_id=1, source_target_pairs={{0,4},{4,0},{8,12},{12,8},{16,20},{20,16},{24,28},{28,24},{1,5},{5... | collective-permute-start | bytes 2457608 | tf_op jit(solution)/shard_map/ppermute | solution.py:899
  150.3 38.3 %collective-permute-start.16 = (bf16[160,2560]{1,0:T(8,128)(2,1)S(1)}, bf16[160,2560]{1,0:T(8,128)(2,1)}, u32[]{:S(2)}, u32[]{:S(2)}) collective-permute-start(bf16[160,2560]{1,0:T(8,128)(2,1)S(1)} %collective-permute-done.15.refs_8_), channel_id=1, source_target_pairs={{0,4},{4,0},{8,12},{12,8},{16,20},{20,16},{24,28},{28,24},{1,5},{5... | collective-permute-start | bytes 2457608 | tf_op jit(solution)/shard_map/ppermute | solution.py:899
  151.8 52.8 %collective-permute-start.18 = (bf16[160,2560]{1,0:T(8,128)(2,1)S(1)}, bf16[160,2560]{1,0:T(8,128)(2,1)}, u32[]{:S(2)}, u32[]{:S(2)}) collective-permute-start(bf16[160,2560]{1,0:T(8,128)(2,1)S(1)} %collective-permute-done.17.refs_10_), channel_id=1, source_target_pairs={{0,4},{4,0},{8,12},{12,8},{16,20},{20,16},{24,28},{28,24},{1,5},{5... | collective-permute-start | bytes 2457608 | tf_op jit(solution)/shard_map/ppermute | solution.py:899
  152.8 51.8 %collective-permute-start.10 = (bf16[208,1280]{1,0:T(8,128)(2,1)}, bf16[208,1280]{1,0:T(8,128)(2,1)S(1)}, u32[]{:S(2)}, u32[]{:S(2)}) collective-permute-start(bf16[208,1280]{1,0:T(8,128)(2,1)} %get-tuple-element.86.refs_0_), channel_id=1, source_target_pairs={{0,1},{1,0},{2,3},{3,2},{4,5},{5,4},{6,7},{7,6},{8,9},{9,8},{10,11... | collective-permute-start | bytes 1597448 | tf_op jit(solution)/shard_map/ppermute | solution.py:935
  161.4 43.2 %collective-permute-start.11 = (bf16[208,1280]{1,0:T(8,128)(2,1)}, bf16[208,1280]{1,0:T(8,128)(2,1)}, u32[]{:S(2)}, u32[]{:S(2)}) collective-permute-start(bf16[208,1280]{1,0:T(8,128)(2,1)} %collective-permute-done.9.refs_1_), channel_id=1, source_target_pairs={{0,1},{1,0},{2,3},{3,2},{4,5},{5,4},{6,7},{7,6},{8,9},{9,8},{10,11... | collective-permute-start | bytes 1597448 | tf_op jit(solution)/shard_map/ppermute | solution.py:935
  226.4 218.0 %reduce-scatter.5.cloned.1.call-start = ((), (), s32[]{:S(2)}) async-start(), calls=%async_computation.3 | async-start | bytes 2662400 | tf_op jit(solution)/shard_map/reduce_scatter | solution.py:1044
  245.1 22.8 %collective-permute-start.20 = (bf16[208,1280]{1,0:T(8,128)(2,1)S(1)}, bf16[208,1280]{1,0:T(8,128)(2,1)S(1)}, u32[]{:S(2)}, u32[]{:S(2)}) collective-permute-start(bf16[208,1280]{1,0:T(8,128)(2,1)S(1)} %add_convert_fusion.4), channel_id=1, source_target_pairs={{0,2},{1,3},{2,0},{3,1},{4,6},{5,7},{6,4},{7,5},{8,10},{9,11},{10,... | collective-permute-start | bytes 1597448 | tf_op jit(solution)/shard_map/ppermute | solution.py:929
  271.8 14.1 %collective-permute-start.21 = (bf16[208,1280]{1,0:T(8,128)(2,1)}, bf16[208,1280]{1,0:T(8,128)(2,1)S(1)}, u32[]{:S(2)}, u32[]{:S(2)}) collective-permute-start(bf16[208,1280]{1,0:T(8,128)(2,1)} %get-tuple-element.93.refs_0_), channel_id=1, source_target_pairs={{0,2},{1,3},{2,0},{3,1},{4,6},{5,7},{6,4},{7,5},{8,10},{9,11},{10,... | collective-permute-start | bytes 1597448 | tf_op jit(solution)/shard_map/ppermute | solution.py:934
  309.5 15.0 %collective-permute-start.24 = (bf16[416,1280]{1,0:T(8,128)(2,1)}, bf16[416,1280]{1,0:T(8,128)(2,1)}, u32[]{:S(2)}, u32[]{:S(2)}) collective-permute-start(bf16[416,1280]{1,0:T(8,128)(2,1)} %get-tuple-element.97), channel_id=1, source_target_pairs={{0,1},{1,0},{2,3},{3,2},{4,5},{5,4},{6,7},{7,6},{8,9},{9,8},{10,11... | collective-permute-start | bytes 3194888 | tf_op jit(solution)/shard_map/ppermute | solution.py:927
  309.7 17.5 %collective-permute-start.34 = (bf16[416,1280]{1,0:T(8,128)(2,1)}, bf16[416,1280]{1,0:T(8,128)(2,1)S(1)}, u32[]{:S(2)}, u32[]{:S(2)}) collective-permute-start(bf16[416,1280]{1,0:T(8,128)(2,1)} %get-tuple-element.105), channel_id=1, source_target_pairs={{0,1},{1,0},{2,3},{3,2},{4,5},{5,4},{6,7},{7,6},{8,9},{9,8},{10,11... | collective-permute-start | bytes 3194888 | tf_op jit(solution)/shard_map/ppermute | solution.py:927
  322.9 83.8 %collective-permute-start.57 = (bf16[4,160,1280]{2,1,0:T(8,128)(2,1)}, bf16[4,160,1280]{2,1,0:T(8,128)(2,1)}, u32[]{:S(2)}, u32[]{:S(2)}) collective-permute-start(bf16[4,160,1280]{2,1,0:T(8,128)(2,1)} %get-tuple-element.139), channel_id=1, source_target_pairs={{0,4},{4,0},{8,12},{12,8},{16,20},{20,16},{24,28},{28,24},{1,5},{5... | collective-permute-start | bytes 4915208 | tf_op jit(solution)/shard_map/ppermute | solution.py:916
  324.4 227.1 %all-gather.2.cloned.1.call-start = ((), (), s32[]{:S(2)}) async-start(), calls=%async_computation.4 | async-start | bytes 5324800 | tf_op jit(solution)/shard_map/all_gather | solution.py:1047
  326.6 15.5 %collective-permute-start.25 = (bf16[208,1280]{1,0:T(8,128)(2,1)}, bf16[208,1280]{1,0:T(8,128)(2,1)S(1)}, u32[]{:S(2)}, u32[]{:S(2)}) collective-permute-start(bf16[208,1280]{1,0:T(8,128)(2,1)} %add_convert_fusion.3), channel_id=1, source_target_pairs={{0,2},{1,3},{2,0},{3,1},{4,6},{5,7},{6,4},{7,5},{8,10},{9,11},{10,... | collective-permute-start | bytes 1597448 | tf_op jit(solution)/shard_map/ppermute | solution.py:929
  327.3 36.3 %collective-permute-start.35 = (bf16[208,1280]{1,0:T(8,128)(2,1)S(1)}, bf16[208,1280]{1,0:T(8,128)(2,1)S(1)}, u32[]{:S(2)}, u32[]{:S(2)}) collective-permute-start(bf16[208,1280]{1,0:T(8,128)(2,1)S(1)} %add_convert_fusion.1), channel_id=1, source_target_pairs={{0,2},{1,3},{2,0},{3,1},{4,6},{5,7},{6,4},{7,5},{8,10},{9,11},{10,... | collective-permute-start | bytes 1597448 | tf_op jit(solution)/shard_map/ppermute | solution.py:929
  341.5 88.9 %collective-permute-start.53 = (bf16[4,160,1280]{2,1,0:T(8,128)(2,1)}, bf16[4,160,1280]{2,1,0:T(8,128)(2,1)}, u32[]{:S(2)}, u32[]{:S(2)}) collective-permute-start(bf16[4,160,1280]{2,1,0:T(8,128)(2,1)} %get-tuple-element.135), channel_id=1, source_target_pairs={{0,4},{4,0},{8,12},{12,8},{16,20},{20,16},{24,28},{28,24},{1,5},{5... | collective-permute-start | bytes 4915208 | tf_op jit(solution)/shard_map/ppermute | solution.py:916
  347.0 29.0 %collective-permute-start.26 = (bf16[208,1280]{1,0:T(8,128)(2,1)}, bf16[208,1280]{1,0:T(8,128)(2,1)S(1)}, u32[]{:S(2)}, u32[]{:S(2)}) collective-permute-start(bf16[208,1280]{1,0:T(8,128)(2,1)} %get-tuple-element.98.refs_0_), channel_id=1, source_target_pairs={{0,2},{1,3},{2,0},{3,1},{4,6},{5,7},{6,4},{7,5},{8,10},{9,11},{10,... | collective-permute-start | bytes 1597448 | tf_op jit(solution)/shard_map/ppermute | solution.py:934
  368.6 17.7 %collective-permute-start.36 = (bf16[208,1280]{1,0:T(8,128)(2,1)}, bf16[208,1280]{1,0:T(8,128)(2,1)S(1)}, u32[]{:S(2)}, u32[]{:S(2)}) collective-permute-start(bf16[208,1280]{1,0:T(8,128)(2,1)} %get-tuple-element.106.refs_0_), channel_id=1, source_target_pairs={{0,2},{1,3},{2,0},{3,1},{4,6},{5,7},{6,4},{7,5},{8,10},{9,11},{10,... | collective-permute-start | bytes 1597448 | tf_op jit(solution)/shard_map/ppermute | solution.py:934
  369.4 16.9 %collective-permute-start.27 = (bf16[208,1280]{1,0:T(8,128)(2,1)S(1)}, bf16[208,1280]{1,0:T(8,128)(2,1)S(1)}, u32[]{:S(2)}, u32[]{:S(2)}) collective-permute-start(bf16[208,1280]{1,0:T(8,128)(2,1)S(1)} %copy-done.28), channel_id=1, source_target_pairs={{0,1},{1,0},{2,3},{3,2},{4,5},{5,4},{6,7},{7,6},{8,9},{9,8},{10,11... | collective-permute-start | bytes 1597448 | tf_op jit(solution)/shard_map/ppermute | solution.py:935
  386.3 23.5 %collective-permute-start.37 = (bf16[208,1280]{1,0:T(8,128)(2,1)}, bf16[208,1280]{1,0:T(8,128)(2,1)S(1)}, u32[]{:S(2)}, u32[]{:S(2)}) collective-permute-start(bf16[208,1280]{1,0:T(8,128)(2,1)} %get-tuple-element.106.refs_0_), channel_id=1, source_target_pairs={{0,1},{1,0},{2,3},{3,2},{4,5},{5,4},{6,7},{7,6},{8,9},{9,8},{10,11... | collective-permute-start | bytes 1597448 | tf_op jit(solution)/shard_map/ppermute | solution.py:935
  386.4 23.5 %collective-permute-start.38 = (bf16[208,1280]{1,0:T(8,128)(2,1)S(1)}, bf16[208,1280]{1,0:T(8,128)(2,1)S(1)}, u32[]{:S(2)}, u32[]{:S(2)}) collective-permute-start(bf16[208,1280]{1,0:T(8,128)(2,1)S(1)} %collective-permute-done.36.refs_1_), channel_id=1, source_target_pairs={{0,1},{1,0},{2,3},{3,2},{4,5},{5,4},{6,7},{7,6},{8,9},{9,8},{10,11... | collective-permute-start | bytes 1597448 | tf_op jit(solution)/shard_map/ppermute | solution.py:935
  406.5 31.2 %collective-permute-start.29 = (bf16[416,1280]{1,0:T(8,128)(2,1)}, bf16[416,1280]{1,0:T(8,128)(2,1)S(1)}, u32[]{:S(2)}, u32[]{:S(2)}) collective-permute-start(bf16[416,1280]{1,0:T(8,128)(2,1)} %get-tuple-element.101), channel_id=1, source_target_pairs={{0,1},{1,0},{2,3},{3,2},{4,5},{5,4},{6,7},{7,6},{8,9},{9,8},{10,11... | collective-permute-start | bytes 3194888 | tf_op jit(solution)/shard_map/ppermute | solution.py:927
  408.7 25.4 %collective-permute-start.58 = (bf16[160,1280]{1,0:T(8,128)(2,1)}, bf16[160,1280]{1,0:T(8,128)(2,1)S(1)}, u32[]{:S(2)}, u32[]{:S(2)}) collective-permute-start(bf16[160,1280]{1,0:T(8,128)(2,1)} %fusion.9), channel_id=1, source_target_pairs={{0,8},{4,12},{8,16},{12,20},{16,24},{20,28},{24,0},{28,4},{1,9},{5... | collective-permute-start | bytes 1228808 | tf_op jit(solution)/shard_map/ppermute | solution.py:918
  432.3 16.7 %collective-permute-start.54 = (bf16[160,1280]{1,0:T(8,128)(2,1)}, bf16[160,1280]{1,0:T(8,128)(2,1)}, u32[]{:S(2)}, u32[]{:S(2)}) collective-permute-start(bf16[160,1280]{1,0:T(8,128)(2,1)} %fusion.8), channel_id=1, source_target_pairs={{0,8},{4,12},{8,16},{12,20},{16,24},{20,28},{24,0},{28,4},{1,9},{5... | collective-permute-start | bytes 1228808 | tf_op jit(solution)/shard_map/ppermute | solution.py:918
  436.1 41.7 %collective-permute-start.59 = (bf16[160,1280]{1,0:T(8,128)(2,1)}, bf16[160,1280]{1,0:T(8,128)(2,1)}, u32[]{:S(2)}, u32[]{:S(2)}) collective-permute-start(bf16[160,1280]{1,0:T(8,128)(2,1)} %fusion), channel_id=1, source_target_pairs={{0,8},{4,12},{8,16},{12,20},{16,24},{20,28},{24,0},{28,4},{1,9},{5... | collective-permute-start | bytes 1228808 | tf_op jit(solution)/shard_map/ppermute | solution.py:919
  438.8 30.6 %collective-permute-start.30 = (bf16[208,1280]{1,0:T(8,128)(2,1)}, bf16[208,1280]{1,0:T(8,128)(2,1)}, u32[]{:S(2)}, u32[]{:S(2)}) collective-permute-start(bf16[208,1280]{1,0:T(8,128)(2,1)} %add_convert_fusion.2), channel_id=1, source_target_pairs={{0,2},{1,3},{2,0},{3,1},{4,6},{5,7},{6,4},{7,5},{8,10},{9,11},{10,... | collective-permute-start | bytes 1597448 | tf_op jit(solution)/shard_map/ppermute | solution.py:929
  440.5 32.6 %collective-permute-start.40 = (bf16[208,1280]{1,0:T(8,128)(2,1)}, bf16[208,1280]{1,0:T(8,128)(2,1)}, u32[]{:S(2)}, u32[]{:S(2)}) collective-permute-start(bf16[208,1280]{1,0:T(8,128)(2,1)} %add_convert_fusion), channel_id=1, source_target_pairs={{0,2},{1,3},{2,0},{3,1},{4,6},{5,7},{6,4},{7,5},{8,10},{9,11},{10,... | collective-permute-start | bytes 1597448 | tf_op jit(solution)/shard_map/ppermute | solution.py:929
  450.3 30.1 %collective-permute-start.55 = (bf16[160,1280]{1,0:T(8,128)(2,1)S(1)}, bf16[160,1280]{1,0:T(8,128)(2,1)S(1)}, u32[]{:S(2)}, u32[]{:S(2)}) collective-permute-start(bf16[160,1280]{1,0:T(8,128)(2,1)S(1)} %fusion.3), channel_id=1, source_target_pairs={{0,8},{4,12},{8,16},{12,20},{16,24},{20,28},{24,0},{28,4},{1,9},{5... | collective-permute-start | bytes 1228808 | tf_op jit(solution)/shard_map/ppermute | solution.py:919
  467.9 37.3 %collective-permute-start.49 = (bf16[4,160,1280]{2,1,0:T(8,128)(2,1)}, bf16[4,160,1280]{2,1,0:T(8,128)(2,1)}, u32[]{:S(2)}, u32[]{:S(2)}) collective-permute-start(bf16[4,160,1280]{2,1,0:T(8,128)(2,1)} %get-tuple-element.129), channel_id=1, source_target_pairs={{0,4},{4,0},{8,12},{12,8},{16,20},{20,16},{24,28},{28,24},{1,5},{5... | collective-permute-start | bytes 4915208 | tf_op jit(solution)/shard_map/ppermute | solution.py:916
  479.3 29.8 %collective-permute-start.60 = (bf16[160,1280]{1,0:T(8,128)(2,1)S(1)}, bf16[160,1280]{1,0:T(8,128)(2,1)S(1)}, u32[]{:S(2)}, u32[]{:S(2)}) collective-permute-start(bf16[160,1280]{1,0:T(8,128)(2,1)S(1)} %fusion.1), channel_id=1, source_target_pairs={{0,8},{4,12},{8,16},{12,20},{16,24},{20,28},{24,0},{28,4},{1,9},{5... | collective-permute-start | bytes 1228808 | tf_op jit(solution)/shard_map/ppermute | solution.py:920
  481.6 40.7 %collective-permute-start.56 = (bf16[160,1280]{1,0:T(8,128)(2,1)S(1)}, bf16[160,1280]{1,0:T(8,128)(2,1)S(1)}, u32[]{:S(2)}, u32[]{:S(2)}) collective-permute-start(bf16[160,1280]{1,0:T(8,128)(2,1)S(1)} %fusion.4), channel_id=1, source_target_pairs={{0,8},{4,12},{8,16},{12,20},{16,24},{20,28},{24,0},{28,4},{1,9},{5... | collective-permute-start | bytes 1228808 | tf_op jit(solution)/shard_map/ppermute | solution.py:920
  486.9 20.3 %collective-permute-start.46 = (f32[160,128]{1,0:T(8,128)S(1)}, f32[160,128]{1,0:T(8,128)S(1)}, u32[]{:S(2)}, u32[]{:S(2)}) collective-permute-start(f32[160,128]{1,0:T(8,128)S(1)} %fusion.15), channel_id=1, source_target_pairs={{0,4},{4,0},{8,12},{12,8},{16,20},{20,16},{24,28},{28,24},{1,5},{5... | collective-permute-start | bytes 245768 | tf_op jit(solution)/shard_map/ppermute | solution.py:945
  511.3 16.7 %collective-permute-start.31 = (bf16[208,1280]{1,0:T(8,128)(2,1)}, bf16[208,1280]{1,0:T(8,128)(2,1)}, u32[]{:S(2)}, u32[]{:S(2)}) collective-permute-start(bf16[208,1280]{1,0:T(8,128)(2,1)} %get-tuple-element.103.refs_0_), channel_id=1, source_target_pairs={{0,2},{1,3},{2,0},{3,1},{4,6},{5,7},{6,4},{7,5},{8,10},{9,11},{10,... | collective-permute-start | bytes 1597448 | tf_op jit(solution)/shard_map/ppermute | solution.py:934
  511.5 21.3 %collective-permute-start.41 = (bf16[208,1280]{1,0:T(8,128)(2,1)S(1)}, bf16[208,1280]{1,0:T(8,128)(2,1)S(1)}, u32[]{:S(2)}, u32[]{:S(2)}) collective-permute-start(bf16[208,1280]{1,0:T(8,128)(2,1)S(1)} %copy-done.19), channel_id=1, source_target_pairs={{0,2},{1,3},{2,0},{3,1},{4,6},{5,7},{6,4},{7,5},{8,10},{9,11},{10,... | collective-permute-start | bytes 1597448 | tf_op jit(solution)/shard_map/ppermute | solution.py:934
  524.3 17.8 %collective-permute-start.32 = (bf16[208,1280]{1,0:T(8,128)(2,1)}, bf16[208,1280]{1,0:T(8,128)(2,1)S(1)}, u32[]{:S(2)}, u32[]{:S(2)}) collective-permute-start(bf16[208,1280]{1,0:T(8,128)(2,1)} %get-tuple-element.103.refs_0_), channel_id=1, source_target_pairs={{0,1},{1,0},{2,3},{3,2},{4,5},{5,4},{6,7},{7,6},{8,9},{9,8},{10,11... | collective-permute-start | bytes 1597448 | tf_op jit(solution)/shard_map/ppermute | solution.py:935
  528.0 14.2 %collective-permute-start.33 = (bf16[208,1280]{1,0:T(8,128)(2,1)}, bf16[208,1280]{1,0:T(8,128)(2,1)S(1)}, u32[]{:S(2)}, u32[]{:S(2)}) collective-permute-start(bf16[208,1280]{1,0:T(8,128)(2,1)} %collective-permute-done.31.refs_1_), channel_id=1, source_target_pairs={{0,1},{1,0},{2,3},{3,2},{4,5},{5,4},{6,7},{7,6},{8,9},{9,8},{10,11... | collective-permute-start | bytes 1597448 | tf_op jit(solution)/shard_map/ppermute | solution.py:935
  534.5 13.8 %collective-permute-start.52 = (bf16[160,1280]{1,0:T(8,128)(2,1)S(1)}, bf16[160,1280]{1,0:T(8,128)(2,1)}, u32[]{:S(2)}, u32[]{:S(2)}) collective-permute-start(bf16[160,1280]{1,0:T(8,128)(2,1)S(1)} %fusion.6), channel_id=1, source_target_pairs={{0,8},{4,12},{8,16},{12,20},{16,24},{20,28},{24,0},{28,4},{1,9},{5... | collective-permute-start | bytes 1228808 | tf_op jit(solution)/shard_map/ppermute | solution.py:920
  (74 other events, 1165.5 us)
Sparse Core Ops, SparseCore 0:
  226.5 39.7 reduce-scatter.2
  324.5 42.2 reduce-scatter.4
  449.0 41.2 all-gather.1

commit v3 on v2

--- a/solution.py
+++ b/solution.py
@@ -44,6 +44,12 @@
     return pltpu.CompilerParams(vmem_limit_bytes=megabytes * 2**20)
 
 
+def cost(micros):
+    return pl.CostEstimate(
+        flops=int(micros * 0.05e9), bytes_accessed=int(micros * 1.0e4), transcendentals=0
+    )
+
+
 def struct(shape, dtype):
     return jax.ShapeDtypeStruct(shape, dtype)
 
@@ -70,29 +76,33 @@
     return centred * rstd, rstd
 
 
-def prepare_kernel(order, places, lives, x_ref, top_ref, gain_ref, shift_ref, *outs):
-    rows_ref, normed_ref, grad_ref, valid_ref = outs
-    slot = order[pl.program_id(0)]
+def token_valid(spot, live):
     token = lax.broadcasted_iota(jnp.int32, (WTOK, 1), 0)
     row = (token * 9363) >> 17
     col = token - row * WIN
-    spot = places[slot]
     high = spot // GRID * WIN
     wide = spot % GRID * WIN
-    inside = (high + row < SIDE) & (wide + col < SIDE) & (lives[slot] == 1)
-    valid = jnp.where(inside, 1.0, 0.0).astype(F32)
-    x = x_ref[0]
-    xhat, _ = norm_parts(x.astype(F32))
-    normed = (xhat * gain_ref[...] + shift_ref[...]) * valid
-    empty = jnp.zeros((ROWS - WTOK, x.shape[1]), F32)
-    normed_ref[...] = jnp.concatenate([normed, empty], axis=0).astype(BF16)
-    grad = top_ref[0].astype(F32) * valid
-    grad_ref[...] = jnp.concatenate([grad, empty], axis=0).astype(BF16)
-    rows_ref[...] = jnp.concatenate([x.astype(F32), empty], axis=0).astype(BF16)
-    valid_ref[...] = jnp.concatenate([valid, empty[:, :1]], axis=0)
-
-
-def prepare(order, places, lives, x, top, gain, shift):
+    inside = (high + row < SIDE) & (wide + col < SIDE) & (live == 1)
+    return jnp.where(inside, 1.0, 0.0).astype(F32)
+
+
+def pad_rows(values):
+    empty = jnp.zeros((ROWS - WTOK, values.shape[1]), F32)
+    return jnp.concatenate([values, empty], axis=0)
+
+
+def prepare_kernel(order, places, lives, x_ref, gain_ref, shift_ref, *outs):
+    rows_ref, normed_ref, valid_ref = outs
+    slot = order[pl.program_id(0)]
+    valid = token_valid(places[slot], lives[slot])
+    x = x_ref[0].astype(F32)
+    xhat, _ = norm_parts(x)
+    normed_ref[...] = pad_rows((xhat * gain_ref[...] + shift_ref[...]) * valid).astype(BF16)
+    rows_ref[...] = pad_rows(x).astype(BF16)
+    valid_ref[...] = pad_rows(valid)
+
+
+def prepare(order, places, lives, x, gain, shift):
     count = order.shape[0]
     width = x.shape[2]
     window = pl.BlockSpec((1, WTOK, width), lambda i, order, *_: (order[i], 0, 0))
@@ -102,13 +112,38 @@
         grid_spec=pltpu.PrefetchScalarGridSpec(
             num_scalar_prefetch=3,
             grid=(count,),
-            in_specs=[window, window, whole(gain), whole(shift)],
-            out_specs=[block] * 3 + [pl.BlockSpec((ROWS, 1), lambda i, *_: (i, 0))],
+            in_specs=[window, whole(gain), whole(shift)],
+            out_specs=[block] * 2 + [pl.BlockSpec((ROWS, 1), lambda i, *_: (i, 0))],
         ),
-        out_shape=[struct((count * ROWS, width), BF16)] * 3 + [struct((count * ROWS, 1), F32)],
+        out_shape=[struct((count * ROWS, width), BF16)] * 2 + [struct((count * ROWS, 1), F32)],
         compiler_params=params(60),
+        cost_estimate=cost(9),
         name="prepare",
-    )(order, places, lives, x, top, gain, shift)
+    )(order, places, lives, x, gain, shift)
+
+
+def mask_kernel(order, places, lives, top_ref, grad_ref):
+    slot = order[pl.program_id(0)]
+    valid = token_valid(places[slot], lives[slot])
+    grad_ref[...] = pad_rows(top_ref[0].astype(F32) * valid).astype(BF16)
+
+
+def mask_rows(order, places, lives, top):
+    count = order.shape[0]
+    width = top.shape[2]
+    return pl.pallas_call(
+        mask_kernel,
+        grid_spec=pltpu.PrefetchScalarGridSpec(
+            num_scalar_prefetch=3,
+            grid=(count,),
+            in_specs=[pl.BlockSpec((1, WTOK, width), lambda i, order, *_: (order[i], 0, 0))],
+            out_specs=pl.BlockSpec((ROWS, width), lambda i, *_: (i, 0)),
+        ),
+        out_shape=struct((count * ROWS, width), BF16),
+        compiler_params=params(60),
+        cost_estimate=cost(6),
+        name="mask_rows",
+    )(order, places, lives, top)
 
 
 def top_rows(shape):
@@ -148,6 +183,7 @@
         out_specs=[top_rows(shape)] * 2,
         out_shape=[struct(shape, F32), struct(shape, BF16)],
         compiler_params=params(60),
+        cost_estimate=cost(3),
         name="norm_two",
     )(*parts, x, bias, gain, shift)
 
@@ -168,6 +204,7 @@
         out_specs=top_rows(after.shape),
         out_shape=struct(after.shape, BF16),
         compiler_params=params(60),
+        cost_estimate=cost(2.5),
         name="finish",
     )(*parts, after, valid, bias)
 
@@ -206,6 +243,7 @@
         out_specs=[top_rows(after.shape)] * 2 + [whole(sums)],
         out_shape=[struct(after.shape, F32), struct(after.shape, BF16), sums],
         compiler_params=params(60),
+        cost_estimate=cost(4),
         name="norm_two_back",
     )(*parts, after, top, gain)
 
@@ -232,6 +270,7 @@
         out_specs=[top_rows(shape), whole(sums)],
         out_shape=[struct(shape, BF16), sums],
         compiler_params=params(60),
+        cost_estimate=cost(3.5),
         name="norm_one_back",
     )(*parts, x, valid, grad, gain)
 
@@ -277,6 +316,7 @@
         ),
         out_shape=[struct((rows, wide), BF16)] * 3 + [struct((width, 4 * wide), BF16)],
         compiler_params=params(60),
+        cost_estimate=cost(14),
         name="qkv",
     )(offsets, *pieces, x, bias)
 
@@ -423,6 +463,7 @@
         ]
         + shapes,
         compiler_params=params(60),
+        cost_estimate=cost(13.5),
         name="attend",
     )(q, k, v, rel_high, rel_low, marks, weights)
 
@@ -539,16 +580,18 @@
         + specs,
         out_shape=[struct((rows, 3 * heads * HD), BF16), branch, rel, sums] + shapes,
         compiler_params=params(60),
+        cost_estimate=cost(18.5),
         name="attend_back",
     )(*pieces, q, k, v, shares, rel_high, marks, weights)
 
 
-def mlp_kernel(count, weights, split, offsets, order, *refs):
+def mlp_kernel(count, weights, split, offsets, *refs):
     pieces = refs[:count]
     weight_pieces = refs[count : count + weights]
     refs = refs[count + weights :]
-    top_ref, bias_ref, active_ref, hidden_ref, normed_ref, sum_ref, out_ref = refs[:7]
-    backs = refs[7:-3]
+    top_ref, bias_ref, after_ref, down_bias_ref = refs[:4]
+    active_ref, hidden_ref, normed_ref, sum_ref = refs[4:8]
+    backs, outs = (refs[8:10], refs[10:12]) if split else (refs[8:9], refs[9:10])
     up, down, sems = refs[-3:]
     step = pl.program_id(0)
     block = top_ref.shape[0]
@@ -596,26 +639,26 @@
     hidden_ref[...] = grad
     sum_ref[...] += jnp.sum(grad.astype(F32), axis=0, keepdims=True)
     back = dot_nt(grad, up[...]).astype(BF16)
+    result = dot_nt(active, down[...])
     if split:
 
         @pl.when(step == 0)
         def _():
             backs[1][...] = back
+            outs[1][...] = result.astype(BF16)
 
         @pl.when(step == 1)
         def _():
             backs[0][...] = back
+            own = result[:ROWS] + after_ref[...] + down_bias_ref[...]
+            outs[0][:ROWS] = own.astype(BF16)
+            outs[0][ROWS:] = result[ROWS:].astype(BF16)
     else:
         backs[0][...] = back
-    result = dot_nt(active, down[...]).astype(BF16)
-    for index in range(block // ROWS):
-        target = order[place * (block // ROWS) + index]
-        out_ref[pl.ds(pl.multiple_of(target * ROWS, 16), ROWS), :] = result[
-            index * ROWS : (index + 1) * ROWS
-        ]
-
-
-def mlp(offsets, order, pieces, weight_pieces, top, part, bias, split):
+        outs[0][...] = result.astype(BF16)
+
+
+def mlp(offsets, pieces, weight_pieces, top, part, bias, after, down_bias, split):
     rows = sum(piece.shape[0] for piece in pieces)
     width = pieces[0].shape[1]
     units = weight_pieces[0].shape[1] // 2
@@ -637,31 +680,37 @@
     return pl.pallas_call(
         partial(mlp_kernel, len(pieces), len(weight_pieces), split),
         grid_spec=pltpu.PrefetchScalarGridSpec(
-            num_scalar_prefetch=2,
+            num_scalar_prefetch=1,
             grid=(blocks,),
             in_specs=[whole(piece) for piece in pieces]
             + [ANY] * len(weight_pieces)
             + [
                 pl.BlockSpec((block, width), lambda i, *_: (part * blocks + place(i), 0)),
                 whole(bias),
+                whole(after),
+                whole(down_bias),
             ],
-            out_specs=[wide, wide, whole(normed), whole(sums), whole(normed)] + back_specs,
+            out_specs=[wide, wide, whole(normed), whole(sums)] + back_specs * 2,
             scratch_shapes=[
                 pltpu.VMEM((width, units), BF16),
                 pltpu.VMEM((width, units), BF16),
                 pltpu.SemaphoreType.DMA((2, len(weight_pieces))),
             ],
         ),
-        out_shape=[struct((rows, units), BF16)] * 2 + [normed, sums, normed] + back_shapes,
+        out_shape=[struct((rows, units), BF16)] * 2 + [normed, sums] + back_shapes * 2,
         compiler_params=params(60),
+        cost_estimate=cost(21),
         name="mlp",
-    )(offsets, order, *pieces, *weight_pieces, top, bias)
+    )(offsets, *pieces, *weight_pieces, top, bias, after, down_bias)
 
 
 def weight_grad_kernel(sizes, share, targets, *refs):
     count = 2 * sum(sizes)
     operands = refs[:count]
-    send_ref, keep_ref, result, sems = refs[count:]
+    outs, (result, sems) = refs[count:-2], refs[-2:]
+    pair_ref = outs[-1] if len(outs) != 2 else None
+    send_ref, keep_ref = outs[:2] if len(outs) > 1 else (None, None)
+    lead = send_ref.shape[2] if len(outs) > 1 else 0
     step = pl.program_id(0)
     steps = pl.num_programs(0)
     chunk = operands[0].shape[1]
@@ -681,25 +730,45 @@
 
     def copy(index, out, slot):
         return pltpu.make_async_copy(
-            result.at[pl.ds(pl.multiple_of(index * share, 16), share)], out.at[slot], sems.at[index]
+            result.at[pl.ds(pl.multiple_of(index * share, 16), share), pl.ds(0, lead)],
+            out.at[slot],
+            sems.at[0, index],
+        )
+
+    def pair_copy(index, slot):
+        return pltpu.make_async_copy(
+            result.at[
+                pl.ds(pl.multiple_of(index * share, 16), share),
+                pl.ds(lead, result.shape[1] - lead),
+            ],
+            pair_ref.at[lax.rem(slot, 4), 1 - slot // 4],
+            sems.at[1, index],
         )
 
     for piece in range(pieces):
         index = step * pieces + piece
         slot = targets[index]
 
-        @pl.when(slot < 4)
-        def _():
-            copy(index, send_ref, slot).start()
-
-        @pl.when(slot >= 4)
-        def _():
-            copy(index, keep_ref, slot - 4).start()
+        if lead:
+
+            @pl.when(slot < 4)
+            def _():
+                copy(index, send_ref, slot).start()
+
+            @pl.when(slot >= 4)
+            def _():
+                copy(index, keep_ref, slot - 4).start()
+
+        if pair_ref is not None:
+            pair_copy(index, slot).start()
 
     @pl.when(step == steps - 1)
     def _():
         for index in range(8):
-            copy(index, send_ref, 0).wait()
+            if lead:
+                copy(index, send_ref, 0).wait()
+            if pair_ref is not None:
+                pair_copy(index, 0).wait()
 
 
 def plain_grad_kernel(sizes, *refs):
@@ -718,7 +787,7 @@
         first += span
 
 
-def weight_grad(targets, groups, share):
+def weight_grad(targets, groups, share, lead=None):
     operands, specs = [], []
     chunk = 640 if targets is not None else 256
     total_cols = 0
@@ -739,23 +808,29 @@
                 out_specs=pl.BlockSpec((chunk, total_cols), lambda i: (i, 0)),
                 out_shape=struct((width, total_cols), BF16),
                 compiler_params=params(60),
-                name="weight_grad",
+                cost_estimate=cost(13),
+        name="weight_grad",
             )(*operands)
         ]
+    lead = total_cols if lead is None else lead
+    shapes = [struct((4, share, lead), BF16)] * 2 if lead else []
+    if lead < total_cols:
+        shapes.append(struct((4, 2, share, total_cols - lead), BF16))
     return pl.pallas_call(
         partial(weight_grad_kernel, sizes, share),
         grid_spec=pltpu.PrefetchScalarGridSpec(
             num_scalar_prefetch=1,
             grid=(width // chunk,),
             in_specs=specs,
-            out_specs=[ANY] * 2,
+            out_specs=[ANY] * len(shapes),
             scratch_shapes=[
                 pltpu.VMEM((width, total_cols), BF16),
-                pltpu.SemaphoreType.DMA((8,)),
+                pltpu.SemaphoreType.DMA((2, 8)),
             ],
         ),
-        out_shape=[struct((4, share, total_cols), BF16)] * 2,
+        out_shape=shapes,
         compiler_params=params(60),
+        cost_estimate=cost(13),
         name="weight_grad",
     )(targets, *operands)
 
@@ -791,8 +866,53 @@
         out_shape=struct((rows, width), F32),
         input_output_aliases={} if held is None else {5: 0},
         compiler_params=params(60),
+        cost_estimate=cost(4.5),
         name="place_windows",
     )(order, *operands)
+
+
+def output_kernel(part, order, places, lives, *refs):
+    pieces, out_ref, buffer, rounded, sem = refs[:4], refs[-4], refs[-3], refs[-2], refs[-1]
+    rows = buffer.shape[0]
+    for me in range(4):
+
+        @pl.when(order[0] == me)
+        def _(me=me):
+            for index, step in enumerate((0, 2, 1, 3)):
+                slot = me ^ step
+                valid = token_valid(places[4 * part + slot], lives[4 * part + slot])
+                value = pieces[index][:WTOK].astype(F32) * valid
+                buffer[slot * WTOK : (slot + 1) * WTOK] = value
+
+    rounded[...] = buffer[...].astype(BF16)
+    copy = pltpu.make_async_copy(rounded, out_ref.at[pl.ds(part * rows, rows)], sem)
+    copy.start()
+    copy.wait()
+
+
+def write_output(part, order, places, lives, pieces, rows, held):
+    width = pieces[0].shape[1]
+    operands = list(pieces) + ([] if held is None else [held])
+    shape = (4 * WTOK, width)
+    return pl.pallas_call(
+        partial(output_kernel, part),
+        grid_spec=pltpu.PrefetchScalarGridSpec(
+            num_scalar_prefetch=3,
+            grid=(1,),
+            in_specs=[whole(piece) for piece in pieces] + [ANY] * (len(operands) - 4),
+            out_specs=ANY,
+            scratch_shapes=[
+                pltpu.VMEM(shape, F32),
+                pltpu.VMEM(shape, BF16),
+                pltpu.SemaphoreType.DMA(()),
+            ],
+        ),
+        out_shape=struct((rows, width), BF16),
+        input_output_aliases={} if held is None else {7: 0},
+        compiler_params=params(60),
+        cost_estimate=cost(5),
+        name="write_output",
+    )(order, places, lives, *operands)
 
 
 def key_marks(heads):
@@ -841,6 +961,14 @@
     for value in values[1:]:
         out = out + value
     return out
+
+
+def tie(value, *others):
+    return lax.optimization_barrier((value,) + others)[0]
+
+
+def sync(*values):
+    return lax.optimization_barrier(values)
 
 
 def body(
@@ -874,7 +1002,7 @@
     wide = (cols + 127) // 128 * 128
     units = up_weight.shape[1]
     slots = window_place.shape[0]
-    rings = data_parts == 8 and model_parts == 4 and slots % 4 == 0
+    rings = data_parts == 8 and model_parts == 4 and slots == 8
     padded = (slots + model_parts - 1) // model_parts * model_parts
     halves = padded // 4 if rings else 1
     windows = padded // halves
@@ -891,12 +1019,7 @@
         over_core = partial(lax.ppermute, axis_name="mp", perm=[(m, m ^ 1) for m in range(4)])
 
     def gather(piece):
-        if not rings:
-            return [lax.all_gather(piece, "dp", axis=0, tiled=True)]
-        line = [piece]
-        for _ in range(3):
-            line.append(over_z(line[-1]))
-        return [item for held in line for item in (held, over_x(held))]
+        return [lax.all_gather(piece, "dp", axis=0, tiled=True)]
 
     if rings:
         offsets = []
@@ -908,31 +1031,19 @@
         offsets = jnp.zeros((1,), jnp.int32)
 
     def scatter(parts):
-        if not rings:
-            return lax.psum_scatter(
-                parts[0], "dp", scatter_dimension=0, tiled=True
-            ).astype(F32)
-        send, keep = parts
-        came = over_x(send)
-        sums = [keep[k].astype(F32) + came[k].astype(F32) for k in range(4)]
-        moving = over_z(sums[3].astype(BF16))
-        moving = over_z((sums[2] + moving.astype(F32)).astype(BF16))
-        moving = over_z((sums[1] + moving.astype(F32)).astype(BF16))
-        return sums[0] + moving.astype(F32)
+        return lax.psum_scatter(parts[0], "dp", scatter_dimension=0, tiled=True).astype(F32)
+
+    def joined(*values):
+        total_value = values[0].astype(F32)
+        for value in values[1:]:
+            total_value = total_value + value.astype(F32)
+        return total_value.astype(BF16)
 
     def rows_scatter(parts):
-        if not rings:
-            return [lax.psum_scatter(parts[0], "mp", scatter_dimension=0, tiled=True)]
-        keep, send = parts
-        came = over_core(send)
-        passed = (keep[ROWS:].astype(F32) + came[ROWS:].astype(F32)).astype(BF16)
-        return [keep, came, over_y(passed)]
+        return [lax.psum_scatter(parts[0], "mp", scatter_dimension=0, tiled=True)]
 
     def rows_gather(own):
-        if not rings:
-            return [lax.all_gather(own, "mp", axis=0, tiled=True)]
-        across = over_y(own)
-        return [own, across, over_core(own), over_core(across)]
+        return [lax.all_gather(own, "mp", axis=0, tiled=True)]
 
     def sum_all(vector):
         if not rings:
@@ -941,7 +1052,7 @@
             vector = vector + lax.ppermute(
                 vector, "mp", [(m, m ^ step) for m in range(4)]
             )
-        for step in (1, 2, 4):
+        for step in (2, 4, 1):
             vector = vector + lax.ppermute(
                 vector, "dp", [(d, d ^ step) for d in range(8)]
             )
@@ -952,8 +1063,7 @@
         return lax.dynamic_slice_in_dim(array, model_index * rows, rows, 0)
 
     first_piece = jnp.concatenate([qkv_weight[0], qkv_weight[1], qkv_weight[2], proj_weight.T], 1)
-    first_weights = gather(first_piece)
-    other_weights = gather(jnp.concatenate([down_weight.T, up_weight], 1))
+    other_piece = jnp.concatenate([down_weight.T, up_weight], 1)
 
     row = lambda v: v.reshape(1, -1)
     gain_one, shift_one = row(norm_one_gain), row(norm_one_shift)
@@ -987,117 +1097,261 @@
         array = array.reshape((slots, WTOK) + array.shape[1:])
         return jnp.pad(array, [(0, padded - slots)] + [(0, 0)] * (array.ndim - 1))
 
-    rows_in, normed, grad_top, valid = prepare(
-        places,
-        jnp.pad(window_place, (0, padded - slots)),
-        jnp.pad(slot_live, (0, padded - slots)),
-        by_window(block_input),
-        by_window(cotangent),
-        gain_one,
-        shift_one,
-    )
-    if rings:
-        own_in, own_top, own_valid = rows_in, grad_top, valid
-        at = [4 * part for part in range(halves)]
+    places_all = jnp.pad(window_place, (0, padded - slots))
+    lives_all = jnp.pad(slot_live, (0, padded - slots))
+    blocks = [(part, part_rows) for part in range(halves)]
+
+    def start(x):
+        return prepare(places, places_all, lives_all, x, gain_one, shift_one)
+
+    def masked(top):
+        return mask_rows(places, places_all, lives_all, top)
+
+    def attention(part, q, k, v, weights):
+        return attend(heads, part, windows, split, q, k, v, rel_high, rel_low, marks, weights)
+
+    def attention_back(part, pieces, q, k, v, shares, weights):
+        return attend_back(
+            heads, part, windows, split, pieces, q, k, v, shares, rel_high, marks, weights
+        )
+
+    def down_groups(mlps):
+        return [[(grad_top, *blocks[i], mlps[i][0]) for i in range(halves)]]
+
+    def up_groups(mlps):
+        return [[(mlps[i][2], 0, part_rows, mlps[i][1]) for i in range(halves)]]
+
+    def first_groups(backs, attended):
+        return [
+            [(normed, *blocks[i], backs[i][0]) for i in range(halves)],
+            [(backs[i][1], 0, part_rows, attended[i][0]) for i in range(halves)],
+        ]
+
+    x_windows, top_windows = by_window(block_input), by_window(cotangent)
+    if not rings:
+        first_weights, other_weights = gather(first_piece), gather(other_piece)
+        rows_in, normed, valid = start(x_windows)
+        grad_top = masked(top_windows)
+        own_in, own_top, own_valid = own_slice(rows_in), own_slice(grad_top), own_slice(valid)
+        q, k, v, weights = project(offsets, first_weights, normed, bias_qkv, cols, wide)
+        attended = [attention(0, q, k, v, weights)]
+        after, normed_two = norm_two(
+            rows_scatter(attended[0][2:]), own_in, 0, row(proj_bias), gain_two, shift_two
+        )
+        none = jnp.zeros((1, 128), F32)
+        mlps = [
+            mlp(
+                offsets,
+                rows_gather(normed_two),
+                other_weights,
+                grad_top,
+                0,
+                up_local,
+                none,
+                none,
+                False,
+            )
+        ]
+        grad_after, branch, sums = norm_two_back(
+            rows_scatter(mlps[0][4:5]), after, own_top, 0, gain_two
+        )
+        sums_two = [sums]
+        result = mlps[0][5]
+        own = finish(rows_scatter([result]), after, own_valid, 0, row(down_bias))
+
+        def unpad(array):
+            array = array.reshape(padded, ROWS, width)[:slots, :WTOK]
+            return array.reshape(slots * WTOK, width)
+
+        block_output = unpad(rows_gather(own)[0])
+        down_grad = scatter(weight_grad(None, down_groups(mlps), share))
+        up_grad = scatter(weight_grad(None, up_groups(mlps), share))
+        backs = [attention_back(0, rows_gather(branch), q, k, v, attended[0][1], weights)]
+        own, sums = norm_one_back(
+            rows_scatter(backs[0][4:]), own_in, own_valid, 0, grad_after, gain_one
+        )
+        sums_one = [sums]
+        input_grad = unpad(rows_gather(own)[0]).astype(F32)
+        first_grad = scatter(weight_grad(None, first_groups(backs, attended), share))
     else:
-        own_in, own_top, own_valid = own_slice(rows_in), own_slice(grad_top), own_slice(valid)
-        at = [0]
-
-    q, k, v, weights = project(offsets, first_weights, normed, bias_qkv, cols, wide)
-    attended = [
-        attend(heads, part, windows, split, q, k, v, rel_high, rel_low, marks, weights)
-        for part in range(halves)
-    ]
-    afters, normed_twos = [], []
-    for part in range(halves):
-        parts = rows_scatter(attended[part][2:])
-        after, normed_two = norm_two(
-            parts, own_in, at[part], row(proj_bias), gain_two, shift_two
-        )
-        afters.append(after)
-        normed_twos.append(rows_gather(normed_two))
-
-    mlps = [
-        mlp(
-            offsets,
-            local,
-            normed_twos[part],
-            other_weights,
-            grad_top,
-            part,
-            up_local,
-            bool(split),
-        )
-        for part in range(halves)
-    ]
-    grad_afters, branches, sums_two = [], [], []
-    for part in range(halves):
-        parts = rows_scatter(mlps[part][5:])
-        grad_after, branch, sums = norm_two_back(
-            parts, afters[part], own_top, at[part], gain_two
-        )
-        grad_afters.append(grad_after)
-        branches.append(rows_gather(branch))
-        sums_two.append(sums)
-    out_pieces = []
-    for part in range(halves):
-        result = lax.psum_scatter(mlps[part][4], "mp", scatter_dimension=0, tiled=True)
-        own = finish([result], afters[part], own_valid, at[part], row(down_bias))
-        out_pieces.append(own)
-    full = lax.all_gather(jnp.concatenate(out_pieces, 0), "mp", axis=0, tiled=True)
-    if rings:
-        full = full.reshape(4, halves, ROWS, width).swapaxes(0, 1)
-    full = full.reshape(padded, ROWS, width)
-    block_output = full[:slots, :WTOK].reshape(slots * WTOK, width)
-
-    blocks = [(part, part_rows) for part in range(halves)]
-    down_grad = scatter(
-        weight_grad(
-            targets, [[(grad_top, *blocks[i], mlps[i][0]) for i in range(halves)]], share
-        )
-    )
-    up_grad = scatter(
-        weight_grad(
-            targets, [[(mlps[i][2], 0, part_rows, mlps[i][1]) for i in range(halves)]], share
-        )
-    )
-
-    backs = [
-        attend_back(
-            heads,
-            part,
-            windows,
-            split,
-            branches[part],
-            q,
-            k,
-            v,
-            attended[part][1],
-            rel_high,
-            marks,
-            weights,
-        )
-        for part in range(halves)
-    ]
-    sums_one = []
-    input_grad = None
-    for part in range(halves):
-        parts = rows_scatter(backs[part][4:])
-        own, sums = norm_one_back(
-            parts, own_in, own_valid, at[part], grad_afters[part], gain_one
-        )
-        sums_one.append(sums)
-        gathered = rows_gather(own)
-        if rings:
-            input_grad = place_windows(part, local, gathered, slots * WTOK, input_grad)
-        else:
-            full = gathered[0].reshape(padded, ROWS, width)[:slots, :WTOK]
-            input_grad = full.reshape(slots * WTOK, width).astype(F32)
-    groups = [
-        [(normed, *blocks[i], backs[i][0]) for i in range(halves)],
-        [(backs[i][1], 0, part_rows, attended[i][0]) for i in range(halves)],
-    ]
-    first_grad = scatter(weight_grad(targets, groups, share))
+        def second_norm(part, keep, came, crossed):
+            return norm_two(
+                [keep, came, crossed], rows_in, 4 * part, row(proj_bias), gain_two, shift_two
+            )
+
+        def second_back(part, after, keep, came, crossed):
+            return norm_two_back([keep, came, crossed], after, grad_top, 4 * part, gain_two)
+
+        def first_back(part, grad_after, keep, came, crossed):
+            return norm_one_back(
+                [keep, came, crossed], rows_in, valid, 4 * part, grad_after, gain_one
+            )
+
+        def spread(own, across):
+            return [own, across, over_core(own), over_core(across)]
+
+        def to_core(keep, send):
+            came = over_core(send)
+            return came, joined(keep[ROWS:], came[ROWS:])
+
+        bias_row = row(down_bias)
+
+        z1, x0 = over_z(first_piece), over_x(first_piece)
+        z1, x0, x_windows, top_windows, other_piece, rel_high, rel_low = sync(
+            z1, x0, x_windows, top_windows, other_piece, rel_high, rel_low
+        )
+        z2, x1 = over_z(z1), over_x(z1)
+        rows_in, normed, valid = start(x_windows)
+        z2, x1, normed, top_windows = sync(z2, x1, normed, top_windows)
+        z3, x2 = over_z(z2), over_x(z2)
+        grad_top = masked(top_windows)
+        z3, x2, normed, grad_top, other_piece = sync(z3, x2, normed, grad_top, other_piece)
+        x3 = over_x(z3)
+        oz1 = over_z(other_piece)
+        x3, normed, other_late = sync(x3, normed, other_piece)
+        ox0 = over_x(other_late)
+        first_weights = [first_piece, x0, z1, x1, z2, x2, z3, x3]
+        q, k, v, weights = project(offsets, first_weights, normed, bias_qkv, cols, wide)
+        oz1, ox0, q = sync(oz1, ox0, q)
+
+        oz2, ox1 = over_z(oz1), over_x(oz1)
+        a0 = attention(0, q, k, v, weights)
+        oz2, ox1, a0 = sync(oz2, ox1, a0)
+        oz3, ox2 = over_z(oz2), over_x(oz2)
+        came0, passed0 = to_core(a0[2], a0[3])
+        crossed0 = over_y(passed0)
+        a1 = attention(1, tie(q, passed0), k, v, weights)
+        oz3, ox2, crossed0, a1 = sync(oz3, ox2, crossed0, a1)
+        ox3 = over_x(oz3)
+        after0, own0 = second_norm(0, a0[2], came0, crossed0)
+        across0 = over_y(own0)
+        came1, passed1 = to_core(a1[2], a1[3])
+        crossed1 = over_y(tie(passed1, own0))
+        attended = [a0, a1]
+        ox3, across0, crossed1 = sync(ox3, across0, crossed1)
+        other_weights = [other_piece, ox0, oz1, ox1, oz2, ox2, oz3, ox3]
+        after1, own1 = second_norm(1, a1[2], came1, crossed1)
+        across1 = over_y(own1)
+        pieces0 = spread(own0, across0)
+        pieces0[0] = tie(pieces0[0], own1)
+
+        m0 = mlp(offsets, pieces0, other_weights, grad_top, 0, up_local, after0, bias_row, True)
+        across1, m0 = sync(across1, m0)
+        pieces1 = spread(own1, across1)
+        came0, passed0 = to_core(m0[4], m0[5])
+        crossed0 = over_y(passed0)
+        pieces1[0] = tie(pieces1[0], passed0)
+        m1 = mlp(offsets, pieces1, other_weights, grad_top, 1, up_local, after1, bias_row, True)
+        crossed0, m1 = sync(crossed0, m1)
+        mlps = [m0, m1]
+        grad_after0, branch0, sums0 = second_back(0, after0, m0[4], came0, crossed0)
+        came1, passed1 = to_core(m1[4], m1[5])
+        across0 = over_y(branch0)
+        crossed1 = over_y(tie(passed1, branch0))
+        left = tie(m0, branch0, passed1)
+        (down_pairs,) = weight_grad(targets, down_groups([left, m1]), share, 0)
+        down_pairs = sync(down_pairs)[0]
+        down_held = over_z(down_pairs[3])
+        up_send, up_keep = weight_grad(
+            targets, up_groups([tie(m0, down_pairs), m1]), share
+        )
+        across0, crossed1, down_held, up_send, up_keep = sync(
+            across0, crossed1, down_held, up_send, up_keep
+        )
+
+        grad_after1, branch1, sums1 = second_back(1, after1, m1[4], came1, crossed1)
+        sums_two = [sums0, sums1]
+        across1 = over_y(branch1)
+        branches0 = spread(branch0, across0)
+        out_came0, out_passed0 = to_core(m0[6], tie(m0[7], branch1))
+        out_crossed0 = over_y(out_passed0)
+        down_held = over_z(joined(down_pairs[2], down_held))
+        up_came_high = over_x(up_send[2:])
+        branches0[0] = tie(branches0[0], branch1, out_passed0)
+        b0 = attention_back(0, branches0, q, k, v, a0[1], weights)
+        across1, out_crossed0, down_held, up_came_high, b0 = sync(
+            across1, out_crossed0, down_held, up_came_high, b0
+        )
+        branches1 = spread(branch1, across1)
+        came0, passed0 = to_core(b0[4], b0[5])
+        crossed0 = over_y(passed0)
+        out_came1, out_passed1 = to_core(m1[6], tie(m1[7], passed0))
+        out_crossed1 = over_y(out_passed1)
+        down_held = over_z(joined(down_pairs[1], down_held))
+        up_came_low = over_x(up_send[:2])
+        branches1[0] = tie(branches1[0], out_passed1)
+        b1 = attention_back(1, branches1, q, k, v, a1[1], weights)
+        crossed0, out_crossed1, down_held, up_came_low, b1 = sync(
+            crossed0, out_crossed1, down_held, up_came_low, b1
+        )
+        backs = [b0, b1]
+        own0, one0 = first_back(0, grad_after0, b0[4], came0, crossed0)
+        in_across0 = over_y(own0)
+        came1, passed1 = to_core(b1[4], b1[5])
+        crossed1 = over_y(tie(passed1, own0))
+        down_last = joined(down_pairs[0], down_held)
+        down_other = over_x(down_last[1])
+        up_held = over_z(joined(up_keep[3], up_came_high[1]))
+        left = tie(b0, own0, passed1, down_last)
+        first_send, first_keep, first_pairs = weight_grad(
+            targets, first_groups([left, b1], attended), share, 3 * cols // 128 * 128
+        )
+        in_across0, crossed1, down_other, up_held, first_send, first_keep, first_pairs = sync(
+            in_across0, crossed1, down_other, up_held, first_send, first_keep, first_pairs
+        )
+
+        first_came = over_x(first_send)
+        pair_held = over_z(first_pairs[3])
+        own1, one1 = first_back(1, grad_after1, b1[4], came1, crossed1)
+        sums_one = [one0, one1]
+        in_across1 = over_y(own1)
+        in_pieces0 = spread(own0, in_across0)
+        up_held = over_z(joined(up_keep[2], up_came_high[0], up_held))
+        pair_held = over_z(joined(first_pairs[2], pair_held))
+        out_own0 = joined(m0[6][:ROWS], out_came0[:ROWS], out_crossed0)
+        out_own1 = joined(m1[6][:ROWS], out_came1[:ROWS], out_crossed1)
+        out_across0, out_across1 = over_y(tie(out_own0, own1)), over_y(tie(out_own1, own1))
+        input_grad = place_windows(0, local, in_pieces0, slots * WTOK, None)
+        in_across1, up_held, pair_held, first_came, input_grad = sync(
+            in_across1, up_held, pair_held, first_came, input_grad
+        )
+        first_held = over_z(joined(first_keep[3], first_came[3]))
+        pair_held = over_z(joined(first_pairs[1], pair_held))
+        up_held = over_z(joined(up_keep[1], up_came_low[1], up_held))
+        in_pieces1 = spread(own1, in_across1)
+        input_grad = place_windows(1, local, in_pieces1, slots * WTOK, input_grad)
+        first_held, pair_held, up_held, input_grad, out_across0, out_across1 = sync(
+            first_held, pair_held, up_held, input_grad, out_across0, out_across1
+        )
+        first_held = over_z(joined(first_keep[2], first_came[2], first_held))
+        pair_last = joined(first_pairs[0], pair_held)
+        pair_other = over_x(pair_last[1])
+        out_pieces0 = spread(out_own0, out_across0)
+        block_output = write_output(
+            0, local, places_all, lives_all, out_pieces0, slots * WTOK, None
+        )
+        first_held, pair_other, block_output = sync(first_held, pair_other, block_output)
+        first_held = over_z(joined(first_keep[1], first_came[1], first_held))
+        out_pieces1 = spread(out_own1, out_across1)
+        block_output = write_output(
+            1, local, places_all, lives_all, out_pieces1, slots * WTOK, block_output
+        )
+
+        def last(*values):
+            out = values[0].astype(F32)
+            for value in values[1:]:
+                out = out + value.astype(F32)
+            return out
+
+        down_grad = last(down_pairs[0, 0], down_held[0], down_other)
+        up_grad = last(up_keep[0], up_came_low[0], up_held)
+        first_grad = jnp.concatenate(
+            [
+                last(first_keep[0], first_came[0], first_held),
+                last(first_pairs[0, 0], pair_held[0], pair_other),
+            ],
+            axis=1,
+        )
 
     two = add_all(sums_two)
     one = add_all(sums_one)

time: 575 us -> 475 us (0.83)
  waiting for transfers between devices: 218 us -> 107 us
  other arithmetic: 35.1 us -> 49.2 us
  between operations: 14.9 us -> 2.17 us
  Pallas kernels: 209 us -> 220 us
  local copies, waits for them, and re-layouts: 44 us -> 37 us
    ppermute x56 -> x71, waiting for transfers between devices: 211 us -> 84.2 us  [the longest x1 12 us: body(): across0 = over_y(own0)]
    ppermute x3, waiting for transfers between devices: 3.34 us -> 22 us  [sum_all(): lax.ppermute(vector, 'dp', [(d, d ^ step) for d in range(8)])]
    convert_element_type x15 -> x21, other arithmetic: 22 us -> 35.7 us  [joined(): return total_value.astype(BF16)]
    ppermute x56 -> x71, starting transfers between devices: 38 us -> 50.6 us  [the longest x2 4.57 us: body(): z1, x0 = (over_z(first_piece), over_x(first_piece))]
    pallas_call x2 -> x3, Pallas kernels: 4.74 us -> 16.3 us  [the longest x2 8.55 us: write_output(): pl.pallas_call(partial(output_kernel, part), grid_spec=pltpu.PrefetchScal...]
    reshape x2 -> x0, local copies, waits for them, and re-layouts: 7.36 us -> none  [the longest x1 4.88 us: body(): block_output = full[:slots, :WTOK].reshape(slots * WTOK, width)]
    ppermute x3, starting transfers between devices: 8.48 us -> 1.22 us  [sum_all(): lax.ppermute(vector, 'dp', [(d, d ^ step) for d in range(8)])]
  transfers between devices with their start and end apart: 64 -> 76, of which waited for: 22 -> 26; matrix products, arithmetic and copies ran while one was open for 10% -> 15% of each run, Pallas kernels for 33% -> 44%
where the time goes in v3:
time: 475 us; the launch traced here: 468 us
  Pallas kernels  220 us (46%)
  waiting for transfers between devices  107 us (23%)
  starting transfers between devices  53.1 us (11%)
  other arithmetic  49.2 us (10%)
  local copies, waits for them, and re-layouts  37 us (8%)
    pallas_call x2, Pallas kernels, mlp(): pl.pallas_call(partial(mlp_kernel, len(pieces), len(weight_pieces), split...  45.2 us
    pallas_call x3, Pallas kernels, weight_grad(): pl.pallas_call(partial(weight_grad_kernel, sizes, share), grid_spec=pltpu...  39.3 us
    pallas_call x2, Pallas kernels, attend_back(): pl.pallas_call(partial(attend_back_kernel, heads, windows, split, len(pie...  37.2 us
    convert_element_type x21, other arithmetic, joined(): return total_value.astype(BF16)  35.7 us
    pallas_call x2, Pallas kernels, attend(): pl.pallas_call(partial(attend_kernel, heads, split), grid=(windows,), in_...  27.4 us
    ppermute x3, waiting for transfers between devices, sum_all(): lax.ppermute(vector, 'dp', [(d, d ^ step) for d in range(8)])  22 us
    pallas_call x1, Pallas kernels, project(): pl.pallas_call(partial(qkv_kernel, len(pieces), cols), grid_spec=pltpu.Pr...  14 us
    ppermute x1, waiting for transfers between devices, body(): across0 = over_y(own0)  12 us
  transfers between devices with their start and end apart: 76, of which 26 were waited for; matrix products, arithmetic and copies ran while one was open for 15% of the time, Pallas kernels for 44%

profile of v3, /device:TPU:0, one launch (start us, length us, event | category | flops | bytes accessed | tf_op | source)
XLA Modules:
  0.0 467.9 jit_solution(857974777141655849)
XLA Ops:
  2.9 3.1 collective-permute-start
  8.8 4.9 %reshape.164.x_ref = bf16[8,196,1280]{2,1,0:T(8,128)(2,1)} reshape(bf16[1568,1280]{1,0:T(8,128)(2,1)} %param.19) | data formatting | bytes 8028160 | tf_op jit(solution)/shard_map/reshape | solution.py:1097
  13.8 5.0 %reshape.165.top_ref = bf16[8,196,1280]{2,1,0:T(8,128)(2,1)} reshape(bf16[1568,1280]{1,0:T(8,128)(2,1)} %param.36) | data formatting | bytes 8028160 | tf_op jit(solution)/shard_map/reshape | solution.py:1097
  22.8 9.6 %prepare.1 = (bf16[1664,1280]{1,0:T(8,128)(2,1)}, bf16[1664,1280]{1,0:T(8,128)(2,1)}, f32[1664,1]{1,0:T(8,128)}) custom-call(s32[8]{0:T(128)} %stack.112.order, s32[8]{0:T(128)} %places.7, s32[8]{0:T(128)} %lives.7, bf16[8,196,1280]{2,1,0:T(8,128)(2,1)} %reshape.164.x_ref, f32[1,1280]{1,0:T(1,128)} %reshape.166.gain_ref.refs_6_, f32[1,1280]{1,0:T(1,128)} %reshape.167.shift_ref), custom_call_target="tpu_custom_call" | custom-call | flops 450000000 | bytes 90000 | tf_op jit(solution)/shard_map/prepare/pallas_call | solution.py:110
  35.6 7.7 %mask_rows.1.refs_12_.refs_4_.refs_0_.refs_2_ = bf16[1664,1280]{1,0:T(8,128)(2,1)} custom-call(s32[8]{0:T(128)} %stack.112.order, s32[8]{0:T(128)} %places.7, s32[8]{0:T(128)} %lives.7, bf16[8,196,1280]{2,1,0:T(8,128)(2,1)} %reshape.165.top_ref), custom_call_target="tpu_custom_call" | custom-call | flops 300000000 | bytes 60000 | tf_op jit(solution)/shard_map/mask_rows/pallas_call | solution.py:134
  45.9 8.1 %collective-permute-done.7.refs_7_ = bf16[160,1280]{1,0:T(8,128)(2,1)S(1)} collective-permute-done((bf16[160,1280]{1,0:T(8,128)(2,1)S(1)}, bf16[160,1280]{1,0:T(8,128)(2,1)S(1)}, u32[]{:S(2)}, u32[]{:S(2)}) %collective-permute-start.7) | collective-permute-done | bytes 409632 | tf_op jit(solution)/shard_map/ppermute | solution.py:1209
  57.1 14.0 %qkv.1 = (bf16[1664,384]{1,0:T(8,128)(2,1)}, bf16[1664,384]{1,0:T(8,128)(2,1)}, bf16[1664,384]{1,0:T(8,128)(2,1)}, bf16[1280,1536]{1,0:T(8,128)(2,1)}) custom-call(s32[8]{0:T(128)} %stack.121.offsets, bf16[160,1280]{1,0:T(8,128)(2,1)} %copy-done.22, bf16[160,1280]{1,0:T(8,128)(2,1)} %copy-done.52, bf16[160,1280]{1,0:T(8,128)(2,1)} %copy-done.51, ...), custom_call_target="tpu_custom_call" | custom-call | flops 700000000 | bytes 140000 | tf_op jit(solution)/shard_map/qkv/pallas_call | solution.py:304
  74.0 13.7 %attend.2 = (bf16[832,320]{1,0:T(8,128)(2,1)}, bf16[832,1024]{1,0:T(8,128)(2,1)}, bf16[416,1280]{1,0:T(8,128)(2,1)}, bf16[416,1280]{1,0:T(8,128)(2,1)}) custom-call(bf16[1664,384]{1,0:T(8,128)(2,1)} %get-tuple-element.229.q_ref.refs_4_, bf16[1664,384]{1,0:T(8,128)(2,1)} %get-tuple-element.217.k_ref.refs_5_, ...), custom_call_target="tpu_custom_call" | custom-call | flops 675000000 | bytes 135000 | tf_op jit(solution)/shard_map/attend/pallas_call | solution.py:443
  96.8 13.7 %attend.3 = (bf16[832,320]{1,0:T(8,128)(2,1)}, bf16[832,1024]{1,0:T(8,128)(2,1)}, bf16[416,1280]{1,0:T(8,128)(2,1)}, bf16[416,1280]{1,0:T(8,128)(2,1)}) custom-call(bf16[1664,384]{1,0:T(8,128)(2,1)} %get-tuple-element.229.q_ref.refs_4_, bf16[1664,384]{1,0:T(8,128)(2,1)} %get-tuple-element.217.k_ref.refs_5_, ...), custom_call_target="tpu_custom_call" | custom-call | flops 675000000 | bytes 135000 | tf_op jit(solution)/shard_map/attend/pallas_call | solution.py:443
  115.4 3.1 norm_two.2
  121.8 12.0 %collective-permute-done.17.refs_1_ = bf16[208,1280]{1,0:T(8,128)(2,1)} collective-permute-done((bf16[208,1280]{1,0:T(8,128)(2,1)}, bf16[208,1280]{1,0:T(8,128)(2,1)}, u32[]{:S(2)}, u32[]{:S(2)}) %collective-permute-start.17) | collective-permute-done | bytes 532512 | tf_op jit(solution)/shard_map/ppermute | solution.py:1227
  134.6 9.6 %collective-permute-done.18.refs_2_ = bf16[208,1280]{1,0:T(8,128)(2,1)S(1)} collective-permute-done((bf16[208,1280]{1,0:T(8,128)(2,1)S(1)}, bf16[208,1280]{1,0:T(8,128)(2,1)S(1)}, u32[]{:S(2)}, u32[]{:S(2)}) %collective-permute-start.18) | collective-permute-done | bytes 532512 | tf_op jit(solution)/shard_map/ppermute | solution.py:1229
  145.1 3.0 norm_two.3
  152.6 22.5 %mlp.2 = (bf16[832,1280]{1,0:T(8,128)(2,1)}, bf16[832,1280]{1,0:T(8,128)(2,1)}, bf16[832,1280]{1,0:T(8,128)(2,1)}, f32[1,1280]{1,0:T(1,128)}, bf16[416,1280]{1,0...) custom-call(s32[8]{0:T(128)} %stack.121.offsets, ...), custom_call_target="tpu_custom_call" | custom-call | flops 1050000000 | bytes 210000 | tf_op jit(solution)/shard_map/mlp/pallas_call | solution.py:680
  175.7 2.9 collective-permute-done.22.refs_1_
  178.7 2.3 add_convert_fusion.7
  182.5 22.7 %mlp.3 = (bf16[832,1280]{1,0:T(8,128)(2,1)}, bf16[832,1280]{1,0:T(8,128)(2,1)}, bf16[832,1280]{1,0:T(8,128)(2,1)}, f32[1,1280]{1,0:T(1,128)}, bf16[416,1280]{1,0...) custom-call(s32[8]{0:T(128)} %stack.121.offsets, ...), custom_call_target="tpu_custom_call" | custom-call | flops 1050000000 | bytes 210000 | tf_op jit(solution)/shard_map/mlp/pallas_call | solution.py:680
  206.1 4.2 norm_two_back.2
  210.4 12.1 %weight_grad.3 = bf16[4,2,160,1280]{3,2,1,0:T(8,128)(2,1)} custom-call(s32[8]{0:T(128)} %stack.131.targets, bf16[1664,1280]{1,0:T(8,128)(2,1)} %mask_rows.1.refs_12_.refs_4_.refs_0_.refs_2_, bf16[832,1280]{1,0:T(8,128)(2,1)} %get-tuple-element.285.refs_1_, bf16[1664,1280]{1,0:T(8,128)(2,1)} %mask_rows.1.refs_12_.refs_4_.refs_0_.refs_2_, ...), custom_call_target="tpu_custom_call" | custom-call | flops 650000000 | bytes 130000 | tf_op jit(solution)/shard_map/weight_grad/pallas_call | solution.py:819
  226.0 12.3 %weight_grad.4 = (bf16[4,160,1280]{2,1,0:T(8,128)(2,1)}, bf16[4,160,1280]{2,1,0:T(8,128)(2,1)}) custom-call(s32[8]{0:T(128)} %stack.131.targets, bf16[832,1280]{1,0:T(8,128)(2,1)} %get-tuple-element.287.refs_0_, bf16[832,1280]{1,0:T(8,128)(2,1)} %get-tuple-element.288.refs_1_, bf16[832,1280]{1,0:T(8,128)(2,1)} %get-tuple-element.289.refs_2_, ...), custom_call_target="tpu_custom_call" | custom-call | flops 650000000 | bytes 130000 | tf_op jit(solution)/shard_map/weight_grad/pallas_call | solution.py:819
  239.1 10.8 %collective-permute-done.28.refs_2_ = bf16[208,1280]{1,0:T(8,128)(2,1)S(1)} collective-permute-done((bf16[208,1280]{1,0:T(8,128)(2,1)S(1)}, bf16[208,1280]{1,0:T(8,128)(2,1)S(1)}, u32[]{:S(2)}, u32[]{:S(2)}) %collective-permute-start.28) | collective-permute-done | bytes 532512 | tf_op jit(solution)/shard_map/ppermute | solution.py:1250
  251.0 4.3 norm_two_back.3
  256.8 2.3 fusion.2
  264.2 18.5 %attend_back.2 = (bf16[832,960]{1,0:T(8,128)(2,1)}, bf16[832,1280]{1,0:T(8,128)(2,1)}, f32[256,384]{1,0:T(8,128)}, f32[1,1152]{1,0:T(1,128)}, bf16[416,1280]{1,0:T(8,128)(2,1)}, /*index=5*/bf16[416,1280]{1,0:T(8,128)(2,1)}) custom-call(bf16[208,1280]{1,0:T(8,128)(2,1)} %get-tuple-element.298.refs_0_, bf16[208,1280]{1,0:T(8,128)(2,1)} %copy-done.37, ...), custom_call_target="tpu_custom_call" | custom-call | flops 925000000 | bytes 185000 | tf_op jit(solution)/shard_map/attend_back/pallas_call | solution.py:561
  282.9 2.8 collective-permute-done.37.refs_1_
  289.9 2.3 fusion.1
  292.2 2.1 collective-permute-start.41
  298.2 18.7 %attend_back.3 = (bf16[832,960]{1,0:T(8,128)(2,1)}, bf16[832,1280]{1,0:T(8,128)(2,1)}, f32[256,384]{1,0:T(8,128)}, f32[1,1152]{1,0:T(1,128)}, bf16[416,1280]{1,0:T(8,128)(2,1)}, /*index=5*/bf16[416,1280]{1,0:T(8,128)(2,1)}) custom-call(bf16[208,1280]{1,0:T(8,128)(2,1)} %get-tuple-element.311.refs_0_, bf16[208,1280]{1,0:T(8,128)(2,1)} %collective-permute-done.30.refs_1_, ...), custom_call_target="tpu_custom_call" | custom-call | flops 925000000 | bytes 185000 | tf_op jit(solution)/shard_map/attend_back/pallas_call | solution.py:561
  316.9 3.6 collective-permute-done.40
  323.1 2.1 collective-permute-start.49
  325.2 3.6 norm_one_back.2
  338.1 14.9 %weight_grad.5 = (bf16[4,160,896]{2,1,0:T(8,128)(2,1)}, bf16[4,160,896]{2,1,0:T(8,128)(2,1)}, bf16[4,2,160,384]{3,2,1,0:T(8,128)(2,1)}) custom-call(s32[8]{0:T(128)} %stack.131.targets, bf16[1664,1280]{1,0:T(8,128)(2,1)} %get-tuple-element.213.refs_8_.refs_0_.refs_2_, bf16[832,960]{1,0:T(8,128)(2,1)} %get-tuple-element.335.refs_1_, ...), custom_call_target="tpu_custom_call" | custom-call | flops 650000000 | bytes 130000 | tf_op jit(solution)/shard_map/weight_grad/pallas_call | solution.py:819
  354.8 3.7 norm_one_back.3
  359.4 2.5 add_convert_fusion.refs_0_
  370.1 4.9 %collective-permute-done.72 = f32[160,128]{1,0:T(8,128)S(1)} collective-permute-done((f32[160,128]{1,0:T(8,128)S(1)}, f32[160,128]{1,0:T(8,128)S(1)}, u32[]{:S(2)}, u32[]{:S(2)}) %collective-permute-start.72) | collective-permute-done | bytes 81952 | tf_op jit(solution)/shard_map/ppermute | solution.py:1056
  375.1 2.2 fusion.4
  377.3 3.1 collective-permute-done.73
  381.1 2.2 fusion.6
  383.3 13.9 %collective-permute-done.74 = f32[160,128]{1,0:T(8,128)S(1)} collective-permute-done((f32[160,128]{1,0:T(8,128)S(1)}, f32[160,128]{1,0:T(8,128)S(1)}, u32[]{:S(2)}, u32[]{:S(2)}) %collective-permute-start.74) | collective-permute-done | bytes 81952 | tf_op jit(solution)/shard_map/ppermute | solution.py:1056
  401.3 4.6 place_windows.2.refs_4_
  406.0 5.2 %collective-permute-done.51 = bf16[160,1280]{1,0:T(8,128)(2,1)S(1)} collective-permute-done((bf16[160,1280]{1,0:T(8,128)(2,1)}, bf16[160,1280]{1,0:T(8,128)(2,1)S(1)}, u32[]{:S(2)}, u32[]{:S(2)}) %collective-permute-start.51) | collective-permute-done | bytes 409632 | tf_op jit(solution)/shard_map/ppermute | solution.py:1309
  423.5 4.5 place_windows.3
  428.1 3.9 collective-permute-done.63.refs_1_
  432.0 7.7 %collective-permute-done.58 = bf16[2,160,384]{2,1,0:T(8,128)(2,1)} collective-permute-done((bf16[2,160,384]{2,1,0:T(8,128)(2,1)}, bf16[2,160,384]{2,1,0:T(8,128)(2,1)}, u32[]{:S(2)}, u32[]{:S(2)}) %collective-permute-start.58) | collective-permute-done | bytes 245792 | tf_op jit(solution)/shard_map/ppermute | solution.py:1319
  445.4 4.3 write_output.2.refs_4_
  449.7 3.2 collective-permute-done.66
  457.1 4.3 write_output.3
  462.4 2.1 collective-permute-done.75
  (367 shorter events, 121.0 us)
Async XLA Ops:
  2.9 15.9 %collective-permute-start = (bf16[160,1280]{1,0:T(8,128)(2,1)S(1)}, bf16[160,1280]{1,0:T(8,128)(2,1)S(1)}, u32[]{:S(2)}, u32[]{:S(2)}) collective-permute-start(bf16[160,1280]{1,0:T(8,128)(2,1)S(1)} %concatenate.15.refs_0_), channel_id=1, source_target_pairs={{0,8},{4,12},{8,16},{12,20},{16,24},{20,28},{24,0},{28,4},{1,9},{5... | collective-permute-start | bytes 1228808 | tf_op jit(solution)/shard_map/ppermute | solution.py:1199
  6.0 12.8 %collective-permute-start.1 = (bf16[160,1280]{1,0:T(8,128)(2,1)S(1)}, bf16[160,1280]{1,0:T(8,128)(2,1)S(1)}, u32[]{:S(2)}, u32[]{:S(2)}) collective-permute-start(bf16[160,1280]{1,0:T(8,128)(2,1)S(1)} %concatenate.15.refs_0_), channel_id=1, source_target_pairs={{0,4},{4,0},{8,12},{12,8},{16,20},{20,16},{24,28},{28,24},{1,5},{5... | collective-permute-start | bytes 1228808 | tf_op jit(solution)/shard_map/ppermute | solution.py:1199
  18.9 13.5 %collective-permute-start.2 = (bf16[160,1280]{1,0:T(8,128)(2,1)S(1)}, bf16[160,1280]{1,0:T(8,128)(2,1)S(1)}, u32[]{:S(2)}, u32[]{:S(2)}) collective-permute-start(bf16[160,1280]{1,0:T(8,128)(2,1)S(1)} %collective-permute-done.refs_2_), channel_id=1, source_target_pairs={{0,8},{4,12},{8,16},{12,20},{16,24},{20,28},{24,0},{28,4},{1,9},{5... | collective-permute-start | bytes 1228808 | tf_op jit(solution)/shard_map/ppermute | solution.py:1203
  45.9 25.2 %collective-permute-start.6 = (bf16[160,2560]{1,0:T(8,128)(2,1)S(1)}, bf16[160,2560]{1,0:T(8,128)(2,1)S(1)}, u32[]{:S(2)}, u32[]{:S(2)}) collective-permute-start(bf16[160,2560]{1,0:T(8,128)(2,1)S(1)} %pad_maximum_fusion.refs_4_), channel_id=1, source_target_pairs={{0,8},{4,12},{8,16},{12,20},{16,24},{20,28},{24,0},{28,4},{1,9},{5... | collective-permute-start | bytes 2457608 | tf_op jit(solution)/shard_map/ppermute | solution.py:1210
  54.0 18.2 %collective-permute-start.8 = (bf16[160,2560]{1,0:T(8,128)(2,1)S(1)}, bf16[160,2560]{1,0:T(8,128)(2,1)S(1)}, u32[]{:S(2)}, u32[]{:S(2)}) collective-permute-start(bf16[160,2560]{1,0:T(8,128)(2,1)S(1)} %pad_maximum_fusion.refs_4_), channel_id=1, source_target_pairs={{0,4},{4,0},{8,12},{12,8},{16,20},{20,16},{24,28},{28,24},{1,5},{5... | collective-permute-start | bytes 2457608 | tf_op jit(solution)/shard_map/ppermute | solution.py:1212
  72.2 17.2 %collective-permute-start.9 = (bf16[160,2560]{1,0:T(8,128)(2,1)S(1)}, bf16[160,2560]{1,0:T(8,128)(2,1)S(1)}, u32[]{:S(2)}, u32[]{:S(2)}) collective-permute-start(bf16[160,2560]{1,0:T(8,128)(2,1)S(1)} %collective-permute-done.6.refs_6_), channel_id=1, source_target_pairs={{0,8},{4,12},{8,16},{12,20},{16,24},{20,28},{24,0},{28,4},{1,9},{5... | collective-permute-start | bytes 2457608 | tf_op jit(solution)/shard_map/ppermute | solution.py:1217
  72.2 17.2 %collective-permute-start.10 = (bf16[160,2560]{1,0:T(8,128)(2,1)S(1)}, bf16[160,2560]{1,0:T(8,128)(2,1)S(1)}, u32[]{:S(2)}, u32[]{:S(2)}) collective-permute-start(bf16[160,2560]{1,0:T(8,128)(2,1)S(1)} %collective-permute-done.6.refs_6_), channel_id=1, source_target_pairs={{0,4},{4,0},{8,12},{12,8},{16,20},{20,16},{24,28},{28,24},{1,5},{5... | collective-permute-start | bytes 2457608 | tf_op jit(solution)/shard_map/ppermute | solution.py:1217
  89.4 22.6 %collective-permute-start.11 = (bf16[160,2560]{1,0:T(8,128)(2,1)S(1)}, bf16[160,2560]{1,0:T(8,128)(2,1)S(1)}, u32[]{:S(2)}, u32[]{:S(2)}) collective-permute-start(bf16[160,2560]{1,0:T(8,128)(2,1)S(1)} %collective-permute-done.9.refs_8_), channel_id=1, source_target_pairs={{0,8},{4,12},{8,16},{12,20},{16,24},{20,28},{24,0},{28,4},{1,9},{5... | collective-permute-start | bytes 2457608 | tf_op jit(solution)/shard_map/ppermute | solution.py:1220
  89.7 22.4 %collective-permute-start.12 = (bf16[160,2560]{1,0:T(8,128)(2,1)S(1)}, bf16[160,2560]{1,0:T(8,128)(2,1)S(1)}, u32[]{:S(2)}, u32[]{:S(2)}) collective-permute-start(bf16[160,2560]{1,0:T(8,128)(2,1)S(1)} %collective-permute-done.9.refs_8_), channel_id=1, source_target_pairs={{0,4},{4,0},{8,12},{12,8},{16,20},{20,16},{24,28},{28,24},{1,5},{5... | collective-permute-start | bytes 2457608 | tf_op jit(solution)/shard_map/ppermute | solution.py:1220
  95.3 16.8 %collective-permute-start.14 = (bf16[208,1280]{1,0:T(8,128)(2,1)}, bf16[208,1280]{1,0:T(8,128)(2,1)S(1)}, u32[]{:S(2)}, u32[]{:S(2)}) collective-permute-start(bf16[208,1280]{1,0:T(8,128)(2,1)} %add_convert_fusion.9), channel_id=1, source_target_pairs={{0,2},{1,3},{2,0},{3,1},{4,6},{5,7},{6,4},{7,5},{8,10},{9,11},{10,... | collective-permute-start | bytes 1597448 | tf_op jit(solution)/shard_map/ppermute | solution.py:1222
  114.1 20.5 %collective-permute-start.16 = (bf16[160,2560]{1,0:T(8,128)(2,1)S(1)}, bf16[160,2560]{1,0:T(8,128)(2,1)S(1)}, u32[]{:S(2)}, u32[]{:S(2)}) collective-permute-start(bf16[160,2560]{1,0:T(8,128)(2,1)S(1)} %collective-permute-done.11.refs_10_), channel_id=1, source_target_pairs={{0,4},{4,0},{8,12},{12,8},{16,20},{20,16},{24,28},{28,24},{1,5},{5... | collective-permute-start | bytes 2457608 | tf_op jit(solution)/shard_map/ppermute | solution.py:1225
  118.5 15.3 %collective-permute-start.17 = (bf16[208,1280]{1,0:T(8,128)(2,1)}, bf16[208,1280]{1,0:T(8,128)(2,1)}, u32[]{:S(2)}, u32[]{:S(2)}) collective-permute-start(bf16[208,1280]{1,0:T(8,128)(2,1)} %get-tuple-element.243.refs_0_), channel_id=1, source_target_pairs={{0,2},{1,3},{2,0},{3,1},{4,6},{5,7},{6,4},{7,5},{8,10},{9,11},{10,... | collective-permute-start | bytes 1597448 | tf_op jit(solution)/shard_map/ppermute | solution.py:1227
  121.3 23.0 %collective-permute-start.18 = (bf16[208,1280]{1,0:T(8,128)(2,1)S(1)}, bf16[208,1280]{1,0:T(8,128)(2,1)S(1)}, u32[]{:S(2)}, u32[]{:S(2)}) collective-permute-start(bf16[208,1280]{1,0:T(8,128)(2,1)S(1)} %add_convert_fusion.8), channel_id=1, source_target_pairs={{0,2},{1,3},{2,0},{3,1},{4,6},{5,7},{6,4},{7,5},{8,10},{9,11},{10,... | collective-permute-start | bytes 1597448 | tf_op jit(solution)/shard_map/ppermute | solution.py:1229
  121.8 29.8 %collective-permute-start.20 = (bf16[208,1280]{1,0:T(8,128)(2,1)}, bf16[208,1280]{1,0:T(8,128)(2,1)S(1)}, u32[]{:S(2)}, u32[]{:S(2)}) collective-permute-start(bf16[208,1280]{1,0:T(8,128)(2,1)} %get-tuple-element.243.refs_0_), channel_id=1, source_target_pairs={{0,1},{1,0},{2,3},{3,2},{4,5},{5,4},{6,7},{7,6},{8,9},{9,8},{10,11... | collective-permute-start | bytes 1597448 | tf_op jit(solution)/shard_map/ppermute | solution.py:1191
  148.1 27.0 %collective-permute-start.19 = (bf16[208,1280]{1,0:T(8,128)(2,1)}, bf16[208,1280]{1,0:T(8,128)(2,1)S(1)}, u32[]{:S(2)}, u32[]{:S(2)}) collective-permute-start(bf16[208,1280]{1,0:T(8,128)(2,1)} %get-tuple-element.261.refs_0_), channel_id=1, source_target_pairs={{0,2},{1,3},{2,0},{3,1},{4,6},{5,7},{6,4},{7,5},{8,10},{9,11},{10,... | collective-permute-start | bytes 1597448 | tf_op jit(solution)/shard_map/ppermute | solution.py:1234
  181.0 24.3 %collective-permute-start.23 = (bf16[208,1280]{1,0:T(8,128)(2,1)}, bf16[208,1280]{1,0:T(8,128)(2,1)S(1)}, u32[]{:S(2)}, u32[]{:S(2)}) collective-permute-start(bf16[208,1280]{1,0:T(8,128)(2,1)} %add_convert_fusion.7), channel_id=1, source_target_pairs={{0,2},{1,3},{2,0},{3,1},{4,6},{5,7},{6,4},{7,5},{8,10},{9,11},{10,... | collective-permute-start | bytes 1597448 | tf_op jit(solution)/shard_map/ppermute | solution.py:1242
  223.8 26.1 %collective-permute-start.29 = (bf16[2,160,1280]{2,1,0:T(8,128)(2,1)S(1)}, bf16[2,160,1280]{2,1,0:T(8,128)(2,1)S(1)}, u32[]{:S(2)}, u32[]{:S(2)}) collective-permute-start(bf16[2,160,1280]{2,1,0:T(8,128)(2,1)S(1)} %slice_bitcast_fusion.3), channel_id=1, source_target_pairs={{0,8},{4,12},{8,16},{12,20},{16,24},{20,28},{24,0},{28,4},{1,9},{5... | collective-permute-start | bytes 2457608 | tf_op jit(solution)/shard_map/ppermute | solution.py:1254
  223.9 15.2 %collective-permute-start.27 = (bf16[208,1280]{1,0:T(8,128)(2,1)}, bf16[208,1280]{1,0:T(8,128)(2,1)S(1)}, u32[]{:S(2)}, u32[]{:S(2)}) collective-permute-start(bf16[208,1280]{1,0:T(8,128)(2,1)} %get-tuple-element.298.refs_0_), channel_id=1, source_target_pairs={{0,2},{1,3},{2,0},{3,1},{4,6},{5,7},{6,4},{7,5},{8,10},{9,11},{10,... | collective-permute-start | bytes 1597448 | tf_op jit(solution)/shard_map/ppermute | solution.py:1249
  225.5 24.4 %collective-permute-start.28 = (bf16[208,1280]{1,0:T(8,128)(2,1)S(1)}, bf16[208,1280]{1,0:T(8,128)(2,1)S(1)}, u32[]{:S(2)}, u32[]{:S(2)}) collective-permute-start(bf16[208,1280]{1,0:T(8,128)(2,1)S(1)} %add_convert_fusion.6), channel_id=1, source_target_pairs={{0,2},{1,3},{2,0},{3,1},{4,6},{5,7},{6,4},{7,5},{8,10},{9,11},{10,... | collective-permute-start | bytes 1597448 | tf_op jit(solution)/shard_map/ppermute | solution.py:1250
  226.0 37.3 %collective-permute-start.35 = (bf16[208,1280]{1,0:T(8,128)(2,1)}, bf16[208,1280]{1,0:T(8,128)(2,1)}, u32[]{:S(2)}, u32[]{:S(2)}) collective-permute-start(bf16[208,1280]{1,0:T(8,128)(2,1)} %get-tuple-element.298.refs_0_), channel_id=1, source_target_pairs={{0,1},{1,0},{2,3},{3,2},{4,5},{5,4},{6,7},{7,6},{8,9},{9,8},{10,11... | collective-permute-start | bytes 1597448 | tf_op jit(solution)/shard_map/ppermute | solution.py:1191
  255.2 27.4 %collective-permute-start.30 = (bf16[208,1280]{1,0:T(8,128)(2,1)}, bf16[208,1280]{1,0:T(8,128)(2,1)}, u32[]{:S(2)}, u32[]{:S(2)}) collective-permute-start(bf16[208,1280]{1,0:T(8,128)(2,1)} %get-tuple-element.311.refs_0_), channel_id=1, source_target_pairs={{0,2},{1,3},{2,0},{3,1},{4,6},{5,7},{6,4},{7,5},{8,10},{9,11},{10,... | collective-permute-start | bytes 1597448 | tf_op jit(solution)/shard_map/ppermute | solution.py:1264
  259.1 23.6 %collective-permute-start.33 = (bf16[2,160,1280]{2,1,0:T(8,128)(2,1)}, bf16[2,160,1280]{2,1,0:T(8,128)(2,1)}, u32[]{:S(2)}, u32[]{:S(2)}) collective-permute-start(bf16[2,160,1280]{2,1,0:T(8,128)(2,1)} %fusion.2), channel_id=1, source_target_pairs={{0,8},{4,12},{8,16},{12,20},{16,24},{20,28},{24,0},{28,4},{1,9},{5... | collective-permute-start | bytes 2457608 | tf_op jit(solution)/shard_map/ppermute | solution.py:1268
  260.7 22.0 %collective-permute-start.34 = (bf16[2,160,1280]{2,1,0:T(8,128)(2,1)}, bf16[2,160,1280]{2,1,0:T(8,128)(2,1)}, u32[]{:S(2)}, u32[]{:S(2)}) collective-permute-start(bf16[2,160,1280]{2,1,0:T(8,128)(2,1)} %get-tuple-element.381), channel_id=1, source_target_pairs={{0,4},{4,0},{8,12},{12,8},{16,20},{20,16},{24,28},{28,24},{1,5},{5... | collective-permute-start | bytes 2457608 | tf_op jit(solution)/shard_map/ppermute | solution.py:1269
  263.2 19.5 %collective-permute-start.32 = (bf16[208,1280]{1,0:T(8,128)(2,1)}, bf16[208,1280]{1,0:T(8,128)(2,1)}, u32[]{:S(2)}, u32[]{:S(2)}) collective-permute-start(bf16[208,1280]{1,0:T(8,128)(2,1)} %add_convert_fusion.5), channel_id=1, source_target_pairs={{0,2},{1,3},{2,0},{3,1},{4,6},{5,7},{6,4},{7,5},{8,10},{9,11},{10,... | collective-permute-start | bytes 1597448 | tf_op jit(solution)/shard_map/ppermute | solution.py:1267
  289.2 27.7 %collective-permute-start.42 = (bf16[2,160,1280]{2,1,0:T(8,128)(2,1)}, bf16[2,160,1280]{2,1,0:T(8,128)(2,1)}, u32[]{:S(2)}, u32[]{:S(2)}) collective-permute-start(bf16[2,160,1280]{2,1,0:T(8,128)(2,1)} %get-tuple-element.380), channel_id=1, source_target_pairs={{0,4},{4,0},{8,12},{12,8},{16,20},{20,16},{24,28},{28,24},{1,5},{5... | collective-permute-start | bytes 2457608 | tf_op jit(solution)/shard_map/ppermute | solution.py:1281
  292.2 24.7 %collective-permute-start.41 = (bf16[2,160,1280]{2,1,0:T(8,128)(2,1)}, bf16[2,160,1280]{2,1,0:T(8,128)(2,1)}, u32[]{:S(2)}, u32[]{:S(2)}) collective-permute-start(bf16[2,160,1280]{2,1,0:T(8,128)(2,1)} %fusion.1), channel_id=1, source_target_pairs={{0,8},{4,12},{8,16},{12,20},{16,24},{20,28},{24,0},{28,4},{1,9},{5... | collective-permute-start | bytes 2457608 | tf_op jit(solution)/shard_map/ppermute | solution.py:1280
  294.3 22.6 %collective-permute-start.39 = (bf16[208,1280]{1,0:T(8,128)(2,1)}, bf16[208,1280]{1,0:T(8,128)(2,1)S(1)}, u32[]{:S(2)}, u32[]{:S(2)}) collective-permute-start(bf16[208,1280]{1,0:T(8,128)(2,1)} %add_convert_fusion.4), channel_id=1, source_target_pairs={{0,2},{1,3},{2,0},{3,1},{4,6},{5,7},{6,4},{7,5},{8,10},{9,11},{10,... | collective-permute-start | bytes 1597448 | tf_op jit(solution)/shard_map/ppermute | solution.py:1277
  297.2 23.3 %collective-permute-start.40 = (bf16[208,1280]{1,0:T(8,128)(2,1)}, bf16[208,1280]{1,0:T(8,128)(2,1)}, u32[]{:S(2)}, u32[]{:S(2)}) collective-permute-start(bf16[208,1280]{1,0:T(8,128)(2,1)} %add_convert_fusion.3), channel_id=1, source_target_pairs={{0,2},{1,3},{2,0},{3,1},{4,6},{5,7},{6,4},{7,5},{8,10},{9,11},{10,... | collective-permute-start | bytes 1597448 | tf_op jit(solution)/shard_map/ppermute | solution.py:1279
  323.1 29.9 %collective-permute-start.49 = (bf16[160,1280]{1,0:T(8,128)(2,1)}, bf16[160,1280]{1,0:T(8,128)(2,1)}, u32[]{:S(2)}, u32[]{:S(2)}) collective-permute-start(bf16[160,1280]{1,0:T(8,128)(2,1)} %fusion.11), channel_id=1, source_target_pairs={{0,8},{4,12},{8,16},{12,20},{16,24},{20,28},{24,0},{28,4},{1,9},{5... | collective-permute-start | bytes 1228808 | tf_op jit(solution)/shard_map/ppermute | solution.py:1294
  328.9 24.2 %collective-permute-start.45 = (bf16[208,1280]{1,0:T(8,128)(2,1)}, bf16[208,1280]{1,0:T(8,128)(2,1)}, u32[]{:S(2)}, u32[]{:S(2)}) collective-permute-start(bf16[208,1280]{1,0:T(8,128)(2,1)} %get-tuple-element.324.refs_0_), channel_id=1, source_target_pairs={{0,2},{1,3},{2,0},{3,1},{4,6},{5,7},{6,4},{7,5},{8,10},{9,11},{10,... | collective-permute-start | bytes 1597448 | tf_op jit(solution)/shard_map/ppermute | solution.py:1289
  333.4 21.4 %collective-permute-start.47 = (bf16[208,1280]{1,0:T(8,128)(2,1)}, bf16[208,1280]{1,0:T(8,128)(2,1)}, u32[]{:S(2)}, u32[]{:S(2)}) collective-permute-start(bf16[208,1280]{1,0:T(8,128)(2,1)} %add_convert_fusion.1), channel_id=1, source_target_pairs={{0,2},{1,3},{2,0},{3,1},{4,6},{5,7},{6,4},{7,5},{8,10},{9,11},{10,... | collective-permute-start | bytes 1597448 | tf_op jit(solution)/shard_map/ppermute | solution.py:1291
  335.2 17.9 %collective-permute-start.48 = (bf16[160,1280]{1,0:T(8,128)(2,1)}, bf16[160,1280]{1,0:T(8,128)(2,1)}, u32[]{:S(2)}, u32[]{:S(2)}) collective-permute-start(bf16[160,1280]{1,0:T(8,128)(2,1)} %slice_bitcast_fusion.5), channel_id=1, source_target_pairs={{0,4},{4,0},{8,12},{12,8},{16,20},{20,16},{24,28},{28,24},{1,5},{5... | collective-permute-start | bytes 1228808 | tf_op jit(solution)/shard_map/ppermute | solution.py:1293
  361.9 37.6 %collective-permute-start.55 = (bf16[208,1280]{1,0:T(8,128)(2,1)}, bf16[208,1280]{1,0:T(8,128)(2,1)}, u32[]{:S(2)}, u32[]{:S(2)}) collective-permute-start(bf16[208,1280]{1,0:T(8,128)(2,1)} %get-tuple-element.324.refs_0_), channel_id=1, source_target_pairs={{0,1},{1,0},{2,3},{3,2},{4,5},{5,4},{6,7},{7,6},{8,9},{9,8},{10,11... | collective-permute-start | bytes 1597448 | tf_op jit(solution)/shard_map/ppermute | solution.py:1191
  365.5 49.5 %collective-permute-start.50 = (bf16[208,1280]{1,0:T(8,128)(2,1)}, bf16[208,1280]{1,0:T(8,128)(2,1)}, u32[]{:S(2)}, u32[]{:S(2)}) collective-permute-start(bf16[208,1280]{1,0:T(8,128)(2,1)} %get-tuple-element.347.refs_0_), channel_id=1, source_target_pairs={{0,2},{1,3},{2,0},{3,1},{4,6},{5,7},{6,4},{7,5},{8,10},{9,11},{10,... | collective-permute-start | bytes 1597448 | tf_op jit(solution)/shard_map/ppermute | solution.py:1307
  367.4 13.1 %collective-permute-start.52 = (bf16[2,160,384]{2,1,0:T(8,128)(2,1)S(1)}, bf16[2,160,384]{2,1,0:T(8,128)(2,1)S(1)}, u32[]{:S(2)}, u32[]{:S(2)}) collective-permute-start(bf16[2,160,384]{2,1,0:T(8,128)(2,1)S(1)} %get-tuple-element.383), channel_id=1, source_target_pairs={{0,8},{4,12},{8,16},{12,20},{16,24},{20,28},{24,0},{28,4},{1,9},{5... | collective-permute-start | bytes 737288 | tf_op jit(solution)/shard_map/ppermute | solution.py:1304
  369.3 45.7 %collective-permute-start.54 = (bf16[4,160,896]{2,1,0:T(8,128)(2,1)}, bf16[4,160,896]{2,1,0:T(8,128)(2,1)}, u32[]{:S(2)}, u32[]{:S(2)}) collective-permute-start(bf16[4,160,896]{2,1,0:T(8,128)(2,1)} %get-tuple-element.350), channel_id=1, source_target_pairs={{0,4},{4,0},{8,12},{12,8},{16,20},{20,16},{24,28},{28,24},{1,5},{5... | collective-permute-start | bytes 3440648 | tf_op jit(solution)/shard_map/ppermute | solution.py:1303
  380.4 20.1 %collective-permute-start.56 = (bf16[208,1280]{1,0:T(8,128)(2,1)}, bf16[208,1280]{1,0:T(8,128)(2,1)S(1)}, u32[]{:S(2)}, u32[]{:S(2)}) collective-permute-start(bf16[208,1280]{1,0:T(8,128)(2,1)} %collective-permute-done.45.refs_1_), channel_id=1, source_target_pairs={{0,1},{1,0},{2,3},{3,2},{4,5},{5,4},{6,7},{7,6},{8,9},{9,8},{10,11... | collective-permute-start | bytes 1597448 | tf_op jit(solution)/shard_map/ppermute | solution.py:1191
  380.4 16.8 %collective-permute-start.74 = (f32[160,128]{1,0:T(8,128)S(1)}, f32[160,128]{1,0:T(8,128)S(1)}, u32[]{:S(2)}, u32[]{:S(2)}) collective-permute-start(f32[160,128]{1,0:T(8,128)S(1)} %add.408), channel_id=1, source_target_pairs={{0,4},{4,0},{8,12},{12,8},{16,20},{20,16},{24,28},{28,24},{1,5},{5... | collective-permute-start | bytes 245768 | tf_op jit(solution)/shard_map/ppermute | solution.py:1056
  397.2 14.0 %collective-permute-start.51 = (bf16[160,1280]{1,0:T(8,128)(2,1)}, bf16[160,1280]{1,0:T(8,128)(2,1)S(1)}, u32[]{:S(2)}, u32[]{:S(2)}) collective-permute-start(bf16[160,1280]{1,0:T(8,128)(2,1)} %fusion.6), channel_id=1, source_target_pairs={{0,8},{4,12},{8,16},{12,20},{16,24},{20,28},{24,0},{28,4},{1,9},{5... | collective-permute-start | bytes 1228808 | tf_op jit(solution)/shard_map/ppermute | solution.py:1309
  399.5 14.4 %collective-permute-start.53 = (bf16[2,160,384]{2,1,0:T(8,128)(2,1)}, bf16[2,160,384]{2,1,0:T(8,128)(2,1)}, u32[]{:S(2)}, u32[]{:S(2)}) collective-permute-start(bf16[2,160,384]{2,1,0:T(8,128)(2,1)} %fusion.10), channel_id=1, source_target_pairs={{0,8},{4,12},{8,16},{12,20},{16,24},{20,28},{24,0},{28,4},{1,9},{5... | collective-permute-start | bytes 737288 | tf_op jit(solution)/shard_map/ppermute | solution.py:1310
  401.3 17.5 %collective-permute-start.60 = (bf16[208,1280]{1,0:T(8,128)(2,1)}, bf16[208,1280]{1,0:T(8,128)(2,1)}, u32[]{:S(2)}, u32[]{:S(2)}) collective-permute-start(bf16[208,1280]{1,0:T(8,128)(2,1)} %get-tuple-element.347.refs_0_), channel_id=1, source_target_pairs={{0,1},{1,0},{2,3},{3,2},{4,5},{5,4},{6,7},{7,6},{8,9},{9,8},{10,11... | collective-permute-start | bytes 1597448 | tf_op jit(solution)/shard_map/ppermute | solution.py:1191
  411.2 16.8 %collective-permute-start.62 = (bf16[208,1280]{1,0:T(8,128)(2,1)S(1)}, bf16[208,1280]{1,0:T(8,128)(2,1)}, u32[]{:S(2)}, u32[]{:S(2)}) collective-permute-start(bf16[208,1280]{1,0:T(8,128)(2,1)S(1)} %copy-done.19), channel_id=1, source_target_pairs={{0,2},{1,3},{2,0},{3,1},{4,6},{5,7},{6,4},{7,5},{8,10},{9,11},{10,... | collective-permute-start | bytes 1597448 | tf_op jit(solution)/shard_map/ppermute | solution.py:1313
  413.9 18.0 %collective-permute-start.63 = (bf16[208,1280]{1,0:T(8,128)(2,1)S(1)}, bf16[208,1280]{1,0:T(8,128)(2,1)S(1)}, u32[]{:S(2)}, u32[]{:S(2)}) collective-permute-start(bf16[208,1280]{1,0:T(8,128)(2,1)S(1)} %copy-done.18), channel_id=1, source_target_pairs={{0,2},{1,3},{2,0},{3,1},{4,6},{5,7},{6,4},{7,5},{8,10},{9,11},{10,... | collective-permute-start | bytes 1597448 | tf_op jit(solution)/shard_map/ppermute | solution.py:1313
  416.8 22.8 %collective-permute-start.57 = (bf16[160,896]{1,0:T(8,128)(2,1)}, bf16[160,896]{1,0:T(8,128)(2,1)}, u32[]{:S(2)}, u32[]{:S(2)}) collective-permute-start(bf16[160,896]{1,0:T(8,128)(2,1)} %fusion.12), channel_id=1, source_target_pairs={{0,8},{4,12},{8,16},{12,20},{16,24},{20,28},{24,0},{28,4},{1,9},{5... | collective-permute-start | bytes 860168 | tf_op jit(solution)/shard_map/ppermute | solution.py:1318
  418.8 20.9 %collective-permute-start.59 = (bf16[160,1280]{1,0:T(8,128)(2,1)}, bf16[160,1280]{1,0:T(8,128)(2,1)S(1)}, u32[]{:S(2)}, u32[]{:S(2)}) collective-permute-start(bf16[160,1280]{1,0:T(8,128)(2,1)} %fusion.5), channel_id=1, source_target_pairs={{0,8},{4,12},{8,16},{12,20},{16,24},{20,28},{24,0},{28,4},{1,9},{5... | collective-permute-start | bytes 1228808 | tf_op jit(solution)/shard_map/ppermute | solution.py:1320
  420.6 19.0 %collective-permute-start.58 = (bf16[2,160,384]{2,1,0:T(8,128)(2,1)}, bf16[2,160,384]{2,1,0:T(8,128)(2,1)}, u32[]{:S(2)}, u32[]{:S(2)}) collective-permute-start(bf16[2,160,384]{2,1,0:T(8,128)(2,1)} %fusion.9), channel_id=1, source_target_pairs={{0,8},{4,12},{8,16},{12,20},{16,24},{20,28},{24,0},{28,4},{1,9},{5... | collective-permute-start | bytes 737288 | tf_op jit(solution)/shard_map/ppermute | solution.py:1319
  428.0 17.2 %collective-permute-start.68 = (bf16[208,1280]{1,0:T(8,128)(2,1)S(1)}, bf16[208,1280]{1,0:T(8,128)(2,1)}, u32[]{:S(2)}, u32[]{:S(2)}) collective-permute-start(bf16[208,1280]{1,0:T(8,128)(2,1)S(1)} %copy-done.19), channel_id=1, source_target_pairs={{0,1},{1,0},{2,3},{3,2},{4,5},{5,4},{6,7},{7,6},{8,9},{9,8},{10,11... | collective-permute-start | bytes 1597448 | tf_op jit(solution)/shard_map/ppermute | solution.py:1191
  432.0 24.3 %collective-permute-start.64 = (bf16[208,1280]{1,0:T(8,128)(2,1)S(1)}, bf16[208,1280]{1,0:T(8,128)(2,1)}, u32[]{:S(2)}, u32[]{:S(2)}) collective-permute-start(bf16[208,1280]{1,0:T(8,128)(2,1)S(1)} %copy-done.18), channel_id=1, source_target_pairs={{0,1},{1,0},{2,3},{3,2},{4,5},{5,4},{6,7},{7,6},{8,9},{9,8},{10,11... | collective-permute-start | bytes 1597448 | tf_op jit(solution)/shard_map/ppermute | solution.py:1191
  (102 other events, 827.9 us)

commit v4 on v3

--- a/solution.py
+++ b/solution.py
@@ -19,7 +19,7 @@
 EPS = 1e-06
 F32 = jnp.float32
 BF16 = jnp.bfloat16
-ANY = pl.BlockSpec(memory_space=pltpu.HBM)
+ANY = pl.BlockSpec(memory_space=pl.ANY)
 highest = lax.Precision.HIGHEST
 
 
@@ -91,32 +91,47 @@
     return jnp.concatenate([values, empty], axis=0)
 
 
-def prepare_kernel(order, places, lives, x_ref, gain_ref, shift_ref, *outs):
-    rows_ref, normed_ref, valid_ref = outs
-    slot = order[pl.program_id(0)]
+def prepare_kernel(every, order, places, lives, x_ref, gain_ref, shift_ref, *outs):
+    rows_ref, own_ref, normed_ref, valid_ref = outs
+    step = pl.program_id(0)
+    slot = order[step]
     valid = token_valid(places[slot], lives[slot])
     x = x_ref[0].astype(F32)
     xhat, _ = norm_parts(x)
     normed_ref[...] = pad_rows((xhat * gain_ref[...] + shift_ref[...]) * valid).astype(BF16)
-    rows_ref[...] = pad_rows(x).astype(BF16)
     valid_ref[...] = pad_rows(valid)
 
-
-def prepare(order, places, lives, x, gain, shift):
+    @pl.when(lax.rem(step, every) == 0)
+    def _():
+        rows_ref[...] = pad_rows(x).astype(BF16)
+        own_ref[...] = pad_rows(valid)
+
+
+def prepare(order, places, lives, x, gain, shift, every):
     count = order.shape[0]
     width = x.shape[2]
     window = pl.BlockSpec((1, WTOK, width), lambda i, order, *_: (order[i], 0, 0))
     block = pl.BlockSpec((ROWS, width), lambda i, *_: (i, 0))
     return pl.pallas_call(
-        prepare_kernel,
+        partial(prepare_kernel, every),
         grid_spec=pltpu.PrefetchScalarGridSpec(
             num_scalar_prefetch=3,
             grid=(count,),
             in_specs=[window, whole(gain), whole(shift)],
-            out_specs=[block] * 2 + [pl.BlockSpec((ROWS, 1), lambda i, *_: (i, 0))],
+            out_specs=[
+                pl.BlockSpec((ROWS, width), lambda i, *_: (i // every, 0)),
+                pl.BlockSpec((ROWS, 1), lambda i, *_: (i // every, 0)),
+                block,
+                pl.BlockSpec((ROWS, 1), lambda i, *_: (i, 0)),
+            ],
         ),
-        out_shape=[struct((count * ROWS, width), BF16)] * 2 + [struct((count * ROWS, 1), F32)],
-        compiler_params=params(60),
+        out_shape=[
+            struct((count // every * ROWS, width), BF16),
+            struct((count // every * ROWS, 1), F32),
+            struct((count * ROWS, width), BF16),
+            struct((count * ROWS, 1), F32),
+        ],
+        compiler_params=params(12),
         cost_estimate=cost(9),
         name="prepare",
     )(order, places, lives, x, gain, shift)
@@ -140,7 +155,7 @@
             out_specs=pl.BlockSpec((ROWS, width), lambda i, *_: (i, 0)),
         ),
         out_shape=struct((count * ROWS, width), BF16),
-        compiler_params=params(60),
+        compiler_params=params(12),
         cost_estimate=cost(6),
         name="mask_rows",
     )(order, places, lives, top)
@@ -182,7 +197,7 @@
         + [row_block(shape, at), whole(bias), whole(gain), whole(shift)],
         out_specs=[top_rows(shape)] * 2,
         out_shape=[struct(shape, F32), struct(shape, BF16)],
-        compiler_params=params(60),
+        compiler_params=params(14),
         cost_estimate=cost(3),
         name="norm_two",
     )(*parts, x, bias, gain, shift)
@@ -203,7 +218,7 @@
         + [row_block((after.shape[0], 1), at), whole(bias)],
         out_specs=top_rows(after.shape),
         out_shape=struct(after.shape, BF16),
-        compiler_params=params(60),
+        compiler_params=params(14),
         cost_estimate=cost(2.5),
         name="finish",
     )(*parts, after, valid, bias)
@@ -242,65 +257,67 @@
         + [row_block(after.shape, at), whole(gain)],
         out_specs=[top_rows(after.shape)] * 2 + [whole(sums)],
         out_shape=[struct(after.shape, F32), struct(after.shape, BF16), sums],
-        compiler_params=params(60),
+        compiler_params=params(14),
         cost_estimate=cost(4),
         name="norm_two_back",
     )(*parts, after, top, gain)
 
 
-def norm_one_back_kernel(count, *refs):
-    parts = refs[:count]
-    x_ref, valid_ref, grad_ref, gain_ref, out_ref, sums_ref = refs[count:]
-    rows = x_ref.shape[0]
-    upstream = total(parts, rows) * valid_ref[...]
-    xhat, rstd = norm_parts(x_ref[...].astype(F32))
-    out_ref[...] = (grad_ref[...] + norm_back(upstream, xhat, rstd, gain_ref[...])).astype(BF16)
-    sums_ref[0:1] = jnp.sum(upstream * xhat, axis=0, keepdims=True)
-    sums_ref[1:2] = jnp.sum(upstream, axis=0, keepdims=True)
-
-
-def norm_one_back(parts, x, valid, at, grad, gain):
-    shape = grad.shape
-    sums = struct((2, shape[1]), F32)
+def norm_one_back_kernel(counts, *refs):
+    x_ref, valid_ref, gain_ref, out_ref = refs[-4:]
+    at = 0
+    for part, count in enumerate(counts):
+        parts, grad_ref = refs[at : at + count], refs[at + count]
+        at += count + 1
+        rows = slice(part * ROWS, part * ROWS + ROWS)
+        upstream = total(parts, ROWS) * valid_ref[rows]
+        xhat, rstd = norm_parts(x_ref[rows].astype(F32))
+        grad = grad_ref[...] + norm_back(upstream, xhat, rstd, gain_ref[...])
+        out_ref[rows] = grad.astype(BF16)
+
+
+def norm_one_back(windows, x, valid, gain):
+    shape = (ROWS, x.shape[1])
+    operands, specs = [], []
+    for parts, grad in windows:
+        operands += [part[0] for part in parts] + [grad]
+        specs += [
+            pl.BlockSpec(shape, lambda i, at=at: (at, 0)) for at in (part[1] for part in parts)
+        ]
+        specs.append(whole(grad))
     return pl.pallas_call(
-        partial(norm_one_back_kernel, len(parts)),
+        partial(norm_one_back_kernel, [len(parts) for parts, _ in windows]),
         grid=(1,),
-        in_specs=[top_rows(shape)] * len(parts)
-        + [row_block(shape, at), row_block((shape[0], 1), at), top_rows(shape), whole(gain)],
-        out_specs=[top_rows(shape), whole(sums)],
-        out_shape=[struct(shape, BF16), sums],
-        compiler_params=params(60),
-        cost_estimate=cost(3.5),
+        in_specs=specs + [whole(x), whole(valid), whole(gain)],
+        out_specs=whole(x),
+        out_shape=struct(x.shape, BF16),
+        compiler_params=params(20),
+        cost_estimate=cost(3.5 * len(windows)),
         name="norm_one_back",
-    )(*parts, x, valid, grad, gain)
+    )(*operands, x, valid, gain)
 
 
 def qkv_kernel(count, cols, offsets, *refs):
     pieces = refs[:count]
-    x_ref, bias_ref, q_ref, k_ref, v_ref, w_ref, buffer, sems = refs[count:]
+    x_ref, bias_ref, q_ref, k_ref, v_ref, w_ref, sems = refs[count:]
     wide = q_ref.shape[1]
 
     @pl.when(pl.program_id(0) == 0)
     def _():
-        assemble(offsets, pieces, buffer, sems)
-        for slot in range(4):
-            base = slot * wide
-            w_ref[:, base : base + cols] = buffer[:, slot * cols : (slot + 1) * cols]
-            if wide > cols:
-                w_ref[:, base + cols : base + wide] = jnp.zeros(
-                    (w_ref.shape[0], wide - cols), BF16
-                )
-
-    x = x_ref[...]
+        assemble(offsets, pieces, w_ref, sems)
+
+    result = (dot(x_ref[...], w_ref[:, wide:]) + bias_ref[...]).astype(BF16)
     for slot, ref in enumerate((q_ref, k_ref, v_ref)):
-        span = slice(slot * wide, (slot + 1) * wide)
-        ref[...] = (dot(x, w_ref[:, span]) + bias_ref[:, span]).astype(BF16)
+        ref[:, :cols] = result[:, slot * cols : (slot + 1) * cols]
+        if wide > cols:
+            ref[:, cols:] = jnp.zeros((ref.shape[0], wide - cols), BF16)
 
 
 def project(offsets, pieces, x, bias, cols, wide):
     rows, width = x.shape
     step = 2 * ROWS
     block = pl.BlockSpec((step, wide), lambda i, *_: (i, 0))
+    total_cols = wide + 3 * cols
     return pl.pallas_call(
         partial(qkv_kernel, len(pieces), cols),
         grid_spec=pltpu.PrefetchScalarGridSpec(
@@ -308,14 +325,11 @@
             grid=(rows // step,),
             in_specs=[ANY] * len(pieces)
             + [pl.BlockSpec((step, width), lambda i, *_: (i, 0)), whole(bias)],
-            out_specs=[block, block, block, pl.BlockSpec((width, 4 * wide), lambda i, *_: (0, 0))],
-            scratch_shapes=[
-                pltpu.VMEM((width, 4 * cols), BF16),
-                pltpu.SemaphoreType.DMA((len(pieces),)),
-            ],
+            out_specs=[block, block, block, pl.BlockSpec((width, total_cols), lambda i, *_: (0, 0))],
+            scratch_shapes=[pltpu.SemaphoreType.DMA((len(pieces),))],
         ),
-        out_shape=[struct((rows, wide), BF16)] * 3 + [struct((width, 4 * wide), BF16)],
-        compiler_params=params(60),
+        out_shape=[struct((rows, wide), BF16)] * 3 + [struct((width, total_cols), BF16)],
+        compiler_params=params(28),
         cost_estimate=cost(14),
         name="qkv",
     )(offsets, *pieces, x, bias)
@@ -450,7 +464,7 @@
             whole(rel_high),
             whole(rel_low),
             whole(marks),
-            pl.BlockSpec((width, wide), lambda i: (0, 3)),
+            pl.BlockSpec((width, wide), lambda i: (0, 0)),
         ],
         out_specs=[
             pl.BlockSpec((ROWS, heads * HD), lambda i: (place(i), 0)),
@@ -462,7 +476,7 @@
             struct((windows * ROWS, heads * 256), BF16),
         ]
         + shapes,
-        compiler_params=params(60),
+        compiler_params=params(16),
         cost_estimate=cost(13.5),
         name="attend",
     )(q, k, v, rel_high, rel_low, marks, weights)
@@ -471,8 +485,9 @@
 def attend_back_kernel(heads, windows, split, count, *refs):
     pieces = refs[:count]
     q_ref, k_ref, v_ref, shares_ref, rh_ref, mark_ref, w_ref = refs[count : count + 7]
-    grads_ref, branch_ref, rel_ref, sum_ref = refs[count + 7 : count + 11]
-    outs = refs[count + 11 :]
+    normed_ref, valid_ref = refs[count + 7 : count + 9]
+    grads_ref, branch_ref, rel_ref, sum_ref, norm_ref = refs[count + 9 : count + 14]
+    outs = refs[count + 14 :]
     step = pl.program_id(0)
 
     @pl.when(step == 0)
@@ -483,12 +498,13 @@
             start += piece.shape[0]
         rel_ref[...] = jnp.zeros(rel_ref.shape, F32)
         sum_ref[...] = jnp.zeros(sum_ref.shape, F32)
+        norm_ref[...] = jnp.zeros(norm_ref.shape, F32)
 
     place = lax.rem(step + split, windows) if split else step
     q, k, v = q_ref[...], k_ref[...], v_ref[...]
     wide = q.shape[1]
     top = branch_ref[pl.ds(pl.multiple_of(place * ROWS, 16), ROWS), :]
-    grad_mixed = dot(top, w_ref[:, 3 * wide :]).astype(BF16)
+    grad_mixed = dot(top, w_ref[:, :wide]).astype(BF16)
     grad_q, grad_k, grad_v = ([None] * (wide // 128) for _ in range(3))
     grad_bias = None
     for head, span in enumerate(head_spans(heads, wide)):
@@ -522,12 +538,12 @@
     grad_v = jnp.concatenate(grad_v, axis=1).astype(BF16)
     cols = heads * HD
     for slot, grad in enumerate((grad_q, grad_k, grad_v)):
-        cut = slice(slot * wide, (slot + 1) * wide)
         grads_ref[:, slot * cols : (slot + 1) * cols] = grad[:, :cols]
-        sum_ref[:, cut] += jnp.sum(grad.astype(F32), axis=0, keepdims=True)
-    partial_sum = dot_nt(
-        jnp.concatenate([grad_q, grad_k, grad_v], axis=1), w_ref[:, : 3 * wide]
-    )
+    packed_grads = grads_ref[...]
+    sum_ref[...] += jnp.sum(packed_grads.astype(F32), axis=0, keepdims=True)
+    partial_sum = dot_nt(packed_grads, w_ref[:, wide:])
+    norm_ref[0:1] += jnp.sum(partial_sum * normed_ref[...].astype(F32), axis=0, keepdims=True)
+    norm_ref[1:2] += jnp.sum(partial_sum * valid_ref[...], axis=0, keepdims=True)
     result = partial_sum.astype(BF16)
     if split:
         keep_ref, send_ref = outs
@@ -544,7 +560,7 @@
 
 
 def attend_back(
-    heads, part, windows, split, pieces, q, k, v, shares, rel_high, marks, weights
+    heads, part, windows, split, pieces, q, k, v, shares, rel_high, marks, weights, normed, valid
 ):
     wide = q.shape[1]
     width = weights.shape[0]
@@ -557,7 +573,8 @@
     rows = windows * ROWS
     branch = struct((rows, width), BF16)
     rel = struct((256, wide), F32)
-    sums = struct((1, 3 * wide), F32)
+    sums = struct((1, 3 * heads * HD), F32)
+    norms = struct((2, width), F32)
     return pl.pallas_call(
         partial(attend_back_kernel, heads, windows, split, len(pieces)),
         grid=(windows,),
@@ -570,30 +587,34 @@
             whole(rel_high),
             whole(marks),
             whole(weights),
+            pl.BlockSpec((ROWS, width), lambda i: (part * windows + place(i), 0)),
+            pl.BlockSpec((ROWS, 1), lambda i: (part * windows + place(i), 0)),
         ],
         out_specs=[
             pl.BlockSpec((ROWS, 3 * heads * HD), lambda i: (place(i), 0)),
             whole(branch),
             whole(rel),
             whole(sums),
+            whole(norms),
         ]
         + specs,
-        out_shape=[struct((rows, 3 * heads * HD), BF16), branch, rel, sums] + shapes,
-        compiler_params=params(60),
+        out_shape=[struct((rows, 3 * heads * HD), BF16), branch, rel, sums, norms] + shapes,
+        compiler_params=params(28),
         cost_estimate=cost(18.5),
         name="attend_back",
-    )(*pieces, q, k, v, shares, rel_high, marks, weights)
+    )(*pieces, q, k, v, shares, rel_high, marks, weights, normed, valid)
 
 
 def mlp_kernel(count, weights, split, offsets, *refs):
     pieces = refs[:count]
     weight_pieces = refs[count : count + weights]
     refs = refs[count + weights :]
-    top_ref, bias_ref, after_ref, down_bias_ref = refs[:4]
-    active_ref, hidden_ref, normed_ref, sum_ref = refs[4:8]
-    backs, outs = (refs[8:10], refs[10:12]) if split else (refs[8:9], refs[9:10])
-    up, down, sems = refs[-3:]
+    after_any, top_ref, bias_ref, down_bias_ref = refs[:4]
+    active_ref, hidden_ref, normed_any, sum_ref = refs[4:8]
+    outs = refs[8 : 12 if split else 10]
+    up, down, normed_ref, after_ref, send_ref, out_send_ref, sems, row_sems = refs[len(outs) + 8 :]
     step = pl.program_id(0)
+    steps = pl.num_programs(0)
     block = top_ref.shape[0]
     units = up.shape[1]
     copies = []
@@ -609,18 +630,30 @@
                     sems.at[half, index],
                 )
             )
+    row_copies, start = [], 0
+    for index, piece in enumerate(pieces):
+        rows = piece.shape[0]
+        row_copies.append(
+            pltpu.make_async_copy(
+                piece, normed_ref.at[pl.ds(start, rows)], row_sems.at[index]
+            )
+        )
+        start += rows
+    normed_out = pltpu.make_async_copy(normed_ref, normed_any, row_sems.at[count])
+    after_in = pltpu.make_async_copy(after_any, after_ref, row_sems.at[count + 1])
+    if split:
+        send_out = pltpu.make_async_copy(send_ref, outs[1], row_sems.at[count + 2])
+        out_send_out = pltpu.make_async_copy(out_send_ref, outs[3], row_sems.at[count + 3])
 
     @pl.when(step == 0)
     def _():
-        for copy in copies[1] + copies[0]:
+        for copy in row_copies + copies[1] + copies[0]:
             copy.start()
-        start = 0
-        for piece in pieces:
-            normed_ref[start : start + piece.shape[0]] = piece[...]
-            start += piece.shape[0]
+        after_in.start()
         sum_ref[...] = jnp.zeros(sum_ref.shape, F32)
-        for copy in copies[1]:
+        for copy in row_copies + copies[1]:
             copy.wait()
+        normed_out.start()
 
     place = 1 - step if split else step
     normed = normed_ref[pl.ds(pl.multiple_of(place * block, 16), block), :]
@@ -644,18 +677,31 @@
 
         @pl.when(step == 0)
         def _():
-            backs[1][...] = back
-            outs[1][...] = result.astype(BF16)
+            send_ref[...] = back
+            out_send_ref[...] = result.astype(BF16)
+            send_out.start()
+            out_send_out.start()
+            after_in.wait()
 
         @pl.when(step == 1)
         def _():
-            backs[0][...] = back
+            outs[0][...] = back
             own = result[:ROWS] + after_ref[...] + down_bias_ref[...]
-            outs[0][:ROWS] = own.astype(BF16)
-            outs[0][ROWS:] = result[ROWS:].astype(BF16)
+            outs[2][:ROWS] = own.astype(BF16)
+            outs[2][ROWS:] = result[ROWS:].astype(BF16)
+            send_out.wait()
+            out_send_out.wait()
     else:
-        backs[0][...] = back
-        outs[0][...] = result.astype(BF16)
+        outs[0][...] = back
+        outs[1][...] = result.astype(BF16)
+
+        @pl.when(step == 0)
+        def _():
+            after_in.wait()
+
+    @pl.when(step == steps - 1)
+    def _():
+        normed_out.wait()
 
 
 def mlp(offsets, pieces, weight_pieces, top, part, bias, after, down_bias, split):
@@ -673,44 +719,47 @@
     wide = pl.BlockSpec((block, units), lambda i, *_: (place(i), 0))
     back = struct((block, width), BF16)
     if split:
-        back_specs, back_shapes = [whole(back)] * 2, [back] * 2
+        back_specs, back_shapes = [whole(back), ANY] * 2, [back] * 4
     else:
-        back_specs = [pl.BlockSpec((block, width), lambda i, *_: (i, 0))]
-        back_shapes = [normed]
+        back_specs = [pl.BlockSpec((block, width), lambda i, *_: (i, 0))] * 2
+        back_shapes = [normed] * 2
     return pl.pallas_call(
         partial(mlp_kernel, len(pieces), len(weight_pieces), split),
         grid_spec=pltpu.PrefetchScalarGridSpec(
             num_scalar_prefetch=1,
             grid=(blocks,),
-            in_specs=[whole(piece) for piece in pieces]
-            + [ANY] * len(weight_pieces)
+            in_specs=[ANY] * (len(pieces) + len(weight_pieces) + 1)
             + [
                 pl.BlockSpec((block, width), lambda i, *_: (part * blocks + place(i), 0)),
                 whole(bias),
-                whole(after),
                 whole(down_bias),
             ],
-            out_specs=[wide, wide, whole(normed), whole(sums)] + back_specs * 2,
+            out_specs=[wide, wide, ANY, whole(sums)] + back_specs,
             scratch_shapes=[
                 pltpu.VMEM((width, units), BF16),
                 pltpu.VMEM((width, units), BF16),
+                pltpu.VMEM((rows, width), BF16),
+                pltpu.VMEM(after.shape, F32),
+                pltpu.VMEM((block, width), BF16),
+                pltpu.VMEM((block, width), BF16),
                 pltpu.SemaphoreType.DMA((2, len(weight_pieces))),
+                pltpu.SemaphoreType.DMA((len(pieces) + 4,)),
             ],
         ),
-        out_shape=[struct((rows, units), BF16)] * 2 + [normed, sums] + back_shapes * 2,
-        compiler_params=params(60),
+        out_shape=[struct((rows, units), BF16)] * 2 + [normed, sums] + back_shapes,
+        compiler_params=params(48),
         cost_estimate=cost(21),
         name="mlp",
-    )(offsets, *pieces, *weight_pieces, top, bias, after, down_bias)
+    )(offsets, *pieces, *weight_pieces, after, top, bias, down_bias)
 
 
 def weight_grad_kernel(sizes, share, targets, *refs):
     count = 2 * sum(sizes)
     operands = refs[:count]
     outs, (result, sems) = refs[count:-2], refs[-2:]
-    pair_ref = outs[-1] if len(outs) != 2 else None
-    send_ref, keep_ref = outs[:2] if len(outs) > 1 else (None, None)
-    lead = send_ref.shape[2] if len(outs) > 1 else 0
+    high_ref, low_ref, keep_ref = outs[:3] if len(outs) > 1 else (None,) * 3
+    pair_ref = outs[-1] if len(outs) != 3 else None
+    lead = 0 if keep_ref is None else keep_ref.shape[2]
     step = pl.program_id(0)
     steps = pl.num_programs(0)
     chunk = operands[0].shape[1]
@@ -751,9 +800,13 @@
 
         if lead:
 
-            @pl.when(slot < 4)
+            @pl.when(slot < 2)
             def _():
-                copy(index, send_ref, slot).start()
+                copy(index, low_ref, slot).start()
+
+            @pl.when((slot >= 2) & (slot < 4))
+            def _():
+                copy(index, high_ref, slot - 2).start()
 
             @pl.when(slot >= 4)
             def _():
@@ -766,7 +819,7 @@
     def _():
         for index in range(8):
             if lead:
-                copy(index, send_ref, 0).wait()
+                copy(index, keep_ref, 0).wait()
             if pair_ref is not None:
                 pair_copy(index, 0).wait()
 
@@ -807,13 +860,13 @@
                 in_specs=specs,
                 out_specs=pl.BlockSpec((chunk, total_cols), lambda i: (i, 0)),
                 out_shape=struct((width, total_cols), BF16),
-                compiler_params=params(60),
+                compiler_params=params(36),
                 cost_estimate=cost(13),
         name="weight_grad",
             )(*operands)
         ]
     lead = total_cols if lead is None else lead
-    shapes = [struct((4, share, lead), BF16)] * 2 if lead else []
+    shapes = [struct((count, share, lead), BF16) for count in (2, 2, 4)] if lead else []
     if lead < total_cols:
         shapes.append(struct((4, 2, share, total_cols - lead), BF16))
     return pl.pallas_call(
@@ -829,90 +882,118 @@
             ],
         ),
         out_shape=shapes,
-        compiler_params=params(60),
+        compiler_params=params(36),
         cost_estimate=cost(13),
         name="weight_grad",
     )(targets, *operands)
 
 
-def place_kernel(part, order, *refs):
-    pieces, out_ref, buffer, sem = refs[:4], refs[-3], refs[-2], refs[-1]
-    rows = buffer.shape[0]
+def combine_kernel(layout, *refs):
+    outs = refs[len(refs) - len(layout) :]
+    at = 0
+    for cells, out in zip(layout, outs):
+        for row, lane, rows, lanes, terms in cells:
+            value = None
+            for lead, first in terms:
+                term = refs[at][(0,) * lead + (slice(None), slice(first, first + lanes))]
+                at += 1
+                value = term.astype(F32) if value is None else value + term.astype(F32)
+            out[row : row + rows, lane : lane + lanes] = value.astype(BF16)
+
+
+def combine(*outs):
+    operands, specs, layout = [], [], []
+    for _, cells in outs:
+        layout.append([])
+        for row, lane, rows, lanes, terms in cells:
+            places = []
+            for array, index, first in terms:
+                lead = array.ndim - 2
+                block = (1,) * lead + (rows, array.shape[-1])
+                place = tuple(index) + (0,) * (array.ndim - len(index))
+                operands.append(array)
+                specs.append(pl.BlockSpec(block, lambda i, place=place: place))
+                places.append((lead, first))
+            layout[-1].append((row, lane, rows, lanes, places))
+    shapes = [struct(shape, BF16) for shape, _ in outs]
+    return pl.pallas_call(
+        partial(combine_kernel, layout),
+        grid=(1,),
+        in_specs=specs,
+        out_specs=[whole(shape) for shape in shapes],
+        out_shape=shapes,
+        compiler_params=params(16),
+        cost_estimate=cost(2),
+        name="combine",
+    )(*operands)
+
+
+def place_kernel(order, *refs):
+    pieces, out_ref = refs[:4], refs[4]
     for me in range(4):
 
         @pl.when(order[0] == me)
         def _(me=me):
-            for index, step in enumerate((0, 2, 1, 3)):
-                start = (me ^ step) * WTOK
-                buffer[start : start + WTOK] = pieces[index][:WTOK].astype(F32)
-
-    copy = pltpu.make_async_copy(buffer, out_ref.at[pl.ds(part * rows, rows)], sem)
-    copy.start()
-    copy.wait()
-
-
-def place_windows(part, order, pieces, rows, held):
-    width = pieces[0].shape[1]
-    operands = list(pieces) + ([] if held is None else [held])
+            for part in range(pieces[0].shape[0] // ROWS):
+                for index, step in enumerate((0, 2, 1, 3)):
+                    start = (4 * part + (me ^ step)) * WTOK
+                    value = pieces[index][part * ROWS : part * ROWS + WTOK]
+                    out_ref[start : start + WTOK] = value.astype(F32)
+
+
+def place_windows(order, pieces):
+    height, width = pieces[0].shape
+    rows = height // ROWS * 4 * WTOK
+    lanes = width // 2
     return pl.pallas_call(
-        partial(place_kernel, part),
+        place_kernel,
         grid_spec=pltpu.PrefetchScalarGridSpec(
             num_scalar_prefetch=1,
-            grid=(1,),
-            in_specs=[whole(piece) for piece in pieces] + [ANY] * (len(operands) - 4),
-            out_specs=ANY,
-            scratch_shapes=[pltpu.VMEM((4 * WTOK, width), F32), pltpu.SemaphoreType.DMA(())],
+            grid=(2,),
+            in_specs=[pl.BlockSpec((height, lanes), lambda i, *_: (0, i))] * 4,
+            out_specs=pl.BlockSpec((rows, lanes), lambda i, *_: (0, i)),
         ),
         out_shape=struct((rows, width), F32),
-        input_output_aliases={} if held is None else {5: 0},
-        compiler_params=params(60),
-        cost_estimate=cost(4.5),
+        compiler_params=params(32),
+        cost_estimate=cost(7),
         name="place_windows",
-    )(order, *operands)
-
-
-def output_kernel(part, order, places, lives, *refs):
-    pieces, out_ref, buffer, rounded, sem = refs[:4], refs[-4], refs[-3], refs[-2], refs[-1]
-    rows = buffer.shape[0]
+    )(order, *pieces)
+
+
+def output_kernel(order, places, lives, *refs):
+    pieces, out_ref, buffer = refs[:4], refs[4], refs[5]
     for me in range(4):
 
         @pl.when(order[0] == me)
         def _(me=me):
-            for index, step in enumerate((0, 2, 1, 3)):
-                slot = me ^ step
-                valid = token_valid(places[4 * part + slot], lives[4 * part + slot])
-                value = pieces[index][:WTOK].astype(F32) * valid
-                buffer[slot * WTOK : (slot + 1) * WTOK] = value
-
-    rounded[...] = buffer[...].astype(BF16)
-    copy = pltpu.make_async_copy(rounded, out_ref.at[pl.ds(part * rows, rows)], sem)
-    copy.start()
-    copy.wait()
-
-
-def write_output(part, order, places, lives, pieces, rows, held):
-    width = pieces[0].shape[1]
-    operands = list(pieces) + ([] if held is None else [held])
-    shape = (4 * WTOK, width)
+            for part in range(pieces[0].shape[0] // ROWS):
+                for index, step in enumerate((0, 2, 1, 3)):
+                    slot = 4 * part + (me ^ step)
+                    value = pieces[index][part * ROWS : part * ROWS + WTOK].astype(F32)
+                    value = value * token_valid(places[slot], lives[slot])
+                    buffer[slot * WTOK : (slot + 1) * WTOK] = value
+
+    out_ref[...] = buffer[...].astype(BF16)
+
+
+def write_output(order, places, lives, pieces):
+    height, width = pieces[0].shape
+    rows = height // ROWS * 4 * WTOK
+    lanes = width // 2
     return pl.pallas_call(
-        partial(output_kernel, part),
+        output_kernel,
         grid_spec=pltpu.PrefetchScalarGridSpec(
             num_scalar_prefetch=3,
-            grid=(1,),
-            in_specs=[whole(piece) for piece in pieces] + [ANY] * (len(operands) - 4),
-            out_specs=ANY,
-            scratch_shapes=[
-                pltpu.VMEM(shape, F32),
-                pltpu.VMEM(shape, BF16),
-                pltpu.SemaphoreType.DMA(()),
-            ],
+            grid=(2,),
+            in_specs=[pl.BlockSpec((height, lanes), lambda i, *_: (0, i))] * 4,
+            out_specs=pl.BlockSpec((rows, lanes), lambda i, *_: (0, i)),
+            scratch_shapes=[pltpu.VMEM((rows, lanes), F32)],
         ),
         out_shape=struct((rows, width), BF16),
-        input_output_aliases={} if held is None else {7: 0},
-        compiler_params=params(60),
-        cost_estimate=cost(5),
+        compiler_params=params(32),
+        cost_estimate=cost(7),
         name="write_output",
-    )(order, places, lives, *operands)
+    )(order, places, lives, *pieces)
 
 
 def key_marks(heads):
@@ -1033,43 +1114,31 @@
     def scatter(parts):
         return lax.psum_scatter(parts[0], "dp", scatter_dimension=0, tiled=True).astype(F32)
 
-    def joined(*values):
-        total_value = values[0].astype(F32)
-        for value in values[1:]:
-            total_value = total_value + value.astype(F32)
-        return total_value.astype(BF16)
-
     def rows_scatter(parts):
         return [lax.psum_scatter(parts[0], "mp", scatter_dimension=0, tiled=True)]
 
     def rows_gather(own):
         return [lax.all_gather(own, "mp", axis=0, tiled=True)]
-
-    def sum_all(vector):
-        if not rings:
-            return lax.psum(vector, ("dp", "mp"))
-        for step in (1, 2):
-            vector = vector + lax.ppermute(
-                vector, "mp", [(m, m ^ step) for m in range(4)]
-            )
-        for step in (2, 4, 1):
-            vector = vector + lax.ppermute(
-                vector, "dp", [(d, d ^ step) for d in range(8)]
-            )
-        return vector
 
     def own_slice(array):
         rows = array.shape[0] // model_parts
         return lax.dynamic_slice_in_dim(array, model_index * rows, rows, 0)
 
-    first_piece = jnp.concatenate([qkv_weight[0], qkv_weight[1], qkv_weight[2], proj_weight.T], 1)
+    first_piece = jnp.concatenate(
+        [
+            jnp.pad(proj_weight.T, ((0, 0), (0, wide - cols))),
+            qkv_weight[0],
+            qkv_weight[1],
+            qkv_weight[2],
+        ],
+        axis=1,
+    )
     other_piece = jnp.concatenate([down_weight.T, up_weight], 1)
 
     row = lambda v: v.reshape(1, -1)
     gain_one, shift_one = row(norm_one_gain), row(norm_one_shift)
     gain_two, shift_two = row(norm_two_gain), row(norm_two_shift)
     bias_local = lax.dynamic_slice_in_dim(qv_bias, model_index * cols, cols, 1)
-    bias_local = jnp.pad(bias_local, [(0, 0), (0, wide - cols)])
     bias_qkv = row(jnp.stack([bias_local[0], jnp.zeros_like(bias_local[0]), bias_local[1]]))
     up_local = row(lax.dynamic_slice_in_dim(up_bias, model_index * units, units, 0))
     rel_high, rel_low = rel_operand(rel_height, rel_width, heads, wide)
@@ -1102,7 +1171,8 @@
     blocks = [(part, part_rows) for part in range(halves)]
 
     def start(x):
-        return prepare(places, places_all, lives_all, x, gain_one, shift_one)
+        every = 4 if rings else 1
+        return prepare(places, places_all, lives_all, x, gain_one, shift_one, every)
 
     def masked(top):
         return mask_rows(places, places_all, lives_all, top)
@@ -1112,7 +1182,20 @@
 
     def attention_back(part, pieces, q, k, v, shares, weights):
         return attend_back(
-            heads, part, windows, split, pieces, q, k, v, shares, rel_high, marks, weights
+            heads,
+            part,
+            windows,
+            split,
+            pieces,
+            q,
+            k,
+            v,
+            shares,
+            rel_high,
+            marks,
+            weights,
+            normed,
+            valid,
         )
 
     def down_groups(mlps):
@@ -1127,18 +1210,34 @@
             [(backs[i][1], 0, part_rows, attended[i][0]) for i in range(halves)],
         ]
 
-    x_windows, top_windows = by_window(block_input), by_window(cotangent)
+    def bundle(sums_two, backs, mlps):
+        qv_sums = add_all([item[3] for item in backs]).reshape(3, cols)[0::2]
+        rel_sums = rel_result(add_all([item[2] for item in backs]), heads)
+        up_sums = add_all([item[3] for item in mlps]).reshape(units)
+        qv_full = lax.dynamic_update_slice_in_dim(
+            jnp.zeros((2, width), F32), qv_sums, model_index * cols, 1
+        )
+        up_full = lax.dynamic_update_slice_in_dim(
+            jnp.zeros(up_bias.shape, F32), up_sums, model_index * units, 0
+        )
+        norms = add_all([item[4] for item in backs])
+        arrays = [norms, add_all(sums_two), up_full, qv_full, *rel_sums]
+        flat = jnp.concatenate([array.reshape(-1) for array in arrays])
+        count = (flat.size + 1023) // 1024 * 1024
+        return jnp.pad(flat, (0, count - flat.size)).reshape(-1, 128)
+
+    x_windows = by_window(block_input)
     if not rings:
         first_weights, other_weights = gather(first_piece), gather(other_piece)
-        rows_in, normed, valid = start(x_windows)
-        grad_top = masked(top_windows)
-        own_in, own_top, own_valid = own_slice(rows_in), own_slice(grad_top), own_slice(valid)
+        rows_in, own_valid, normed, valid = start(x_windows)
+        grad_top = masked(by_window(cotangent))
+        own_in, own_top, own_valid = own_slice(rows_in), own_slice(grad_top), own_slice(own_valid)
         q, k, v, weights = project(offsets, first_weights, normed, bias_qkv, cols, wide)
         attended = [attention(0, q, k, v, weights)]
         after, normed_two = norm_two(
             rows_scatter(attended[0][2:]), own_in, 0, row(proj_bias), gain_two, shift_two
         )
-        none = jnp.zeros((1, 128), F32)
+        none = jnp.zeros((8, 128), F32)
         mlps = [
             mlp(
                 offsets,
@@ -1148,7 +1247,7 @@
                 0,
                 up_local,
                 none,
-                none,
+                row(down_bias),
                 False,
             )
         ]
@@ -1167,48 +1266,47 @@
         down_grad = scatter(weight_grad(None, down_groups(mlps), share))
         up_grad = scatter(weight_grad(None, up_groups(mlps), share))
         backs = [attention_back(0, rows_gather(branch), q, k, v, attended[0][1], weights)]
-        own, sums = norm_one_back(
-            rows_scatter(backs[0][4:]), own_in, own_valid, 0, grad_after, gain_one
-        )
-        sums_one = [sums]
+        parts = [(part, 0) for part in rows_scatter(backs[0][5:])]
+        own = norm_one_back([(parts, grad_after)], own_in, own_valid, gain_one)
         input_grad = unpad(rows_gather(own)[0]).astype(F32)
         first_grad = scatter(weight_grad(None, first_groups(backs, attended), share))
+        vector = lax.psum(bundle(sums_two, backs, mlps), ("dp", "mp"))
     else:
         def second_norm(part, keep, came, crossed):
             return norm_two(
-                [keep, came, crossed], rows_in, 4 * part, row(proj_bias), gain_two, shift_two
+                [keep, came, crossed], rows_in, part, bias_proj, gain_two, shift_two
             )
 
         def second_back(part, after, keep, came, crossed):
             return norm_two_back([keep, came, crossed], after, grad_top, 4 * part, gain_two)
 
-        def first_back(part, grad_after, keep, came, crossed):
-            return norm_one_back(
-                [keep, came, crossed], rows_in, valid, 4 * part, grad_after, gain_one
-            )
-
         def spread(own, across):
             return [own, across, over_core(own), over_core(across)]
 
-        def to_core(keep, send):
-            came = over_core(send)
-            return came, joined(keep[ROWS:], came[ROWS:])
-
-        bias_row = row(down_bias)
+        rows = (ROWS, width)
+
+        def second(keep, came, at=0):
+            return (at, 0, *rows, [(keep, (1,), 0), (came, (1,), 0)])
 
         z1, x0 = over_z(first_piece), over_x(first_piece)
-        z1, x0, x_windows, top_windows, other_piece, rel_high, rel_low = sync(
-            z1, x0, x_windows, top_windows, other_piece, rel_high, rel_low
+        z1, x0, x_windows, other_piece, rel_high, rel_low, cotangent = sync(
+            z1, x0, x_windows, other_piece, rel_high, rel_low, cotangent
         )
         z2, x1 = over_z(z1), over_x(z1)
-        rows_in, normed, valid = start(x_windows)
-        z2, x1, normed, top_windows = sync(z2, x1, normed, top_windows)
+        rows_in, own_valid, normed, valid = start(x_windows)
+        z2, x1, normed, cotangent, gain_two, shift_two, bias_proj, bias_down = sync(
+            z2, x1, normed, cotangent, gain_two, shift_two, row(proj_bias), row(down_bias)
+        )
         z3, x2 = over_z(z2), over_x(z2)
-        grad_top = masked(top_windows)
-        z3, x2, normed, grad_top, other_piece = sync(z3, x2, normed, grad_top, other_piece)
+        z3, x2, normed, top_windows, other_piece = sync(
+            z3, x2, normed, by_window(cotangent), other_piece
+        )
         x3 = over_x(z3)
         oz1 = over_z(other_piece)
-        x3, normed, other_late = sync(x3, normed, other_piece)
+        grad_top = masked(top_windows)
+        x3, normed, grad_top, other_late, gain_two, shift_two, bias_proj, bias_down = sync(
+            x3, normed, grad_top, other_piece, gain_two, shift_two, bias_proj, bias_down
+        )
         ox0 = over_x(other_late)
         first_weights = [first_piece, x0, z1, x1, z2, x2, z3, x3]
         q, k, v, weights = project(offsets, first_weights, normed, bias_qkv, cols, wide)
@@ -1218,124 +1316,252 @@
         a0 = attention(0, q, k, v, weights)
         oz2, ox1, a0 = sync(oz2, ox1, a0)
         oz3, ox2 = over_z(oz2), over_x(oz2)
-        came0, passed0 = to_core(a0[2], a0[3])
+        came0 = over_core(a0[3])
+        (passed0,) = combine((rows, [second(a0[2], came0)]))
         crossed0 = over_y(passed0)
         a1 = attention(1, tie(q, passed0), k, v, weights)
         oz3, ox2, crossed0, a1 = sync(oz3, ox2, crossed0, a1)
         ox3 = over_x(oz3)
-        after0, own0 = second_norm(0, a0[2], came0, crossed0)
+        came1 = over_core(a1[3])
+        (passed1,) = combine((rows, [second(a1[2], came1)]))
+        crossed1 = over_y(passed1)
+        after0, own0 = second_norm(0, tie(a0[2], passed1), came0, crossed0)
         across0 = over_y(own0)
-        came1, passed1 = to_core(a1[2], a1[3])
-        crossed1 = over_y(tie(passed1, own0))
         attended = [a0, a1]
-        ox3, across0, crossed1 = sync(ox3, across0, crossed1)
+        after1, own1 = second_norm(1, tie(a1[2], own0), came1, crossed1)
+        ox3, across0, own1 = sync(ox3, across0, own1)
         other_weights = [other_piece, ox0, oz1, ox1, oz2, ox2, oz3, ox3]
-        after1, own1 = second_norm(1, a1[2], came1, crossed1)
         across1 = over_y(own1)
         pieces0 = spread(own0, across0)
-        pieces0[0] = tie(pieces0[0], own1)
-
-        m0 = mlp(offsets, pieces0, other_weights, grad_top, 0, up_local, after0, bias_row, True)
+
+        m0 = mlp(offsets, pieces0, other_weights, grad_top, 0, up_local, after0, bias_down, True)
         across1, m0 = sync(across1, m0)
         pieces1 = spread(own1, across1)
-        came0, passed0 = to_core(m0[4], m0[5])
+        came0, out_came0 = over_core(m0[5]), over_core(m0[7])
+        (passed0,) = combine((rows, [second(m0[4], came0)]))
         crossed0 = over_y(passed0)
         pieces1[0] = tie(pieces1[0], passed0)
-        m1 = mlp(offsets, pieces1, other_weights, grad_top, 1, up_local, after1, bias_row, True)
-        crossed0, m1 = sync(crossed0, m1)
+        m1 = mlp(offsets, pieces1, other_weights, grad_top, 1, up_local, after1, bias_down, True)
+        crossed0, out_came0, m1 = sync(crossed0, out_came0, m1)
         mlps = [m0, m1]
+        came1, out_came1 = over_core(m1[5]), over_core(m1[7])
         grad_after0, branch0, sums0 = second_back(0, after0, m0[4], came0, crossed0)
-        came1, passed1 = to_core(m1[4], m1[5])
         across0 = over_y(branch0)
-        crossed1 = over_y(tie(passed1, branch0))
-        left = tie(m0, branch0, passed1)
+        passed1, out_passed = combine(
+            (rows, [second(tie(m1[4], branch0), came1)]),
+            (
+                (2 * ROWS, width),
+                [second(m0[6], out_came0), second(m1[6], out_came1, ROWS)],
+            ),
+        )
+        left = tie(m0, passed1)
         (down_pairs,) = weight_grad(targets, down_groups([left, m1]), share, 0)
-        down_pairs = sync(down_pairs)[0]
+        across0, passed1, down_pairs = sync(across0, passed1, down_pairs)
+        crossed1 = over_y(passed1)
+        branches0 = spread(branch0, across0)
+        left = tie(m0, down_pairs)
+        up_high, up_low, up_keep = weight_grad(targets, up_groups([left, m1]), share)
+        crossed1, branches0, up_high, up_low, up_keep = sync(
+            crossed1, branches0, up_high, up_low, up_keep
+        )
+
+        up_came_high = over_x(up_high)
         down_held = over_z(down_pairs[3])
-        up_send, up_keep = weight_grad(
-            targets, up_groups([tie(m0, down_pairs), m1]), share
-        )
-        across0, crossed1, down_held, up_send, up_keep = sync(
-            across0, crossed1, down_held, up_send, up_keep
-        )
-
         grad_after1, branch1, sums1 = second_back(1, after1, m1[4], came1, crossed1)
         sums_two = [sums0, sums1]
         across1 = over_y(branch1)
-        branches0 = spread(branch0, across0)
-        out_came0, out_passed0 = to_core(m0[6], tie(m0[7], branch1))
-        out_crossed0 = over_y(out_passed0)
-        down_held = over_z(joined(down_pairs[2], down_held))
-        up_came_high = over_x(up_send[2:])
-        branches0[0] = tie(branches0[0], branch1, out_passed0)
+        branches0[0] = tie(branches0[0], branch1)
         b0 = attention_back(0, branches0, q, k, v, a0[1], weights)
-        across1, out_crossed0, down_held, up_came_high, b0 = sync(
-            across1, out_crossed0, down_held, up_came_high, b0
-        )
+        across1, up_came_high, down_held, b0, out_passed = sync(
+            across1, up_came_high, down_held, b0, out_passed
+        )
+        out_crossed = over_y(out_passed)
         branches1 = spread(branch1, across1)
-        came0, passed0 = to_core(b0[4], b0[5])
+        came0 = over_core(b0[6])
+        up_came_low = over_x(up_low)
+
+        def down_cells(k, held, lane):
+            return [
+                (0, half * units, share, units, [(down_pairs, (k, half), 0), (held, at, first)])
+                for half, (at, first) in enumerate(lane)
+            ]
+
+        passed0, held = combine(
+            (rows, [second(b0[5], came0)]),
+            (
+                (share, 3 * units),
+                down_cells(2, down_held, [((0,), 0), ((1,), 0)])
+                + [
+                    (
+                        0,
+                        2 * units,
+                        share,
+                        units,
+                        [(up_keep, (3,), 0), (up_came_high, (1,), 0)],
+                    )
+                ],
+            ),
+        )
         crossed0 = over_y(passed0)
-        out_came1, out_passed1 = to_core(m1[6], tie(m1[7], passed0))
-        out_crossed1 = over_y(out_passed1)
-        down_held = over_z(joined(down_pairs[1], down_held))
-        up_came_low = over_x(up_send[:2])
-        branches1[0] = tie(branches1[0], out_passed1)
+        held = over_z(held)
+        branches1[0] = tie(branches1[0], passed0)
         b1 = attention_back(1, branches1, q, k, v, a1[1], weights)
-        crossed0, out_crossed1, down_held, up_came_low, b1 = sync(
-            crossed0, out_crossed1, down_held, up_came_low, b1
+        crossed0, held, up_came_low, out_crossed, b1 = sync(
+            crossed0, held, up_came_low, out_crossed, b1
         )
         backs = [b0, b1]
-        own0, one0 = first_back(0, grad_after0, b0[4], came0, crossed0)
-        in_across0 = over_y(own0)
-        came1, passed1 = to_core(b1[4], b1[5])
-        crossed1 = over_y(tie(passed1, own0))
-        down_last = joined(down_pairs[0], down_held)
-        down_other = over_x(down_last[1])
-        up_held = over_z(joined(up_keep[3], up_came_high[1]))
-        left = tie(b0, own0, passed1, down_last)
-        first_send, first_keep, first_pairs = weight_grad(
-            targets, first_groups([left, b1], attended), share, 3 * cols // 128 * 128
-        )
-        in_across0, crossed1, down_other, up_held, first_send, first_keep, first_pairs = sync(
-            in_across0, crossed1, down_other, up_held, first_send, first_keep, first_pairs
-        )
-
-        first_came = over_x(first_send)
-        pair_held = over_z(first_pairs[3])
-        own1, one1 = first_back(1, grad_after1, b1[4], came1, crossed1)
-        sums_one = [one0, one1]
-        in_across1 = over_y(own1)
-        in_pieces0 = spread(own0, in_across0)
-        up_held = over_z(joined(up_keep[2], up_came_high[0], up_held))
-        pair_held = over_z(joined(first_pairs[2], pair_held))
-        out_own0 = joined(m0[6][:ROWS], out_came0[:ROWS], out_crossed0)
-        out_own1 = joined(m1[6][:ROWS], out_came1[:ROWS], out_crossed1)
-        out_across0, out_across1 = over_y(tie(out_own0, own1)), over_y(tie(out_own1, own1))
-        input_grad = place_windows(0, local, in_pieces0, slots * WTOK, None)
-        in_across1, up_held, pair_held, first_came, input_grad = sync(
-            in_across1, up_held, pair_held, first_came, input_grad
-        )
-        first_held = over_z(joined(first_keep[3], first_came[3]))
-        pair_held = over_z(joined(first_pairs[1], pair_held))
-        up_held = over_z(joined(up_keep[1], up_came_low[1], up_held))
-        in_pieces1 = spread(own1, in_across1)
-        input_grad = place_windows(1, local, in_pieces1, slots * WTOK, input_grad)
-        first_held, pair_held, up_held, input_grad, out_across0, out_across1 = sync(
-            first_held, pair_held, up_held, input_grad, out_across0, out_across1
-        )
-        first_held = over_z(joined(first_keep[2], first_came[2], first_held))
-        pair_last = joined(first_pairs[0], pair_held)
-        pair_other = over_x(pair_last[1])
-        out_pieces0 = spread(out_own0, out_across0)
-        block_output = write_output(
-            0, local, places_all, lives_all, out_pieces0, slots * WTOK, None
-        )
-        first_held, pair_other, block_output = sync(first_held, pair_other, block_output)
-        first_held = over_z(joined(first_keep[1], first_came[1], first_held))
-        out_pieces1 = spread(out_own1, out_across1)
-        block_output = write_output(
-            1, local, places_all, lives_all, out_pieces1, slots * WTOK, block_output
-        )
+        came1 = over_core(b1[6])
+        vector = bundle(sums_two, backs, mlps)
+        vector_came = lax.ppermute(vector, "mp", [(m, m ^ 1) for m in range(4)])
+        came1, vector_came, vector = sync(came1, vector_came, vector)
+        vector = vector + vector_came
+        vector_came = lax.ppermute(vector, "mp", [(m, m ^ 2) for m in range(4)])
+        passed1, out_own, down_held, up_held = combine(
+            (rows, [second(tie(b1[5], vector), came1)]),
+            (
+                (2 * ROWS, width),
+                [
+                    (
+                        part * ROWS,
+                        0,
+                        *rows,
+                        [(keep, (0,), 0), (came, (0,), 0), (out_crossed, (part,), 0)],
+                    )
+                    for part, (keep, came) in enumerate(((m0[6], out_came0), (m1[6], out_came1)))
+                ],
+            ),
+            (
+                (share, 2 * units),
+                down_cells(1, held, [((0,), 0), ((0,), units)]),
+            ),
+            (
+                (share, units),
+                [
+                    (
+                        0,
+                        0,
+                        share,
+                        units,
+                        [(up_keep, (2,), 0), (up_came_high, (0,), 0), (held, (0,), 2 * units)],
+                    )
+                ],
+            ),
+        )
+        crossed1 = over_y(passed1)
+        down_held = over_z(down_held)
+        left = tie(b0, passed1)
+        lead = 3 * cols // 128 * 128
+        rest = 4 * cols - lead
+        firsts = weight_grad(targets, first_groups([left, b1], attended), share, lead)
+        crossed1, down_held, up_held, vector, vector_came, firsts = sync(
+            crossed1, down_held, up_held, vector, vector_came, firsts
+        )
+        first_high, first_low, first_keep, first_pairs = firsts
+        vector = vector + vector_came
+
+        def pair_cells(k, lane, held=None, first=0):
+            cells = []
+            for half in range(2):
+                terms = [(first_pairs, (k, half), 0)]
+                if held is not None:
+                    terms.append((held, (0,), first + half * rest))
+                cells.append((0, lane + half * rest, share, rest, terms))
+            return cells
+
+        first_came_high = over_x(first_high)
+        (held_sum,) = combine(
+            (
+                (share, 2 * rest + units),
+                pair_cells(3, 0) + [(0, 2 * rest, share, units, [(up_held, (0,), 0)])],
+            )
+        )
+        held = over_z(held_sum)
+        vector_came = lax.ppermute(vector, "dp", [(d, d ^ 2) for d in range(8)])
+        own = norm_one_back(
+            [
+                ([(b0[5], 0), (came0, 0), (tie(crossed0, held_sum), 0)], grad_after0),
+                ([(b1[5], 0), (came1, 0), (crossed1, 0)], grad_after1),
+            ],
+            rows_in,
+            own_valid,
+            gain_one,
+        )
+        in_across = over_y(own)
+        first_came_high, held, vector_came, own = sync(first_came_high, held, vector_came, own)
+        vector = vector + vector_came
+        first_came_low = over_x(first_low)
+        held, down_other = combine(
+            (
+                (share, lead + 2 * rest + units),
+                [(0, 0, share, lead, [(first_keep, (3,), 0), (first_came_high, (1,), 0)])]
+                + pair_cells(2, lead, held, 0)
+                + [
+                    (
+                        0,
+                        lead + 2 * rest,
+                        share,
+                        units,
+                        [(up_keep, (1,), 0), (up_came_low, (1,), 0), (held, (0,), 2 * rest)],
+                    )
+                ],
+            ),
+            (
+                (share, units),
+                [(0, 0, share, units, [(down_pairs, (0, 1), 0), (down_held, (0,), units)])],
+            ),
+        )
+        held = over_z(held)
+        down_other = over_x(down_other)
+        vector_came = lax.ppermute(vector, "dp", [(d, d ^ 4) for d in range(8)])
+        first_came_low, held, vector_came, down_other, in_across, out_own = sync(
+            first_came_low, held, vector_came, down_other, in_across, out_own
+        )
+        vector = vector + vector_came
+        up_last = held[:, lead + 2 * rest :]
+        (held,) = combine(
+            (
+                (share, lead + 2 * rest),
+                [
+                    (
+                        0,
+                        0,
+                        share,
+                        lead,
+                        [(first_keep, (2,), 0), (first_came_high, (0,), 0), (held, (0,), 0)],
+                    )
+                ]
+                + pair_cells(1, lead, held, lead),
+            ),
+        )
+        held = over_z(held)
+        vector_came = lax.ppermute(vector, "dp", [(d, d ^ 1) for d in range(8)])
+        out_across = over_y(out_own)
+        in_pieces = spread(own, in_across)
+        input_grad = place_windows(local, in_pieces)
+        held, vector_came, input_grad = sync(held, vector_came, input_grad)
+        out_pieces = spread(out_own, out_across)
+        block_output = write_output(local, places_all, lives_all, out_pieces)
+        vector = vector + vector_came
+        first_held, pair_other = combine(
+            (
+                (share, lead),
+                [
+                    (
+                        0,
+                        0,
+                        share,
+                        lead,
+                        [(first_keep, (1,), 0), (first_came_low, (1,), 0), (held, (0,), 0)],
+                    )
+                ],
+            ),
+            (
+                (share, rest),
+                [(0, 0, share, rest, [(first_pairs, (0, 1), 0), (held, (0,), lead + rest)])],
+            ),
+        )
+        pair_other = over_x(pair_other)
+        first_held = over_z(first_held)
 
         def last(*values):
             out = values[0].astype(F32)
@@ -1343,50 +1569,33 @@
                 out = out + value.astype(F32)
             return out
 
-        down_grad = last(down_pairs[0, 0], down_held[0], down_other)
-        up_grad = last(up_keep[0], up_came_low[0], up_held)
+        down_grad = last(down_pairs[0, 0], down_held[:, :units], down_other)
+        up_grad = last(up_keep[0], up_came_low[0], up_last)
         first_grad = jnp.concatenate(
             [
-                last(first_keep[0], first_came[0], first_held),
-                last(first_pairs[0, 0], pair_held[0], pair_other),
+                last(first_keep[0], first_came_low[0], first_held),
+                last(first_pairs[0, 0], held[:, lead : lead + rest], pair_other),
             ],
             axis=1,
         )
 
-    two = add_all(sums_two)
-    one = add_all(sums_one)
-    qv_sums = add_all([item[3] for item in backs]).reshape(3, wide)[0::2, :cols]
-    rel_sums = rel_result(add_all([item[2] for item in backs]), heads)
-    up_sums = add_all([item[3] for item in mlps]).reshape(units)
-    qv_full = lax.dynamic_update_slice_in_dim(
-        jnp.zeros((2, width), F32), qv_sums, model_index * cols, 1
-    )
-    up_full = lax.dynamic_update_slice_in_dim(
-        jnp.zeros(up_bias.shape, F32), up_sums, model_index * units, 0
-    )
-
-    def sum_bundle(arrays):
-        sizes = [array.size for array in arrays]
-        flat = jnp.concatenate([array.reshape(-1) for array in arrays])
-        count = (flat.size + 1023) // 1024 * 1024
-        flat = jnp.pad(flat, (0, count - flat.size)).reshape(-1, 128)
-        flat = sum_all(flat).reshape(-1)
-        outs, at = [], 0
-        for array, size in zip(arrays, sizes):
-            outs.append(flat[at : at + size].reshape(array.shape))
-            at += size
-        return outs
-
-    two_sums, up_bias_grad, one_sums, qv_bias_grad, height_grad, width_grad = sum_bundle(
-        [two, up_full, one, qv_full, rel_sums[0], rel_sums[1]]
-    )
+    shapes = [(2, width), (4, width), (up_bias.size,), (2, width), (RELN, HD), (RELN, HD)]
+    outs, at = [], 0
+    flat = vector.reshape(-1)
+    for shape in shapes:
+        size = int(np.prod(shape))
+        outs.append(flat[at : at + size].reshape(shape))
+        at += size
+    one_sums, two_sums, up_bias_grad, qv_bias_grad, height_grad, width_grad = outs
+    shift_one_grad = one_sums[1]
+    gain_one_grad = (one_sums[0] - norm_one_shift * shift_one_grad) / norm_one_gain
     qkv_grad = jnp.stack([first_grad[:, slot * cols : (slot + 1) * cols] for slot in range(3)])
     proj_grad = first_grad[:, 3 * cols :].T
     return (
         block_output,
         input_grad,
-        one_sums[0],
-        one_sums[1],
+        gain_one_grad,
+        shift_one_grad,
         qkv_grad,
         qv_bias_grad,
         proj_grad,

time: 475 us -> 431 us (0.907)
  Pallas kernels: 220 us -> 161 us
  local copies, waits for them, and re-layouts: 37 us -> 78.9 us
  other arithmetic: 49.2 us -> 9.96 us
  waiting for transfers between devices: 107 us -> 128 us
  starting transfers between devices: 53.1 us -> 44.7 us
    unnamed x152 -> x288, local copies, waits for them, and re-layouts: 9.41 us -> 60.1 us
    convert_element_type x21 -> x0, other arithmetic: 35.7 us -> none  [joined(): return total_value.astype(BF16)]
    pallas_call x7 -> x14, Pallas kernels: 34.5 us -> 23.8 us  [the longest x10 7.2 us: combine(): pl.pallas_call(partial(combine_kernel, layout), grid=(1,), in_specs=specs...]
    ppermute x3, waiting for transfers between devices: 0.01 us -> 9.88 us  [body(): crossed0 = over_y(passed0)]
    pallas_call x2, Pallas kernels: 37.2 us -> 27.8 us  [attend_back(): pl.pallas_call(partial(attend_back_kernel, heads, windows, split, len(pie...]
    pallas_call x3, Pallas kernels: 39.3 us -> 31.2 us  [weight_grad(): pl.pallas_call(partial(weight_grad_kernel, sizes, share), grid_spec=pltpu...]
    pallas_call x2, Pallas kernels: 27.4 us -> 21.1 us  [attend(): pl.pallas_call(partial(attend_kernel, heads, split), grid=(windows,), in_...]
    pallas_call x1, Pallas kernels: 7.71 us -> 1.76 us  [mask_rows(): pl.pallas_call(mask_kernel, grid_spec=pltpu.PrefetchScalarGridSpec(num_sc...]
  transfers between devices with their start and end apart: 76 -> 65, of which waited for: 26 -> 28; matrix products, arithmetic and copies ran while one was open for 15% -> 6% of each run, Pallas kernels for 44% -> 36%
where the time goes in v4:
time: 431 us; the launch traced here: 425 us
  Pallas kernels  161 us (37%)
  waiting for transfers between devices  128 us (30%)
  local copies, waits for them, and re-layouts  78.9 us (18%)
  starting transfers between devices  44.7 us (10%)
  other arithmetic  9.96 us (2%)
    unnamed x288, local copies, waits for them, and re-layouts  60.1 us
    pallas_call x2, Pallas kernels, mlp(): pl.pallas_call(partial(mlp_kernel, len(pieces), len(weight_pieces), split...  40.3 us
    pallas_call x3, Pallas kernels, weight_grad(): pl.pallas_call(partial(weight_grad_kernel, sizes, share), grid_spec=pltpu...  31.2 us
    pallas_call x2, Pallas kernels, attend_back(): pl.pallas_call(partial(attend_back_kernel, heads, windows, split, len(pie...  27.8 us
    pallas_call x2, Pallas kernels, attend(): pl.pallas_call(partial(attend_kernel, heads, split), grid=(windows,), in_...  21.1 us
    ppermute x1, waiting for transfers between devices, body(): first_came_low = over_x(first_low)  13.2 us
    ppermute x3, waiting for transfers between devices, body(): crossed1 = over_y(passed1)  12.7 us
    ppermute x1, waiting for transfers between devices, body(): vector_came = lax.ppermute(vector, 'dp', [(d, d ^ 4) for d in range(8)])  12.2 us
  transfers between devices with their start and end apart: 65, of which 28 were waited for; matrix products, arithmetic and copies ran while one was open for 6% of the time, Pallas kernels for 36%

profile of v4, /device:TPU:0, one launch (start us, length us, event | category | flops | bytes accessed | tf_op | source)
XLA Modules:
  0.0 425.0 jit_solution(15082367053079562555)
XLA Ops:
  2.9 3.1 collective-permute-start
  7.9 5.0 %reshape.127.x_ref = bf16[8,196,1280]{2,1,0:T(8,128)(2,1)} reshape(bf16[1568,1280]{1,0:T(8,128)(2,1)} %param.19) | data formatting | bytes 8028160 | tf_op jit(solution)/shard_map/reshape | solution.py:1166
  13.8 4.6 %collective-permute-done.refs_2_ = bf16[160,1344]{1,0:T(8,128)(2,1)} collective-permute-done((bf16[160,1344]{1,0:T(8,128)(2,1)S(1)}, bf16[160,1344]{1,0:T(8,128)(2,1)}, u32[]{:S(2)}, u32[]{:S(2)}) %collective-permute-start) | collective-permute-done | bytes 430112 | tf_op jit(solution)/shard_map/ppermute | solution.py:1291
  21.8 2.2 copy-done.16
  24.0 4.4 %prepare.1 = (bf16[416,1280]{1,0:T(8,128)(2,1)S(1)}, f32[416,1]{1,0:T(8,128)S(1)}, bf16[1664,1280]{1,0:T(8,128)(2,1)S(1)}, f32[1664,1]{1,0:T(8,128)S(1)}) custom-call(s32[8]{0:T(128)S(1)} %stack.112.order, s32[8]{0:T(128)S(1)} %copy-done.108, s32[8]{0:T(128)S(1)} %copy-done.110, bf16[8,196,1280]{2,1,0:T(8,128)(2,1)S(1)} %copy-done.16, ...), custom_call_target="tpu_custom_call" | custom-call | flops 450000000 | bytes 90000 | tf_op jit(solution)/shard_map/prepare/pallas_call | solution.py:115
  28.3 2.0 copy-done.2
  31.0 1.8 collective-permute-done.2.refs_4_
  34.2 4.9 %reshape.134.top_ref = bf16[8,196,1280]{2,1,0:T(8,128)(2,1)} reshape(bf16[1568,1280]{1,0:T(8,128)(2,1)} %param.36) | data formatting | bytes 8028160 | tf_op jit(solution)/shard_map/reshape | solution.py:1166
  39.1 6.5 %collective-permute-done.4.refs_6_ = bf16[160,1344]{1,0:T(8,128)(2,1)} collective-permute-done((bf16[160,1344]{1,0:T(8,128)(2,1)}, bf16[160,1344]{1,0:T(8,128)(2,1)}, u32[]{:S(2)}, u32[]{:S(2)}) %collective-permute-start.4) | collective-permute-done | bytes 430112 | tf_op jit(solution)/shard_map/ppermute | solution.py:1300
  46.6 2.2 copy-done.17
  50.5 2.0 copy-done
  52.4 3.1 collective-permute-done.7.refs_7_
  58.4 2.2 copy-done.3
  62.7 8.1 %qkv.1 = (bf16[1664,384]{1,0:T(8,128)(2,1)S(1)}, bf16[1664,384]{1,0:T(8,128)(2,1)S(1)}, bf16[1664,384]{1,0:T(8,128)(2,1)S(1)}, bf16[1280,1344]{1,0:T(8,128)(2,1)S(1)}) custom-call(s32[8]{0:T(128)S(1)} %stack.121.offsets, bf16[160,1344]{1,0:T(8,128)(2,1)S(1)} %concatenate.15.refs_0_, bf16[160,1344]{1,0:T(8,128)(2,1)S(1)} %copy-done.95, ...), custom_call_target="tpu_custom_call" | custom-call | flops 700000000 | bytes 140000 | tf_op jit(solution)/shard_map/qkv/pallas_call | solution.py:321
  70.9 2.5 collective-permute-done.8.refs_5_
  75.1 10.5 %attend.2 = (bf16[832,320]{1,0:T(8,128)(2,1)S(1)}, bf16[832,1024]{1,0:T(8,128)(2,1)S(1)}, bf16[416,1280]{1,0:T(8,128)(2,1)S(1)}, bf16[416,1280]{1,0:T(8,128)(2,1)S(1)}) custom-call(bf16[1664,384]{1,0:T(8,128)(2,1)S(1)} %get-tuple-element.266.q_ref.refs_4_, bf16[1664,384]{1,0:T(8,128)(2,1)S(1)} %get-tuple-element.254.k_ref.refs_5_, ...), custom_call_target="tpu_custom_call" | custom-call | flops 675000000 | bytes 135000 | tf_op jit(solution)/shard_map/attend/pallas_call | solution.py:457
  86.9 3.7 collective-permute-done.10.refs_7_
  90.6 1.9 collective-permute-done.9.refs_8_
  96.6 10.6 %attend.3 = (bf16[832,320]{1,0:T(8,128)(2,1)S(1)}, bf16[832,1024]{1,0:T(8,128)(2,1)S(1)}, bf16[416,1280]{1,0:T(8,128)(2,1)S(1)}, bf16[416,1280]{1,0:T(8,128)(2,1)S(1)}) custom-call(bf16[1664,384]{1,0:T(8,128)(2,1)S(1)} %get-tuple-element.266.q_ref.refs_4_, bf16[1664,384]{1,0:T(8,128)(2,1)S(1)} %get-tuple-element.254.k_ref.refs_5_, ...), custom_call_target="tpu_custom_call" | custom-call | flops 675000000 | bytes 135000 | tf_op jit(solution)/shard_map/attend/pallas_call | solution.py:457
  108.4 6.7 %collective-permute-done.11.refs_10_ = bf16[160,2560]{1,0:T(8,128)(2,1)S(1)} collective-permute-done((bf16[160,2560]{1,0:T(8,128)(2,1)S(1)}, bf16[160,2560]{1,0:T(8,128)(2,1)S(1)}, u32[]{:S(2)}, u32[]{:S(2)}) %collective-permute-start.11) | collective-permute-done | bytes 819232 | tf_op jit(solution)/shard_map/ppermute | solution.py:1318
  121.5 11.5 %collective-permute-done.18.refs_2_ = bf16[208,1280]{1,0:T(8,128)(2,1)S(1)} collective-permute-done((bf16[208,1280]{1,0:T(8,128)(2,1)S(1)}, bf16[208,1280]{1,0:T(8,128)(2,1)S(1)}, u32[]{:S(2)}, u32[]{:S(2)}) %collective-permute-start.18) | collective-permute-done | bytes 532512 | tf_op jit(solution)/shard_map/ppermute | solution.py:1327
  135.9 7.9 %collective-permute-done.17.refs_1_ = bf16[208,1280]{1,0:T(8,128)(2,1)} collective-permute-done((bf16[208,1280]{1,0:T(8,128)(2,1)}, bf16[208,1280]{1,0:T(8,128)(2,1)}, u32[]{:S(2)}, u32[]{:S(2)}) %collective-permute-start.17) | collective-permute-done | bytes 532512 | tf_op jit(solution)/shard_map/ppermute | solution.py:1329
  148.9 20.0 %mlp.2 = (bf16[832,1280]{1,0:T(8,128)(2,1)}, bf16[832,1280]{1,0:T(8,128)(2,1)}, bf16[832,1280]{1,0:T(8,128)(2,1)}, f32[1,1280]{1,0:T(1,128)S(1)}, bf16[416,1280]...) custom-call(s32[8]{0:T(128)S(1)} %stack.121.offsets, ...), custom_call_target="tpu_custom_call" | custom-call | flops 1050000000 | bytes 210000 | tf_op jit(solution)/shard_map/mlp/pallas_call | solution.py:726
  170.0 1.9 collective-permute-done.22.refs_1_
  175.0 20.3 %mlp.3 = (bf16[832,1280]{1,0:T(8,128)(2,1)}, bf16[832,1280]{1,0:T(8,128)(2,1)}, bf16[832,1280]{1,0:T(8,128)(2,1)}, f32[1,1280]{1,0:T(1,128)S(1)}, bf16[416,1280]...) custom-call(s32[8]{0:T(128)S(1)} %stack.121.offsets, ...), custom_call_target="tpu_custom_call" | custom-call | flops 1050000000 | bytes 210000 | tf_op jit(solution)/shard_map/mlp/pallas_call | solution.py:726
  195.9 2.0 norm_two_back.2
  202.8 2.4 combine.13
  206.2 2.2 copy-done.1
  208.4 10.0 %weight_grad.3.refs_2_.refs_4_.refs_8_.refs_10_.refs_9_ = bf16[4,2,160,1280]{3,2,1,0:T(8,128)(2,1)S(1)} custom-call(s32[8]{0:T(128)S(1)} %stack.131.targets, bf16[1664,1280]{1,0:T(8,128)(2,1)S(1)} %copy-done.1, bf16[832,1280]{1,0:T(8,128)(2,1)S(1)} %copy-done.59, bf16[1664,1280]{1,0:T(8,128)(2,1)S(1)} %copy-done.1, bf16[832,1280]{1,0:T(8,128)(2,1)S(1)} %copy-done.62), custom_call_target="tpu_custom_call" | custom-call | flops 650000000 | bytes 130000 | tf_op jit(solution)/shard_map/weight_grad/pallas_call | solution.py:872
  220.6 10.5 %weight_grad.4 = (bf16[2,160,1280]{2,1,0:T(8,128)(2,1)S(1)}, bf16[2,160,1280]{2,1,0:T(8,128)(2,1)S(1)}, bf16[4,160,1280]{2,1,0:T(8,128)(2,1)S(1)}) custom-call(s32[8]{0:T(128)S(1)} %stack.131.targets, bf16[832,1280]{1,0:T(8,128)(2,1)S(1)} %copy-done.66, bf16[832,1280]{1,0:T(8,128)(2,1)S(1)} %copy-done.65, bf16[832,1280]{1,0:T(8,128)(2,1)S(1)} %copy-done.68, ...), custom_call_target="tpu_custom_call" | custom-call | flops 650000000 | bytes 130000 | tf_op jit(solution)/shard_map/weight_grad/pallas_call | solution.py:872
  234.1 2.6 norm_two_back.3
  240.2 14.0 %attend_back.2 = (bf16[832,960]{1,0:T(8,128)(2,1)S(1)}, bf16[832,1280]{1,0:T(8,128)(2,1)S(1)}, f32[256,384]{1,0:T(8,128)S(1)}, f32[1,960]{1,0:T(1,128)S(1)}, f32...) custom-call(bf16[208,1280]{1,0:T(8,128)(2,1)} %get-tuple-element.344.refs_0_, ...), custom_call_target="tpu_custom_call" | custom-call | flops 925000000 | bytes 185000 | tf_op jit(solution)/shard_map/attend_back/pallas_call | solution.py:578
  254.4 2.7 collective-permute-done.36.refs_1_
  262.2 13.8 %attend_back.3 = (bf16[832,960]{1,0:T(8,128)(2,1)S(1)}, bf16[832,1280]{1,0:T(8,128)(2,1)S(1)}, f32[256,384]{1,0:T(8,128)S(1)}, f32[1,960]{1,0:T(1,128)S(1)}, f32...) custom-call(bf16[208,1280]{1,0:T(8,128)(2,1)S(1)} %get-tuple-element.367.refs_0_, ...), custom_call_target="tpu_custom_call" | custom-call | flops 925000000 | bytes 185000 | tf_op jit(solution)/shard_map/attend_back/pallas_call | solution.py:578
  281.2 3.3 collective-permute-done.40.refs_4_.refs_7_
  285.5 9.9 %collective-permute-done.37.refs_2_ = bf16[208,1280]{1,0:T(8,128)(2,1)S(1)} collective-permute-done((bf16[208,1280]{1,0:T(8,128)(2,1)S(1)}, bf16[208,1280]{1,0:T(8,128)(2,1)S(1)}, u32[]{:S(2)}, u32[]{:S(2)}) %collective-permute-start.37) | collective-permute-done | bytes 532512 | tf_op jit(solution)/shard_map/ppermute | solution.py:1405
  301.9 1.8 copy-done.14
  312.3 3.3 combine.15
  315.6 2.3 collective-permute-start.46
  326.5 10.7 %weight_grad.5 = (bf16[2,160,896]{2,1,0:T(8,128)(2,1)S(1)}, bf16[2,160,896]{2,1,0:T(8,128)(2,1)S(1)}, bf16[4,160,896]{2,1,0:T(8,128)(2,1)S(1)}, bf16[4,2,160,384]{3,2,1,0:T(8,128)(2,1)S(1)}) custom-call(s32[8]{0:T(128)S(1)} %copy-done.103, bf16[1664,1280]{1,0:T(8,128)(2,1)S(1)} %bitcast.86, bf16[832,960]{1,0:T(8,128)(2,1)S(1)} %copy-done.77, ...), custom_call_target="tpu_custom_call" | custom-call | flops 650000000 | bytes 130000 | tf_op jit(solution)/shard_map/weight_grad/pallas_call | solution.py:872
  340.9 3.0 norm_one_back.1.refs_0_
  347.1 11.6 %collective-permute-done.51 = f32[160,128]{1,0:T(8,128)S(1)} collective-permute-done((f32[160,128]{1,0:T(8,128)S(1)}, f32[160,128]{1,0:T(8,128)S(1)}, u32[]{:S(2)}, u32[]{:S(2)}) %collective-permute-start.51) | collective-permute-done | bytes 81952 | tf_op jit(solution)/shard_map/ppermute | solution.py:1479
  361.9 13.2 %collective-permute-done.48.refs_1_ = bf16[2,160,896]{2,1,0:T(8,128)(2,1)S(1)} collective-permute-done((bf16[2,160,896]{2,1,0:T(8,128)(2,1)S(1)}, bf16[2,160,896]{2,1,0:T(8,128)(2,1)S(1)}, u32[]{:S(2)}, u32[]{:S(2)}) %collective-permute-start.48) | collective-permute-done | bytes 573472 | tf_op jit(solution)/shard_map/ppermute | solution.py:1492
  375.0 12.2 %collective-permute-done.53 = f32[160,128]{1,0:T(8,128)S(1)} collective-permute-done((f32[160,128]{1,0:T(8,128)S(1)}, f32[160,128]{1,0:T(8,128)S(1)}, u32[]{:S(2)}, u32[]{:S(2)}) %collective-permute-start.53) | collective-permute-done | bytes 81952 | tf_op jit(solution)/shard_map/ppermute | solution.py:1515
  391.3 4.6 %place_windows.1 = f32[1568,1280]{1,0:T(8,128)} custom-call(s32[4]{0:T(128)S(1)} %pad_add_fusion.1.order, bf16[416,1280]{1,0:T(8,128)(2,1)S(1)} %norm_one_back.1.refs_0_, bf16[416,1280]{1,0:T(8,128)(2,1)S(1)} %collective-permute-done.55.refs_1_, bf16[416,1280]{1,0:T(8,128)(2,1)S(1)} %collective-permute-done.61.refs_2_, ...), custom_call_target="tpu_custom_call" | custom-call | flops 350000000 | bytes 70000 | tf_op jit(solution)/shard_map/place_windows/pallas_call | solution.py:948
  395.8 8.9 %collective-permute-done.59.refs_2_.refs_4_ = bf16[160,1664]{1,0:T(8,128)(2,1)S(1)} collective-permute-done((bf16[160,1664]{1,0:T(8,128)(2,1)S(1)}, bf16[160,1664]{1,0:T(8,128)(2,1)S(1)}, u32[]{:S(2)}, u32[]{:S(2)}) %collective-permute-start.59) | collective-permute-done | bytes 532512 | tf_op jit(solution)/shard_map/ppermute | solution.py:1536
  408.5 6.3 %collective-permute-done.56.refs_1_ = bf16[416,1280]{1,0:T(8,128)(2,1)} collective-permute-done((bf16[416,1280]{1,0:T(8,128)(2,1)}, bf16[416,1280]{1,0:T(8,128)(2,1)}, u32[]{:S(2)}, u32[]{:S(2)}) %collective-permute-start.56) | collective-permute-done | bytes 1064992 | tf_op jit(solution)/shard_map/ppermute | solution.py:1538
  420.0 4.8 %write_output.1 = bf16[1568,1280]{1,0:T(8,128)(2,1)} custom-call(s32[4]{0:T(128)S(1)} %pad_add_fusion.1.order, s32[8]{0:T(128)S(1)} %copy-done.109, s32[8]{0:T(128)S(1)} %copy-done.111, bf16[416,1280]{1,0:T(8,128)(2,1)} %get-tuple-element.430.refs_0_, bf16[416,1280]{1,0:T(8,128)(2,1)} %collective-permute-done.56.refs_1_, ...), custom_call_target="tpu_custom_call" | custom-call | flops 350000000 | bytes 70000 | tf_op jit(solution)/shard_map/write_output/pallas_call | solution.py:983
  (469 shorter events, 117.7 us)
Async XLA Ops:
  2.9 15.6 %collective-permute-start = (bf16[160,1344]{1,0:T(8,128)(2,1)S(1)}, bf16[160,1344]{1,0:T(8,128)(2,1)}, u32[]{:S(2)}, u32[]{:S(2)}) collective-permute-start(bf16[160,1344]{1,0:T(8,128)(2,1)S(1)} %concatenate.15.refs_0_), channel_id=1, source_target_pairs={{0,8},{4,12},{8,16},{12,20},{16,24},{20,28},{24,0},{28,4},{1,9},{5... | collective-permute-start | bytes 1290248 | tf_op jit(solution)/shard_map/ppermute | solution.py:1291
  5.9 12.5 %collective-permute-start.1 = (bf16[160,1344]{1,0:T(8,128)(2,1)S(1)}, bf16[160,1344]{1,0:T(8,128)(2,1)S(1)}, u32[]{:S(2)}, u32[]{:S(2)}) collective-permute-start(bf16[160,1344]{1,0:T(8,128)(2,1)S(1)} %concatenate.15.refs_0_), channel_id=1, source_target_pairs={{0,4},{4,0},{8,12},{12,8},{16,20},{20,16},{24,28},{28,24},{1,5},{5... | collective-permute-start | bytes 1290248 | tf_op jit(solution)/shard_map/ppermute | solution.py:1291
  19.2 13.6 %collective-permute-start.2 = (bf16[160,1344]{1,0:T(8,128)(2,1)}, bf16[160,1344]{1,0:T(8,128)(2,1)}, u32[]{:S(2)}, u32[]{:S(2)}) collective-permute-start(bf16[160,1344]{1,0:T(8,128)(2,1)} %collective-permute-done.refs_2_), channel_id=1, source_target_pairs={{0,8},{4,12},{8,16},{12,20},{16,24},{20,28},{24,0},{28,4},{1,9},{5... | collective-permute-start | bytes 1290248 | tf_op jit(solution)/shard_map/ppermute | solution.py:1295
  20.1 12.7 %collective-permute-start.3 = (bf16[160,1344]{1,0:T(8,128)(2,1)}, bf16[160,1344]{1,0:T(8,128)(2,1)}, u32[]{:S(2)}, u32[]{:S(2)}) collective-permute-start(bf16[160,1344]{1,0:T(8,128)(2,1)} %collective-permute-done.refs_2_), channel_id=1, source_target_pairs={{0,4},{4,0},{8,12},{12,8},{16,20},{20,16},{24,28},{28,24},{1,5},{5... | collective-permute-start | bytes 1290248 | tf_op jit(solution)/shard_map/ppermute | solution.py:1295
  32.8 12.7 %collective-permute-start.4 = (bf16[160,1344]{1,0:T(8,128)(2,1)}, bf16[160,1344]{1,0:T(8,128)(2,1)}, u32[]{:S(2)}, u32[]{:S(2)}) collective-permute-start(bf16[160,1344]{1,0:T(8,128)(2,1)} %collective-permute-done.2.refs_4_), channel_id=1, source_target_pairs={{0,8},{4,12},{8,16},{12,20},{16,24},{20,28},{24,0},{28,4},{1,9},{5... | collective-permute-start | bytes 1290248 | tf_op jit(solution)/shard_map/ppermute | solution.py:1300
  32.8 12.7 %collective-permute-start.5 = (bf16[160,1344]{1,0:T(8,128)(2,1)}, bf16[160,1344]{1,0:T(8,128)(2,1)}, u32[]{:S(2)}, u32[]{:S(2)}) collective-permute-start(bf16[160,1344]{1,0:T(8,128)(2,1)} %collective-permute-done.2.refs_4_), channel_id=1, source_target_pairs={{0,4},{4,0},{8,12},{12,8},{16,20},{20,16},{24,28},{28,24},{1,5},{5... | collective-permute-start | bytes 1290248 | tf_op jit(solution)/shard_map/ppermute | solution.py:1300
  46.6 24.3 %collective-permute-start.6 = (bf16[160,2560]{1,0:T(8,128)(2,1)S(1)}, bf16[160,2560]{1,0:T(8,128)(2,1)}, u32[]{:S(2)}, u32[]{:S(2)}) collective-permute-start(bf16[160,2560]{1,0:T(8,128)(2,1)S(1)} %pad_maximum_fusion.refs_4_), channel_id=1, source_target_pairs={{0,8},{4,12},{8,16},{12,20},{16,24},{20,28},{24,0},{28,4},{1,9},{5... | collective-permute-start | bytes 2457608 | tf_op jit(solution)/shard_map/ppermute | solution.py:1305
  56.3 17.1 %collective-permute-start.8 = (bf16[160,2560]{1,0:T(8,128)(2,1)S(1)}, bf16[160,2560]{1,0:T(8,128)(2,1)S(1)}, u32[]{:S(2)}, u32[]{:S(2)}) collective-permute-start(bf16[160,2560]{1,0:T(8,128)(2,1)S(1)} %pad_maximum_fusion.refs_4_), channel_id=1, source_target_pairs={{0,4},{4,0},{8,12},{12,8},{16,20},{20,16},{24,28},{28,24},{1,5},{5... | collective-permute-start | bytes 2457608 | tf_op jit(solution)/shard_map/ppermute | solution.py:1310
  74.3 16.3 %collective-permute-start.10 = (bf16[160,2560]{1,0:T(8,128)(2,1)}, bf16[160,2560]{1,0:T(8,128)(2,1)S(1)}, u32[]{:S(2)}, u32[]{:S(2)}) collective-permute-start(bf16[160,2560]{1,0:T(8,128)(2,1)} %collective-permute-done.6.refs_6_), channel_id=1, source_target_pairs={{0,4},{4,0},{8,12},{12,8},{16,20},{20,16},{24,28},{28,24},{1,5},{5... | collective-permute-start | bytes 2457608 | tf_op jit(solution)/shard_map/ppermute | solution.py:1315
  75.1 17.4 %collective-permute-start.9 = (bf16[160,2560]{1,0:T(8,128)(2,1)}, bf16[160,2560]{1,0:T(8,128)(2,1)S(1)}, u32[]{:S(2)}, u32[]{:S(2)}) collective-permute-start(bf16[160,2560]{1,0:T(8,128)(2,1)} %collective-permute-done.6.refs_6_), channel_id=1, source_target_pairs={{0,8},{4,12},{8,16},{12,20},{16,24},{20,28},{24,0},{28,4},{1,9},{5... | collective-permute-start | bytes 2457608 | tf_op jit(solution)/shard_map/ppermute | solution.py:1315
  92.5 22.6 %collective-permute-start.11 = (bf16[160,2560]{1,0:T(8,128)(2,1)S(1)}, bf16[160,2560]{1,0:T(8,128)(2,1)S(1)}, u32[]{:S(2)}, u32[]{:S(2)}) collective-permute-start(bf16[160,2560]{1,0:T(8,128)(2,1)S(1)} %collective-permute-done.9.refs_8_), channel_id=1, source_target_pairs={{0,8},{4,12},{8,16},{12,20},{16,24},{20,28},{24,0},{28,4},{1,9},{5... | collective-permute-start | bytes 2457608 | tf_op jit(solution)/shard_map/ppermute | solution.py:1318
  92.7 22.4 %collective-permute-start.12 = (bf16[160,2560]{1,0:T(8,128)(2,1)S(1)}, bf16[160,2560]{1,0:T(8,128)(2,1)S(1)}, u32[]{:S(2)}, u32[]{:S(2)}) collective-permute-start(bf16[160,2560]{1,0:T(8,128)(2,1)S(1)} %collective-permute-done.9.refs_8_), channel_id=1, source_target_pairs={{0,4},{4,0},{8,12},{12,8},{16,20},{20,16},{24,28},{28,24},{1,5},{5... | collective-permute-start | bytes 2457608 | tf_op jit(solution)/shard_map/ppermute | solution.py:1318
  95.3 19.8 %collective-permute-start.14 = (bf16[208,1280]{1,0:T(8,128)(2,1)S(1)}, bf16[208,1280]{1,0:T(8,128)(2,1)S(1)}, u32[]{:S(2)}, u32[]{:S(2)}) collective-permute-start(bf16[208,1280]{1,0:T(8,128)(2,1)S(1)} %combine.10), channel_id=1, source_target_pairs={{0,2},{1,3},{2,0},{3,1},{4,6},{5,7},{6,4},{7,5},{8,10},{9,11},{10,... | collective-permute-start | bytes 1597448 | tf_op jit(solution)/shard_map/ppermute | solution.py:1321
  115.2 20.7 %collective-permute-start.15 = (bf16[160,2560]{1,0:T(8,128)(2,1)S(1)}, bf16[160,2560]{1,0:T(8,128)(2,1)S(1)}, u32[]{:S(2)}, u32[]{:S(2)}) collective-permute-start(bf16[160,2560]{1,0:T(8,128)(2,1)S(1)} %collective-permute-done.11.refs_10_), channel_id=1, source_target_pairs={{0,4},{4,0},{8,12},{12,8},{16,20},{20,16},{24,28},{28,24},{1,5},{5... | collective-permute-start | bytes 2457608 | tf_op jit(solution)/shard_map/ppermute | solution.py:1324
  118.0 15.0 %collective-permute-start.18 = (bf16[208,1280]{1,0:T(8,128)(2,1)S(1)}, bf16[208,1280]{1,0:T(8,128)(2,1)S(1)}, u32[]{:S(2)}, u32[]{:S(2)}) collective-permute-start(bf16[208,1280]{1,0:T(8,128)(2,1)S(1)} %combine.11), channel_id=1, source_target_pairs={{0,2},{1,3},{2,0},{3,1},{4,6},{5,7},{6,4},{7,5},{8,10},{9,11},{10,... | collective-permute-start | bytes 1597448 | tf_op jit(solution)/shard_map/ppermute | solution.py:1327
  120.7 23.0 %collective-permute-start.17 = (bf16[208,1280]{1,0:T(8,128)(2,1)}, bf16[208,1280]{1,0:T(8,128)(2,1)}, u32[]{:S(2)}, u32[]{:S(2)}) collective-permute-start(bf16[208,1280]{1,0:T(8,128)(2,1)} %get-tuple-element.280.refs_0_), channel_id=1, source_target_pairs={{0,2},{1,3},{2,0},{3,1},{4,6},{5,7},{6,4},{7,5},{8,10},{9,11},{10,... | collective-permute-start | bytes 1597448 | tf_op jit(solution)/shard_map/ppermute | solution.py:1329
  121.5 24.2 %collective-permute-start.20 = (bf16[208,1280]{1,0:T(8,128)(2,1)}, bf16[208,1280]{1,0:T(8,128)(2,1)}, u32[]{:S(2)}, u32[]{:S(2)}) collective-permute-start(bf16[208,1280]{1,0:T(8,128)(2,1)} %get-tuple-element.280.refs_0_), channel_id=1, source_target_pairs={{0,1},{1,0},{2,3},{3,2},{4,5},{5,4},{6,7},{7,6},{8,9},{9,8},{10,11... | collective-permute-start | bytes 1597448 | tf_op jit(solution)/shard_map/ppermute | solution.py:1284
  143.8 25.2 %collective-permute-start.19 = (bf16[208,1280]{1,0:T(8,128)(2,1)S(1)}, bf16[208,1280]{1,0:T(8,128)(2,1)}, u32[]{:S(2)}, u32[]{:S(2)}) collective-permute-start(bf16[208,1280]{1,0:T(8,128)(2,1)S(1)} %get-tuple-element.303.refs_0_), channel_id=1, source_target_pairs={{0,2},{1,3},{2,0},{3,1},{4,6},{5,7},{6,4},{7,5},{8,10},{9,11},{10,... | collective-permute-start | bytes 1597448 | tf_op jit(solution)/shard_map/ppermute | solution.py:1334
  169.1 26.2 %collective-permute-start.24 = (bf16[416,1280]{1,0:T(8,128)(2,1)}, bf16[416,1280]{1,0:T(8,128)(2,1)S(1)}, u32[]{:S(2)}, u32[]{:S(2)}) collective-permute-start(bf16[416,1280]{1,0:T(8,128)(2,1)} %get-tuple-element.302), channel_id=1, source_target_pairs={{0,1},{1,0},{2,3},{3,2},{4,5},{5,4},{6,7},{7,6},{8,9},{9,8},{10,11... | collective-permute-start | bytes 3194888 | tf_op jit(solution)/shard_map/ppermute | solution.py:1340
  173.2 22.1 %collective-permute-start.23 = (bf16[208,1280]{1,0:T(8,128)(2,1)S(1)}, bf16[208,1280]{1,0:T(8,128)(2,1)S(1)}, u32[]{:S(2)}, u32[]{:S(2)}) collective-permute-start(bf16[208,1280]{1,0:T(8,128)(2,1)S(1)} %combine.12), channel_id=1, source_target_pairs={{0,2},{1,3},{2,0},{3,1},{4,6},{5,7},{6,4},{7,5},{8,10},{9,11},{10,... | collective-permute-start | bytes 1597448 | tf_op jit(solution)/shard_map/ppermute | solution.py:1342
  198.9 19.5 %collective-permute-start.28 = (bf16[208,1280]{1,0:T(8,128)(2,1)}, bf16[208,1280]{1,0:T(8,128)(2,1)}, u32[]{:S(2)}, u32[]{:S(2)}) collective-permute-start(bf16[208,1280]{1,0:T(8,128)(2,1)} %get-tuple-element.344.refs_0_), channel_id=1, source_target_pairs={{0,2},{1,3},{2,0},{3,1},{4,6},{5,7},{6,4},{7,5},{8,10},{9,11},{10,... | collective-permute-start | bytes 1597448 | tf_op jit(solution)/shard_map/ppermute | solution.py:1349
  200.2 31.8 %collective-permute-start.31 = (bf16[208,1280]{1,0:T(8,128)(2,1)}, bf16[208,1280]{1,0:T(8,128)(2,1)S(1)}, u32[]{:S(2)}, u32[]{:S(2)}) collective-permute-start(bf16[208,1280]{1,0:T(8,128)(2,1)} %get-tuple-element.344.refs_0_), channel_id=1, source_target_pairs={{0,1},{1,0},{2,3},{3,2},{4,5},{5,4},{6,7},{7,6},{8,9},{9,8},{10,11... | collective-permute-start | bytes 1597448 | tf_op jit(solution)/shard_map/ppermute | solution.py:1284
  218.4 14.8 %collective-permute-start.30 = (bf16[208,1280]{1,0:T(8,128)(2,1)}, bf16[208,1280]{1,0:T(8,128)(2,1)S(1)}, u32[]{:S(2)}, u32[]{:S(2)}) collective-permute-start(bf16[208,1280]{1,0:T(8,128)(2,1)} %get-tuple-element.330), channel_id=1, source_target_pairs={{0,2},{1,3},{2,0},{3,1},{4,6},{5,7},{6,4},{7,5},{8,10},{9,11},{10,... | collective-permute-start | bytes 1597448 | tf_op jit(solution)/shard_map/ppermute | solution.py:1360
  219.4 13.8 %collective-permute-start.32 = (bf16[208,1280]{1,0:T(8,128)(2,1)}, bf16[208,1280]{1,0:T(8,128)(2,1)S(1)}, u32[]{:S(2)}, u32[]{:S(2)}) collective-permute-start(bf16[208,1280]{1,0:T(8,128)(2,1)} %collective-permute-done.28.refs_1_), channel_id=1, source_target_pairs={{0,1},{1,0},{2,3},{3,2},{4,5},{5,4},{6,7},{7,6},{8,9},{9,8},{10,11... | collective-permute-start | bytes 1597448 | tf_op jit(solution)/shard_map/ppermute | solution.py:1284
  220.5 33.8 %collective-permute-start.35 = (bf16[2,160,1280]{2,1,0:T(8,128)(2,1)}, bf16[2,160,1280]{2,1,0:T(8,128)(2,1)S(1)}, u32[]{:S(2)}, u32[]{:S(2)}) collective-permute-start(bf16[2,160,1280]{2,1,0:T(8,128)(2,1)} %slice_bitcast_fusion), channel_id=1, source_target_pairs={{0,8},{4,12},{8,16},{12,20},{16,24},{20,28},{24,0},{28,4},{1,9},{5... | collective-permute-start | bytes 2457608 | tf_op jit(solution)/shard_map/ppermute | solution.py:1369
  233.2 21.1 %collective-permute-start.34 = (bf16[2,160,1280]{2,1,0:T(8,128)(2,1)}, bf16[2,160,1280]{2,1,0:T(8,128)(2,1)S(1)}, u32[]{:S(2)}, u32[]{:S(2)}) collective-permute-start(bf16[2,160,1280]{2,1,0:T(8,128)(2,1)} %copy-done.118), channel_id=1, source_target_pairs={{0,4},{4,0},{8,12},{12,8},{16,20},{20,16},{24,28},{28,24},{1,5},{5... | collective-permute-start | bytes 2457608 | tf_op jit(solution)/shard_map/ppermute | solution.py:1368
  237.8 16.5 %collective-permute-start.33 = (bf16[208,1280]{1,0:T(8,128)(2,1)S(1)}, bf16[208,1280]{1,0:T(8,128)(2,1)S(1)}, u32[]{:S(2)}, u32[]{:S(2)}) collective-permute-start(bf16[208,1280]{1,0:T(8,128)(2,1)S(1)} %get-tuple-element.367.refs_0_), channel_id=1, source_target_pairs={{0,2},{1,3},{2,0},{3,1},{4,6},{5,7},{6,4},{7,5},{8,10},{9,11},{10,... | collective-permute-start | bytes 1597448 | tf_op jit(solution)/shard_map/ppermute | solution.py:1372
  258.1 38.1 %collective-permute-start.38 = (bf16[160,3840]{1,0:T(8,128)(2,1)S(1)}, bf16[160,3840]{1,0:T(8,128)(2,1)S(1)}, u32[]{:S(2)}, u32[]{:S(2)}) collective-permute-start(bf16[160,3840]{1,0:T(8,128)(2,1)S(1)} %get-tuple-element.364), channel_id=1, source_target_pairs={{0,8},{4,12},{8,16},{12,20},{16,24},{20,28},{24,0},{28,4},{1,9},{5... | collective-permute-start | bytes 3686408 | tf_op jit(solution)/shard_map/ppermute | solution.py:1406
  258.2 26.3 %collective-permute-start.40 = (bf16[416,1280]{1,0:T(8,128)(2,1)S(1)}, bf16[416,1280]{1,0:T(8,128)(2,1)S(1)}, u32[]{:S(2)}, u32[]{:S(2)}) collective-permute-start(bf16[416,1280]{1,0:T(8,128)(2,1)S(1)} %copy-done.117), channel_id=1, source_target_pairs={{0,2},{1,3},{2,0},{3,1},{4,6},{5,7},{6,4},{7,5},{8,10},{9,11},{10,... | collective-permute-start | bytes 3194888 | tf_op jit(solution)/shard_map/ppermute | solution.py:1378
  259.3 21.0 %collective-permute-start.39 = (bf16[2,160,1280]{2,1,0:T(8,128)(2,1)S(1)}, bf16[2,160,1280]{2,1,0:T(8,128)(2,1)S(1)}, u32[]{:S(2)}, u32[]{:S(2)}) collective-permute-start(bf16[2,160,1280]{2,1,0:T(8,128)(2,1)S(1)} %get-tuple-element.365), channel_id=1, source_target_pairs={{0,4},{4,0},{8,12},{12,8},{16,20},{20,16},{24,28},{28,24},{1,5},{5... | collective-permute-start | bytes 2457608 | tf_op jit(solution)/shard_map/ppermute | solution.py:1381
  260.3 35.1 %collective-permute-start.37 = (bf16[208,1280]{1,0:T(8,128)(2,1)S(1)}, bf16[208,1280]{1,0:T(8,128)(2,1)S(1)}, u32[]{:S(2)}, u32[]{:S(2)}) collective-permute-start(bf16[208,1280]{1,0:T(8,128)(2,1)S(1)} %get-tuple-element.363), channel_id=1, source_target_pairs={{0,2},{1,3},{2,0},{3,1},{4,6},{5,7},{6,4},{7,5},{8,10},{9,11},{10,... | collective-permute-start | bytes 1597448 | tf_op jit(solution)/shard_map/ppermute | solution.py:1405
  315.6 22.8 %collective-permute-start.46 = (bf16[160,2560]{1,0:T(8,128)(2,1)}, bf16[160,2560]{1,0:T(8,128)(2,1)S(1)}, u32[]{:S(2)}, u32[]{:S(2)}) collective-permute-start(bf16[160,2560]{1,0:T(8,128)(2,1)} %get-tuple-element.395), channel_id=1, source_target_pairs={{0,8},{4,12},{8,16},{12,20},{16,24},{20,28},{24,0},{28,4},{1,9},{5... | collective-permute-start | bytes 2457608 | tf_op jit(solution)/shard_map/ppermute | solution.py:1451
  317.8 19.5 %collective-permute-start.45 = (bf16[208,1280]{1,0:T(8,128)(2,1)}, bf16[208,1280]{1,0:T(8,128)(2,1)S(1)}, u32[]{:S(2)}, u32[]{:S(2)}) collective-permute-start(bf16[208,1280]{1,0:T(8,128)(2,1)} %get-tuple-element.394), channel_id=1, source_target_pairs={{0,2},{1,3},{2,0},{3,1},{4,6},{5,7},{6,4},{7,5},{8,10},{9,11},{10,... | collective-permute-start | bytes 1597448 | tf_op jit(solution)/shard_map/ppermute | solution.py:1450
  318.7 18.6 %collective-permute-start.47 = (f32[160,128]{1,0:T(8,128)}, f32[160,128]{1,0:T(8,128)S(1)}, u32[]{:S(2)}, u32[]{:S(2)}) collective-permute-start(f32[160,128]{1,0:T(8,128)} %add.278), channel_id=1, source_target_pairs={{0,2},{1,3},{2,0},{3,1},{4,6},{5,7},{6,4},{7,5},{8,10},{9,11},{10,... | collective-permute-start | bytes 245768 | tf_op jit(solution)/shard_map/ppermute | solution.py:1418
  338.4 20.2 %collective-permute-start.50 = (bf16[160,2048]{1,0:T(8,128)(2,1)S(1)}, bf16[160,2048]{1,0:T(8,128)(2,1)S(1)}, u32[]{:S(2)}, u32[]{:S(2)}) collective-permute-start(bf16[160,2048]{1,0:T(8,128)(2,1)S(1)} %combine.16), channel_id=1, source_target_pairs={{0,8},{4,12},{8,16},{12,20},{16,24},{20,28},{24,0},{28,4},{1,9},{5... | collective-permute-start | bytes 1966088 | tf_op jit(solution)/shard_map/ppermute | solution.py:1478
  339.9 18.8 %collective-permute-start.49 = (bf16[2,160,896]{2,1,0:T(8,128)(2,1)S(1)}, bf16[2,160,896]{2,1,0:T(8,128)(2,1)S(1)}, u32[]{:S(2)}, u32[]{:S(2)}) collective-permute-start(bf16[2,160,896]{2,1,0:T(8,128)(2,1)S(1)} %get-tuple-element.411), channel_id=1, source_target_pairs={{0,4},{4,0},{8,12},{12,8},{16,20},{20,16},{24,28},{28,24},{1,5},{5... | collective-permute-start | bytes 1720328 | tf_op jit(solution)/shard_map/ppermute | solution.py:1471
  343.9 43.4 %collective-permute-start.55 = (bf16[416,1280]{1,0:T(8,128)(2,1)S(1)}, bf16[416,1280]{1,0:T(8,128)(2,1)S(1)}, u32[]{:S(2)}, u32[]{:S(2)}) collective-permute-start(bf16[416,1280]{1,0:T(8,128)(2,1)S(1)} %norm_one_back.1.refs_0_), channel_id=1, source_target_pairs={{0,2},{1,3},{2,0},{3,1},{4,6},{5,7},{6,4},{7,5},{8,10},{9,11},{10,... | collective-permute-start | bytes 3194888 | tf_op jit(solution)/shard_map/ppermute | solution.py:1489
  345.9 12.8 %collective-permute-start.51 = (f32[160,128]{1,0:T(8,128)S(1)}, f32[160,128]{1,0:T(8,128)S(1)}, u32[]{:S(2)}, u32[]{:S(2)}) collective-permute-start(f32[160,128]{1,0:T(8,128)S(1)} %add.279), channel_id=1, source_target_pairs={{0,8},{4,12},{8,0},{12,4},{16,24},{20,28},{24,16},{28,20},{1,9},{5... | collective-permute-start | bytes 245768 | tf_op jit(solution)/shard_map/ppermute | solution.py:1479
  359.1 28.2 %collective-permute-start.52 = (bf16[160,2944]{1,0:T(8,128)(2,1)S(1)}, bf16[160,2944]{1,0:T(8,128)(2,1)S(1)}, u32[]{:S(2)}, u32[]{:S(2)}) collective-permute-start(bf16[160,2944]{1,0:T(8,128)(2,1)S(1)} %get-tuple-element.426), channel_id=1, source_target_pairs={{0,8},{4,12},{8,16},{12,20},{16,24},{20,28},{24,0},{28,4},{1,9},{5... | collective-permute-start | bytes 2826248 | tf_op jit(solution)/shard_map/ppermute | solution.py:1513
  359.1 15.9 %collective-permute-start.48 = (bf16[2,160,896]{2,1,0:T(8,128)(2,1)S(1)}, bf16[2,160,896]{2,1,0:T(8,128)(2,1)S(1)}, u32[]{:S(2)}, u32[]{:S(2)}) collective-permute-start(bf16[2,160,896]{2,1,0:T(8,128)(2,1)S(1)} %get-tuple-element.409), channel_id=1, source_target_pairs={{0,4},{4,0},{8,12},{12,8},{16,20},{20,16},{24,28},{28,24},{1,5},{5... | collective-permute-start | bytes 1720328 | tf_op jit(solution)/shard_map/ppermute | solution.py:1492
  360.3 27.0 %collective-permute-start.54 = (bf16[160,1280]{1,0:T(8,128)(2,1)S(1)}, bf16[160,1280]{1,0:T(8,128)(2,1)S(1)}, u32[]{:S(2)}, u32[]{:S(2)}) collective-permute-start(bf16[160,1280]{1,0:T(8,128)(2,1)S(1)} %get-tuple-element.428), channel_id=1, source_target_pairs={{0,4},{4,0},{8,12},{12,8},{16,20},{20,16},{24,28},{28,24},{1,5},{5... | collective-permute-start | bytes 1228808 | tf_op jit(solution)/shard_map/ppermute | solution.py:1514
  361.2 26.0 %collective-permute-start.53 = (f32[160,128]{1,0:T(8,128)S(1)}, f32[160,128]{1,0:T(8,128)S(1)}, u32[]{:S(2)}, u32[]{:S(2)}) collective-permute-start(f32[160,128]{1,0:T(8,128)S(1)} %add.280), channel_id=1, source_target_pairs={{0,16},{4,20},{8,24},{12,28},{16,0},{20,4},{24,8},{28,12},{1,17},{... | collective-permute-start | bytes 245768 | tf_op jit(solution)/shard_map/ppermute | solution.py:1515
  375.0 16.2 %collective-permute-start.61 = (bf16[416,1280]{1,0:T(8,128)(2,1)S(1)}, bf16[416,1280]{1,0:T(8,128)(2,1)S(1)}, u32[]{:S(2)}, u32[]{:S(2)}) collective-permute-start(bf16[416,1280]{1,0:T(8,128)(2,1)S(1)} %norm_one_back.1.refs_0_), channel_id=1, source_target_pairs={{0,1},{1,0},{2,3},{3,2},{4,5},{5,4},{6,7},{7,6},{8,9},{9,8},{10,11... | collective-permute-start | bytes 3194888 | tf_op jit(solution)/shard_map/ppermute | solution.py:1284
  388.7 16.1 %collective-permute-start.59 = (bf16[160,1664]{1,0:T(8,128)(2,1)S(1)}, bf16[160,1664]{1,0:T(8,128)(2,1)S(1)}, u32[]{:S(2)}, u32[]{:S(2)}) collective-permute-start(bf16[160,1664]{1,0:T(8,128)(2,1)S(1)} %combine.18), channel_id=1, source_target_pairs={{0,8},{4,12},{8,16},{12,20},{16,24},{20,28},{24,0},{28,4},{1,9},{5... | collective-permute-start | bytes 1597448 | tf_op jit(solution)/shard_map/ppermute | solution.py:1536
  388.8 26.0 %collective-permute-start.56 = (bf16[416,1280]{1,0:T(8,128)(2,1)}, bf16[416,1280]{1,0:T(8,128)(2,1)}, u32[]{:S(2)}, u32[]{:S(2)}) collective-permute-start(bf16[416,1280]{1,0:T(8,128)(2,1)} %get-tuple-element.430.refs_0_), channel_id=1, source_target_pairs={{0,2},{1,3},{2,0},{3,1},{4,6},{5,7},{6,4},{7,5},{8,10},{9,11},{10,... | collective-permute-start | bytes 3194888 | tf_op jit(solution)/shard_map/ppermute | solution.py:1538
  391.3 28.7 %collective-permute-start.57 = (bf16[416,1280]{1,0:T(8,128)(2,1)}, bf16[416,1280]{1,0:T(8,128)(2,1)S(1)}, u32[]{:S(2)}, u32[]{:S(2)}) collective-permute-start(bf16[416,1280]{1,0:T(8,128)(2,1)} %get-tuple-element.430.refs_0_), channel_id=1, source_target_pairs={{0,1},{1,0},{2,3},{3,2},{4,5},{5,4},{6,7},{7,6},{8,9},{9,8},{10,11... | collective-permute-start | bytes 3194888 | tf_op jit(solution)/shard_map/ppermute | solution.py:1284
  405.6 10.4 %collective-permute-start.64 = (bf16[160,384]{1,0:T(8,128)(2,1)S(1)}, bf16[160,384]{1,0:T(8,128)(2,1)S(1)}, u32[]{:S(2)}, u32[]{:S(2)}) collective-permute-start(bf16[160,384]{1,0:T(8,128)(2,1)S(1)} %get-tuple-element.440), channel_id=1, source_target_pairs={{0,4},{4,0},{8,12},{12,8},{16,20},{20,16},{24,28},{28,24},{1,5},{5... | collective-permute-start | bytes 368648 | tf_op jit(solution)/shard_map/ppermute | solution.py:1563
  406.6 10.5 %collective-permute-start.63 = (bf16[160,896]{1,0:T(8,128)(2,1)S(1)}, bf16[160,896]{1,0:T(8,128)(2,1)}, u32[]{:S(2)}, u32[]{:S(2)}) collective-permute-start(bf16[160,896]{1,0:T(8,128)(2,1)S(1)} %get-tuple-element.439), channel_id=1, source_target_pairs={{0,8},{4,12},{8,16},{12,20},{16,24},{20,28},{24,0},{28,4},{1,9},{5... | collective-permute-start | bytes 860168 | tf_op jit(solution)/shard_map/ppermute | solution.py:1564
  (160 other events, 1450.0 us)

commit v5 on v4

--- a/solution.py
+++ b/solution.py
@@ -131,7 +131,7 @@
             struct((count * ROWS, width), BF16),
             struct((count * ROWS, 1), F32),
         ],
-        compiler_params=params(12),
+        compiler_params=params(63),
         cost_estimate=cost(9),
         name="prepare",
     )(order, places, lives, x, gain, shift)
@@ -155,7 +155,7 @@
             out_specs=pl.BlockSpec((ROWS, width), lambda i, *_: (i, 0)),
         ),
         out_shape=struct((count * ROWS, width), BF16),
-        compiler_params=params(12),
+        compiler_params=params(63),
         cost_estimate=cost(6),
         name="mask_rows",
     )(order, places, lives, top)
@@ -753,13 +753,16 @@
     )(offsets, *pieces, *weight_pieces, after, top, bias, down_bias)
 
 
-def weight_grad_kernel(sizes, share, targets, *refs):
+SEND_PARTS = {2: ((2, 3), (0, 1)), 3: ((3,), (1, 2), (0,))}
+
+
+def weight_grad_kernel(sizes, share, sends, targets, *refs):
     count = 2 * sum(sizes)
     operands = refs[:count]
     outs, (result, sems) = refs[count:-2], refs[-2:]
-    high_ref, low_ref, keep_ref = outs[:3] if len(outs) > 1 else (None,) * 3
-    pair_ref = outs[-1] if len(outs) != 3 else None
-    lead = 0 if keep_ref is None else keep_ref.shape[2]
+    keep_ref = outs[sends] if sends else None
+    pair_ref = None if sends else outs[0]
+    lead = keep_ref.shape[2] if sends else 0
     step = pl.program_id(0)
     steps = pl.num_programs(0)
     chunk = operands[0].shape[1]
@@ -800,13 +803,11 @@
 
         if lead:
 
-            @pl.when(slot < 2)
-            def _():
-                copy(index, low_ref, slot).start()
-
-            @pl.when((slot >= 2) & (slot < 4))
-            def _():
-                copy(index, high_ref, slot - 2).start()
+            for out, slots in zip(outs, SEND_PARTS[sends]):
+
+                @pl.when((slot >= slots[0]) & (slot <= slots[-1]))
+                def _(out=out, slots=slots):
+                    copy(index, out, slot - slots[0]).start()
 
             @pl.when(slot >= 4)
             def _():
@@ -840,7 +841,7 @@
         first += span
 
 
-def weight_grad(targets, groups, share, lead=None):
+def weight_grad(targets, groups, share, sends=0):
     operands, specs = [], []
     chunk = 640 if targets is not None else 256
     total_cols = 0
@@ -865,12 +866,13 @@
         name="weight_grad",
             )(*operands)
         ]
-    lead = total_cols if lead is None else lead
-    shapes = [struct((count, share, lead), BF16) for count in (2, 2, 4)] if lead else []
-    if lead < total_cols:
-        shapes.append(struct((4, 2, share, total_cols - lead), BF16))
+    if sends:
+        counts = [len(slots) for slots in SEND_PARTS[sends]] + [4]
+        shapes = [struct((count, share, total_cols), BF16) for count in counts]
+    else:
+        shapes = [struct((4, 2, share, total_cols), BF16)]
     return pl.pallas_call(
-        partial(weight_grad_kernel, sizes, share),
+        partial(weight_grad_kernel, sizes, share, sends),
         grid_spec=pltpu.PrefetchScalarGridSpec(
             num_scalar_prefetch=1,
             grid=(width // chunk,),
@@ -1347,38 +1349,24 @@
         came1, out_came1 = over_core(m1[5]), over_core(m1[7])
         grad_after0, branch0, sums0 = second_back(0, after0, m0[4], came0, crossed0)
         across0 = over_y(branch0)
-        passed1, out_passed = combine(
+        passed1, out_passed0, out_passed1 = combine(
             (rows, [second(tie(m1[4], branch0), came1)]),
-            (
-                (2 * ROWS, width),
-                [second(m0[6], out_came0), second(m1[6], out_came1, ROWS)],
-            ),
+            (rows, [second(m0[6], out_came0)]),
+            (rows, [second(m1[6], out_came1)]),
         )
         left = tie(m0, passed1)
-        (down_pairs,) = weight_grad(targets, down_groups([left, m1]), share, 0)
+        (down_pairs,) = weight_grad(targets, down_groups([left, m1]), share)
         across0, passed1, down_pairs = sync(across0, passed1, down_pairs)
         crossed1 = over_y(passed1)
         branches0 = spread(branch0, across0)
         left = tie(m0, down_pairs)
-        up_high, up_low, up_keep = weight_grad(targets, up_groups([left, m1]), share)
+        up_high, up_low, up_keep = weight_grad(targets, up_groups([left, m1]), share, 2)
+        down_held = over_z(down_pairs[3])
         crossed1, branches0, up_high, up_low, up_keep = sync(
             crossed1, branches0, up_high, up_low, up_keep
         )
 
         up_came_high = over_x(up_high)
-        down_held = over_z(down_pairs[3])
-        grad_after1, branch1, sums1 = second_back(1, after1, m1[4], came1, crossed1)
-        sums_two = [sums0, sums1]
-        across1 = over_y(branch1)
-        branches0[0] = tie(branches0[0], branch1)
-        b0 = attention_back(0, branches0, q, k, v, a0[1], weights)
-        across1, up_came_high, down_held, b0, out_passed = sync(
-            across1, up_came_high, down_held, b0, out_passed
-        )
-        out_crossed = over_y(out_passed)
-        branches1 = spread(branch1, across1)
-        came0 = over_core(b0[6])
-        up_came_low = over_x(up_low)
 
         def down_cells(k, held, lane):
             return [
@@ -1386,28 +1374,34 @@
                 for half, (at, first) in enumerate(lane)
             ]
 
+        grad_after1, branch1, sums1 = second_back(1, after1, m1[4], came1, crossed1)
+        sums_two = [sums0, sums1]
+        across1 = over_y(branch1)
+        (down_held,) = combine(
+            (
+                (share, 2 * units),
+                down_cells(2, tie(down_held, branch1), [((0,), 0), ((1,), 0)]),
+            )
+        )
+        branches0[0] = tie(branches0[0], down_held)
+        down_held = over_z(down_held)
+        b0 = attention_back(0, branches0, q, k, v, a0[1], weights)
+        across1, up_came_high, down_held, b0 = sync(across1, up_came_high, down_held, b0)
+        branches1 = spread(branch1, across1)
+        came0 = over_core(b0[6])
+        up_came_low = over_x(up_low)
+
         passed0, held = combine(
             (rows, [second(b0[5], came0)]),
-            (
-                (share, 3 * units),
-                down_cells(2, down_held, [((0,), 0), ((1,), 0)])
-                + [
-                    (
-                        0,
-                        2 * units,
-                        share,
-                        units,
-                        [(up_keep, (3,), 0), (up_came_high, (1,), 0)],
-                    )
-                ],
-            ),
+            ((share, 2 * units), down_cells(1, down_held, [((0,), 0), ((0,), units)])),
         )
         crossed0 = over_y(passed0)
         held = over_z(held)
         branches1[0] = tie(branches1[0], passed0)
+        out_crossed0 = over_y(tie(out_passed0, passed0))
         b1 = attention_back(1, branches1, q, k, v, a1[1], weights)
-        crossed0, held, up_came_low, out_crossed, b1 = sync(
-            crossed0, held, up_came_low, out_crossed, b1
+        crossed0, held, up_came_low, out_crossed0, b1 = sync(
+            crossed0, held, up_came_low, out_crossed0, b1
         )
         backs = [b0, b1]
         came1 = over_core(b1[6])
@@ -1416,24 +1410,34 @@
         came1, vector_came, vector = sync(came1, vector_came, vector)
         vector = vector + vector_came
         vector_came = lax.ppermute(vector, "mp", [(m, m ^ 2) for m in range(4)])
-        passed1, out_own, down_held, up_held = combine(
-            (rows, [second(tie(b1[5], vector), came1)]),
+        vector_came, vector, held = sync(vector_came, vector, held)
+        vector = vector + vector_came
+        vector_came = lax.ppermute(vector, "dp", [(d, d ^ 2) for d in range(8)])
+        down_held = held
+        passed1, down_other, up_held = combine(
+            (rows, [second(b1[5], came1)]),
             (
-                (2 * ROWS, width),
-                [
-                    (
-                        part * ROWS,
-                        0,
-                        *rows,
-                        [(keep, (0,), 0), (came, (0,), 0), (out_crossed, (part,), 0)],
-                    )
-                    for part, (keep, came) in enumerate(((m0[6], out_came0), (m1[6], out_came1)))
-                ],
+                (share, units),
+                [(0, 0, share, units, [(down_pairs, (0, 1), 0), (down_held, (0,), units)])],
             ),
             (
-                (share, 2 * units),
-                down_cells(1, held, [((0,), 0), ((0,), units)]),
+                (share, units),
+                [(0, 0, share, units, [(up_keep, (3,), 0), (up_came_high, (1,), 0)])],
             ),
+        )
+        crossed1 = over_y(passed1)
+        up_held, down_other = over_z(up_held), over_x(down_other)
+        left = tie(b0, passed1)
+        out_crossed1 = over_y(tie(out_passed1, passed1))
+        firsts = weight_grad(targets, first_groups([left, b1], attended), share, 3)
+        crossed1, down_other, up_held, vector, vector_came, firsts = sync(
+            crossed1, down_other, up_held, vector, vector_came, firsts
+        )
+        first_three, first_two, first_last, first_keep = firsts
+        vector = vector + vector_came
+
+        came_three = over_x(first_three)
+        (up_sum,) = combine(
             (
                 (share, units),
                 [
@@ -1442,44 +1446,15 @@
                         0,
                         share,
                         units,
-                        [(up_keep, (2,), 0), (up_came_high, (0,), 0), (held, (0,), 2 * units)],
+                        [(up_keep, (2,), 0), (up_came_high, (0,), 0), (up_held, (0,), 0)],
                     )
                 ],
-            ),
-        )
-        crossed1 = over_y(passed1)
-        down_held = over_z(down_held)
-        left = tie(b0, passed1)
-        lead = 3 * cols // 128 * 128
-        rest = 4 * cols - lead
-        firsts = weight_grad(targets, first_groups([left, b1], attended), share, lead)
-        crossed1, down_held, up_held, vector, vector_came, firsts = sync(
-            crossed1, down_held, up_held, vector, vector_came, firsts
-        )
-        first_high, first_low, first_keep, first_pairs = firsts
-        vector = vector + vector_came
-
-        def pair_cells(k, lane, held=None, first=0):
-            cells = []
-            for half in range(2):
-                terms = [(first_pairs, (k, half), 0)]
-                if held is not None:
-                    terms.append((held, (0,), first + half * rest))
-                cells.append((0, lane + half * rest, share, rest, terms))
-            return cells
-
-        first_came_high = over_x(first_high)
-        (held_sum,) = combine(
-            (
-                (share, 2 * rest + units),
-                pair_cells(3, 0) + [(0, 2 * rest, share, units, [(up_held, (0,), 0)])],
             )
         )
-        held = over_z(held_sum)
-        vector_came = lax.ppermute(vector, "dp", [(d, d ^ 2) for d in range(8)])
+        held = over_z(up_sum)
         own = norm_one_back(
             [
-                ([(b0[5], 0), (came0, 0), (tie(crossed0, held_sum), 0)], grad_after0),
+                ([(b0[5], 0), (came0, 0), (tie(crossed0, up_sum), 0)], grad_after0),
                 ([(b1[5], 0), (came1, 0), (crossed1, 0)], grad_after1),
             ],
             rows_in,
@@ -1487,81 +1462,72 @@
             gain_one,
         )
         in_across = over_y(own)
-        first_came_high, held, vector_came, own = sync(first_came_high, held, vector_came, own)
-        vector = vector + vector_came
-        first_came_low = over_x(first_low)
-        held, down_other = combine(
+        (out_own,) = combine(
             (
-                (share, lead + 2 * rest + units),
-                [(0, 0, share, lead, [(first_keep, (3,), 0), (first_came_high, (1,), 0)])]
-                + pair_cells(2, lead, held, 0)
-                + [
+                (2 * ROWS, width),
+                [
                     (
+                        part * ROWS,
                         0,
-                        lead + 2 * rest,
-                        share,
-                        units,
-                        [(up_keep, (1,), 0), (up_came_low, (1,), 0), (held, (0,), 2 * rest)],
+                        *rows,
+                        [(keep, (0,), 0), (came, (0,), 0), (crossed, (0,), 0)],
+                    )
+                    for part, (keep, came, crossed) in enumerate(
+                        (
+                            (m0[6], out_came0, tie(out_crossed0, own)),
+                            (m1[6], out_came1, out_crossed1),
+                        )
                     )
                 ],
             ),
-            (
-                (share, units),
-                [(0, 0, share, units, [(down_pairs, (0, 1), 0), (down_held, (0,), units)])],
-            ),
-        )
-        held = over_z(held)
-        down_other = over_x(down_other)
-        vector_came = lax.ppermute(vector, "dp", [(d, d ^ 4) for d in range(8)])
-        first_came_low, held, vector_came, down_other, in_across, out_own = sync(
-            first_came_low, held, vector_came, down_other, in_across, out_own
-        )
-        vector = vector + vector_came
-        up_last = held[:, lead + 2 * rest :]
+        )
+        came_three, held, own, out_own, vector = sync(came_three, held, own, out_own, vector)
+        came_two = over_x(first_two)
         (held,) = combine(
             (
-                (share, lead + 2 * rest),
+                (share, 2 * units),
                 [
+                    (0, 0, share, units, [(first_keep, (3,), 0), (came_three, (0,), 0)]),
                     (
                         0,
-                        0,
+                        units,
                         share,
-                        lead,
-                        [(first_keep, (2,), 0), (first_came_high, (0,), 0), (held, (0,), 0)],
-                    )
-                ]
-                + pair_cells(1, lead, held, lead),
+                        units,
+                        [(up_keep, (1,), 0), (up_came_low, (1,), 0), (held, (0,), 0)],
+                    ),
+                ],
             ),
         )
+        held = over_z(held)
+        vector_came = lax.ppermute(vector, "dp", [(d, d ^ 4) for d in range(8)])
+        out_across = over_y(tie(out_own, own))
+        came_two, held, vector_came, in_across = sync(came_two, held, vector_came, in_across)
+        vector = vector + vector_came
+        up_last = held[:, units:]
+
+        def first_cell(k, held):
+            return (
+                0,
+                0,
+                share,
+                4 * cols,
+                [(first_keep, (k,), 0), (came_two, (k - 1,), 0), (held, (0,), 0)],
+            )
+
+        (held,) = combine(((share, 4 * cols), [first_cell(2, held)]))
         held = over_z(held)
         vector_came = lax.ppermute(vector, "dp", [(d, d ^ 1) for d in range(8)])
-        out_across = over_y(out_own)
         in_pieces = spread(own, in_across)
         input_grad = place_windows(local, in_pieces)
         held, vector_came, input_grad = sync(held, vector_came, input_grad)
+        vector = vector + vector_came
+        came_last = over_x(tie(first_last, held))
+        (held,) = combine(((share, 4 * cols), [first_cell(1, held)]))
+        vector = tie(vector, held)
+        held = over_z(held)
+        came_last, out_own, out_across = sync(came_last, out_own, out_across)
         out_pieces = spread(out_own, out_across)
         block_output = write_output(local, places_all, lives_all, out_pieces)
-        vector = vector + vector_came
-        first_held, pair_other = combine(
-            (
-                (share, lead),
-                [
-                    (
-                        0,
-                        0,
-                        share,
-                        lead,
-                        [(first_keep, (1,), 0), (first_came_low, (1,), 0), (held, (0,), 0)],
-                    )
-                ],
-            ),
-            (
-                (share, rest),
-                [(0, 0, share, rest, [(first_pairs, (0, 1), 0), (held, (0,), lead + rest)])],
-            ),
-        )
-        pair_other = over_x(pair_other)
-        first_held = over_z(first_held)
 
         def last(*values):
             out = values[0].astype(F32)
@@ -1571,13 +1537,7 @@
 
         down_grad = last(down_pairs[0, 0], down_held[:, :units], down_other)
         up_grad = last(up_keep[0], up_came_low[0], up_last)
-        first_grad = jnp.concatenate(
-            [
-                last(first_keep[0], first_came_low[0], first_held),
-                last(first_pairs[0, 0], held[:, lead : lead + rest], pair_other),
-            ],
-            axis=1,
-        )
+        first_grad = last(first_keep[0], came_last[0], held)
 
     shapes = [(2, width), (4, width), (up_bias.size,), (2, width), (RELN, HD), (RELN, HD)]
     outs, at = [], 0

time: 431 us -> 407 us (0.944)
  waiting for transfers between devices: 128 us -> 104 us
  local copies, waits for them, and re-layouts: 78.9 us -> 59.3 us
  Pallas kernels: 161 us -> 174 us
  starting transfers between devices: 44.7 us -> 52.6 us
    unnamed x288 -> x260, local copies, waits for them, and re-layouts: 60.1 us -> 38.7 us
    ppermute x8 -> x9, waiting for transfers between devices: 22.7 us -> 10.3 us  [the longest x1 6.32 us: body(): out_across = over_y(tie(out_own, own))]
    ppermute x1, waiting for transfers between devices: 11.6 us -> 0.01 us  [body(): vector_came = lax.ppermute(vector, 'dp', [(d, d ^ 2) for d in range(8)])]
    pallas_call x1, Pallas kernels: 1.76 us -> 7.67 us  [mask_rows(): pl.pallas_call(mask_kernel, grid_spec=pltpu.PrefetchScalarGridSpec(num_sc...]
    ppermute x3, waiting for transfers between devices: 9.88 us -> 4.35 us  [body(): crossed0 = over_y(passed0)]
    pallas_call x1, Pallas kernels: 4.35 us -> 9.4 us  [prepare(): pl.pallas_call(partial(prepare_kernel, every), grid_spec=pltpu.PrefetchSc...]
    ppermute x1, waiting for transfers between devices: 12.2 us -> 17.1 us  [body(): vector_came = lax.ppermute(vector, 'dp', [(d, d ^ 4) for d in range(8)])]
    ppermute x8 -> x9, starting transfers between devices: 7.6 us -> 9.37 us  [the longest x1 1.53 us: body(): out_crossed0 = over_y(tie(out_passed0, passed0))]
  transfers between devices with their start and end apart: 65 -> 67, of which waited for: 28 -> 28; matrix products, arithmetic and copies ran while one was open for 6% -> 7% of each run, Pallas kernels for 36% -> 42%
where the time goes in v5:
time: 407 us; the launch traced here: 401 us
  Pallas kernels  174 us (43%)
  waiting for transfers between devices  104 us (26%)
  local copies, waits for them, and re-layouts  59.3 us (15%)
  starting transfers between devices  52.6 us (13%)
  other arithmetic  8.24 us (2%)
    pallas_call x2, Pallas kernels, mlp(): pl.pallas_call(partial(mlp_kernel, len(pieces), len(weight_pieces), split...  40.5 us
    unnamed x260, local copies, waits for them, and re-layouts  38.7 us
    pallas_call x3, Pallas kernels, weight_grad(): pl.pallas_call(partial(weight_grad_kernel, sizes, share, sends), grid_spe...  32.8 us
    pallas_call x2, Pallas kernels, attend_back(): pl.pallas_call(partial(attend_back_kernel, heads, windows, split, len(pie...  28 us
    pallas_call x2, Pallas kernels, attend(): pl.pallas_call(partial(attend_kernel, heads, split), grid=(windows,), in_...  21.2 us
    ppermute x1, waiting for transfers between devices, body(): vector_came = lax.ppermute(vector, 'dp', [(d, d ^ 4) for d in range(8)])  17.1 us
    ppermute x3, waiting for transfers between devices, body(): crossed1 = over_y(passed1)  11.9 us
    reshape x2, local copies, waits for them, and re-layouts, by_window(): array = array.reshape((slots, WTOK) + array.shape[1:])  9.9 us
  transfers between devices with their start and end apart: 67, of which 28 were waited for; matrix products, arithmetic and copies ran while one was open for 7% of the time, Pallas kernels for 42%

profile of v5, /device:TPU:0, one launch (start us, length us, event | category | flops | bytes accessed | tf_op | source)
XLA Modules:
  0.0 400.6 jit_solution(1828069324292329215)
XLA Ops:
  2.9 3.1 collective-permute-start
  7.9 5.0 %reshape.125.x_ref = bf16[8,196,1280]{2,1,0:T(8,128)(2,1)} reshape(bf16[1568,1280]{1,0:T(8,128)(2,1)} %param.19) | data formatting | bytes 8028160 | tf_op jit(solution)/shard_map/reshape | solution.py:1168
  13.9 4.5 %collective-permute-done.refs_2_ = bf16[160,1344]{1,0:T(8,128)(2,1)} collective-permute-done((bf16[160,1344]{1,0:T(8,128)(2,1)S(1)}, bf16[160,1344]{1,0:T(8,128)(2,1)}, u32[]{:S(2)}, u32[]{:S(2)}) %collective-permute-start) | collective-permute-done | bytes 430112 | tf_op jit(solution)/shard_map/ppermute | solution.py:1293
  23.5 9.4 %prepare.1 = (bf16[416,1280]{1,0:T(8,128)(2,1)}, f32[416,1]{1,0:T(8,128)}, bf16[1664,1280]{1,0:T(8,128)(2,1)}, f32[1664,1]{1,0:T(8,128)}) custom-call(s32[8]{0:T(128)} %stack.112.order, s32[8]{0:T(128)} %places.5, s32[8]{0:T(128)} %lives.5, bf16[8,196,1280]{2,1,0:T(8,128)(2,1)} %reshape.125.x_ref, f32[1,1280]{1,0:T(1,128)} %reshape.126.gain_ref.refs_10_, ...), custom_call_target="tpu_custom_call" | custom-call | flops 450000000 | bytes 90000 | tf_op jit(solution)/shard_map/prepare/pallas_call | solution.py:115
  32.9 1.6 collective-permute-start.4
  35.0 4.9 %reshape.132.top_ref = bf16[8,196,1280]{2,1,0:T(8,128)(2,1)} reshape(bf16[1568,1280]{1,0:T(8,128)(2,1)} %param.36) | data formatting | bytes 8028160 | tf_op jit(solution)/shard_map/reshape | solution.py:1168
  40.0 5.6 %collective-permute-done.4.refs_6_ = bf16[160,1344]{1,0:T(8,128)(2,1)} collective-permute-done((bf16[160,1344]{1,0:T(8,128)(2,1)}, bf16[160,1344]{1,0:T(8,128)(2,1)}, u32[]{:S(2)}, u32[]{:S(2)}) %collective-permute-start.4) | collective-permute-done | bytes 430112 | tf_op jit(solution)/shard_map/ppermute | solution.py:1302
  47.3 7.7 %mask_rows.1.refs_13_.refs_4_.refs_0_.refs_2_ = bf16[1664,1280]{1,0:T(8,128)(2,1)} custom-call(s32[8]{0:T(128)} %stack.112.order, s32[8]{0:T(128)} %places.5, s32[8]{0:T(128)} %lives.5, bf16[8,196,1280]{2,1,0:T(8,128)(2,1)} %reshape.132.top_ref), custom_call_target="tpu_custom_call" | custom-call | flops 300000000 | bytes 60000 | tf_op jit(solution)/shard_map/mask_rows/pallas_call | solution.py:149
  55.0 2.0 collective-permute-done.7.refs_7_
  59.2 2.2 copy-done.1
  64.5 8.2 %qkv.1 = (bf16[1664,384]{1,0:T(8,128)(2,1)S(1)}, bf16[1664,384]{1,0:T(8,128)(2,1)S(1)}, bf16[1664,384]{1,0:T(8,128)(2,1)S(1)}, bf16[1280,1344]{1,0:T(8,128)(2,1)S(1)}) custom-call(s32[8]{0:T(128)S(1)} %stack.121.offsets, bf16[160,1344]{1,0:T(8,128)(2,1)S(1)} %copy-done.63, bf16[160,1344]{1,0:T(8,128)(2,1)S(1)} %copy-done.88, ...), custom_call_target="tpu_custom_call" | custom-call | flops 700000000 | bytes 140000 | tf_op jit(solution)/shard_map/qkv/pallas_call | solution.py:321
  72.7 2.5 collective-permute-done.8.refs_5_
  76.3 10.6 %attend.2 = (bf16[832,320]{1,0:T(8,128)(2,1)S(1)}, bf16[832,1024]{1,0:T(8,128)(2,1)S(1)}, bf16[416,1280]{1,0:T(8,128)(2,1)S(1)}, bf16[416,1280]{1,0:T(8,128)(2,1)S(1)}) custom-call(bf16[1664,384]{1,0:T(8,128)(2,1)S(1)} %get-tuple-element.272.q_ref.refs_4_, bf16[1664,384]{1,0:T(8,128)(2,1)S(1)} %get-tuple-element.260.k_ref.refs_5_, ...), custom_call_target="tpu_custom_call" | custom-call | flops 675000000 | bytes 135000 | tf_op jit(solution)/shard_map/attend/pallas_call | solution.py:457
  86.9 4.3 %collective-permute-done.10.refs_7_ = bf16[160,2560]{1,0:T(8,128)(2,1)S(1)} collective-permute-done((bf16[160,2560]{1,0:T(8,128)(2,1)}, bf16[160,2560]{1,0:T(8,128)(2,1)S(1)}, u32[]{:S(2)}, u32[]{:S(2)}) %collective-permute-start.10) | collective-permute-done | bytes 819232 | tf_op jit(solution)/shard_map/ppermute | solution.py:1317
  94.7 1.6 collective-permute-start.14
  96.3 10.6 %attend.3 = (bf16[832,320]{1,0:T(8,128)(2,1)S(1)}, bf16[832,1024]{1,0:T(8,128)(2,1)S(1)}, bf16[416,1280]{1,0:T(8,128)(2,1)S(1)}, bf16[416,1280]{1,0:T(8,128)(2,1)S(1)}) custom-call(bf16[1664,384]{1,0:T(8,128)(2,1)S(1)} %get-tuple-element.272.q_ref.refs_4_, bf16[1664,384]{1,0:T(8,128)(2,1)S(1)} %get-tuple-element.260.k_ref.refs_5_, ...), custom_call_target="tpu_custom_call" | custom-call | flops 675000000 | bytes 135000 | tf_op jit(solution)/shard_map/attend/pallas_call | solution.py:457
  106.9 7.5 %collective-permute-done.11.refs_10_ = bf16[160,2560]{1,0:T(8,128)(2,1)S(1)} collective-permute-done((bf16[160,2560]{1,0:T(8,128)(2,1)S(1)}, bf16[160,2560]{1,0:T(8,128)(2,1)S(1)}, u32[]{:S(2)}, u32[]{:S(2)}) %collective-permute-start.11) | collective-permute-done | bytes 819232 | tf_op jit(solution)/shard_map/ppermute | solution.py:1320
  117.4 1.6 collective-permute-start.18
  120.9 11.5 %collective-permute-done.18.refs_2_ = bf16[208,1280]{1,0:T(8,128)(2,1)S(1)} collective-permute-done((bf16[208,1280]{1,0:T(8,128)(2,1)S(1)}, bf16[208,1280]{1,0:T(8,128)(2,1)S(1)}, u32[]{:S(2)}, u32[]{:S(2)}) %collective-permute-start.18) | collective-permute-done | bytes 532512 | tf_op jit(solution)/shard_map/ppermute | solution.py:1329
  135.2 7.9 %collective-permute-done.17.refs_1_ = bf16[208,1280]{1,0:T(8,128)(2,1)} collective-permute-done((bf16[208,1280]{1,0:T(8,128)(2,1)}, bf16[208,1280]{1,0:T(8,128)(2,1)}, u32[]{:S(2)}, u32[]{:S(2)}) %collective-permute-start.17) | collective-permute-done | bytes 532512 | tf_op jit(solution)/shard_map/ppermute | solution.py:1331
  145.4 20.1 %mlp.2 = (bf16[832,1280]{1,0:T(8,128)(2,1)}, bf16[832,1280]{1,0:T(8,128)(2,1)}, bf16[832,1280]{1,0:T(8,128)(2,1)}, f32[1,1280]{1,0:T(1,128)S(1)}, bf16[416,1280]...) custom-call(s32[8]{0:T(128)S(1)} %stack.121.offsets, ...), custom_call_target="tpu_custom_call" | custom-call | flops 1050000000 | bytes 210000 | tf_op jit(solution)/shard_map/mlp/pallas_call | solution.py:726
  166.7 1.9 collective-permute-done.22.refs_1_
  171.6 20.3 %mlp.3 = (bf16[832,1280]{1,0:T(8,128)(2,1)}, bf16[832,1280]{1,0:T(8,128)(2,1)}, bf16[832,1280]{1,0:T(8,128)(2,1)}, f32[1,1280]{1,0:T(1,128)S(1)}, bf16[416,1280]...) custom-call(s32[8]{0:T(128)S(1)} %stack.121.offsets, ...), custom_call_target="tpu_custom_call" | custom-call | flops 1050000000 | bytes 210000 | tf_op jit(solution)/shard_map/mlp/pallas_call | solution.py:726
  192.6 1.9 norm_two_back.2
  198.4 1.7 combine.15
  201.7 2.2 copy-done
  204.0 10.0 %weight_grad.3.refs_0_.refs_2_.refs_4_ = bf16[4,2,160,1280]{3,2,1,0:T(8,128)(2,1)S(1)} custom-call(s32[8]{0:T(128)S(1)} %stack.131.targets, bf16[1664,1280]{1,0:T(8,128)(2,1)S(1)} %copy-done, bf16[832,1280]{1,0:T(8,128)(2,1)S(1)} %copy-done.47, bf16[1664,1280]{1,0:T(8,128)(2,1)S(1)} %copy-done, bf16[832,1280]{1,0:T(8,128)(2,1)S(1)} %copy-done.50), custom_call_target="tpu_custom_call" | custom-call | flops 650000000 | bytes 130000 | tf_op jit(solution)/shard_map/weight_grad/pallas_call | solution.py:874
  215.4 2.1 copy-done.55
  217.5 10.8 %weight_grad.4 = (bf16[2,160,1280]{2,1,0:T(8,128)(2,1)}, bf16[2,160,1280]{2,1,0:T(8,128)(2,1)S(1)}, bf16[4,160,1280]{2,1,0:T(8,128)(2,1)S(1)}) custom-call(s32[8]{0:T(128)S(1)} %stack.131.targets, bf16[832,1280]{1,0:T(8,128)(2,1)S(1)} %copy-done.54, bf16[832,1280]{1,0:T(8,128)(2,1)S(1)} %copy-done.53, bf16[832,1280]{1,0:T(8,128)(2,1)S(1)} %copy-done.56, ...), custom_call_target="tpu_custom_call" | custom-call | flops 650000000 | bytes 130000 | tf_op jit(solution)/shard_map/weight_grad/pallas_call | solution.py:874
  229.9 2.4 norm_two_back.3
  233.3 2.6 collective-permute-done.35.refs_1_.refs_3_
  239.3 14.2 %attend_back.2 = (bf16[832,960]{1,0:T(8,128)(2,1)S(1)}, bf16[832,1280]{1,0:T(8,128)(2,1)S(1)}, f32[256,384]{1,0:T(8,128)S(1)}, f32[1,960]{1,0:T(1,128)S(1)}, f32...) custom-call(bf16[208,1280]{1,0:T(8,128)(2,1)} %get-tuple-element.351.refs_0_, ...), custom_call_target="tpu_custom_call" | custom-call | flops 925000000 | bytes 185000 | tf_op jit(solution)/shard_map/attend_back/pallas_call | solution.py:578
  253.5 3.6 collective-permute-done.36.refs_3_.refs_5_
  263.0 13.9 %attend_back.3 = (bf16[832,960]{1,0:T(8,128)(2,1)S(1)}, bf16[832,1280]{1,0:T(8,128)(2,1)S(1)}, f32[256,384]{1,0:T(8,128)S(1)}, f32[1,960]{1,0:T(1,128)S(1)}, f32...) custom-call(bf16[208,1280]{1,0:T(8,128)(2,1)S(1)} %get-tuple-element.372.refs_0_, ...), custom_call_target="tpu_custom_call" | custom-call | flops 925000000 | bytes 185000 | tf_op jit(solution)/shard_map/attend_back/pallas_call | solution.py:578
  282.4 4.3 %collective-permute-done.38.refs_2_ = bf16[208,1280]{1,0:T(8,128)(2,1)S(1)} collective-permute-done((bf16[208,1280]{1,0:T(8,128)(2,1)S(1)}, bf16[208,1280]{1,0:T(8,128)(2,1)S(1)}, u32[]{:S(2)}, u32[]{:S(2)}) %collective-permute-start.38) | collective-permute-done | bytes 532512 | tf_op jit(solution)/shard_map/ppermute | solution.py:1398
  294.1 3.2 collective-permute-done.46
  302.3 2.2 combine.18
  312.5 12.0 %weight_grad.5 = (bf16[1,160,1280]{2,1,0:T(8,128)(2,1)S(1)}, bf16[2,160,1280]{2,1,0:T(8,128)(2,1)S(1)}, bf16[1,160,1280]{2,1,0:T(8,128)(2,1)S(1)}, bf16[4,160,1280]{2,1,0:T(8,128)(2,1)S(1)}) custom-call(s32[8]{0:T(128)S(1)} %stack.131.targets, bf16[1664,1280]{1,0:T(8,128)(2,1)S(1)} %bitcast.81, bf16[832,960]{1,0:T(8,128)(2,1)S(1)} %copy-done.70, ...), custom_call_target="tpu_custom_call" | custom-call | flops 650000000 | bytes 130000 | tf_op jit(solution)/shard_map/weight_grad/pallas_call | solution.py:874
  328.9 3.0 norm_one_back.1.refs_0_
  334.6 2.5 combine.20.refs_0_
  337.1 2.3 collective-permute-done.53.refs_4_
  340.7 3.1 collective-permute-start.55
  345.3 17.1 %collective-permute-done.56 = f32[160,128]{1,0:T(8,128)S(1)} collective-permute-done((f32[160,128]{1,0:T(8,128)S(1)}, f32[160,128]{1,0:T(8,128)S(1)}, u32[]{:S(2)}, u32[]{:S(2)}) %collective-permute-start.56) | collective-permute-done | bytes 81952 | tf_op jit(solution)/shard_map/ppermute | solution.py:1502
  362.5 2.0 fusion.1
  368.3 4.6 %place_windows.1 = f32[1568,1280]{1,0:T(8,128)} custom-call(s32[4]{0:T(128)S(1)} %pad_add_fusion.1.order, bf16[416,1280]{1,0:T(8,128)(2,1)S(1)} %norm_one_back.1.refs_0_, bf16[416,1280]{1,0:T(8,128)(2,1)S(1)} %collective-permute-done.57.refs_1_, bf16[416,1280]{1,0:T(8,128)(2,1)S(1)} %collective-permute-done.60.refs_2_, ...), custom_call_target="tpu_custom_call" | custom-call | flops 350000000 | bytes 70000 | tf_op jit(solution)/shard_map/place_windows/pallas_call | solution.py:950
  372.9 7.5 %collective-permute-done.58.refs_2_ = bf16[160,1280]{1,0:T(8,128)(2,1)S(1)} collective-permute-done((bf16[160,1280]{1,0:T(8,128)(2,1)S(1)}, bf16[160,1280]{1,0:T(8,128)(2,1)S(1)}, u32[]{:S(2)}, u32[]{:S(2)}) %collective-permute-start.58) | collective-permute-done | bytes 409632 | tf_op jit(solution)/shard_map/ppermute | solution.py:1518
  384.3 6.3 %collective-permute-done.63.refs_1_ = bf16[416,1280]{1,0:T(8,128)(2,1)S(1)} collective-permute-done((bf16[416,1280]{1,0:T(8,128)(2,1)}, bf16[416,1280]{1,0:T(8,128)(2,1)S(1)}, u32[]{:S(2)}, u32[]{:S(2)}) %collective-permute-start.63) | collective-permute-done | bytes 1064992 | tf_op jit(solution)/shard_map/ppermute | solution.py:1503
  395.7 4.6 %write_output.1 = bf16[1568,1280]{1,0:T(8,128)(2,1)} custom-call(s32[4]{0:T(128)S(1)} %pad_add_fusion.1.order, s32[8]{0:T(128)S(1)} %copy-done.95, s32[8]{0:T(128)S(1)} %copy-done.96, bf16[416,1280]{1,0:T(8,128)(2,1)} %combine.20.refs_0_, bf16[416,1280]{1,0:T(8,128)(2,1)S(1)} %collective-permute-done.63.refs_1_, ...), custom_call_target="tpu_custom_call" | custom-call | flops 350000000 | bytes 70000 | tf_op jit(solution)/shard_map/write_output/pallas_call | solution.py:985
  (447 shorter events, 103.3 us)
Async XLA Ops:
  2.9 15.6 %collective-permute-start = (bf16[160,1344]{1,0:T(8,128)(2,1)S(1)}, bf16[160,1344]{1,0:T(8,128)(2,1)}, u32[]{:S(2)}, u32[]{:S(2)}) collective-permute-start(bf16[160,1344]{1,0:T(8,128)(2,1)S(1)} %concatenate.12.refs_0_), channel_id=1, source_target_pairs={{0,8},{4,12},{8,16},{12,20},{16,24},{20,28},{24,0},{28,4},{1,9},{5... | collective-permute-start | bytes 1290248 | tf_op jit(solution)/shard_map/ppermute | solution.py:1293
  5.9 12.5 %collective-permute-start.1 = (bf16[160,1344]{1,0:T(8,128)(2,1)S(1)}, bf16[160,1344]{1,0:T(8,128)(2,1)S(1)}, u32[]{:S(2)}, u32[]{:S(2)}) collective-permute-start(bf16[160,1344]{1,0:T(8,128)(2,1)S(1)} %concatenate.12.refs_0_), channel_id=1, source_target_pairs={{0,4},{4,0},{8,12},{12,8},{16,20},{20,16},{24,28},{28,24},{1,5},{5... | collective-permute-start | bytes 1290248 | tf_op jit(solution)/shard_map/ppermute | solution.py:1293
  19.2 13.7 %collective-permute-start.2 = (bf16[160,1344]{1,0:T(8,128)(2,1)}, bf16[160,1344]{1,0:T(8,128)(2,1)}, u32[]{:S(2)}, u32[]{:S(2)}) collective-permute-start(bf16[160,1344]{1,0:T(8,128)(2,1)} %collective-permute-done.refs_2_), channel_id=1, source_target_pairs={{0,8},{4,12},{8,16},{12,20},{16,24},{20,28},{24,0},{28,4},{1,9},{5... | collective-permute-start | bytes 1290248 | tf_op jit(solution)/shard_map/ppermute | solution.py:1297
  20.1 12.8 %collective-permute-start.3 = (bf16[160,1344]{1,0:T(8,128)(2,1)}, bf16[160,1344]{1,0:T(8,128)(2,1)}, u32[]{:S(2)}, u32[]{:S(2)}) collective-permute-start(bf16[160,1344]{1,0:T(8,128)(2,1)} %collective-permute-done.refs_2_), channel_id=1, source_target_pairs={{0,4},{4,0},{8,12},{12,8},{16,20},{20,16},{24,28},{28,24},{1,5},{5... | collective-permute-start | bytes 1290248 | tf_op jit(solution)/shard_map/ppermute | solution.py:1297
  32.9 12.7 %collective-permute-start.4 = (bf16[160,1344]{1,0:T(8,128)(2,1)}, bf16[160,1344]{1,0:T(8,128)(2,1)}, u32[]{:S(2)}, u32[]{:S(2)}) collective-permute-start(bf16[160,1344]{1,0:T(8,128)(2,1)} %collective-permute-done.2.refs_4_), channel_id=1, source_target_pairs={{0,8},{4,12},{8,16},{12,20},{16,24},{20,28},{24,0},{28,4},{1,9},{5... | collective-permute-start | bytes 1290248 | tf_op jit(solution)/shard_map/ppermute | solution.py:1302
  34.5 11.1 %collective-permute-start.5 = (bf16[160,1344]{1,0:T(8,128)(2,1)}, bf16[160,1344]{1,0:T(8,128)(2,1)S(1)}, u32[]{:S(2)}, u32[]{:S(2)}) collective-permute-start(bf16[160,1344]{1,0:T(8,128)(2,1)} %collective-permute-done.2.refs_4_), channel_id=1, source_target_pairs={{0,4},{4,0},{8,12},{12,8},{16,20},{20,16},{24,28},{28,24},{1,5},{5... | collective-permute-start | bytes 1290248 | tf_op jit(solution)/shard_map/ppermute | solution.py:1302
  46.3 10.7 %collective-permute-start.7 = (bf16[160,1344]{1,0:T(8,128)(2,1)}, bf16[160,1344]{1,0:T(8,128)(2,1)}, u32[]{:S(2)}, u32[]{:S(2)}) collective-permute-start(bf16[160,1344]{1,0:T(8,128)(2,1)} %collective-permute-done.4.refs_6_), channel_id=1, source_target_pairs={{0,4},{4,0},{8,12},{12,8},{16,20},{20,16},{24,28},{28,24},{1,5},{5... | collective-permute-start | bytes 1290248 | tf_op jit(solution)/shard_map/ppermute | solution.py:1306
  47.3 25.4 %collective-permute-start.6 = (bf16[160,2560]{1,0:T(8,128)(2,1)S(1)}, bf16[160,2560]{1,0:T(8,128)(2,1)}, u32[]{:S(2)}, u32[]{:S(2)}) collective-permute-start(bf16[160,2560]{1,0:T(8,128)(2,1)S(1)} %pad_maximum_fusion.refs_4_), channel_id=1, source_target_pairs={{0,8},{4,12},{8,16},{12,20},{16,24},{20,28},{24,0},{28,4},{1,9},{5... | collective-permute-start | bytes 2457608 | tf_op jit(solution)/shard_map/ppermute | solution.py:1307
  57.0 18.2 %collective-permute-start.8 = (bf16[160,2560]{1,0:T(8,128)(2,1)S(1)}, bf16[160,2560]{1,0:T(8,128)(2,1)S(1)}, u32[]{:S(2)}, u32[]{:S(2)}) collective-permute-start(bf16[160,2560]{1,0:T(8,128)(2,1)S(1)} %pad_maximum_fusion.refs_4_), channel_id=1, source_target_pairs={{0,4},{4,0},{8,12},{12,8},{16,20},{20,16},{24,28},{28,24},{1,5},{5... | collective-permute-start | bytes 2457608 | tf_op jit(solution)/shard_map/ppermute | solution.py:1312
  75.2 16.0 %collective-permute-start.10 = (bf16[160,2560]{1,0:T(8,128)(2,1)}, bf16[160,2560]{1,0:T(8,128)(2,1)S(1)}, u32[]{:S(2)}, u32[]{:S(2)}) collective-permute-start(bf16[160,2560]{1,0:T(8,128)(2,1)} %collective-permute-done.6.refs_6_), channel_id=1, source_target_pairs={{0,4},{4,0},{8,12},{12,8},{16,20},{20,16},{24,28},{28,24},{1,5},{5... | collective-permute-start | bytes 2457608 | tf_op jit(solution)/shard_map/ppermute | solution.py:1317
  76.2 15.6 %collective-permute-start.9 = (bf16[160,2560]{1,0:T(8,128)(2,1)}, bf16[160,2560]{1,0:T(8,128)(2,1)S(1)}, u32[]{:S(2)}, u32[]{:S(2)}) collective-permute-start(bf16[160,2560]{1,0:T(8,128)(2,1)} %collective-permute-done.6.refs_6_), channel_id=1, source_target_pairs={{0,8},{4,12},{8,16},{12,20},{16,24},{20,28},{24,0},{28,4},{1,9},{5... | collective-permute-start | bytes 2457608 | tf_op jit(solution)/shard_map/ppermute | solution.py:1317
  91.8 22.6 %collective-permute-start.11 = (bf16[160,2560]{1,0:T(8,128)(2,1)S(1)}, bf16[160,2560]{1,0:T(8,128)(2,1)S(1)}, u32[]{:S(2)}, u32[]{:S(2)}) collective-permute-start(bf16[160,2560]{1,0:T(8,128)(2,1)S(1)} %collective-permute-done.9.refs_8_), channel_id=1, source_target_pairs={{0,8},{4,12},{8,16},{12,20},{16,24},{20,28},{24,0},{28,4},{1,9},{5... | collective-permute-start | bytes 2457608 | tf_op jit(solution)/shard_map/ppermute | solution.py:1320
  92.0 22.4 %collective-permute-start.12 = (bf16[160,2560]{1,0:T(8,128)(2,1)S(1)}, bf16[160,2560]{1,0:T(8,128)(2,1)S(1)}, u32[]{:S(2)}, u32[]{:S(2)}) collective-permute-start(bf16[160,2560]{1,0:T(8,128)(2,1)S(1)} %collective-permute-done.9.refs_8_), channel_id=1, source_target_pairs={{0,4},{4,0},{8,12},{12,8},{16,20},{20,16},{24,28},{28,24},{1,5},{5... | collective-permute-start | bytes 2457608 | tf_op jit(solution)/shard_map/ppermute | solution.py:1320
  94.7 19.8 %collective-permute-start.14 = (bf16[208,1280]{1,0:T(8,128)(2,1)S(1)}, bf16[208,1280]{1,0:T(8,128)(2,1)S(1)}, u32[]{:S(2)}, u32[]{:S(2)}) collective-permute-start(bf16[208,1280]{1,0:T(8,128)(2,1)S(1)} %combine.12), channel_id=1, source_target_pairs={{0,2},{1,3},{2,0},{3,1},{4,6},{5,7},{6,4},{7,5},{8,10},{9,11},{10,... | collective-permute-start | bytes 1597448 | tf_op jit(solution)/shard_map/ppermute | solution.py:1323
  114.5 20.7 %collective-permute-start.15 = (bf16[160,2560]{1,0:T(8,128)(2,1)S(1)}, bf16[160,2560]{1,0:T(8,128)(2,1)S(1)}, u32[]{:S(2)}, u32[]{:S(2)}) collective-permute-start(bf16[160,2560]{1,0:T(8,128)(2,1)S(1)} %collective-permute-done.11.refs_10_), channel_id=1, source_target_pairs={{0,4},{4,0},{8,12},{12,8},{16,20},{20,16},{24,28},{28,24},{1,5},{5... | collective-permute-start | bytes 2457608 | tf_op jit(solution)/shard_map/ppermute | solution.py:1326
  117.4 15.0 %collective-permute-start.18 = (bf16[208,1280]{1,0:T(8,128)(2,1)S(1)}, bf16[208,1280]{1,0:T(8,128)(2,1)S(1)}, u32[]{:S(2)}, u32[]{:S(2)}) collective-permute-start(bf16[208,1280]{1,0:T(8,128)(2,1)S(1)} %combine.13), channel_id=1, source_target_pairs={{0,2},{1,3},{2,0},{3,1},{4,6},{5,7},{6,4},{7,5},{8,10},{9,11},{10,... | collective-permute-start | bytes 1597448 | tf_op jit(solution)/shard_map/ppermute | solution.py:1329
  120.4 22.7 %collective-permute-start.17 = (bf16[208,1280]{1,0:T(8,128)(2,1)}, bf16[208,1280]{1,0:T(8,128)(2,1)}, u32[]{:S(2)}, u32[]{:S(2)}) collective-permute-start(bf16[208,1280]{1,0:T(8,128)(2,1)} %get-tuple-element.286.refs_0_), channel_id=1, source_target_pairs={{0,2},{1,3},{2,0},{3,1},{4,6},{5,7},{6,4},{7,5},{8,10},{9,11},{10,... | collective-permute-start | bytes 1597448 | tf_op jit(solution)/shard_map/ppermute | solution.py:1331
  120.9 24.5 %collective-permute-start.20 = (bf16[208,1280]{1,0:T(8,128)(2,1)}, bf16[208,1280]{1,0:T(8,128)(2,1)}, u32[]{:S(2)}, u32[]{:S(2)}) collective-permute-start(bf16[208,1280]{1,0:T(8,128)(2,1)} %get-tuple-element.286.refs_0_), channel_id=1, source_target_pairs={{0,1},{1,0},{2,3},{3,2},{4,5},{5,4},{6,7},{7,6},{8,9},{9,8},{10,11... | collective-permute-start | bytes 1597448 | tf_op jit(solution)/shard_map/ppermute | solution.py:1286
  143.1 22.5 %collective-permute-start.19 = (bf16[208,1280]{1,0:T(8,128)(2,1)S(1)}, bf16[208,1280]{1,0:T(8,128)(2,1)}, u32[]{:S(2)}, u32[]{:S(2)}) collective-permute-start(bf16[208,1280]{1,0:T(8,128)(2,1)S(1)} %get-tuple-element.309.refs_0_), channel_id=1, source_target_pairs={{0,2},{1,3},{2,0},{3,1},{4,6},{5,7},{6,4},{7,5},{8,10},{9,11},{10,... | collective-permute-start | bytes 1597448 | tf_op jit(solution)/shard_map/ppermute | solution.py:1336
  165.9 26.1 %collective-permute-start.24 = (bf16[416,1280]{1,0:T(8,128)(2,1)}, bf16[416,1280]{1,0:T(8,128)(2,1)S(1)}, u32[]{:S(2)}, u32[]{:S(2)}) collective-permute-start(bf16[416,1280]{1,0:T(8,128)(2,1)} %get-tuple-element.308), channel_id=1, source_target_pairs={{0,1},{1,0},{2,3},{3,2},{4,5},{5,4},{6,7},{7,6},{8,9},{9,8},{10,11... | collective-permute-start | bytes 3194888 | tf_op jit(solution)/shard_map/ppermute | solution.py:1342
  169.9 22.1 %collective-permute-start.23 = (bf16[208,1280]{1,0:T(8,128)(2,1)S(1)}, bf16[208,1280]{1,0:T(8,128)(2,1)S(1)}, u32[]{:S(2)}, u32[]{:S(2)}) collective-permute-start(bf16[208,1280]{1,0:T(8,128)(2,1)S(1)} %combine.14), channel_id=1, source_target_pairs={{0,2},{1,3},{2,0},{3,1},{4,6},{5,7},{6,4},{7,5},{8,10},{9,11},{10,... | collective-permute-start | bytes 1597448 | tf_op jit(solution)/shard_map/ppermute | solution.py:1344
  195.6 18.4 %collective-permute-start.28 = (bf16[208,1280]{1,0:T(8,128)(2,1)}, bf16[208,1280]{1,0:T(8,128)(2,1)}, u32[]{:S(2)}, u32[]{:S(2)}) collective-permute-start(bf16[208,1280]{1,0:T(8,128)(2,1)} %get-tuple-element.351.refs_0_), channel_id=1, source_target_pairs={{0,2},{1,3},{2,0},{3,1},{4,6},{5,7},{6,4},{7,5},{8,10},{9,11},{10,... | collective-permute-start | bytes 1597448 | tf_op jit(solution)/shard_map/ppermute | solution.py:1351
  214.1 21.9 %collective-permute-start.35 = (bf16[2,160,1280]{2,1,0:T(8,128)(2,1)S(1)}, bf16[2,160,1280]{2,1,0:T(8,128)(2,1)S(1)}, u32[]{:S(2)}, u32[]{:S(2)}) collective-permute-start(bf16[2,160,1280]{2,1,0:T(8,128)(2,1)S(1)} %slice_bitcast_fusion), channel_id=1, source_target_pairs={{0,8},{4,12},{8,16},{12,20},{16,24},{20,28},{24,0},{28,4},{1,9},{5... | collective-permute-start | bytes 2457608 | tf_op jit(solution)/shard_map/ppermute | solution.py:1364
  214.2 14.2 %collective-permute-start.31 = (bf16[208,1280]{1,0:T(8,128)(2,1)}, bf16[208,1280]{1,0:T(8,128)(2,1)S(1)}, u32[]{:S(2)}, u32[]{:S(2)}) collective-permute-start(bf16[208,1280]{1,0:T(8,128)(2,1)} %get-tuple-element.351.refs_0_), channel_id=1, source_target_pairs={{0,1},{1,0},{2,3},{3,2},{4,5},{5,4},{6,7},{7,6},{8,9},{9,8},{10,11... | collective-permute-start | bytes 1597448 | tf_op jit(solution)/shard_map/ppermute | solution.py:1286
  214.2 14.5 %collective-permute-start.30 = (bf16[208,1280]{1,0:T(8,128)(2,1)S(1)}, bf16[208,1280]{1,0:T(8,128)(2,1)S(1)}, u32[]{:S(2)}, u32[]{:S(2)}) collective-permute-start(bf16[208,1280]{1,0:T(8,128)(2,1)S(1)} %get-tuple-element.336), channel_id=1, source_target_pairs={{0,2},{1,3},{2,0},{3,1},{4,6},{5,7},{6,4},{7,5},{8,10},{9,11},{10,... | collective-permute-start | bytes 1597448 | tf_op jit(solution)/shard_map/ppermute | solution.py:1360
  215.3 13.4 %collective-permute-start.32 = (bf16[208,1280]{1,0:T(8,128)(2,1)}, bf16[208,1280]{1,0:T(8,128)(2,1)S(1)}, u32[]{:S(2)}, u32[]{:S(2)}) collective-permute-start(bf16[208,1280]{1,0:T(8,128)(2,1)} %collective-permute-done.28.refs_1_), channel_id=1, source_target_pairs={{0,1},{1,0},{2,3},{3,2},{4,5},{5,4},{6,7},{7,6},{8,9},{9,8},{10,11... | collective-permute-start | bytes 1597448 | tf_op jit(solution)/shard_map/ppermute | solution.py:1286
  228.8 24.8 %collective-permute-start.34 = (bf16[2,160,1280]{2,1,0:T(8,128)(2,1)}, bf16[2,160,1280]{2,1,0:T(8,128)(2,1)S(1)}, u32[]{:S(2)}, u32[]{:S(2)}) collective-permute-start(bf16[2,160,1280]{2,1,0:T(8,128)(2,1)} %get-tuple-element.348), channel_id=1, source_target_pairs={{0,4},{4,0},{8,12},{12,8},{16,20},{20,16},{24,28},{28,24},{1,5},{5... | collective-permute-start | bytes 2457608 | tf_op jit(solution)/shard_map/ppermute | solution.py:1369
  236.2 21.0 %collective-permute-start.36 = (bf16[160,2560]{1,0:T(8,128)(2,1)S(1)}, bf16[160,2560]{1,0:T(8,128)(2,1)S(1)}, u32[]{:S(2)}, u32[]{:S(2)}) collective-permute-start(bf16[160,2560]{1,0:T(8,128)(2,1)S(1)} %combine.16), channel_id=1, source_target_pairs={{0,8},{4,12},{8,16},{12,20},{16,24},{20,28},{24,0},{28,4},{1,9},{5... | collective-permute-start | bytes 2457608 | tf_op jit(solution)/shard_map/ppermute | solution.py:1387
  236.3 17.3 %collective-permute-start.33 = (bf16[208,1280]{1,0:T(8,128)(2,1)S(1)}, bf16[208,1280]{1,0:T(8,128)(2,1)S(1)}, u32[]{:S(2)}, u32[]{:S(2)}) collective-permute-start(bf16[208,1280]{1,0:T(8,128)(2,1)S(1)} %get-tuple-element.372.refs_0_), channel_id=1, source_target_pairs={{0,2},{1,3},{2,0},{3,1},{4,6},{5,7},{6,4},{7,5},{8,10},{9,11},{10,... | collective-permute-start | bytes 1597448 | tf_op jit(solution)/shard_map/ppermute | solution.py:1379
  257.7 22.9 %collective-permute-start.40 = (bf16[2,160,1280]{2,1,0:T(8,128)(2,1)S(1)}, bf16[2,160,1280]{2,1,0:T(8,128)(2,1)S(1)}, u32[]{:S(2)}, u32[]{:S(2)}) collective-permute-start(bf16[2,160,1280]{2,1,0:T(8,128)(2,1)S(1)} %copy-done.98), channel_id=1, source_target_pairs={{0,4},{4,0},{8,12},{12,8},{16,20},{20,16},{24,28},{28,24},{1,5},{5... | collective-permute-start | bytes 2457608 | tf_op jit(solution)/shard_map/ppermute | solution.py:1392
  260.8 26.8 %collective-permute-start.39 = (bf16[160,2560]{1,0:T(8,128)(2,1)S(1)}, bf16[160,2560]{1,0:T(8,128)(2,1)S(1)}, u32[]{:S(2)}, u32[]{:S(2)}) collective-permute-start(bf16[160,2560]{1,0:T(8,128)(2,1)S(1)} %get-tuple-element.368), channel_id=1, source_target_pairs={{0,8},{4,12},{8,16},{12,20},{16,24},{20,28},{24,0},{28,4},{1,9},{5... | collective-permute-start | bytes 2457608 | tf_op jit(solution)/shard_map/ppermute | solution.py:1399
  261.0 20.6 %collective-permute-start.41 = (bf16[208,1280]{1,0:T(8,128)(2,1)S(1)}, bf16[208,1280]{1,0:T(8,128)(2,1)S(1)}, u32[]{:S(2)}, u32[]{:S(2)}) collective-permute-start(bf16[208,1280]{1,0:T(8,128)(2,1)S(1)} %copy-done.103), channel_id=1, source_target_pairs={{0,2},{1,3},{2,0},{3,1},{4,6},{5,7},{6,4},{7,5},{8,10},{9,11},{10,... | collective-permute-start | bytes 1597448 | tf_op jit(solution)/shard_map/ppermute | solution.py:1401
  262.5 24.3 %collective-permute-start.38 = (bf16[208,1280]{1,0:T(8,128)(2,1)S(1)}, bf16[208,1280]{1,0:T(8,128)(2,1)S(1)}, u32[]{:S(2)}, u32[]{:S(2)}) collective-permute-start(bf16[208,1280]{1,0:T(8,128)(2,1)S(1)} %get-tuple-element.367), channel_id=1, source_target_pairs={{0,2},{1,3},{2,0},{3,1},{4,6},{5,7},{6,4},{7,5},{8,10},{9,11},{10,... | collective-permute-start | bytes 1597448 | tf_op jit(solution)/shard_map/ppermute | solution.py:1398
  304.5 20.8 %collective-permute-start.47 = (bf16[208,1280]{1,0:T(8,128)(2,1)S(1)}, bf16[208,1280]{1,0:T(8,128)(2,1)S(1)}, u32[]{:S(2)}, u32[]{:S(2)}) collective-permute-start(bf16[208,1280]{1,0:T(8,128)(2,1)S(1)} %get-tuple-element.400), channel_id=1, source_target_pairs={{0,2},{1,3},{2,0},{3,1},{4,6},{5,7},{6,4},{7,5},{8,10},{9,11},{10,... | collective-permute-start | bytes 1597448 | tf_op jit(solution)/shard_map/ppermute | solution.py:1428
  306.0 19.3 %collective-permute-start.48 = (bf16[160,1280]{1,0:T(8,128)(2,1)}, bf16[160,1280]{1,0:T(8,128)(2,1)}, u32[]{:S(2)}, u32[]{:S(2)}) collective-permute-start(bf16[160,1280]{1,0:T(8,128)(2,1)} %get-tuple-element.401), channel_id=1, source_target_pairs={{0,4},{4,0},{8,12},{12,8},{16,20},{20,16},{24,28},{28,24},{1,5},{5... | collective-permute-start | bytes 1228808 | tf_op jit(solution)/shard_map/ppermute | solution.py:1429
  307.1 18.2 %collective-permute-start.49 = (bf16[160,1280]{1,0:T(8,128)(2,1)S(1)}, bf16[160,1280]{1,0:T(8,128)(2,1)S(1)}, u32[]{:S(2)}, u32[]{:S(2)}) collective-permute-start(bf16[160,1280]{1,0:T(8,128)(2,1)S(1)} %get-tuple-element.402), channel_id=1, source_target_pairs={{0,8},{4,12},{8,16},{12,20},{16,24},{20,28},{24,0},{28,4},{1,9},{5... | collective-permute-start | bytes 1228808 | tf_op jit(solution)/shard_map/ppermute | solution.py:1429
  307.1 27.5 %collective-permute-start.54 = (bf16[208,1280]{1,0:T(8,128)(2,1)}, bf16[208,1280]{1,0:T(8,128)(2,1)S(1)}, u32[]{:S(2)}, u32[]{:S(2)}) collective-permute-start(bf16[208,1280]{1,0:T(8,128)(2,1)} %copy-done.101), channel_id=1, source_target_pairs={{0,2},{1,3},{2,0},{3,1},{4,6},{5,7},{6,4},{7,5},{8,10},{9,11},{10,... | collective-permute-start | bytes 1597448 | tf_op jit(solution)/shard_map/ppermute | solution.py:1431
  307.6 17.6 %collective-permute-start.50 = (f32[160,128]{1,0:T(8,128)S(1)}, f32[160,128]{1,0:T(8,128)S(1)}, u32[]{:S(2)}, u32[]{:S(2)}) collective-permute-start(f32[160,128]{1,0:T(8,128)S(1)} %add.273), channel_id=1, source_target_pairs={{0,8},{4,12},{8,0},{12,4},{16,24},{20,28},{24,16},{28,20},{1,9},{5... | collective-permute-start | bytes 245768 | tf_op jit(solution)/shard_map/ppermute | solution.py:1415
  326.3 13.1 %collective-permute-start.53 = (bf16[160,1280]{1,0:T(8,128)(2,1)S(1)}, bf16[160,1280]{1,0:T(8,128)(2,1)S(1)}, u32[]{:S(2)}, u32[]{:S(2)}) collective-permute-start(bf16[160,1280]{1,0:T(8,128)(2,1)S(1)} %combine.19), channel_id=1, source_target_pairs={{0,8},{4,12},{8,16},{12,20},{16,24},{20,28},{24,0},{28,4},{1,9},{5... | collective-permute-start | bytes 1228808 | tf_op jit(solution)/shard_map/ppermute | solution.py:1454
  327.8 12.6 %collective-permute-start.52 = (bf16[1,160,1280]{2,1,0:T(8,128)(2,1)}, bf16[1,160,1280]{2,1,0:T(8,128)(2,1)S(1)}, u32[]{:S(2)}, u32[]{:S(2)}) collective-permute-start(bf16[1,160,1280]{2,1,0:T(8,128)(2,1)} %copy-done.106), channel_id=1, source_target_pairs={{0,4},{4,0},{8,12},{12,8},{16,20},{20,16},{24,28},{28,24},{1,5},{5... | collective-permute-start | bytes 1228808 | tf_op jit(solution)/shard_map/ppermute | solution.py:1439
  331.9 30.5 %collective-permute-start.57 = (bf16[416,1280]{1,0:T(8,128)(2,1)S(1)}, bf16[416,1280]{1,0:T(8,128)(2,1)S(1)}, u32[]{:S(2)}, u32[]{:S(2)}) collective-permute-start(bf16[416,1280]{1,0:T(8,128)(2,1)S(1)} %norm_one_back.1.refs_0_), channel_id=1, source_target_pairs={{0,2},{1,3},{2,0},{3,1},{4,6},{5,7},{6,4},{7,5},{8,10},{9,11},{10,... | collective-permute-start | bytes 3194888 | tf_op jit(solution)/shard_map/ppermute | solution.py:1464
  333.4 28.9 %collective-permute-start.51 = (bf16[2,160,1280]{2,1,0:T(8,128)(2,1)S(1)}, bf16[2,160,1280]{2,1,0:T(8,128)(2,1)S(1)}, u32[]{:S(2)}, u32[]{:S(2)}) collective-permute-start(bf16[2,160,1280]{2,1,0:T(8,128)(2,1)S(1)} %copy-done.100), channel_id=1, source_target_pairs={{0,4},{4,0},{8,12},{12,8},{16,20},{20,16},{24,28},{28,24},{1,5},{5... | collective-permute-start | bytes 2457608 | tf_op jit(solution)/shard_map/ppermute | solution.py:1485
  340.7 21.7 %collective-permute-start.55 = (bf16[160,2560]{1,0:T(8,128)(2,1)S(1)}, bf16[160,2560]{1,0:T(8,128)(2,1)S(1)}, u32[]{:S(2)}, u32[]{:S(2)}) collective-permute-start(bf16[160,2560]{1,0:T(8,128)(2,1)S(1)} %combine.21), channel_id=1, source_target_pairs={{0,8},{4,12},{8,16},{12,20},{16,24},{20,28},{24,0},{28,4},{1,9},{5... | collective-permute-start | bytes 2457608 | tf_op jit(solution)/shard_map/ppermute | solution.py:1501
  343.8 18.6 %collective-permute-start.56 = (f32[160,128]{1,0:T(8,128)S(1)}, f32[160,128]{1,0:T(8,128)S(1)}, u32[]{:S(2)}, u32[]{:S(2)}) collective-permute-start(f32[160,128]{1,0:T(8,128)S(1)} %add.274), channel_id=1, source_target_pairs={{0,16},{4,20},{8,24},{12,28},{16,0},{20,4},{24,8},{28,12},{1,17},{... | collective-permute-start | bytes 245768 | tf_op jit(solution)/shard_map/ppermute | solution.py:1502
  345.3 23.0 %collective-permute-start.60 = (bf16[416,1280]{1,0:T(8,128)(2,1)S(1)}, bf16[416,1280]{1,0:T(8,128)(2,1)S(1)}, u32[]{:S(2)}, u32[]{:S(2)}) collective-permute-start(bf16[416,1280]{1,0:T(8,128)(2,1)S(1)} %norm_one_back.1.refs_0_), channel_id=1, source_target_pairs={{0,1},{1,0},{2,3},{3,2},{4,5},{5,4},{6,7},{7,6},{8,9},{9,8},{10,11... | collective-permute-start | bytes 3194888 | tf_op jit(solution)/shard_map/ppermute | solution.py:1286
  364.5 26.1 %collective-permute-start.63 = (bf16[416,1280]{1,0:T(8,128)(2,1)}, bf16[416,1280]{1,0:T(8,128)(2,1)S(1)}, u32[]{:S(2)}, u32[]{:S(2)}) collective-permute-start(bf16[416,1280]{1,0:T(8,128)(2,1)} %combine.20.refs_0_), channel_id=1, source_target_pairs={{0,2},{1,3},{2,0},{3,1},{4,6},{5,7},{6,4},{7,5},{8,10},{9,11},{10,... | collective-permute-start | bytes 3194888 | tf_op jit(solution)/shard_map/ppermute | solution.py:1503
  367.2 13.1 %collective-permute-start.58 = (bf16[160,1280]{1,0:T(8,128)(2,1)S(1)}, bf16[160,1280]{1,0:T(8,128)(2,1)S(1)}, u32[]{:S(2)}, u32[]{:S(2)}) collective-permute-start(bf16[160,1280]{1,0:T(8,128)(2,1)S(1)} %combine.22), channel_id=1, source_target_pairs={{0,8},{4,12},{8,16},{12,20},{16,24},{20,28},{24,0},{28,4},{1,9},{5... | collective-permute-start | bytes 1228808 | tf_op jit(solution)/shard_map/ppermute | solution.py:1518
  380.5 12.3 %collective-permute-start.66 = (bf16[160,1280]{1,0:T(8,128)(2,1)S(1)}, bf16[160,1280]{1,0:T(8,128)(2,1)S(1)}, u32[]{:S(2)}, u32[]{:S(2)}) collective-permute-start(bf16[160,1280]{1,0:T(8,128)(2,1)S(1)} %combine.23), channel_id=1, source_target_pairs={{0,8},{4,12},{8,16},{12,20},{16,24},{20,28},{24,0},{28,4},{1,9},{5... | collective-permute-start | bytes 1228808 | tf_op jit(solution)/shard_map/ppermute | solution.py:1527
  (148 other events, 1152.8 us)

commit v6 on v5

--- a/solution.py
+++ b/solution.py
@@ -418,16 +418,16 @@
     mixed_ref[...] = mixed[:, :cols]
     branch = dot_nt(mixed, w_ref[...]).astype(BF16)
     if split:
-        keep_ref, send_ref = outs[2:]
         step = pl.program_id(0)
-
-        @pl.when(step < split)
-        def _():
-            send_ref[...] = branch
+        for sent in range(split):
+
+            @pl.when(step == sent)
+            def _(sent=sent):
+                outs[3 + sent][...] = branch
 
         @pl.when(step >= split)
         def _():
-            keep_ref[...] = branch
+            outs[2][...] = branch
     else:
         outs[2][...] = branch
 
@@ -454,6 +454,9 @@
 
     block = pl.BlockSpec((ROWS, wide), lambda i: (part * windows + place(i), 0))
     specs, shapes = split_specs(windows, split, width)
+    if split:
+        one = struct((ROWS, width), BF16)
+        specs, shapes = specs[:1] + [whole(one)] * split, shapes[:1] + [one] * split
     return pl.pallas_call(
         partial(attend_kernel, heads, split),
         grid=(windows,),
@@ -1318,32 +1321,34 @@
         a0 = attention(0, q, k, v, weights)
         oz2, ox1, a0 = sync(oz2, ox1, a0)
         oz3, ox2 = over_z(oz2), over_x(oz2)
-        came0 = over_core(a0[3])
-        (passed0,) = combine((rows, [second(a0[2], came0)]))
+        came0, came_y = over_core(a0[3]), over_core(a0[4])
+        (passed0,) = combine((rows, [(0, 0, *rows, [(a0[2], (1,), 0), (came_y, (0,), 0)])]))
         crossed0 = over_y(passed0)
         a1 = attention(1, tie(q, passed0), k, v, weights)
-        oz3, ox2, crossed0, a1 = sync(oz3, ox2, crossed0, a1)
-        ox3 = over_x(oz3)
-        came1 = over_core(a1[3])
-        (passed1,) = combine((rows, [second(a1[2], came1)]))
+        crossed0, a1 = sync(crossed0, a1)
+        came_y, came1 = over_core(a1[4]), over_core(a1[3])
+        (passed1,) = combine((rows, [(0, 0, *rows, [(a1[2], (1,), 0), (came_y, (0,), 0)])]))
         crossed1 = over_y(passed1)
-        after0, own0 = second_norm(0, tie(a0[2], passed1), came0, crossed0)
+        after0, own0 = second_norm(0, tie(a0[2], passed1, came1), came0, crossed0)
         across0 = over_y(own0)
+        oz3, ox2 = sync(oz3, ox2, own0)[:2]
+        ox3, ox4 = over_x(oz3[: share // 2]), over_x(oz3[share // 2 :])
         attended = [a0, a1]
         after1, own1 = second_norm(1, tie(a1[2], own0), came1, crossed1)
-        ox3, across0, own1 = sync(ox3, across0, own1)
-        other_weights = [other_piece, ox0, oz1, ox1, oz2, ox2, oz3, ox3]
+        ox3, ox4, across0, own1 = sync(ox3, ox4, across0, own1)
+        other_weights = [other_piece, ox0, oz1, ox1, oz2, ox2, oz3, ox3, ox4]
+        other_offsets = jnp.concatenate([offsets, offsets[7:] + share // 2])
         across1 = over_y(own1)
-        pieces0 = spread(own0, across0)
-
-        m0 = mlp(offsets, pieces0, other_weights, grad_top, 0, up_local, after0, bias_down, True)
+        pieces0 = spread(tie(own0, own1), across0)
+
+        m0 = mlp(other_offsets, pieces0, other_weights, grad_top, 0, up_local, after0, bias_down, True)
         across1, m0 = sync(across1, m0)
         pieces1 = spread(own1, across1)
         came0, out_came0 = over_core(m0[5]), over_core(m0[7])
         (passed0,) = combine((rows, [second(m0[4], came0)]))
         crossed0 = over_y(passed0)
         pieces1[0] = tie(pieces1[0], passed0)
-        m1 = mlp(offsets, pieces1, other_weights, grad_top, 1, up_local, after1, bias_down, True)
+        m1 = mlp(other_offsets, pieces1, other_weights, grad_top, 1, up_local, after1, bias_down, True)
         crossed0, out_came0, m1 = sync(crossed0, out_came0, m1)
         mlps = [m0, m1]
         came1, out_came1 = over_core(m1[5]), over_core(m1[7])
@@ -1410,9 +1415,6 @@
         came1, vector_came, vector = sync(came1, vector_came, vector)
         vector = vector + vector_came
         vector_came = lax.ppermute(vector, "mp", [(m, m ^ 2) for m in range(4)])
-        vector_came, vector, held = sync(vector_came, vector, held)
-        vector = vector + vector_came
-        vector_came = lax.ppermute(vector, "dp", [(d, d ^ 2) for d in range(8)])
         down_held = held
         passed1, down_other, up_held = combine(
             (rows, [second(b1[5], came1)]),
@@ -1430,11 +1432,8 @@
         left = tie(b0, passed1)
         out_crossed1 = over_y(tie(out_passed1, passed1))
         firsts = weight_grad(targets, first_groups([left, b1], attended), share, 3)
-        crossed1, down_other, up_held, vector, vector_came, firsts = sync(
-            crossed1, down_other, up_held, vector, vector_came, firsts
-        )
+        crossed1, down_other, up_held, firsts = sync(crossed1, down_other, up_held, firsts)
         first_three, first_two, first_last, first_keep = firsts
-        vector = vector + vector_came
 
         came_three = over_x(first_three)
         (up_sum,) = combine(
@@ -1461,7 +1460,7 @@
             own_valid,
             gain_one,
         )
-        in_across = over_y(own)
+        in_across = over_y(tie(own, vector_came))
         (out_own,) = combine(
             (
                 (2 * ROWS, width),
@@ -1481,7 +1480,10 @@
                 ],
             ),
         )
-        came_three, held, own, out_own, vector = sync(came_three, held, own, out_own, vector)
+        came_three, held, own, out_own, vector, vector_came = sync(
+            came_three, held, own, out_own, vector, vector_came
+        )
+        vector = vector + vector_came
         came_two = over_x(first_two)
         (held,) = combine(
             (
@@ -1499,7 +1501,7 @@
             ),
         )
         held = over_z(held)
-        vector_came = lax.ppermute(vector, "dp", [(d, d ^ 4) for d in range(8)])
+        vector_came = lax.ppermute(vector, "dp", [(d, d ^ 2) for d in range(8)])
         out_across = over_y(tie(out_own, own))
         came_two, held, vector_came, in_across = sync(came_two, held, vector_came, in_across)
         vector = vector + vector_came
@@ -1516,15 +1518,16 @@
 
         (held,) = combine(((share, 4 * cols), [first_cell(2, held)]))
         held = over_z(held)
-        vector_came = lax.ppermute(vector, "dp", [(d, d ^ 1) for d in range(8)])
+        vector_came = lax.ppermute(vector, "dp", [(d, d ^ 4) for d in range(8)])
         in_pieces = spread(own, in_across)
         input_grad = place_windows(local, in_pieces)
         held, vector_came, input_grad = sync(held, vector_came, input_grad)
         vector = vector + vector_came
+        vector_came = lax.ppermute(vector, "dp", [(d, d ^ 1) for d in range(8)])
         came_last = over_x(tie(first_last, held))
         (held,) = combine(((share, 4 * cols), [first_cell(1, held)]))
-        vector = tie(vector, held)
         held = over_z(held)
+        vector = vector + vector_came
         came_last, out_own, out_across = sync(came_last, out_own, out_across)
         out_pieces = spread(out_own, out_across)
         block_output = write_output(local, places_all, lives_all, out_pieces)

time: 407 us -> 398 us (0.978)
  waiting for transfers between devices: 104 us -> 94 us
    ppermute x1, waiting for transfers between devices: 0.01 us -> 17.5 us  [body(): vector_came = lax.ppermute(vector, 'dp', [(d, d ^ 2) for d in range(8)])]
    ppermute x1, waiting for transfers between devices: 17.1 us -> 7.52 us  [body(): vector_came = lax.ppermute(vector, 'dp', [(d, d ^ 4) for d in range(8)])]
    ppermute x4 -> x7, waiting for transfers between devices: 3.61 us -> 12.9 us  [the longest x2 9.27 us: body(): ox3, ox4 = (over_x(oz3[:share // 2]), over_x(oz3[share // 2:]))]
    ppermute x4, waiting for transfers between devices: 7.92 us -> 0.01 us  [body(): held = over_z(held)]
    ppermute x1, waiting for transfers between devices: 7.88 us -> 0.01 us  [body(): across0 = over_y(own0)]
    ppermute x3, waiting for transfers between devices: 11.9 us -> 7.04 us  [body(): crossed1 = over_y(passed1)]
    ppermute x2, waiting for transfers between devices: 7.53 us -> 2.98 us  [body(): oz3, ox2 = (over_z(oz2), over_x(oz2))]
  transfers between devices with their start and end apart: 67 -> 70, of which waited for: 28 -> 34; matrix products, arithmetic and copies ran while one was open for 7% -> 7% of each run, Pallas kernels for 42% -> 43%
where the time goes in v6:
time: 398 us; the launch traced here: 391 us
  Pallas kernels  174 us (44%)
  waiting for transfers between devices  94 us (24%)
  local copies, waits for them, and re-layouts  62.9 us (16%)
  starting transfers between devices  49.3 us (12%)
  other arithmetic  8.23 us (2%)
    unnamed x260, local copies, waits for them, and re-layouts  42.2 us
    pallas_call x2, Pallas kernels, mlp(): pl.pallas_call(partial(mlp_kernel, len(pieces), len(weight_pieces), split...  40.6 us
    pallas_call x3, Pallas kernels, weight_grad(): pl.pallas_call(partial(weight_grad_kernel, sizes, share, sends), grid_spe...  32.8 us
    pallas_call x2, Pallas kernels, attend_back(): pl.pallas_call(partial(attend_back_kernel, heads, windows, split, len(pie...  28 us
    pallas_call x2, Pallas kernels, attend(): pl.pallas_call(partial(attend_kernel, heads, split), grid=(windows,), in_...  21.2 us
    ppermute x1, waiting for transfers between devices, body(): vector_came = lax.ppermute(vector, 'dp', [(d, d ^ 2) for d in range(8)])  17.5 us
    reshape x2, local copies, waits for them, and re-layouts, by_window(): array = array.reshape((slots, WTOK) + array.shape[1:])  9.89 us
    pallas_call x1, Pallas kernels, prepare(): pl.pallas_call(partial(prepare_kernel, every), grid_spec=pltpu.PrefetchSc...  9.41 us
  transfers between devices with their start and end apart: 70, of which 34 were waited for; matrix products, arithmetic and copies ran while one was open for 7% of the time, Pallas kernels for 43%

profile of v6, /device:TPU:0, one launch (start us, length us, event | category | flops | bytes accessed | tf_op | source)
XLA Modules:
  0.0 391.0 jit_solution(2233775815291361724)
XLA Ops:
  2.9 3.1 collective-permute-start
  7.9 5.0 %reshape.125.x_ref = bf16[8,196,1280]{2,1,0:T(8,128)(2,1)} reshape(bf16[1568,1280]{1,0:T(8,128)(2,1)} %param.19) | data formatting | bytes 8028160 | tf_op jit(solution)/shard_map/reshape | solution.py:1171
  13.9 4.5 %collective-permute-done.refs_2_ = bf16[160,1344]{1,0:T(8,128)(2,1)} collective-permute-done((bf16[160,1344]{1,0:T(8,128)(2,1)S(1)}, bf16[160,1344]{1,0:T(8,128)(2,1)}, u32[]{:S(2)}, u32[]{:S(2)}) %collective-permute-start) | collective-permute-done | bytes 430112 | tf_op jit(solution)/shard_map/ppermute | solution.py:1296
  23.5 9.4 %prepare.1 = (bf16[416,1280]{1,0:T(8,128)(2,1)}, f32[416,1]{1,0:T(8,128)}, bf16[1664,1280]{1,0:T(8,128)(2,1)}, f32[1664,1]{1,0:T(8,128)}) custom-call(s32[8]{0:T(128)} %stack.112.order, s32[8]{0:T(128)} %places.5, s32[8]{0:T(128)} %lives.5, bf16[8,196,1280]{2,1,0:T(8,128)(2,1)} %reshape.125.x_ref, f32[1,1280]{1,0:T(1,128)} %reshape.126.gain_ref.refs_10_, ...), custom_call_target="tpu_custom_call" | custom-call | flops 450000000 | bytes 90000 | tf_op jit(solution)/shard_map/prepare/pallas_call | solution.py:115
  32.9 1.6 collective-permute-start.4
  35.0 4.9 %reshape.132.top_ref = bf16[8,196,1280]{2,1,0:T(8,128)(2,1)} reshape(bf16[1568,1280]{1,0:T(8,128)(2,1)} %param.36) | data formatting | bytes 8028160 | tf_op jit(solution)/shard_map/reshape | solution.py:1171
  40.0 5.6 %collective-permute-done.4.refs_6_ = bf16[160,1344]{1,0:T(8,128)(2,1)} collective-permute-done((bf16[160,1344]{1,0:T(8,128)(2,1)}, bf16[160,1344]{1,0:T(8,128)(2,1)}, u32[]{:S(2)}, u32[]{:S(2)}) %collective-permute-start.4) | collective-permute-done | bytes 430112 | tf_op jit(solution)/shard_map/ppermute | solution.py:1305
  47.3 7.7 %mask_rows.1.refs_14_.refs_4_.refs_0_.refs_2_ = bf16[1664,1280]{1,0:T(8,128)(2,1)} custom-call(s32[8]{0:T(128)} %stack.112.order, s32[8]{0:T(128)} %places.5, s32[8]{0:T(128)} %lives.5, bf16[8,196,1280]{2,1,0:T(8,128)(2,1)} %reshape.132.top_ref), custom_call_target="tpu_custom_call" | custom-call | flops 300000000 | bytes 60000 | tf_op jit(solution)/shard_map/mask_rows/pallas_call | solution.py:149
  55.0 2.1 collective-permute-done.7.refs_7_
  59.2 2.2 copy-done.1
  64.5 8.2 %qkv.1 = (bf16[1664,384]{1,0:T(8,128)(2,1)S(1)}, bf16[1664,384]{1,0:T(8,128)(2,1)S(1)}, bf16[1664,384]{1,0:T(8,128)(2,1)S(1)}, bf16[1280,1344]{1,0:T(8,128)(2,1)S(1)}) custom-call(s32[8]{0:T(128)S(1)} %stack.121.offsets, bf16[160,1344]{1,0:T(8,128)(2,1)S(1)} %copy-done.61, bf16[160,1344]{1,0:T(8,128)(2,1)S(1)} %copy-done.88, ...), custom_call_target="tpu_custom_call" | custom-call | flops 700000000 | bytes 140000 | tf_op jit(solution)/shard_map/qkv/pallas_call | solution.py:321
  72.7 2.5 collective-permute-done.8.refs_5_
  76.3 10.6 %attend.2 = (bf16[832,320]{1,0:T(8,128)(2,1)S(1)}, bf16[832,1024]{1,0:T(8,128)(2,1)S(1)}, bf16[416,1280]{1,0:T(8,128)(2,1)S(1)}, bf16[208,1280]{1,0:T(8,128)(2,1)S(1)}, bf16[208,1280]{1,0:T(8,128)(2,1)S(1)}) custom-call(bf16[1664,384]{1,0:T(8,128)(2,1)S(1)} %get-tuple-element.275.q_ref.refs_4_, bf16[1664,384]{1,0:T(8,128)(2,1)S(1)} %get-tuple-element.262.k_ref.refs_5_, ...), custom_call_target="tpu_custom_call" | custom-call | flops 675000000 | bytes 135000 | tf_op jit(solution)/shard_map/attend/pallas_call | solution.py:460
  88.1 3.1 collective-permute-done.10.refs_7_
  91.8 1.9 collective-permute-done.13.refs_1_
  93.9 1.6 collective-permute-start.14
  96.8 10.6 %attend.3 = (bf16[832,320]{1,0:T(8,128)(2,1)S(1)}, bf16[832,1024]{1,0:T(8,128)(2,1)S(1)}, bf16[416,1280]{1,0:T(8,128)(2,1)S(1)}, bf16[208,1280]{1,0:T(8,128)(2,1)S(1)}, bf16[208,1280]{1,0:T(8,128)(2,1)S(1)}) custom-call(bf16[1664,384]{1,0:T(8,128)(2,1)S(1)} %get-tuple-element.275.q_ref.refs_4_, bf16[1664,384]{1,0:T(8,128)(2,1)S(1)} %get-tuple-element.262.k_ref.refs_5_, ...), custom_call_target="tpu_custom_call" | custom-call | flops 675000000 | bytes 135000 | tf_op jit(solution)/shard_map/attend/pallas_call | solution.py:460
  114.4 3.0 collective-permute-done.11.refs_10_
  119.6 6.2 %collective-permute-done.21.refs_2_ = bf16[208,1280]{1,0:T(8,128)(2,1)S(1)} collective-permute-done((bf16[208,1280]{1,0:T(8,128)(2,1)S(1)}, bf16[208,1280]{1,0:T(8,128)(2,1)S(1)}, u32[]{:S(2)}, u32[]{:S(2)}) %collective-permute-start.21) | collective-permute-done | bytes 532512 | tf_op jit(solution)/shard_map/ppermute | solution.py:1331
  127.4 2.5 collective-permute-done.18.refs_11_
  130.0 6.7 %collective-permute-done.19.refs_12_ = bf16[80,2560]{1,0:T(8,128)(2,1)S(1)} collective-permute-done((bf16[80,2560]{1,0:T(8,128)(2,1)S(1)}, bf16[80,2560]{1,0:T(8,128)(2,1)S(1)}, u32[]{:S(2)}, u32[]{:S(2)}) %collective-permute-start.19) | collective-permute-done | bytes 409632 | tf_op jit(solution)/shard_map/ppermute | solution.py:1335
  139.7 20.2 %mlp.2 = (bf16[832,1280]{1,0:T(8,128)(2,1)}, bf16[832,1280]{1,0:T(8,128)(2,1)}, bf16[832,1280]{1,0:T(8,128)(2,1)}, f32[1,1280]{1,0:T(1,128)S(1)}, bf16[416,1280]...) custom-call(s32[9]{0:T(128)S(1)} %concatenate.18.offsets, ...), custom_call_target="tpu_custom_call" | custom-call | flops 1050000000 | bytes 210000 | tf_op jit(solution)/shard_map/mlp/pallas_call | solution.py:729
  161.0 1.9 collective-permute-done.25.refs_1_
  166.0 20.4 %mlp.3 = (bf16[832,1280]{1,0:T(8,128)(2,1)}, bf16[832,1280]{1,0:T(8,128)(2,1)}, bf16[832,1280]{1,0:T(8,128)(2,1)}, f32[1,1280]{1,0:T(1,128)S(1)}, bf16[416,1280]...) custom-call(s32[9]{0:T(128)S(1)} %concatenate.18.offsets, ...), custom_call_target="tpu_custom_call" | custom-call | flops 1050000000 | bytes 210000 | tf_op jit(solution)/shard_map/mlp/pallas_call | solution.py:729
  187.0 1.9 norm_two_back.2
  192.3 1.7 combine.15
  195.7 2.2 copy-done
  197.9 10.0 %weight_grad.3.refs_0_.refs_2_.refs_4_ = bf16[4,2,160,1280]{3,2,1,0:T(8,128)(2,1)S(1)} custom-call(s32[8]{0:T(128)S(1)} %stack.131.targets, bf16[1664,1280]{1,0:T(8,128)(2,1)S(1)} %copy-done, bf16[832,1280]{1,0:T(8,128)(2,1)S(1)} %copy-done.45, bf16[1664,1280]{1,0:T(8,128)(2,1)S(1)} %copy-done, bf16[832,1280]{1,0:T(8,128)(2,1)S(1)} %copy-done.48), custom_call_target="tpu_custom_call" | custom-call | flops 650000000 | bytes 130000 | tf_op jit(solution)/shard_map/weight_grad/pallas_call | solution.py:877
  210.1 1.6 copy-done.53
  211.7 10.8 %weight_grad.4 = (bf16[2,160,1280]{2,1,0:T(8,128)(2,1)}, bf16[2,160,1280]{2,1,0:T(8,128)(2,1)S(1)}, bf16[4,160,1280]{2,1,0:T(8,128)(2,1)S(1)}) custom-call(s32[8]{0:T(128)S(1)} %stack.131.targets, bf16[832,1280]{1,0:T(8,128)(2,1)S(1)} %copy-done.52, bf16[832,1280]{1,0:T(8,128)(2,1)S(1)} %copy-done.51, bf16[832,1280]{1,0:T(8,128)(2,1)S(1)} %copy-done.54, ...), custom_call_target="tpu_custom_call" | custom-call | flops 650000000 | bytes 130000 | tf_op jit(solution)/shard_map/weight_grad/pallas_call | solution.py:877
  224.9 2.4 norm_two_back.3
  228.3 1.9 collective-permute-done.38.refs_1_.refs_3_
  233.5 14.2 %attend_back.2 = (bf16[832,960]{1,0:T(8,128)(2,1)S(1)}, bf16[832,1280]{1,0:T(8,128)(2,1)S(1)}, f32[256,384]{1,0:T(8,128)S(1)}, f32[1,960]{1,0:T(1,128)S(1)}, f32...) custom-call(bf16[208,1280]{1,0:T(8,128)(2,1)} %get-tuple-element.359.refs_0_, ...), custom_call_target="tpu_custom_call" | custom-call | flops 925000000 | bytes 185000 | tf_op jit(solution)/shard_map/attend_back/pallas_call | solution.py:581
  247.8 4.0 %collective-permute-done.39.refs_3_.refs_5_ = bf16[160,2560]{1,0:T(8,128)(2,1)S(1)} collective-permute-done((bf16[160,2560]{1,0:T(8,128)(2,1)S(1)}, bf16[160,2560]{1,0:T(8,128)(2,1)S(1)}, u32[]{:S(2)}, u32[]{:S(2)}) %collective-permute-start.39) | collective-permute-done | bytes 819232 | tf_op jit(solution)/shard_map/ppermute | solution.py:1392
  257.6 13.9 %attend_back.3 = (bf16[832,960]{1,0:T(8,128)(2,1)S(1)}, bf16[832,1280]{1,0:T(8,128)(2,1)S(1)}, f32[256,384]{1,0:T(8,128)S(1)}, f32[1,960]{1,0:T(1,128)S(1)}, f32...) custom-call(bf16[208,1280]{1,0:T(8,128)(2,1)S(1)} %get-tuple-element.380.refs_0_, ...), custom_call_target="tpu_custom_call" | custom-call | flops 925000000 | bytes 185000 | tf_op jit(solution)/shard_map/attend_back/pallas_call | solution.py:581
  276.9 4.4 %collective-permute-done.41.refs_2_ = bf16[208,1280]{1,0:T(8,128)(2,1)S(1)} collective-permute-done((bf16[208,1280]{1,0:T(8,128)(2,1)S(1)}, bf16[208,1280]{1,0:T(8,128)(2,1)S(1)}, u32[]{:S(2)}, u32[]{:S(2)}) %collective-permute-start.41) | collective-permute-done | bytes 532512 | tf_op jit(solution)/shard_map/ppermute | solution.py:1403
  292.0 2.2 combine.18
  302.4 12.0 %weight_grad.5 = (bf16[1,160,1280]{2,1,0:T(8,128)(2,1)S(1)}, bf16[2,160,1280]{2,1,0:T(8,128)(2,1)S(1)}, bf16[1,160,1280]{2,1,0:T(8,128)(2,1)S(1)}, bf16[4,160,1280]{2,1,0:T(8,128)(2,1)S(1)}) custom-call(s32[8]{0:T(128)S(1)} %stack.131.targets, bf16[1664,1280]{1,0:T(8,128)(2,1)S(1)} %bitcast.83, bf16[832,960]{1,0:T(8,128)(2,1)S(1)} %copy-done.68, ...), custom_call_target="tpu_custom_call" | custom-call | flops 650000000 | bytes 130000 | tf_op jit(solution)/shard_map/weight_grad/pallas_call | solution.py:877
  318.6 3.0 norm_one_back.1.refs_0_
  324.1 2.4 combine.20.refs_0_
  326.5 2.3 collective-permute-done.54.refs_4_
  329.5 4.1 %collective-permute-start.57 = (bf16[160,2560]{1,0:T(8,128)(2,1)S(1)}, bf16[160,2560]{1,0:T(8,128)(2,1)S(1)}, u32[]{:S(2)}, u32[]{:S(2)}) collective-permute-start(bf16[160,2560]{1,0:T(8,128)(2,1)S(1)} %combine.21), channel_id=1, source_target_pairs={{0,8},{4,12},{8,16},{12,20},{16,24},{20,28},{24,0},{28,4},{1,9},{5... | collective-permute-start | bytes 2457608 | tf_op jit(solution)/shard_map/ppermute | solution.py:1503
  333.8 17.5 %collective-permute-done.58 = f32[160,128]{1,0:T(8,128)S(1)} collective-permute-done((f32[160,128]{1,0:T(8,128)S(1)}, f32[160,128]{1,0:T(8,128)S(1)}, u32[]{:S(2)}, u32[]{:S(2)}) %collective-permute-start.58) | collective-permute-done | bytes 81952 | tf_op jit(solution)/shard_map/ppermute | solution.py:1504
  352.7 2.0 fusion.1
  355.4 4.6 %place_windows.1 = f32[1568,1280]{1,0:T(8,128)} custom-call(s32[4]{0:T(128)S(1)} %pad_add_fusion.1.order, bf16[416,1280]{1,0:T(8,128)(2,1)S(1)} %norm_one_back.1.refs_0_, bf16[416,1280]{1,0:T(8,128)(2,1)S(1)} %collective-permute-done.59.refs_1_, bf16[416,1280]{1,0:T(8,128)(2,1)S(1)} %collective-permute-done.62.refs_2_, ...), custom_call_target="tpu_custom_call" | custom-call | flops 350000000 | bytes 70000 | tf_op jit(solution)/shard_map/place_windows/pallas_call | solution.py:953
  360.0 7.5 %collective-permute-done.61 = f32[160,128]{1,0:T(8,128)S(1)} collective-permute-done((f32[160,128]{1,0:T(8,128)S(1)}, f32[160,128]{1,0:T(8,128)S(1)}, u32[]{:S(2)}, u32[]{:S(2)}) %collective-permute-start.61) | collective-permute-done | bytes 81952 | tf_op jit(solution)/shard_map/ppermute | solution.py:1521
  374.6 6.2 %collective-permute-done.65.refs_1_ = bf16[416,1280]{1,0:T(8,128)(2,1)S(1)} collective-permute-done((bf16[416,1280]{1,0:T(8,128)(2,1)}, bf16[416,1280]{1,0:T(8,128)(2,1)S(1)}, u32[]{:S(2)}, u32[]{:S(2)}) %collective-permute-start.65) | collective-permute-done | bytes 1064992 | tf_op jit(solution)/shard_map/ppermute | solution.py:1505
  386.2 4.6 %write_output.1 = bf16[1568,1280]{1,0:T(8,128)(2,1)} custom-call(s32[4]{0:T(128)S(1)} %pad_add_fusion.1.order, s32[8]{0:T(128)S(1)} %copy-done.95, s32[8]{0:T(128)S(1)} %copy-done.96, bf16[416,1280]{1,0:T(8,128)(2,1)} %combine.20.refs_0_, bf16[416,1280]{1,0:T(8,128)(2,1)S(1)} %collective-permute-done.65.refs_1_, ...), custom_call_target="tpu_custom_call" | custom-call | flops 350000000 | bytes 70000 | tf_op jit(solution)/shard_map/write_output/pallas_call | solution.py:988
  (455 shorter events, 105.9 us)
Async XLA Ops:
  2.9 15.6 %collective-permute-start = (bf16[160,1344]{1,0:T(8,128)(2,1)S(1)}, bf16[160,1344]{1,0:T(8,128)(2,1)}, u32[]{:S(2)}, u32[]{:S(2)}) collective-permute-start(bf16[160,1344]{1,0:T(8,128)(2,1)S(1)} %concatenate.16.refs_0_), channel_id=1, source_target_pairs={{0,8},{4,12},{8,16},{12,20},{16,24},{20,28},{24,0},{28,4},{1,9},{5... | collective-permute-start | bytes 1290248 | tf_op jit(solution)/shard_map/ppermute | solution.py:1296
  5.9 12.5 %collective-permute-start.1 = (bf16[160,1344]{1,0:T(8,128)(2,1)S(1)}, bf16[160,1344]{1,0:T(8,128)(2,1)S(1)}, u32[]{:S(2)}, u32[]{:S(2)}) collective-permute-start(bf16[160,1344]{1,0:T(8,128)(2,1)S(1)} %concatenate.16.refs_0_), channel_id=1, source_target_pairs={{0,4},{4,0},{8,12},{12,8},{16,20},{20,16},{24,28},{28,24},{1,5},{5... | collective-permute-start | bytes 1290248 | tf_op jit(solution)/shard_map/ppermute | solution.py:1296
  19.2 13.7 %collective-permute-start.2 = (bf16[160,1344]{1,0:T(8,128)(2,1)}, bf16[160,1344]{1,0:T(8,128)(2,1)}, u32[]{:S(2)}, u32[]{:S(2)}) collective-permute-start(bf16[160,1344]{1,0:T(8,128)(2,1)} %collective-permute-done.refs_2_), channel_id=1, source_target_pairs={{0,8},{4,12},{8,16},{12,20},{16,24},{20,28},{24,0},{28,4},{1,9},{5... | collective-permute-start | bytes 1290248 | tf_op jit(solution)/shard_map/ppermute | solution.py:1300
  20.1 12.8 %collective-permute-start.3 = (bf16[160,1344]{1,0:T(8,128)(2,1)}, bf16[160,1344]{1,0:T(8,128)(2,1)}, u32[]{:S(2)}, u32[]{:S(2)}) collective-permute-start(bf16[160,1344]{1,0:T(8,128)(2,1)} %collective-permute-done.refs_2_), channel_id=1, source_target_pairs={{0,4},{4,0},{8,12},{12,8},{16,20},{20,16},{24,28},{28,24},{1,5},{5... | collective-permute-start | bytes 1290248 | tf_op jit(solution)/shard_map/ppermute | solution.py:1300
  32.9 12.7 %collective-permute-start.4 = (bf16[160,1344]{1,0:T(8,128)(2,1)}, bf16[160,1344]{1,0:T(8,128)(2,1)}, u32[]{:S(2)}, u32[]{:S(2)}) collective-permute-start(bf16[160,1344]{1,0:T(8,128)(2,1)} %collective-permute-done.2.refs_4_), channel_id=1, source_target_pairs={{0,8},{4,12},{8,16},{12,20},{16,24},{20,28},{24,0},{28,4},{1,9},{5... | collective-permute-start | bytes 1290248 | tf_op jit(solution)/shard_map/ppermute | solution.py:1305
  34.5 11.1 %collective-permute-start.5 = (bf16[160,1344]{1,0:T(8,128)(2,1)}, bf16[160,1344]{1,0:T(8,128)(2,1)S(1)}, u32[]{:S(2)}, u32[]{:S(2)}) collective-permute-start(bf16[160,1344]{1,0:T(8,128)(2,1)} %collective-permute-done.2.refs_4_), channel_id=1, source_target_pairs={{0,4},{4,0},{8,12},{12,8},{16,20},{20,16},{24,28},{28,24},{1,5},{5... | collective-permute-start | bytes 1290248 | tf_op jit(solution)/shard_map/ppermute | solution.py:1305
  47.3 25.4 %collective-permute-start.6 = (bf16[160,2560]{1,0:T(8,128)(2,1)S(1)}, bf16[160,2560]{1,0:T(8,128)(2,1)}, u32[]{:S(2)}, u32[]{:S(2)}) collective-permute-start(bf16[160,2560]{1,0:T(8,128)(2,1)S(1)} %pad_maximum_fusion.refs_4_), channel_id=1, source_target_pairs={{0,8},{4,12},{8,16},{12,20},{16,24},{20,28},{24,0},{28,4},{1,9},{5... | collective-permute-start | bytes 2457608 | tf_op jit(solution)/shard_map/ppermute | solution.py:1310
  57.1 18.2 %collective-permute-start.8 = (bf16[160,2560]{1,0:T(8,128)(2,1)S(1)}, bf16[160,2560]{1,0:T(8,128)(2,1)S(1)}, u32[]{:S(2)}, u32[]{:S(2)}) collective-permute-start(bf16[160,2560]{1,0:T(8,128)(2,1)S(1)} %pad_maximum_fusion.refs_4_), channel_id=1, source_target_pairs={{0,4},{4,0},{8,12},{12,8},{16,20},{20,16},{24,28},{28,24},{1,5},{5... | collective-permute-start | bytes 2457608 | tf_op jit(solution)/shard_map/ppermute | solution.py:1315
  75.2 16.0 %collective-permute-start.10 = (bf16[160,2560]{1,0:T(8,128)(2,1)}, bf16[160,2560]{1,0:T(8,128)(2,1)S(1)}, u32[]{:S(2)}, u32[]{:S(2)}) collective-permute-start(bf16[160,2560]{1,0:T(8,128)(2,1)} %collective-permute-done.6.refs_6_), channel_id=1, source_target_pairs={{0,4},{4,0},{8,12},{12,8},{16,20},{20,16},{24,28},{28,24},{1,5},{5... | collective-permute-start | bytes 2457608 | tf_op jit(solution)/shard_map/ppermute | solution.py:1320
  76.2 15.6 %collective-permute-start.9 = (bf16[160,2560]{1,0:T(8,128)(2,1)}, bf16[160,2560]{1,0:T(8,128)(2,1)S(1)}, u32[]{:S(2)}, u32[]{:S(2)}) collective-permute-start(bf16[160,2560]{1,0:T(8,128)(2,1)} %collective-permute-done.6.refs_6_), channel_id=1, source_target_pairs={{0,8},{4,12},{8,16},{12,20},{16,24},{20,28},{24,0},{28,4},{1,9},{5... | collective-permute-start | bytes 2457608 | tf_op jit(solution)/shard_map/ppermute | solution.py:1320
  93.9 14.8 %collective-permute-start.14 = (bf16[208,1280]{1,0:T(8,128)(2,1)S(1)}, bf16[208,1280]{1,0:T(8,128)(2,1)S(1)}, u32[]{:S(2)}, u32[]{:S(2)}) collective-permute-start(bf16[208,1280]{1,0:T(8,128)(2,1)S(1)} %combine.12), channel_id=1, source_target_pairs={{0,2},{1,3},{2,0},{3,1},{4,6},{5,7},{6,4},{7,5},{8,10},{9,11},{10,... | collective-permute-start | bytes 1597448 | tf_op jit(solution)/shard_map/ppermute | solution.py:1326
  95.5 22.0 %collective-permute-start.11 = (bf16[160,2560]{1,0:T(8,128)(2,1)S(1)}, bf16[160,2560]{1,0:T(8,128)(2,1)S(1)}, u32[]{:S(2)}, u32[]{:S(2)}) collective-permute-start(bf16[160,2560]{1,0:T(8,128)(2,1)S(1)} %collective-permute-done.9.refs_8_), channel_id=1, source_target_pairs={{0,8},{4,12},{8,16},{12,20},{16,24},{20,28},{24,0},{28,4},{1,9},{5... | collective-permute-start | bytes 2457608 | tf_op jit(solution)/shard_map/ppermute | solution.py:1323
  95.6 21.8 %collective-permute-start.12 = (bf16[160,2560]{1,0:T(8,128)(2,1)S(1)}, bf16[160,2560]{1,0:T(8,128)(2,1)S(1)}, u32[]{:S(2)}, u32[]{:S(2)}) collective-permute-start(bf16[160,2560]{1,0:T(8,128)(2,1)S(1)} %collective-permute-done.9.refs_8_), channel_id=1, source_target_pairs={{0,4},{4,0},{8,12},{12,8},{16,20},{20,16},{24,28},{28,24},{1,5},{5... | collective-permute-start | bytes 2457608 | tf_op jit(solution)/shard_map/ppermute | solution.py:1323
  110.8 15.0 %collective-permute-start.21 = (bf16[208,1280]{1,0:T(8,128)(2,1)S(1)}, bf16[208,1280]{1,0:T(8,128)(2,1)S(1)}, u32[]{:S(2)}, u32[]{:S(2)}) collective-permute-start(bf16[208,1280]{1,0:T(8,128)(2,1)S(1)} %combine.13), channel_id=1, source_target_pairs={{0,2},{1,3},{2,0},{3,1},{4,6},{5,7},{6,4},{7,5},{8,10},{9,11},{10,... | collective-permute-start | bytes 1597448 | tf_op jit(solution)/shard_map/ppermute | solution.py:1331
  113.5 23.2 %collective-permute-start.20 = (bf16[208,1280]{1,0:T(8,128)(2,1)}, bf16[208,1280]{1,0:T(8,128)(2,1)}, u32[]{:S(2)}, u32[]{:S(2)}) collective-permute-start(bf16[208,1280]{1,0:T(8,128)(2,1)} %get-tuple-element.296.refs_0_), channel_id=1, source_target_pairs={{0,2},{1,3},{2,0},{3,1},{4,6},{5,7},{6,4},{7,5},{8,10},{9,11},{10,... | collective-permute-start | bytes 1597448 | tf_op jit(solution)/shard_map/ppermute | solution.py:1333
  117.5 12.5 %collective-permute-start.18 = (bf16[80,2560]{1,0:T(8,128)(2,1)S(1)}, bf16[80,2560]{1,0:T(8,128)(2,1)S(1)}, u32[]{:S(2)}, u32[]{:S(2)}) collective-permute-start(bf16[80,2560]{1,0:T(8,128)(2,1)S(1)} %get-tuple-element.467), channel_id=1, source_target_pairs={{0,4},{4,0},{8,12},{12,8},{16,20},{20,16},{24,28},{28,24},{1,5},{5... | collective-permute-start | bytes 1228808 | tf_op jit(solution)/shard_map/ppermute | solution.py:1335
  118.7 18.0 %collective-permute-start.19 = (bf16[80,2560]{1,0:T(8,128)(2,1)S(1)}, bf16[80,2560]{1,0:T(8,128)(2,1)S(1)}, u32[]{:S(2)}, u32[]{:S(2)}) collective-permute-start(bf16[80,2560]{1,0:T(8,128)(2,1)S(1)} %get-tuple-element.466), channel_id=1, source_target_pairs={{0,4},{4,0},{8,12},{12,8},{16,20},{20,16},{24,28},{28,24},{1,5},{5... | collective-permute-start | bytes 1228808 | tf_op jit(solution)/shard_map/ppermute | solution.py:1335
  137.2 22.7 %collective-permute-start.22 = (bf16[208,1280]{1,0:T(8,128)(2,1)S(1)}, bf16[208,1280]{1,0:T(8,128)(2,1)}, u32[]{:S(2)}, u32[]{:S(2)}) collective-permute-start(bf16[208,1280]{1,0:T(8,128)(2,1)S(1)} %get-tuple-element.317.refs_0_), channel_id=1, source_target_pairs={{0,2},{1,3},{2,0},{3,1},{4,6},{5,7},{6,4},{7,5},{8,10},{9,11},{10,... | collective-permute-start | bytes 1597448 | tf_op jit(solution)/shard_map/ppermute | solution.py:1341
  160.1 26.3 %collective-permute-start.27 = (bf16[416,1280]{1,0:T(8,128)(2,1)}, bf16[416,1280]{1,0:T(8,128)(2,1)S(1)}, u32[]{:S(2)}, u32[]{:S(2)}) collective-permute-start(bf16[416,1280]{1,0:T(8,128)(2,1)} %get-tuple-element.316), channel_id=1, source_target_pairs={{0,1},{1,0},{2,3},{3,2},{4,5},{5,4},{6,7},{7,6},{8,9},{9,8},{10,11... | collective-permute-start | bytes 3194888 | tf_op jit(solution)/shard_map/ppermute | solution.py:1347
  164.3 22.1 %collective-permute-start.26 = (bf16[208,1280]{1,0:T(8,128)(2,1)S(1)}, bf16[208,1280]{1,0:T(8,128)(2,1)S(1)}, u32[]{:S(2)}, u32[]{:S(2)}) collective-permute-start(bf16[208,1280]{1,0:T(8,128)(2,1)S(1)} %combine.14), channel_id=1, source_target_pairs={{0,2},{1,3},{2,0},{3,1},{4,6},{5,7},{6,4},{7,5},{8,10},{9,11},{10,... | collective-permute-start | bytes 1597448 | tf_op jit(solution)/shard_map/ppermute | solution.py:1349
  190.0 17.9 %collective-permute-start.31 = (bf16[208,1280]{1,0:T(8,128)(2,1)}, bf16[208,1280]{1,0:T(8,128)(2,1)}, u32[]{:S(2)}, u32[]{:S(2)}) collective-permute-start(bf16[208,1280]{1,0:T(8,128)(2,1)} %get-tuple-element.359.refs_0_), channel_id=1, source_target_pairs={{0,2},{1,3},{2,0},{3,1},{4,6},{5,7},{6,4},{7,5},{8,10},{9,11},{10,... | collective-permute-start | bytes 1597448 | tf_op jit(solution)/shard_map/ppermute | solution.py:1356
  208.0 22.2 %collective-permute-start.38 = (bf16[2,160,1280]{2,1,0:T(8,128)(2,1)S(1)}, bf16[2,160,1280]{2,1,0:T(8,128)(2,1)S(1)}, u32[]{:S(2)}, u32[]{:S(2)}) collective-permute-start(bf16[2,160,1280]{2,1,0:T(8,128)(2,1)S(1)} %slice_bitcast_fusion), channel_id=1, source_target_pairs={{0,8},{4,12},{8,16},{12,20},{16,24},{20,28},{24,0},{28,4},{1,9},{5... | collective-permute-start | bytes 2457608 | tf_op jit(solution)/shard_map/ppermute | solution.py:1369
  208.9 13.7 %collective-permute-start.34 = (bf16[208,1280]{1,0:T(8,128)(2,1)}, bf16[208,1280]{1,0:T(8,128)(2,1)S(1)}, u32[]{:S(2)}, u32[]{:S(2)}) collective-permute-start(bf16[208,1280]{1,0:T(8,128)(2,1)} %get-tuple-element.359.refs_0_), channel_id=1, source_target_pairs={{0,1},{1,0},{2,3},{3,2},{4,5},{5,4},{6,7},{7,6},{8,9},{9,8},{10,11... | collective-permute-start | bytes 1597448 | tf_op jit(solution)/shard_map/ppermute | solution.py:1289
  208.9 14.5 %collective-permute-start.33 = (bf16[208,1280]{1,0:T(8,128)(2,1)S(1)}, bf16[208,1280]{1,0:T(8,128)(2,1)S(1)}, u32[]{:S(2)}, u32[]{:S(2)}) collective-permute-start(bf16[208,1280]{1,0:T(8,128)(2,1)S(1)} %get-tuple-element.344), channel_id=1, source_target_pairs={{0,2},{1,3},{2,0},{3,1},{4,6},{5,7},{6,4},{7,5},{8,10},{9,11},{10,... | collective-permute-start | bytes 1597448 | tf_op jit(solution)/shard_map/ppermute | solution.py:1365
  209.9 13.5 %collective-permute-start.35 = (bf16[208,1280]{1,0:T(8,128)(2,1)}, bf16[208,1280]{1,0:T(8,128)(2,1)S(1)}, u32[]{:S(2)}, u32[]{:S(2)}) collective-permute-start(bf16[208,1280]{1,0:T(8,128)(2,1)} %collective-permute-done.31.refs_1_), channel_id=1, source_target_pairs={{0,1},{1,0},{2,3},{3,2},{4,5},{5,4},{6,7},{7,6},{8,9},{9,8},{10,11... | collective-permute-start | bytes 1597448 | tf_op jit(solution)/shard_map/ppermute | solution.py:1289
  223.4 24.4 %collective-permute-start.37 = (bf16[2,160,1280]{2,1,0:T(8,128)(2,1)}, bf16[2,160,1280]{2,1,0:T(8,128)(2,1)S(1)}, u32[]{:S(2)}, u32[]{:S(2)}) collective-permute-start(bf16[2,160,1280]{2,1,0:T(8,128)(2,1)} %get-tuple-element.356), channel_id=1, source_target_pairs={{0,4},{4,0},{8,12},{12,8},{16,20},{20,16},{24,28},{28,24},{1,5},{5... | collective-permute-start | bytes 2457608 | tf_op jit(solution)/shard_map/ppermute | solution.py:1374
  230.4 21.3 %collective-permute-start.39 = (bf16[160,2560]{1,0:T(8,128)(2,1)S(1)}, bf16[160,2560]{1,0:T(8,128)(2,1)S(1)}, u32[]{:S(2)}, u32[]{:S(2)}) collective-permute-start(bf16[160,2560]{1,0:T(8,128)(2,1)S(1)} %combine.16), channel_id=1, source_target_pairs={{0,8},{4,12},{8,16},{12,20},{16,24},{20,28},{24,0},{28,4},{1,9},{5... | collective-permute-start | bytes 2457608 | tf_op jit(solution)/shard_map/ppermute | solution.py:1392
  230.5 17.3 %collective-permute-start.36 = (bf16[208,1280]{1,0:T(8,128)(2,1)S(1)}, bf16[208,1280]{1,0:T(8,128)(2,1)S(1)}, u32[]{:S(2)}, u32[]{:S(2)}) collective-permute-start(bf16[208,1280]{1,0:T(8,128)(2,1)S(1)} %get-tuple-element.380.refs_0_), channel_id=1, source_target_pairs={{0,2},{1,3},{2,0},{3,1},{4,6},{5,7},{6,4},{7,5},{8,10},{9,11},{10,... | collective-permute-start | bytes 1597448 | tf_op jit(solution)/shard_map/ppermute | solution.py:1384
  252.3 22.9 %collective-permute-start.43 = (bf16[2,160,1280]{2,1,0:T(8,128)(2,1)S(1)}, bf16[2,160,1280]{2,1,0:T(8,128)(2,1)S(1)}, u32[]{:S(2)}, u32[]{:S(2)}) collective-permute-start(bf16[2,160,1280]{2,1,0:T(8,128)(2,1)S(1)} %copy-done.98), channel_id=1, source_target_pairs={{0,4},{4,0},{8,12},{12,8},{16,20},{20,16},{24,28},{28,24},{1,5},{5... | collective-permute-start | bytes 2457608 | tf_op jit(solution)/shard_map/ppermute | solution.py:1397
  255.4 26.7 %collective-permute-start.42 = (bf16[160,2560]{1,0:T(8,128)(2,1)S(1)}, bf16[160,2560]{1,0:T(8,128)(2,1)S(1)}, u32[]{:S(2)}, u32[]{:S(2)}) collective-permute-start(bf16[160,2560]{1,0:T(8,128)(2,1)S(1)} %get-tuple-element.376), channel_id=1, source_target_pairs={{0,8},{4,12},{8,16},{12,20},{16,24},{20,28},{24,0},{28,4},{1,9},{5... | collective-permute-start | bytes 2457608 | tf_op jit(solution)/shard_map/ppermute | solution.py:1404
  255.5 20.6 %collective-permute-start.44 = (bf16[208,1280]{1,0:T(8,128)(2,1)S(1)}, bf16[208,1280]{1,0:T(8,128)(2,1)S(1)}, u32[]{:S(2)}, u32[]{:S(2)}) collective-permute-start(bf16[208,1280]{1,0:T(8,128)(2,1)S(1)} %copy-done.103), channel_id=1, source_target_pairs={{0,2},{1,3},{2,0},{3,1},{4,6},{5,7},{6,4},{7,5},{8,10},{9,11},{10,... | collective-permute-start | bytes 1597448 | tf_op jit(solution)/shard_map/ppermute | solution.py:1406
  256.0 25.3 %collective-permute-start.41 = (bf16[208,1280]{1,0:T(8,128)(2,1)S(1)}, bf16[208,1280]{1,0:T(8,128)(2,1)S(1)}, u32[]{:S(2)}, u32[]{:S(2)}) collective-permute-start(bf16[208,1280]{1,0:T(8,128)(2,1)S(1)} %get-tuple-element.375), channel_id=1, source_target_pairs={{0,2},{1,3},{2,0},{3,1},{4,6},{5,7},{6,4},{7,5},{8,10},{9,11},{10,... | collective-permute-start | bytes 1597448 | tf_op jit(solution)/shard_map/ppermute | solution.py:1403
  294.2 20.3 %collective-permute-start.49 = (bf16[208,1280]{1,0:T(8,128)(2,1)S(1)}, bf16[208,1280]{1,0:T(8,128)(2,1)S(1)}, u32[]{:S(2)}, u32[]{:S(2)}) collective-permute-start(bf16[208,1280]{1,0:T(8,128)(2,1)S(1)} %get-tuple-element.405), channel_id=1, source_target_pairs={{0,2},{1,3},{2,0},{3,1},{4,6},{5,7},{6,4},{7,5},{8,10},{9,11},{10,... | collective-permute-start | bytes 1597448 | tf_op jit(solution)/shard_map/ppermute | solution.py:1430
  294.6 19.8 %collective-permute-start.50 = (bf16[160,1280]{1,0:T(8,128)(2,1)}, bf16[160,1280]{1,0:T(8,128)(2,1)}, u32[]{:S(2)}, u32[]{:S(2)}) collective-permute-start(bf16[160,1280]{1,0:T(8,128)(2,1)} %get-tuple-element.406), channel_id=1, source_target_pairs={{0,4},{4,0},{8,12},{12,8},{16,20},{20,16},{24,28},{28,24},{1,5},{5... | collective-permute-start | bytes 1228808 | tf_op jit(solution)/shard_map/ppermute | solution.py:1431
  295.7 18.8 %collective-permute-start.51 = (bf16[160,1280]{1,0:T(8,128)(2,1)S(1)}, bf16[160,1280]{1,0:T(8,128)(2,1)S(1)}, u32[]{:S(2)}, u32[]{:S(2)}) collective-permute-start(bf16[160,1280]{1,0:T(8,128)(2,1)S(1)} %get-tuple-element.407), channel_id=1, source_target_pairs={{0,8},{4,12},{8,16},{12,20},{16,24},{20,28},{24,0},{28,4},{1,9},{5... | collective-permute-start | bytes 1228808 | tf_op jit(solution)/shard_map/ppermute | solution.py:1431
  296.2 27.9 %collective-permute-start.55 = (bf16[208,1280]{1,0:T(8,128)(2,1)}, bf16[208,1280]{1,0:T(8,128)(2,1)S(1)}, u32[]{:S(2)}, u32[]{:S(2)}) collective-permute-start(bf16[208,1280]{1,0:T(8,128)(2,1)} %copy-done.101), channel_id=1, source_target_pairs={{0,2},{1,3},{2,0},{3,1},{4,6},{5,7},{6,4},{7,5},{8,10},{9,11},{10,... | collective-permute-start | bytes 1597448 | tf_op jit(solution)/shard_map/ppermute | solution.py:1433
  315.6 13.2 %collective-permute-start.54 = (bf16[160,1280]{1,0:T(8,128)(2,1)S(1)}, bf16[160,1280]{1,0:T(8,128)(2,1)S(1)}, u32[]{:S(2)}, u32[]{:S(2)}) collective-permute-start(bf16[160,1280]{1,0:T(8,128)(2,1)S(1)} %combine.19), channel_id=1, source_target_pairs={{0,8},{4,12},{8,16},{12,20},{16,24},{20,28},{24,0},{28,4},{1,9},{5... | collective-permute-start | bytes 1228808 | tf_op jit(solution)/shard_map/ppermute | solution.py:1453
  316.7 12.6 %collective-permute-start.53 = (bf16[1,160,1280]{2,1,0:T(8,128)(2,1)}, bf16[1,160,1280]{2,1,0:T(8,128)(2,1)S(1)}, u32[]{:S(2)}, u32[]{:S(2)}) collective-permute-start(bf16[1,160,1280]{2,1,0:T(8,128)(2,1)} %copy-done.106), channel_id=1, source_target_pairs={{0,4},{4,0},{8,12},{12,8},{16,20},{20,16},{24,28},{28,24},{1,5},{5... | collective-permute-start | bytes 1228808 | tf_op jit(solution)/shard_map/ppermute | solution.py:1438
  322.3 29.0 %collective-permute-start.59 = (bf16[416,1280]{1,0:T(8,128)(2,1)S(1)}, bf16[416,1280]{1,0:T(8,128)(2,1)S(1)}, u32[]{:S(2)}, u32[]{:S(2)}) collective-permute-start(bf16[416,1280]{1,0:T(8,128)(2,1)S(1)} %norm_one_back.1.refs_0_), channel_id=1, source_target_pairs={{0,2},{1,3},{2,0},{3,1},{4,6},{5,7},{6,4},{7,5},{8,10},{9,11},{10,... | collective-permute-start | bytes 3194888 | tf_op jit(solution)/shard_map/ppermute | solution.py:1463
  323.2 28.2 %collective-permute-start.52 = (bf16[2,160,1280]{2,1,0:T(8,128)(2,1)S(1)}, bf16[2,160,1280]{2,1,0:T(8,128)(2,1)S(1)}, u32[]{:S(2)}, u32[]{:S(2)}) collective-permute-start(bf16[2,160,1280]{2,1,0:T(8,128)(2,1)S(1)} %copy-done.100), channel_id=1, source_target_pairs={{0,4},{4,0},{8,12},{12,8},{16,20},{20,16},{24,28},{28,24},{1,5},{5... | collective-permute-start | bytes 2457608 | tf_op jit(solution)/shard_map/ppermute | solution.py:1487
  329.5 21.8 %collective-permute-start.57 = (bf16[160,2560]{1,0:T(8,128)(2,1)S(1)}, bf16[160,2560]{1,0:T(8,128)(2,1)S(1)}, u32[]{:S(2)}, u32[]{:S(2)}) collective-permute-start(bf16[160,2560]{1,0:T(8,128)(2,1)S(1)} %combine.21), channel_id=1, source_target_pairs={{0,8},{4,12},{8,16},{12,20},{16,24},{20,28},{24,0},{28,4},{1,9},{5... | collective-permute-start | bytes 2457608 | tf_op jit(solution)/shard_map/ppermute | solution.py:1503
  333.7 17.6 %collective-permute-start.58 = (f32[160,128]{1,0:T(8,128)S(1)}, f32[160,128]{1,0:T(8,128)S(1)}, u32[]{:S(2)}, u32[]{:S(2)}) collective-permute-start(f32[160,128]{1,0:T(8,128)S(1)} %add.277), channel_id=1, source_target_pairs={{0,8},{4,12},{8,0},{12,4},{16,24},{20,28},{24,16},{28,20},{1,9},{5... | collective-permute-start | bytes 245768 | tf_op jit(solution)/shard_map/ppermute | solution.py:1504
  333.8 21.6 %collective-permute-start.62 = (bf16[416,1280]{1,0:T(8,128)(2,1)S(1)}, bf16[416,1280]{1,0:T(8,128)(2,1)S(1)}, u32[]{:S(2)}, u32[]{:S(2)}) collective-permute-start(bf16[416,1280]{1,0:T(8,128)(2,1)S(1)} %norm_one_back.1.refs_0_), channel_id=1, source_target_pairs={{0,1},{1,0},{2,3},{3,2},{4,5},{5,4},{6,7},{7,6},{8,9},{9,8},{10,11... | collective-permute-start | bytes 3194888 | tf_op jit(solution)/shard_map/ppermute | solution.py:1289
  351.5 16.0 %collective-permute-start.61 = (f32[160,128]{1,0:T(8,128)S(1)}, f32[160,128]{1,0:T(8,128)S(1)}, u32[]{:S(2)}, u32[]{:S(2)}) collective-permute-start(f32[160,128]{1,0:T(8,128)S(1)} %add.278), channel_id=1, source_target_pairs={{0,16},{4,20},{8,24},{12,28},{16,0},{20,4},{24,8},{28,12},{1,17},{... | collective-permute-start | bytes 245768 | tf_op jit(solution)/shard_map/ppermute | solution.py:1521
  352.7 14.8 %collective-permute-start.60 = (bf16[160,1280]{1,0:T(8,128)(2,1)S(1)}, bf16[160,1280]{1,0:T(8,128)(2,1)S(1)}, u32[]{:S(2)}, u32[]{:S(2)}) collective-permute-start(bf16[160,1280]{1,0:T(8,128)(2,1)S(1)} %combine.22), channel_id=1, source_target_pairs={{0,8},{4,12},{8,16},{12,20},{16,24},{20,28},{24,0},{28,4},{1,9},{5... | collective-permute-start | bytes 1228808 | tf_op jit(solution)/shard_map/ppermute | solution.py:1520
  354.8 26.0 %collective-permute-start.65 = (bf16[416,1280]{1,0:T(8,128)(2,1)}, bf16[416,1280]{1,0:T(8,128)(2,1)S(1)}, u32[]{:S(2)}, u32[]{:S(2)}) collective-permute-start(bf16[416,1280]{1,0:T(8,128)(2,1)} %combine.20.refs_0_), channel_id=1, source_target_pairs={{0,2},{1,3},{2,0},{3,1},{4,6},{5,7},{6,4},{7,5},{8,10},{9,11},{10,... | collective-permute-start | bytes 3194888 | tf_op jit(solution)/shard_map/ppermute | solution.py:1505
  369.8 13.1 %collective-permute-start.69 = (bf16[160,1280]{1,0:T(8,128)(2,1)S(1)}, bf16[160,1280]{1,0:T(8,128)(2,1)S(1)}, u32[]{:S(2)}, u32[]{:S(2)}) collective-permute-start(bf16[160,1280]{1,0:T(8,128)(2,1)S(1)} %combine.23), channel_id=1, source_target_pairs={{0,8},{4,12},{8,16},{12,20},{16,24},{20,28},{24,0},{28,4},{1,9},{5... | collective-permute-start | bytes 1228808 | tf_op jit(solution)/shard_map/ppermute | solution.py:1529
  370.6 11.2 %collective-permute-start.64 = (bf16[1,160,1280]{2,1,0:T(8,128)(2,1)S(1)}, bf16[1,160,1280]{2,1,0:T(8,128)(2,1)S(1)}, u32[]{:S(2)}, u32[]{:S(2)}) collective-permute-start(bf16[1,160,1280]{2,1,0:T(8,128)(2,1)S(1)} %copy-done.105), channel_id=1, source_target_pairs={{0,4},{4,0},{8,12},{12,8},{16,20},{20,16},{24,28},{28,24},{1,5},{5... | collective-permute-start | bytes 1228808 | tf_op jit(solution)/shard_map/ppermute | solution.py:1527
  (151 other events, 1067.3 us)

commit v7 on v6

--- a/solution.py
+++ b/solution.py
@@ -864,7 +864,7 @@
                 in_specs=specs,
                 out_specs=pl.BlockSpec((chunk, total_cols), lambda i: (i, 0)),
                 out_shape=struct((width, total_cols), BF16),
-                compiler_params=params(36),
+                compiler_params=params(32),
                 cost_estimate=cost(13),
         name="weight_grad",
             )(*operands)
@@ -887,7 +887,7 @@
             ],
         ),
         out_shape=shapes,
-        compiler_params=params(36),
+        compiler_params=params(32),
         cost_estimate=cost(13),
         name="weight_grad",
     )(targets, *operands)

time: 398 us -> 394 us (0.990)
    unnamed x260 -> x242, local copies, waits for them, and re-layouts: 42.2 us -> 38.3 us
where the time goes in v7:
time: 394 us; the launch traced here: 388 us
  Pallas kernels  173 us (44%)
  waiting for transfers between devices  96.1 us (24%)
  local copies, waits for them, and re-layouts  59 us (15%)
  starting transfers between devices  50.5 us (13%)
  other arithmetic  7.25 us (2%)
    pallas_call x2, Pallas kernels, mlp(): pl.pallas_call(partial(mlp_kernel, len(pieces), len(weight_pieces), split...  40.5 us
    unnamed x242, local copies, waits for them, and re-layouts  38.3 us
    pallas_call x3, Pallas kernels, weight_grad(): pl.pallas_call(partial(weight_grad_kernel, sizes, share, sends), grid_spe...  32.3 us
    pallas_call x2, Pallas kernels, attend_back(): pl.pallas_call(partial(attend_back_kernel, heads, windows, split, len(pie...  27.9 us
    pallas_call x2, Pallas kernels, attend(): pl.pallas_call(partial(attend_kernel, heads, split), grid=(windows,), in_...  21.2 us
    ppermute x1, waiting for transfers between devices, body(): vector_came = lax.ppermute(vector, 'dp', [(d, d ^ 2) for d in range(8)])  16 us
    reshape x2, local copies, waits for them, and re-layouts, by_window(): array = array.reshape((slots, WTOK) + array.shape[1:])  9.92 us
    pallas_call x1, Pallas kernels, prepare(): pl.pallas_call(partial(prepare_kernel, every), grid_spec=pltpu.PrefetchSc...  9.39 us
  transfers between devices with their start and end apart: 70, of which 34 were waited for; matrix products, arithmetic and copies ran while one was open for 7% of the time, Pallas kernels for 43%

profile of v7, /device:TPU:0, one launch (start us, length us, event | category | flops | bytes accessed | tf_op | source)
XLA Modules:
  0.0 387.8 jit_solution(14223805374988708921)
XLA Ops:
  2.9 3.1 collective-permute-start
  7.9 5.0 %reshape.125.x_ref = bf16[8,196,1280]{2,1,0:T(8,128)(2,1)} reshape(bf16[1568,1280]{1,0:T(8,128)(2,1)} %param.19) | data formatting | bytes 8028160 | tf_op jit(solution)/shard_map/reshape | solution.py:1171
  13.9 4.5 %collective-permute-done.refs_2_ = bf16[160,1344]{1,0:T(8,128)(2,1)} collective-permute-done((bf16[160,1344]{1,0:T(8,128)(2,1)S(1)}, bf16[160,1344]{1,0:T(8,128)(2,1)}, u32[]{:S(2)}, u32[]{:S(2)}) %collective-permute-start) | collective-permute-done | bytes 430112 | tf_op jit(solution)/shard_map/ppermute | solution.py:1296
  23.5 9.4 %prepare.1 = (bf16[416,1280]{1,0:T(8,128)(2,1)}, f32[416,1]{1,0:T(8,128)}, bf16[1664,1280]{1,0:T(8,128)(2,1)}, f32[1664,1]{1,0:T(8,128)}) custom-call(s32[8]{0:T(128)} %stack.112.order, s32[8]{0:T(128)} %places.5, s32[8]{0:T(128)} %lives.5, bf16[8,196,1280]{2,1,0:T(8,128)(2,1)} %reshape.125.x_ref, f32[1,1280]{1,0:T(1,128)} %reshape.126.gain_ref.refs_10_, ...), custom_call_target="tpu_custom_call" | custom-call | flops 450000000 | bytes 90000 | tf_op jit(solution)/shard_map/prepare/pallas_call | solution.py:115
  32.9 1.6 collective-permute-start.4
  35.0 4.9 %reshape.132.top_ref = bf16[8,196,1280]{2,1,0:T(8,128)(2,1)} reshape(bf16[1568,1280]{1,0:T(8,128)(2,1)} %param.36) | data formatting | bytes 8028160 | tf_op jit(solution)/shard_map/reshape | solution.py:1171
  40.0 5.6 %collective-permute-done.4.refs_6_ = bf16[160,1344]{1,0:T(8,128)(2,1)} collective-permute-done((bf16[160,1344]{1,0:T(8,128)(2,1)}, bf16[160,1344]{1,0:T(8,128)(2,1)}, u32[]{:S(2)}, u32[]{:S(2)}) %collective-permute-start.4) | collective-permute-done | bytes 430112 | tf_op jit(solution)/shard_map/ppermute | solution.py:1305
  47.3 7.7 %mask_rows.1.refs_14_.refs_4_.refs_0_.refs_2_ = bf16[1664,1280]{1,0:T(8,128)(2,1)} custom-call(s32[8]{0:T(128)} %stack.112.order, s32[8]{0:T(128)} %places.5, s32[8]{0:T(128)} %lives.5, bf16[8,196,1280]{2,1,0:T(8,128)(2,1)} %reshape.132.top_ref), custom_call_target="tpu_custom_call" | custom-call | flops 300000000 | bytes 60000 | tf_op jit(solution)/shard_map/mask_rows/pallas_call | solution.py:149
  55.0 2.0 collective-permute-done.7.refs_7_
  59.2 2.2 copy-done.1
  64.5 8.2 %qkv.1 = (bf16[1664,384]{1,0:T(8,128)(2,1)S(1)}, bf16[1664,384]{1,0:T(8,128)(2,1)S(1)}, bf16[1664,384]{1,0:T(8,128)(2,1)S(1)}, bf16[1280,1344]{1,0:T(8,128)(2,1)S(1)}) custom-call(s32[8]{0:T(128)S(1)} %stack.121.offsets, bf16[160,1344]{1,0:T(8,128)(2,1)S(1)} %copy-done.61, bf16[160,1344]{1,0:T(8,128)(2,1)S(1)} %copy-done.88, ...), custom_call_target="tpu_custom_call" | custom-call | flops 700000000 | bytes 140000 | tf_op jit(solution)/shard_map/qkv/pallas_call | solution.py:321
  72.7 2.5 collective-permute-done.8.refs_5_
  76.3 10.6 %attend.2 = (bf16[832,320]{1,0:T(8,128)(2,1)S(1)}, bf16[832,1024]{1,0:T(8,128)(2,1)S(1)}, bf16[416,1280]{1,0:T(8,128)(2,1)S(1)}, bf16[208,1280]{1,0:T(8,128)(2,1)S(1)}, bf16[208,1280]{1,0:T(8,128)(2,1)S(1)}) custom-call(bf16[1664,384]{1,0:T(8,128)(2,1)S(1)} %get-tuple-element.275.q_ref.refs_4_, bf16[1664,384]{1,0:T(8,128)(2,1)S(1)} %get-tuple-element.262.k_ref.refs_5_, ...), custom_call_target="tpu_custom_call" | custom-call | flops 675000000 | bytes 135000 | tf_op jit(solution)/shard_map/attend/pallas_call | solution.py:460
  88.2 3.1 collective-permute-done.10.refs_7_
  91.8 1.9 collective-permute-done.13.refs_1_
  93.9 1.6 collective-permute-start.14
  96.8 10.6 %attend.3 = (bf16[832,320]{1,0:T(8,128)(2,1)S(1)}, bf16[832,1024]{1,0:T(8,128)(2,1)S(1)}, bf16[416,1280]{1,0:T(8,128)(2,1)S(1)}, bf16[208,1280]{1,0:T(8,128)(2,1)S(1)}, bf16[208,1280]{1,0:T(8,128)(2,1)S(1)}) custom-call(bf16[1664,384]{1,0:T(8,128)(2,1)S(1)} %get-tuple-element.275.q_ref.refs_4_, bf16[1664,384]{1,0:T(8,128)(2,1)S(1)} %get-tuple-element.262.k_ref.refs_5_, ...), custom_call_target="tpu_custom_call" | custom-call | flops 675000000 | bytes 135000 | tf_op jit(solution)/shard_map/attend/pallas_call | solution.py:460
  114.4 3.0 collective-permute-done.11.refs_10_
  119.6 6.2 %collective-permute-done.21.refs_2_ = bf16[208,1280]{1,0:T(8,128)(2,1)S(1)} collective-permute-done((bf16[208,1280]{1,0:T(8,128)(2,1)S(1)}, bf16[208,1280]{1,0:T(8,128)(2,1)S(1)}, u32[]{:S(2)}, u32[]{:S(2)}) %collective-permute-start.21) | collective-permute-done | bytes 532512 | tf_op jit(solution)/shard_map/ppermute | solution.py:1331
  127.4 2.5 collective-permute-done.18.refs_11_
  130.0 6.7 %collective-permute-done.19.refs_12_ = bf16[80,2560]{1,0:T(8,128)(2,1)S(1)} collective-permute-done((bf16[80,2560]{1,0:T(8,128)(2,1)S(1)}, bf16[80,2560]{1,0:T(8,128)(2,1)S(1)}, u32[]{:S(2)}, u32[]{:S(2)}) %collective-permute-start.19) | collective-permute-done | bytes 409632 | tf_op jit(solution)/shard_map/ppermute | solution.py:1335
  139.7 20.1 %mlp.2 = (bf16[832,1280]{1,0:T(8,128)(2,1)}, bf16[832,1280]{1,0:T(8,128)(2,1)}, bf16[832,1280]{1,0:T(8,128)(2,1)}, f32[1,1280]{1,0:T(1,128)S(1)}, bf16[416,1280]...) custom-call(s32[9]{0:T(128)S(1)} %concatenate.18.offsets, ...), custom_call_target="tpu_custom_call" | custom-call | flops 1050000000 | bytes 210000 | tf_op jit(solution)/shard_map/mlp/pallas_call | solution.py:729
  161.0 1.9 collective-permute-done.25.refs_1_
  165.9 20.3 %mlp.3 = (bf16[832,1280]{1,0:T(8,128)(2,1)}, bf16[832,1280]{1,0:T(8,128)(2,1)}, bf16[832,1280]{1,0:T(8,128)(2,1)}, f32[1,1280]{1,0:T(1,128)S(1)}, bf16[416,1280]...) custom-call(s32[9]{0:T(128)S(1)} %concatenate.18.offsets, ...), custom_call_target="tpu_custom_call" | custom-call | flops 1050000000 | bytes 210000 | tf_op jit(solution)/shard_map/mlp/pallas_call | solution.py:729
  187.0 1.9 norm_two_back.2
  192.2 1.7 combine.15
  194.8 2.2 copy-done
  197.0 10.0 %weight_grad.3.refs_0_.refs_2_.refs_4_ = bf16[4,2,160,1280]{3,2,1,0:T(8,128)(2,1)S(1)} custom-call(s32[8]{0:T(128)S(1)} %stack.131.targets, bf16[1664,1280]{1,0:T(8,128)(2,1)S(1)} %copy-done, bf16[832,1280]{1,0:T(8,128)(2,1)S(1)} %copy-done.45, bf16[1664,1280]{1,0:T(8,128)(2,1)S(1)} %copy-done, bf16[832,1280]{1,0:T(8,128)(2,1)S(1)} %copy-done.48), custom_call_target="tpu_custom_call" | custom-call | flops 650000000 | bytes 130000 | tf_op jit(solution)/shard_map/weight_grad/pallas_call | solution.py:877
  209.2 10.5 %weight_grad.4 = (bf16[2,160,1280]{2,1,0:T(8,128)(2,1)S(1)}, bf16[2,160,1280]{2,1,0:T(8,128)(2,1)S(1)}, bf16[4,160,1280]{2,1,0:T(8,128)(2,1)S(1)}) custom-call(s32[8]{0:T(128)S(1)} %stack.131.targets, bf16[832,1280]{1,0:T(8,128)(2,1)S(1)} %copy-done.52, bf16[832,1280]{1,0:T(8,128)(2,1)S(1)} %copy-done.51, bf16[832,1280]{1,0:T(8,128)(2,1)S(1)} %copy-done.54, ...), custom_call_target="tpu_custom_call" | custom-call | flops 650000000 | bytes 130000 | tf_op jit(solution)/shard_map/weight_grad/pallas_call | solution.py:877
  219.7 2.7 collective-permute-done.33.refs_2_
  224.0 2.4 norm_two_back.3
  227.4 1.9 collective-permute-done.38.refs_1_.refs_3_
  232.6 14.0 %attend_back.2 = (bf16[832,960]{1,0:T(8,128)(2,1)S(1)}, bf16[832,1280]{1,0:T(8,128)(2,1)S(1)}, f32[256,384]{1,0:T(8,128)S(1)}, f32[1,960]{1,0:T(1,128)S(1)}, f32...) custom-call(bf16[208,1280]{1,0:T(8,128)(2,1)} %get-tuple-element.359.refs_0_, ...), custom_call_target="tpu_custom_call" | custom-call | flops 925000000 | bytes 185000 | tf_op jit(solution)/shard_map/attend_back/pallas_call | solution.py:581
  246.7 4.1 %collective-permute-done.39.refs_3_.refs_5_ = bf16[160,2560]{1,0:T(8,128)(2,1)S(1)} collective-permute-done((bf16[160,2560]{1,0:T(8,128)(2,1)S(1)}, bf16[160,2560]{1,0:T(8,128)(2,1)S(1)}, u32[]{:S(2)}, u32[]{:S(2)}) %collective-permute-start.39) | collective-permute-done | bytes 819232 | tf_op jit(solution)/shard_map/ppermute | solution.py:1392
  255.1 1.6 collective-permute-start.41
  256.6 13.8 %attend_back.3 = (bf16[832,960]{1,0:T(8,128)(2,1)S(1)}, bf16[832,1280]{1,0:T(8,128)(2,1)S(1)}, f32[256,384]{1,0:T(8,128)S(1)}, f32[1,960]{1,0:T(1,128)S(1)}, f32...) custom-call(bf16[208,1280]{1,0:T(8,128)(2,1)S(1)} %get-tuple-element.380.refs_0_, ...), custom_call_target="tpu_custom_call" | custom-call | flops 925000000 | bytes 185000 | tf_op jit(solution)/shard_map/attend_back/pallas_call | solution.py:581
  275.9 4.4 %collective-permute-done.41.refs_2_ = bf16[208,1280]{1,0:T(8,128)(2,1)S(1)} collective-permute-done((bf16[208,1280]{1,0:T(8,128)(2,1)S(1)}, bf16[208,1280]{1,0:T(8,128)(2,1)S(1)}, u32[]{:S(2)}, u32[]{:S(2)}) %collective-permute-start.41) | collective-permute-done | bytes 532512 | tf_op jit(solution)/shard_map/ppermute | solution.py:1403
  300.9 11.8 %weight_grad.5 = (bf16[1,160,1280]{2,1,0:T(8,128)(2,1)S(1)}, bf16[2,160,1280]{2,1,0:T(8,128)(2,1)S(1)}, bf16[1,160,1280]{2,1,0:T(8,128)(2,1)}, bf16[4,160,1280]{2,1,0:T(8,128)(2,1)S(1)}) custom-call(s32[8]{0:T(128)S(1)} %stack.131.targets, bf16[1664,1280]{1,0:T(8,128)(2,1)S(1)} %bitcast.83, bf16[832,960]{1,0:T(8,128)(2,1)S(1)} %copy-done.68, ...), custom_call_target="tpu_custom_call" | custom-call | flops 650000000 | bytes 130000 | tf_op jit(solution)/shard_map/weight_grad/pallas_call | solution.py:877
  316.1 3.0 norm_one_back.1.refs_0_
  321.7 2.4 combine.20.refs_0_
  324.1 2.8 collective-permute-done.54.refs_4_
  327.2 4.0 %collective-permute-start.57 = (bf16[160,2560]{1,0:T(8,128)(2,1)S(1)}, bf16[160,2560]{1,0:T(8,128)(2,1)S(1)}, u32[]{:S(2)}, u32[]{:S(2)}) collective-permute-start(bf16[160,2560]{1,0:T(8,128)(2,1)S(1)} %combine.21), channel_id=1, source_target_pairs={{0,8},{4,12},{8,16},{12,20},{16,24},{20,28},{24,0},{28,4},{1,9},{5... | collective-permute-start | bytes 2457608 | tf_op jit(solution)/shard_map/ppermute | solution.py:1503
  331.7 16.0 %collective-permute-done.58 = f32[160,128]{1,0:T(8,128)S(1)} collective-permute-done((f32[160,128]{1,0:T(8,128)S(1)}, f32[160,128]{1,0:T(8,128)S(1)}, u32[]{:S(2)}, u32[]{:S(2)}) %collective-permute-start.58) | collective-permute-done | bytes 81952 | tf_op jit(solution)/shard_map/ppermute | solution.py:1504
  349.1 1.6 collective-permute-start.61
  352.9 4.6 %place_windows.1 = f32[1568,1280]{1,0:T(8,128)} custom-call(s32[4]{0:T(128)S(1)} %pad_add_fusion.1.order, bf16[416,1280]{1,0:T(8,128)(2,1)S(1)} %norm_one_back.1.refs_0_, bf16[416,1280]{1,0:T(8,128)(2,1)S(1)} %collective-permute-done.59.refs_1_, bf16[416,1280]{1,0:T(8,128)(2,1)S(1)} %collective-permute-done.62.refs_2_, ...), custom_call_target="tpu_custom_call" | custom-call | flops 350000000 | bytes 70000 | tf_op jit(solution)/shard_map/place_windows/pallas_call | solution.py:953
  357.4 7.6 %collective-permute-done.61 = f32[160,128]{1,0:T(8,128)S(1)} collective-permute-done((f32[160,128]{1,0:T(8,128)S(1)}, f32[160,128]{1,0:T(8,128)S(1)}, u32[]{:S(2)}, u32[]{:S(2)}) %collective-permute-start.61) | collective-permute-done | bytes 81952 | tf_op jit(solution)/shard_map/ppermute | solution.py:1521
  372.1 5.7 %collective-permute-done.65.refs_1_ = bf16[416,1280]{1,0:T(8,128)(2,1)S(1)} collective-permute-done((bf16[416,1280]{1,0:T(8,128)(2,1)}, bf16[416,1280]{1,0:T(8,128)(2,1)S(1)}, u32[]{:S(2)}, u32[]{:S(2)}) %collective-permute-start.65) | collective-permute-done | bytes 1064992 | tf_op jit(solution)/shard_map/ppermute | solution.py:1505
  383.0 4.6 %write_output.1 = bf16[1568,1280]{1,0:T(8,128)(2,1)} custom-call(s32[4]{0:T(128)S(1)} %pad_add_fusion.1.order, s32[8]{0:T(128)S(1)} %copy-done.95, s32[8]{0:T(128)S(1)} %copy-done.96, bf16[416,1280]{1,0:T(8,128)(2,1)} %combine.20.refs_0_, bf16[416,1280]{1,0:T(8,128)(2,1)S(1)} %collective-permute-done.65.refs_1_, ...), custom_call_target="tpu_custom_call" | custom-call | flops 350000000 | bytes 70000 | tf_op jit(solution)/shard_map/write_output/pallas_call | solution.py:988
  (437 shorter events, 104.9 us)
Async XLA Ops:
  2.9 15.6 %collective-permute-start = (bf16[160,1344]{1,0:T(8,128)(2,1)S(1)}, bf16[160,1344]{1,0:T(8,128)(2,1)}, u32[]{:S(2)}, u32[]{:S(2)}) collective-permute-start(bf16[160,1344]{1,0:T(8,128)(2,1)S(1)} %concatenate.16.refs_0_), channel_id=1, source_target_pairs={{0,8},{4,12},{8,16},{12,20},{16,24},{20,28},{24,0},{28,4},{1,9},{5... | collective-permute-start | bytes 1290248 | tf_op jit(solution)/shard_map/ppermute | solution.py:1296
  5.9 12.5 %collective-permute-start.1 = (bf16[160,1344]{1,0:T(8,128)(2,1)S(1)}, bf16[160,1344]{1,0:T(8,128)(2,1)S(1)}, u32[]{:S(2)}, u32[]{:S(2)}) collective-permute-start(bf16[160,1344]{1,0:T(8,128)(2,1)S(1)} %concatenate.16.refs_0_), channel_id=1, source_target_pairs={{0,4},{4,0},{8,12},{12,8},{16,20},{20,16},{24,28},{28,24},{1,5},{5... | collective-permute-start | bytes 1290248 | tf_op jit(solution)/shard_map/ppermute | solution.py:1296
  19.2 13.7 %collective-permute-start.2 = (bf16[160,1344]{1,0:T(8,128)(2,1)}, bf16[160,1344]{1,0:T(8,128)(2,1)}, u32[]{:S(2)}, u32[]{:S(2)}) collective-permute-start(bf16[160,1344]{1,0:T(8,128)(2,1)} %collective-permute-done.refs_2_), channel_id=1, source_target_pairs={{0,8},{4,12},{8,16},{12,20},{16,24},{20,28},{24,0},{28,4},{1,9},{5... | collective-permute-start | bytes 1290248 | tf_op jit(solution)/shard_map/ppermute | solution.py:1300
  20.1 12.8 %collective-permute-start.3 = (bf16[160,1344]{1,0:T(8,128)(2,1)}, bf16[160,1344]{1,0:T(8,128)(2,1)}, u32[]{:S(2)}, u32[]{:S(2)}) collective-permute-start(bf16[160,1344]{1,0:T(8,128)(2,1)} %collective-permute-done.refs_2_), channel_id=1, source_target_pairs={{0,4},{4,0},{8,12},{12,8},{16,20},{20,16},{24,28},{28,24},{1,5},{5... | collective-permute-start | bytes 1290248 | tf_op jit(solution)/shard_map/ppermute | solution.py:1300
  32.9 12.7 %collective-permute-start.4 = (bf16[160,1344]{1,0:T(8,128)(2,1)}, bf16[160,1344]{1,0:T(8,128)(2,1)}, u32[]{:S(2)}, u32[]{:S(2)}) collective-permute-start(bf16[160,1344]{1,0:T(8,128)(2,1)} %collective-permute-done.2.refs_4_), channel_id=1, source_target_pairs={{0,8},{4,12},{8,16},{12,20},{16,24},{20,28},{24,0},{28,4},{1,9},{5... | collective-permute-start | bytes 1290248 | tf_op jit(solution)/shard_map/ppermute | solution.py:1305
  34.5 11.1 %collective-permute-start.5 = (bf16[160,1344]{1,0:T(8,128)(2,1)}, bf16[160,1344]{1,0:T(8,128)(2,1)S(1)}, u32[]{:S(2)}, u32[]{:S(2)}) collective-permute-start(bf16[160,1344]{1,0:T(8,128)(2,1)} %collective-permute-done.2.refs_4_), channel_id=1, source_target_pairs={{0,4},{4,0},{8,12},{12,8},{16,20},{20,16},{24,28},{28,24},{1,5},{5... | collective-permute-start | bytes 1290248 | tf_op jit(solution)/shard_map/ppermute | solution.py:1305
  47.3 25.4 %collective-permute-start.6 = (bf16[160,2560]{1,0:T(8,128)(2,1)S(1)}, bf16[160,2560]{1,0:T(8,128)(2,1)}, u32[]{:S(2)}, u32[]{:S(2)}) collective-permute-start(bf16[160,2560]{1,0:T(8,128)(2,1)S(1)} %pad_maximum_fusion.refs_4_), channel_id=1, source_target_pairs={{0,8},{4,12},{8,16},{12,20},{16,24},{20,28},{24,0},{28,4},{1,9},{5... | collective-permute-start | bytes 2457608 | tf_op jit(solution)/shard_map/ppermute | solution.py:1310
  57.0 18.2 %collective-permute-start.8 = (bf16[160,2560]{1,0:T(8,128)(2,1)S(1)}, bf16[160,2560]{1,0:T(8,128)(2,1)S(1)}, u32[]{:S(2)}, u32[]{:S(2)}) collective-permute-start(bf16[160,2560]{1,0:T(8,128)(2,1)S(1)} %pad_maximum_fusion.refs_4_), channel_id=1, source_target_pairs={{0,4},{4,0},{8,12},{12,8},{16,20},{20,16},{24,28},{28,24},{1,5},{5... | collective-permute-start | bytes 2457608 | tf_op jit(solution)/shard_map/ppermute | solution.py:1315
  75.2 16.0 %collective-permute-start.10 = (bf16[160,2560]{1,0:T(8,128)(2,1)}, bf16[160,2560]{1,0:T(8,128)(2,1)S(1)}, u32[]{:S(2)}, u32[]{:S(2)}) collective-permute-start(bf16[160,2560]{1,0:T(8,128)(2,1)} %collective-permute-done.6.refs_6_), channel_id=1, source_target_pairs={{0,4},{4,0},{8,12},{12,8},{16,20},{20,16},{24,28},{28,24},{1,5},{5... | collective-permute-start | bytes 2457608 | tf_op jit(solution)/shard_map/ppermute | solution.py:1320
  76.2 15.6 %collective-permute-start.9 = (bf16[160,2560]{1,0:T(8,128)(2,1)}, bf16[160,2560]{1,0:T(8,128)(2,1)S(1)}, u32[]{:S(2)}, u32[]{:S(2)}) collective-permute-start(bf16[160,2560]{1,0:T(8,128)(2,1)} %collective-permute-done.6.refs_6_), channel_id=1, source_target_pairs={{0,8},{4,12},{8,16},{12,20},{16,24},{20,28},{24,0},{28,4},{1,9},{5... | collective-permute-start | bytes 2457608 | tf_op jit(solution)/shard_map/ppermute | solution.py:1320
  93.9 14.8 %collective-permute-start.14 = (bf16[208,1280]{1,0:T(8,128)(2,1)S(1)}, bf16[208,1280]{1,0:T(8,128)(2,1)S(1)}, u32[]{:S(2)}, u32[]{:S(2)}) collective-permute-start(bf16[208,1280]{1,0:T(8,128)(2,1)S(1)} %combine.12), channel_id=1, source_target_pairs={{0,2},{1,3},{2,0},{3,1},{4,6},{5,7},{6,4},{7,5},{8,10},{9,11},{10,... | collective-permute-start | bytes 1597448 | tf_op jit(solution)/shard_map/ppermute | solution.py:1326
  95.5 22.0 %collective-permute-start.11 = (bf16[160,2560]{1,0:T(8,128)(2,1)S(1)}, bf16[160,2560]{1,0:T(8,128)(2,1)S(1)}, u32[]{:S(2)}, u32[]{:S(2)}) collective-permute-start(bf16[160,2560]{1,0:T(8,128)(2,1)S(1)} %collective-permute-done.9.refs_8_), channel_id=1, source_target_pairs={{0,8},{4,12},{8,16},{12,20},{16,24},{20,28},{24,0},{28,4},{1,9},{5... | collective-permute-start | bytes 2457608 | tf_op jit(solution)/shard_map/ppermute | solution.py:1323
  95.6 21.8 %collective-permute-start.12 = (bf16[160,2560]{1,0:T(8,128)(2,1)S(1)}, bf16[160,2560]{1,0:T(8,128)(2,1)S(1)}, u32[]{:S(2)}, u32[]{:S(2)}) collective-permute-start(bf16[160,2560]{1,0:T(8,128)(2,1)S(1)} %collective-permute-done.9.refs_8_), channel_id=1, source_target_pairs={{0,4},{4,0},{8,12},{12,8},{16,20},{20,16},{24,28},{28,24},{1,5},{5... | collective-permute-start | bytes 2457608 | tf_op jit(solution)/shard_map/ppermute | solution.py:1323
  110.8 15.0 %collective-permute-start.21 = (bf16[208,1280]{1,0:T(8,128)(2,1)S(1)}, bf16[208,1280]{1,0:T(8,128)(2,1)S(1)}, u32[]{:S(2)}, u32[]{:S(2)}) collective-permute-start(bf16[208,1280]{1,0:T(8,128)(2,1)S(1)} %combine.13), channel_id=1, source_target_pairs={{0,2},{1,3},{2,0},{3,1},{4,6},{5,7},{6,4},{7,5},{8,10},{9,11},{10,... | collective-permute-start | bytes 1597448 | tf_op jit(solution)/shard_map/ppermute | solution.py:1331
  113.5 23.2 %collective-permute-start.20 = (bf16[208,1280]{1,0:T(8,128)(2,1)}, bf16[208,1280]{1,0:T(8,128)(2,1)}, u32[]{:S(2)}, u32[]{:S(2)}) collective-permute-start(bf16[208,1280]{1,0:T(8,128)(2,1)} %get-tuple-element.296.refs_0_), channel_id=1, source_target_pairs={{0,2},{1,3},{2,0},{3,1},{4,6},{5,7},{6,4},{7,5},{8,10},{9,11},{10,... | collective-permute-start | bytes 1597448 | tf_op jit(solution)/shard_map/ppermute | solution.py:1333
  117.5 12.5 %collective-permute-start.18 = (bf16[80,2560]{1,0:T(8,128)(2,1)S(1)}, bf16[80,2560]{1,0:T(8,128)(2,1)S(1)}, u32[]{:S(2)}, u32[]{:S(2)}) collective-permute-start(bf16[80,2560]{1,0:T(8,128)(2,1)S(1)} %get-tuple-element.467), channel_id=1, source_target_pairs={{0,4},{4,0},{8,12},{12,8},{16,20},{20,16},{24,28},{28,24},{1,5},{5... | collective-permute-start | bytes 1228808 | tf_op jit(solution)/shard_map/ppermute | solution.py:1335
  118.6 18.0 %collective-permute-start.19 = (bf16[80,2560]{1,0:T(8,128)(2,1)S(1)}, bf16[80,2560]{1,0:T(8,128)(2,1)S(1)}, u32[]{:S(2)}, u32[]{:S(2)}) collective-permute-start(bf16[80,2560]{1,0:T(8,128)(2,1)S(1)} %get-tuple-element.466), channel_id=1, source_target_pairs={{0,4},{4,0},{8,12},{12,8},{16,20},{20,16},{24,28},{28,24},{1,5},{5... | collective-permute-start | bytes 1228808 | tf_op jit(solution)/shard_map/ppermute | solution.py:1335
  137.2 22.7 %collective-permute-start.22 = (bf16[208,1280]{1,0:T(8,128)(2,1)S(1)}, bf16[208,1280]{1,0:T(8,128)(2,1)}, u32[]{:S(2)}, u32[]{:S(2)}) collective-permute-start(bf16[208,1280]{1,0:T(8,128)(2,1)S(1)} %get-tuple-element.317.refs_0_), channel_id=1, source_target_pairs={{0,2},{1,3},{2,0},{3,1},{4,6},{5,7},{6,4},{7,5},{8,10},{9,11},{10,... | collective-permute-start | bytes 1597448 | tf_op jit(solution)/shard_map/ppermute | solution.py:1341
  160.1 26.2 %collective-permute-start.27 = (bf16[416,1280]{1,0:T(8,128)(2,1)}, bf16[416,1280]{1,0:T(8,128)(2,1)S(1)}, u32[]{:S(2)}, u32[]{:S(2)}) collective-permute-start(bf16[416,1280]{1,0:T(8,128)(2,1)} %get-tuple-element.316), channel_id=1, source_target_pairs={{0,1},{1,0},{2,3},{3,2},{4,5},{5,4},{6,7},{7,6},{8,9},{9,8},{10,11... | collective-permute-start | bytes 3194888 | tf_op jit(solution)/shard_map/ppermute | solution.py:1347
  164.2 22.1 %collective-permute-start.26 = (bf16[208,1280]{1,0:T(8,128)(2,1)S(1)}, bf16[208,1280]{1,0:T(8,128)(2,1)S(1)}, u32[]{:S(2)}, u32[]{:S(2)}) collective-permute-start(bf16[208,1280]{1,0:T(8,128)(2,1)S(1)} %combine.14), channel_id=1, source_target_pairs={{0,2},{1,3},{2,0},{3,1},{4,6},{5,7},{6,4},{7,5},{8,10},{9,11},{10,... | collective-permute-start | bytes 1597448 | tf_op jit(solution)/shard_map/ppermute | solution.py:1349
  189.9 17.1 %collective-permute-start.31 = (bf16[208,1280]{1,0:T(8,128)(2,1)}, bf16[208,1280]{1,0:T(8,128)(2,1)}, u32[]{:S(2)}, u32[]{:S(2)}) collective-permute-start(bf16[208,1280]{1,0:T(8,128)(2,1)} %get-tuple-element.359.refs_0_), channel_id=1, source_target_pairs={{0,2},{1,3},{2,0},{3,1},{4,6},{5,7},{6,4},{7,5},{8,10},{9,11},{10,... | collective-permute-start | bytes 1597448 | tf_op jit(solution)/shard_map/ppermute | solution.py:1356
  207.1 22.1 %collective-permute-start.38 = (bf16[2,160,1280]{2,1,0:T(8,128)(2,1)S(1)}, bf16[2,160,1280]{2,1,0:T(8,128)(2,1)S(1)}, u32[]{:S(2)}, u32[]{:S(2)}) collective-permute-start(bf16[2,160,1280]{2,1,0:T(8,128)(2,1)S(1)} %slice_bitcast_fusion), channel_id=1, source_target_pairs={{0,8},{4,12},{8,16},{12,20},{16,24},{20,28},{24,0},{28,4},{1,9},{5... | collective-permute-start | bytes 2457608 | tf_op jit(solution)/shard_map/ppermute | solution.py:1369
  207.9 11.8 %collective-permute-start.34 = (bf16[208,1280]{1,0:T(8,128)(2,1)}, bf16[208,1280]{1,0:T(8,128)(2,1)S(1)}, u32[]{:S(2)}, u32[]{:S(2)}) collective-permute-start(bf16[208,1280]{1,0:T(8,128)(2,1)} %get-tuple-element.359.refs_0_), channel_id=1, source_target_pairs={{0,1},{1,0},{2,3},{3,2},{4,5},{5,4},{6,7},{7,6},{8,9},{9,8},{10,11... | collective-permute-start | bytes 1597448 | tf_op jit(solution)/shard_map/ppermute | solution.py:1289
  207.9 14.5 %collective-permute-start.33 = (bf16[208,1280]{1,0:T(8,128)(2,1)S(1)}, bf16[208,1280]{1,0:T(8,128)(2,1)S(1)}, u32[]{:S(2)}, u32[]{:S(2)}) collective-permute-start(bf16[208,1280]{1,0:T(8,128)(2,1)S(1)} %get-tuple-element.344), channel_id=1, source_target_pairs={{0,2},{1,3},{2,0},{3,1},{4,6},{5,7},{6,4},{7,5},{8,10},{9,11},{10,... | collective-permute-start | bytes 1597448 | tf_op jit(solution)/shard_map/ppermute | solution.py:1365
  209.0 13.5 %collective-permute-start.35 = (bf16[208,1280]{1,0:T(8,128)(2,1)}, bf16[208,1280]{1,0:T(8,128)(2,1)S(1)}, u32[]{:S(2)}, u32[]{:S(2)}) collective-permute-start(bf16[208,1280]{1,0:T(8,128)(2,1)} %collective-permute-done.31.refs_1_), channel_id=1, source_target_pairs={{0,1},{1,0},{2,3},{3,2},{4,5},{5,4},{6,7},{7,6},{8,9},{9,8},{10,11... | collective-permute-start | bytes 1597448 | tf_op jit(solution)/shard_map/ppermute | solution.py:1289
  222.5 24.2 %collective-permute-start.37 = (bf16[2,160,1280]{2,1,0:T(8,128)(2,1)S(1)}, bf16[2,160,1280]{2,1,0:T(8,128)(2,1)S(1)}, u32[]{:S(2)}, u32[]{:S(2)}) collective-permute-start(bf16[2,160,1280]{2,1,0:T(8,128)(2,1)S(1)} %get-tuple-element.356), channel_id=1, source_target_pairs={{0,4},{4,0},{8,12},{12,8},{16,20},{20,16},{24,28},{28,24},{1,5},{5... | collective-permute-start | bytes 2457608 | tf_op jit(solution)/shard_map/ppermute | solution.py:1374
  229.5 21.3 %collective-permute-start.39 = (bf16[160,2560]{1,0:T(8,128)(2,1)S(1)}, bf16[160,2560]{1,0:T(8,128)(2,1)S(1)}, u32[]{:S(2)}, u32[]{:S(2)}) collective-permute-start(bf16[160,2560]{1,0:T(8,128)(2,1)S(1)} %combine.16), channel_id=1, source_target_pairs={{0,8},{4,12},{8,16},{12,20},{16,24},{20,28},{24,0},{28,4},{1,9},{5... | collective-permute-start | bytes 2457608 | tf_op jit(solution)/shard_map/ppermute | solution.py:1392
  229.5 17.1 %collective-permute-start.36 = (bf16[208,1280]{1,0:T(8,128)(2,1)S(1)}, bf16[208,1280]{1,0:T(8,128)(2,1)S(1)}, u32[]{:S(2)}, u32[]{:S(2)}) collective-permute-start(bf16[208,1280]{1,0:T(8,128)(2,1)S(1)} %get-tuple-element.380.refs_0_), channel_id=1, source_target_pairs={{0,2},{1,3},{2,0},{3,1},{4,6},{5,7},{6,4},{7,5},{8,10},{9,11},{10,... | collective-permute-start | bytes 1597448 | tf_op jit(solution)/shard_map/ppermute | solution.py:1384
  251.3 22.9 %collective-permute-start.43 = (bf16[2,160,1280]{2,1,0:T(8,128)(2,1)S(1)}, bf16[2,160,1280]{2,1,0:T(8,128)(2,1)S(1)}, u32[]{:S(2)}, u32[]{:S(2)}) collective-permute-start(bf16[2,160,1280]{2,1,0:T(8,128)(2,1)S(1)} %get-tuple-element.377), channel_id=1, source_target_pairs={{0,4},{4,0},{8,12},{12,8},{16,20},{20,16},{24,28},{28,24},{1,5},{5... | collective-permute-start | bytes 2457608 | tf_op jit(solution)/shard_map/ppermute | solution.py:1397
  254.5 26.8 %collective-permute-start.42 = (bf16[160,2560]{1,0:T(8,128)(2,1)S(1)}, bf16[160,2560]{1,0:T(8,128)(2,1)S(1)}, u32[]{:S(2)}, u32[]{:S(2)}) collective-permute-start(bf16[160,2560]{1,0:T(8,128)(2,1)S(1)} %get-tuple-element.376), channel_id=1, source_target_pairs={{0,8},{4,12},{8,16},{12,20},{16,24},{20,28},{24,0},{28,4},{1,9},{5... | collective-permute-start | bytes 2457608 | tf_op jit(solution)/shard_map/ppermute | solution.py:1404
  254.6 20.6 %collective-permute-start.44 = (bf16[208,1280]{1,0:T(8,128)(2,1)S(1)}, bf16[208,1280]{1,0:T(8,128)(2,1)S(1)}, u32[]{:S(2)}, u32[]{:S(2)}) collective-permute-start(bf16[208,1280]{1,0:T(8,128)(2,1)S(1)} %get-tuple-element.379), channel_id=1, source_target_pairs={{0,2},{1,3},{2,0},{3,1},{4,6},{5,7},{6,4},{7,5},{8,10},{9,11},{10,... | collective-permute-start | bytes 1597448 | tf_op jit(solution)/shard_map/ppermute | solution.py:1406
  255.1 25.3 %collective-permute-start.41 = (bf16[208,1280]{1,0:T(8,128)(2,1)S(1)}, bf16[208,1280]{1,0:T(8,128)(2,1)S(1)}, u32[]{:S(2)}, u32[]{:S(2)}) collective-permute-start(bf16[208,1280]{1,0:T(8,128)(2,1)S(1)} %get-tuple-element.375), channel_id=1, source_target_pairs={{0,2},{1,3},{2,0},{3,1},{4,6},{5,7},{6,4},{7,5},{8,10},{9,11},{10,... | collective-permute-start | bytes 1597448 | tf_op jit(solution)/shard_map/ppermute | solution.py:1403
  292.6 20.1 %collective-permute-start.49 = (bf16[208,1280]{1,0:T(8,128)(2,1)S(1)}, bf16[208,1280]{1,0:T(8,128)(2,1)S(1)}, u32[]{:S(2)}, u32[]{:S(2)}) collective-permute-start(bf16[208,1280]{1,0:T(8,128)(2,1)S(1)} %get-tuple-element.405), channel_id=1, source_target_pairs={{0,2},{1,3},{2,0},{3,1},{4,6},{5,7},{6,4},{7,5},{8,10},{9,11},{10,... | collective-permute-start | bytes 1597448 | tf_op jit(solution)/shard_map/ppermute | solution.py:1430
  293.1 19.6 %collective-permute-start.50 = (bf16[160,1280]{1,0:T(8,128)(2,1)S(1)}, bf16[160,1280]{1,0:T(8,128)(2,1)S(1)}, u32[]{:S(2)}, u32[]{:S(2)}) collective-permute-start(bf16[160,1280]{1,0:T(8,128)(2,1)S(1)} %get-tuple-element.406), channel_id=1, source_target_pairs={{0,4},{4,0},{8,12},{12,8},{16,20},{20,16},{24,28},{28,24},{1,5},{5... | collective-permute-start | bytes 1228808 | tf_op jit(solution)/shard_map/ppermute | solution.py:1431
  294.2 18.5 %collective-permute-start.51 = (bf16[160,1280]{1,0:T(8,128)(2,1)S(1)}, bf16[160,1280]{1,0:T(8,128)(2,1)S(1)}, u32[]{:S(2)}, u32[]{:S(2)}) collective-permute-start(bf16[160,1280]{1,0:T(8,128)(2,1)S(1)} %get-tuple-element.407), channel_id=1, source_target_pairs={{0,8},{4,12},{8,16},{12,20},{16,24},{20,28},{24,0},{28,4},{1,9},{5... | collective-permute-start | bytes 1228808 | tf_op jit(solution)/shard_map/ppermute | solution.py:1431
  294.7 27.1 %collective-permute-start.55 = (bf16[208,1280]{1,0:T(8,128)(2,1)}, bf16[208,1280]{1,0:T(8,128)(2,1)S(1)}, u32[]{:S(2)}, u32[]{:S(2)}) collective-permute-start(bf16[208,1280]{1,0:T(8,128)(2,1)} %copy-done.97), channel_id=1, source_target_pairs={{0,2},{1,3},{2,0},{3,1},{4,6},{5,7},{6,4},{7,5},{8,10},{9,11},{10,... | collective-permute-start | bytes 1597448 | tf_op jit(solution)/shard_map/ppermute | solution.py:1433
  313.0 14.0 %collective-permute-start.54 = (bf16[160,1280]{1,0:T(8,128)(2,1)S(1)}, bf16[160,1280]{1,0:T(8,128)(2,1)S(1)}, u32[]{:S(2)}, u32[]{:S(2)}) collective-permute-start(bf16[160,1280]{1,0:T(8,128)(2,1)S(1)} %combine.19), channel_id=1, source_target_pairs={{0,8},{4,12},{8,16},{12,20},{16,24},{20,28},{24,0},{28,4},{1,9},{5... | collective-permute-start | bytes 1228808 | tf_op jit(solution)/shard_map/ppermute | solution.py:1453
  314.1 12.8 %collective-permute-start.53 = (bf16[1,160,1280]{2,1,0:T(8,128)(2,1)S(1)}, bf16[1,160,1280]{2,1,0:T(8,128)(2,1)S(1)}, u32[]{:S(2)}, u32[]{:S(2)}) collective-permute-start(bf16[1,160,1280]{2,1,0:T(8,128)(2,1)S(1)} %get-tuple-element.423), channel_id=1, source_target_pairs={{0,4},{4,0},{8,12},{12,8},{16,20},{20,16},{24,28},{28,24},{1,5},{5... | collective-permute-start | bytes 1228808 | tf_op jit(solution)/shard_map/ppermute | solution.py:1438
  320.2 27.6 %collective-permute-start.59 = (bf16[416,1280]{1,0:T(8,128)(2,1)S(1)}, bf16[416,1280]{1,0:T(8,128)(2,1)S(1)}, u32[]{:S(2)}, u32[]{:S(2)}) collective-permute-start(bf16[416,1280]{1,0:T(8,128)(2,1)S(1)} %norm_one_back.1.refs_0_), channel_id=1, source_target_pairs={{0,2},{1,3},{2,0},{3,1},{4,6},{5,7},{6,4},{7,5},{8,10},{9,11},{10,... | collective-permute-start | bytes 3194888 | tf_op jit(solution)/shard_map/ppermute | solution.py:1463
  320.6 27.2 %collective-permute-start.52 = (bf16[2,160,1280]{2,1,0:T(8,128)(2,1)S(1)}, bf16[2,160,1280]{2,1,0:T(8,128)(2,1)S(1)}, u32[]{:S(2)}, u32[]{:S(2)}) collective-permute-start(bf16[2,160,1280]{2,1,0:T(8,128)(2,1)S(1)} %get-tuple-element.422), channel_id=1, source_target_pairs={{0,4},{4,0},{8,12},{12,8},{16,20},{20,16},{24,28},{28,24},{1,5},{5... | collective-permute-start | bytes 2457608 | tf_op jit(solution)/shard_map/ppermute | solution.py:1487
  327.2 21.8 %collective-permute-start.57 = (bf16[160,2560]{1,0:T(8,128)(2,1)S(1)}, bf16[160,2560]{1,0:T(8,128)(2,1)S(1)}, u32[]{:S(2)}, u32[]{:S(2)}) collective-permute-start(bf16[160,2560]{1,0:T(8,128)(2,1)S(1)} %combine.21), channel_id=1, source_target_pairs={{0,8},{4,12},{8,16},{12,20},{16,24},{20,28},{24,0},{28,4},{1,9},{5... | collective-permute-start | bytes 2457608 | tf_op jit(solution)/shard_map/ppermute | solution.py:1503
  331.2 16.6 %collective-permute-start.58 = (f32[160,128]{1,0:T(8,128)S(1)}, f32[160,128]{1,0:T(8,128)S(1)}, u32[]{:S(2)}, u32[]{:S(2)}) collective-permute-start(f32[160,128]{1,0:T(8,128)S(1)} %add.277), channel_id=1, source_target_pairs={{0,8},{4,12},{8,0},{12,4},{16,24},{20,28},{24,16},{28,20},{1,9},{5... | collective-permute-start | bytes 245768 | tf_op jit(solution)/shard_map/ppermute | solution.py:1504
  331.7 21.1 %collective-permute-start.62 = (bf16[416,1280]{1,0:T(8,128)(2,1)S(1)}, bf16[416,1280]{1,0:T(8,128)(2,1)S(1)}, u32[]{:S(2)}, u32[]{:S(2)}) collective-permute-start(bf16[416,1280]{1,0:T(8,128)(2,1)S(1)} %norm_one_back.1.refs_0_), channel_id=1, source_target_pairs={{0,1},{1,0},{2,3},{3,2},{4,5},{5,4},{6,7},{7,6},{8,9},{9,8},{10,11... | collective-permute-start | bytes 3194888 | tf_op jit(solution)/shard_map/ppermute | solution.py:1289
  349.1 15.9 %collective-permute-start.61 = (f32[160,128]{1,0:T(8,128)S(1)}, f32[160,128]{1,0:T(8,128)S(1)}, u32[]{:S(2)}, u32[]{:S(2)}) collective-permute-start(f32[160,128]{1,0:T(8,128)S(1)} %add.278), channel_id=1, source_target_pairs={{0,16},{4,20},{8,24},{12,28},{16,0},{20,4},{24,8},{28,12},{1,17},{... | collective-permute-start | bytes 245768 | tf_op jit(solution)/shard_map/ppermute | solution.py:1521
  350.9 14.1 %collective-permute-start.60 = (bf16[160,1280]{1,0:T(8,128)(2,1)S(1)}, bf16[160,1280]{1,0:T(8,128)(2,1)S(1)}, u32[]{:S(2)}, u32[]{:S(2)}) collective-permute-start(bf16[160,1280]{1,0:T(8,128)(2,1)S(1)} %combine.22), channel_id=1, source_target_pairs={{0,8},{4,12},{8,16},{12,20},{16,24},{20,28},{24,0},{28,4},{1,9},{5... | collective-permute-start | bytes 1228808 | tf_op jit(solution)/shard_map/ppermute | solution.py:1520
  352.0 25.8 %collective-permute-start.65 = (bf16[416,1280]{1,0:T(8,128)(2,1)}, bf16[416,1280]{1,0:T(8,128)(2,1)S(1)}, u32[]{:S(2)}, u32[]{:S(2)}) collective-permute-start(bf16[416,1280]{1,0:T(8,128)(2,1)} %combine.20.refs_0_), channel_id=1, source_target_pairs={{0,2},{1,3},{2,0},{3,1},{4,6},{5,7},{6,4},{7,5},{8,10},{9,11},{10,... | collective-permute-start | bytes 3194888 | tf_op jit(solution)/shard_map/ppermute | solution.py:1505
  367.0 13.0 %collective-permute-start.69 = (bf16[160,1280]{1,0:T(8,128)(2,1)S(1)}, bf16[160,1280]{1,0:T(8,128)(2,1)S(1)}, u32[]{:S(2)}, u32[]{:S(2)}) collective-permute-start(bf16[160,1280]{1,0:T(8,128)(2,1)S(1)} %combine.23), channel_id=1, source_target_pairs={{0,8},{4,12},{8,16},{12,20},{16,24},{20,28},{24,0},{28,4},{1,9},{5... | collective-permute-start | bytes 1228808 | tf_op jit(solution)/shard_map/ppermute | solution.py:1529
  367.1 11.4 %collective-permute-start.64 = (bf16[1,160,1280]{2,1,0:T(8,128)(2,1)}, bf16[1,160,1280]{2,1,0:T(8,128)(2,1)S(1)}, u32[]{:S(2)}, u32[]{:S(2)}) collective-permute-start(bf16[1,160,1280]{2,1,0:T(8,128)(2,1)} %get-tuple-element.449), channel_id=1, source_target_pairs={{0,4},{4,0},{8,12},{12,8},{16,20},{20,16},{24,28},{28,24},{1,5},{5... | collective-permute-start | bytes 1228808 | tf_op jit(solution)/shard_map/ppermute | solution.py:1527
  (142 other events, 1031.0 us)

commit v8 on v7

--- a/solution.py
+++ b/solution.py
@@ -602,7 +602,7 @@
         ]
         + specs,
         out_shape=[struct((rows, 3 * heads * HD), BF16), branch, rel, sums, norms] + shapes,
-        compiler_params=params(28),
+        compiler_params=params(30),
         cost_estimate=cost(18.5),
         name="attend_back",
     )(*pieces, q, k, v, shares, rel_high, marks, weights, normed, valid)

time: 394 us -> 394 us (level)
  no operation moved by 1% of the time
where the time goes in v8:
time: 394 us; the launch traced here: 388 us
  Pallas kernels  173 us (44%)
  waiting for transfers between devices  94.9 us (24%)
  local copies, waits for them, and re-layouts  60.2 us (15%)
  starting transfers between devices  50.5 us (13%)
  other arithmetic  7.25 us (2%)
    pallas_call x2, Pallas kernels, mlp(): pl.pallas_call(partial(mlp_kernel, len(pieces), len(weight_pieces), split...  40.5 us
    unnamed x242, local copies, waits for them, and re-layouts  39.4 us
    pallas_call x3, Pallas kernels, weight_grad(): pl.pallas_call(partial(weight_grad_kernel, sizes, share, sends), grid_spe...  32.3 us
    pallas_call x2, Pallas kernels, attend_back(): pl.pallas_call(partial(attend_back_kernel, heads, windows, split, len(pie...  27.9 us
    pallas_call x2, Pallas kernels, attend(): pl.pallas_call(partial(attend_kernel, heads, split), grid=(windows,), in_...  21.2 us
    ppermute x1, waiting for transfers between devices, body(): vector_came = lax.ppermute(vector, 'dp', [(d, d ^ 2) for d in range(8)])  16 us
    reshape x2, local copies, waits for them, and re-layouts, by_window(): array = array.reshape((slots, WTOK) + array.shape[1:])  9.92 us
    pallas_call x1, Pallas kernels, prepare(): pl.pallas_call(partial(prepare_kernel, every), grid_spec=pltpu.PrefetchSc...  9.39 us
  transfers between devices with their start and end apart: 70, of which 34 were waited for; matrix products, arithmetic and copies ran while one was open for 7% of the time, Pallas kernels for 43%

profile of v8, /device:TPU:0, one launch (start us, length us, event | category | flops | bytes accessed | tf_op | source)
XLA Modules:
  0.0 387.8 jit_solution(14161958105330622235)
XLA Ops:
  2.9 3.1 collective-permute-start
  7.9 5.0 %reshape.125.x_ref = bf16[8,196,1280]{2,1,0:T(8,128)(2,1)} reshape(bf16[1568,1280]{1,0:T(8,128)(2,1)} %param.19) | data formatting | bytes 8028160 | tf_op jit(solution)/shard_map/reshape | solution.py:1171
  13.9 4.5 %collective-permute-done.refs_2_ = bf16[160,1344]{1,0:T(8,128)(2,1)} collective-permute-done((bf16[160,1344]{1,0:T(8,128)(2,1)S(1)}, bf16[160,1344]{1,0:T(8,128)(2,1)}, u32[]{:S(2)}, u32[]{:S(2)}) %collective-permute-start) | collective-permute-done | bytes 430112 | tf_op jit(solution)/shard_map/ppermute | solution.py:1296
  23.5 9.4 %prepare.1 = (bf16[416,1280]{1,0:T(8,128)(2,1)}, f32[416,1]{1,0:T(8,128)}, bf16[1664,1280]{1,0:T(8,128)(2,1)}, f32[1664,1]{1,0:T(8,128)}) custom-call(s32[8]{0:T(128)} %stack.112.order, s32[8]{0:T(128)} %places.5, s32[8]{0:T(128)} %lives.5, bf16[8,196,1280]{2,1,0:T(8,128)(2,1)} %reshape.125.x_ref, f32[1,1280]{1,0:T(1,128)} %reshape.126.gain_ref.refs_10_, ...), custom_call_target="tpu_custom_call" | custom-call | flops 450000000 | bytes 90000 | tf_op jit(solution)/shard_map/prepare/pallas_call | solution.py:115
  32.9 1.6 collective-permute-start.4
  35.0 4.9 %reshape.132.top_ref = bf16[8,196,1280]{2,1,0:T(8,128)(2,1)} reshape(bf16[1568,1280]{1,0:T(8,128)(2,1)} %param.36) | data formatting | bytes 8028160 | tf_op jit(solution)/shard_map/reshape | solution.py:1171
  40.0 5.6 %collective-permute-done.4.refs_6_ = bf16[160,1344]{1,0:T(8,128)(2,1)} collective-permute-done((bf16[160,1344]{1,0:T(8,128)(2,1)}, bf16[160,1344]{1,0:T(8,128)(2,1)}, u32[]{:S(2)}, u32[]{:S(2)}) %collective-permute-start.4) | collective-permute-done | bytes 430112 | tf_op jit(solution)/shard_map/ppermute | solution.py:1305
  47.3 7.7 %mask_rows.1.refs_14_.refs_4_.refs_0_.refs_2_ = bf16[1664,1280]{1,0:T(8,128)(2,1)} custom-call(s32[8]{0:T(128)} %stack.112.order, s32[8]{0:T(128)} %places.5, s32[8]{0:T(128)} %lives.5, bf16[8,196,1280]{2,1,0:T(8,128)(2,1)} %reshape.132.top_ref), custom_call_target="tpu_custom_call" | custom-call | flops 300000000 | bytes 60000 | tf_op jit(solution)/shard_map/mask_rows/pallas_call | solution.py:149
  55.0 2.0 collective-permute-done.7.refs_7_
  59.2 2.2 copy-done.1
  64.5 8.2 %qkv.1 = (bf16[1664,384]{1,0:T(8,128)(2,1)S(1)}, bf16[1664,384]{1,0:T(8,128)(2,1)S(1)}, bf16[1664,384]{1,0:T(8,128)(2,1)S(1)}, bf16[1280,1344]{1,0:T(8,128)(2,1)S(1)}) custom-call(s32[8]{0:T(128)S(1)} %stack.121.offsets, bf16[160,1344]{1,0:T(8,128)(2,1)S(1)} %copy-done.61, bf16[160,1344]{1,0:T(8,128)(2,1)S(1)} %copy-done.88, ...), custom_call_target="tpu_custom_call" | custom-call | flops 700000000 | bytes 140000 | tf_op jit(solution)/shard_map/qkv/pallas_call | solution.py:321
  72.7 2.5 collective-permute-done.8.refs_5_
  76.3 10.6 %attend.2 = (bf16[832,320]{1,0:T(8,128)(2,1)S(1)}, bf16[832,1024]{1,0:T(8,128)(2,1)S(1)}, bf16[416,1280]{1,0:T(8,128)(2,1)S(1)}, bf16[208,1280]{1,0:T(8,128)(2,1)S(1)}, bf16[208,1280]{1,0:T(8,128)(2,1)S(1)}) custom-call(bf16[1664,384]{1,0:T(8,128)(2,1)S(1)} %get-tuple-element.275.q_ref.refs_4_, bf16[1664,384]{1,0:T(8,128)(2,1)S(1)} %get-tuple-element.262.k_ref.refs_5_, ...), custom_call_target="tpu_custom_call" | custom-call | flops 675000000 | bytes 135000 | tf_op jit(solution)/shard_map/attend/pallas_call | solution.py:460
  88.2 3.1 collective-permute-done.10.refs_7_
  91.8 1.9 collective-permute-done.13.refs_1_
  93.9 1.6 collective-permute-start.14
  96.8 10.6 %attend.3 = (bf16[832,320]{1,0:T(8,128)(2,1)S(1)}, bf16[832,1024]{1,0:T(8,128)(2,1)S(1)}, bf16[416,1280]{1,0:T(8,128)(2,1)S(1)}, bf16[208,1280]{1,0:T(8,128)(2,1)S(1)}, bf16[208,1280]{1,0:T(8,128)(2,1)S(1)}) custom-call(bf16[1664,384]{1,0:T(8,128)(2,1)S(1)} %get-tuple-element.275.q_ref.refs_4_, bf16[1664,384]{1,0:T(8,128)(2,1)S(1)} %get-tuple-element.262.k_ref.refs_5_, ...), custom_call_target="tpu_custom_call" | custom-call | flops 675000000 | bytes 135000 | tf_op jit(solution)/shard_map/attend/pallas_call | solution.py:460
  114.4 3.0 collective-permute-done.11.refs_10_
  119.6 6.2 %collective-permute-done.21.refs_2_ = bf16[208,1280]{1,0:T(8,128)(2,1)S(1)} collective-permute-done((bf16[208,1280]{1,0:T(8,128)(2,1)S(1)}, bf16[208,1280]{1,0:T(8,128)(2,1)S(1)}, u32[]{:S(2)}, u32[]{:S(2)}) %collective-permute-start.21) | collective-permute-done | bytes 532512 | tf_op jit(solution)/shard_map/ppermute | solution.py:1331
  127.4 2.5 collective-permute-done.18.refs_11_
  130.0 6.7 %collective-permute-done.19.refs_12_ = bf16[80,2560]{1,0:T(8,128)(2,1)S(1)} collective-permute-done((bf16[80,2560]{1,0:T(8,128)(2,1)S(1)}, bf16[80,2560]{1,0:T(8,128)(2,1)S(1)}, u32[]{:S(2)}, u32[]{:S(2)}) %collective-permute-start.19) | collective-permute-done | bytes 409632 | tf_op jit(solution)/shard_map/ppermute | solution.py:1335
  139.7 20.1 %mlp.2 = (bf16[832,1280]{1,0:T(8,128)(2,1)}, bf16[832,1280]{1,0:T(8,128)(2,1)}, bf16[832,1280]{1,0:T(8,128)(2,1)}, f32[1,1280]{1,0:T(1,128)S(1)}, bf16[416,1280]...) custom-call(s32[9]{0:T(128)S(1)} %concatenate.18.offsets, ...), custom_call_target="tpu_custom_call" | custom-call | flops 1050000000 | bytes 210000 | tf_op jit(solution)/shard_map/mlp/pallas_call | solution.py:729
  161.0 1.9 collective-permute-done.25.refs_1_
  165.9 20.3 %mlp.3 = (bf16[832,1280]{1,0:T(8,128)(2,1)}, bf16[832,1280]{1,0:T(8,128)(2,1)}, bf16[832,1280]{1,0:T(8,128)(2,1)}, f32[1,1280]{1,0:T(1,128)S(1)}, bf16[416,1280]...) custom-call(s32[9]{0:T(128)S(1)} %concatenate.18.offsets, ...), custom_call_target="tpu_custom_call" | custom-call | flops 1050000000 | bytes 210000 | tf_op jit(solution)/shard_map/mlp/pallas_call | solution.py:729
  187.0 1.9 norm_two_back.2
  192.2 1.7 combine.15
  194.8 2.2 copy-done
  197.0 10.0 %weight_grad.3.refs_0_.refs_2_.refs_4_ = bf16[4,2,160,1280]{3,2,1,0:T(8,128)(2,1)S(1)} custom-call(s32[8]{0:T(128)S(1)} %stack.131.targets, bf16[1664,1280]{1,0:T(8,128)(2,1)S(1)} %copy-done, bf16[832,1280]{1,0:T(8,128)(2,1)S(1)} %copy-done.45, bf16[1664,1280]{1,0:T(8,128)(2,1)S(1)} %copy-done, bf16[832,1280]{1,0:T(8,128)(2,1)S(1)} %copy-done.48), custom_call_target="tpu_custom_call" | custom-call | flops 650000000 | bytes 130000 | tf_op jit(solution)/shard_map/weight_grad/pallas_call | solution.py:877
  209.2 10.5 %weight_grad.4 = (bf16[2,160,1280]{2,1,0:T(8,128)(2,1)S(1)}, bf16[2,160,1280]{2,1,0:T(8,128)(2,1)S(1)}, bf16[4,160,1280]{2,1,0:T(8,128)(2,1)S(1)}) custom-call(s32[8]{0:T(128)S(1)} %stack.131.targets, bf16[832,1280]{1,0:T(8,128)(2,1)S(1)} %copy-done.52, bf16[832,1280]{1,0:T(8,128)(2,1)S(1)} %copy-done.51, bf16[832,1280]{1,0:T(8,128)(2,1)S(1)} %copy-done.54, ...), custom_call_target="tpu_custom_call" | custom-call | flops 650000000 | bytes 130000 | tf_op jit(solution)/shard_map/weight_grad/pallas_call | solution.py:877
  220.9 1.6 collective-permute-done.33.refs_2_
  224.0 2.4 norm_two_back.3
  227.4 1.9 collective-permute-done.38.refs_1_.refs_3_
  232.6 14.0 %attend_back.2 = (bf16[832,960]{1,0:T(8,128)(2,1)S(1)}, bf16[832,1280]{1,0:T(8,128)(2,1)S(1)}, f32[256,384]{1,0:T(8,128)S(1)}, f32[1,960]{1,0:T(1,128)S(1)}, f32...) custom-call(bf16[208,1280]{1,0:T(8,128)(2,1)} %get-tuple-element.359.refs_0_, ...), custom_call_target="tpu_custom_call" | custom-call | flops 925000000 | bytes 185000 | tf_op jit(solution)/shard_map/attend_back/pallas_call | solution.py:581
  246.7 4.1 %collective-permute-done.39.refs_3_.refs_5_ = bf16[160,2560]{1,0:T(8,128)(2,1)S(1)} collective-permute-done((bf16[160,2560]{1,0:T(8,128)(2,1)S(1)}, bf16[160,2560]{1,0:T(8,128)(2,1)S(1)}, u32[]{:S(2)}, u32[]{:S(2)}) %collective-permute-start.39) | collective-permute-done | bytes 819232 | tf_op jit(solution)/shard_map/ppermute | solution.py:1392
  255.1 1.6 collective-permute-start.41
  256.6 13.8 %attend_back.3 = (bf16[832,960]{1,0:T(8,128)(2,1)S(1)}, bf16[832,1280]{1,0:T(8,128)(2,1)S(1)}, f32[256,384]{1,0:T(8,128)S(1)}, f32[1,960]{1,0:T(1,128)S(1)}, f32...) custom-call(bf16[208,1280]{1,0:T(8,128)(2,1)S(1)} %get-tuple-element.380.refs_0_, ...), custom_call_target="tpu_custom_call" | custom-call | flops 925000000 | bytes 185000 | tf_op jit(solution)/shard_map/attend_back/pallas_call | solution.py:581
  275.9 4.4 %collective-permute-done.41.refs_2_ = bf16[208,1280]{1,0:T(8,128)(2,1)S(1)} collective-permute-done((bf16[208,1280]{1,0:T(8,128)(2,1)S(1)}, bf16[208,1280]{1,0:T(8,128)(2,1)S(1)}, u32[]{:S(2)}, u32[]{:S(2)}) %collective-permute-start.41) | collective-permute-done | bytes 532512 | tf_op jit(solution)/shard_map/ppermute | solution.py:1403
  300.9 11.8 %weight_grad.5 = (bf16[1,160,1280]{2,1,0:T(8,128)(2,1)S(1)}, bf16[2,160,1280]{2,1,0:T(8,128)(2,1)S(1)}, bf16[1,160,1280]{2,1,0:T(8,128)(2,1)}, bf16[4,160,1280]{2,1,0:T(8,128)(2,1)S(1)}) custom-call(s32[8]{0:T(128)S(1)} %stack.131.targets, bf16[1664,1280]{1,0:T(8,128)(2,1)S(1)} %bitcast.83, bf16[832,960]{1,0:T(8,128)(2,1)S(1)} %copy-done.68, ...), custom_call_target="tpu_custom_call" | custom-call | flops 650000000 | bytes 130000 | tf_op jit(solution)/shard_map/weight_grad/pallas_call | solution.py:877
  316.1 3.0 norm_one_back.1.refs_0_
  321.7 2.4 combine.20.refs_0_
  324.1 2.8 collective-permute-done.54.refs_4_
  327.2 4.0 %collective-permute-start.57 = (bf16[160,2560]{1,0:T(8,128)(2,1)S(1)}, bf16[160,2560]{1,0:T(8,128)(2,1)S(1)}, u32[]{:S(2)}, u32[]{:S(2)}) collective-permute-start(bf16[160,2560]{1,0:T(8,128)(2,1)S(1)} %combine.21), channel_id=1, source_target_pairs={{0,8},{4,12},{8,16},{12,20},{16,24},{20,28},{24,0},{28,4},{1,9},{5... | collective-permute-start | bytes 2457608 | tf_op jit(solution)/shard_map/ppermute | solution.py:1503
  331.7 16.0 %collective-permute-done.58 = f32[160,128]{1,0:T(8,128)S(1)} collective-permute-done((f32[160,128]{1,0:T(8,128)S(1)}, f32[160,128]{1,0:T(8,128)S(1)}, u32[]{:S(2)}, u32[]{:S(2)}) %collective-permute-start.58) | collective-permute-done | bytes 81952 | tf_op jit(solution)/shard_map/ppermute | solution.py:1504
  349.1 1.6 collective-permute-start.61
  352.9 4.6 %place_windows.1 = f32[1568,1280]{1,0:T(8,128)} custom-call(s32[4]{0:T(128)S(1)} %pad_add_fusion.1.order, bf16[416,1280]{1,0:T(8,128)(2,1)S(1)} %norm_one_back.1.refs_0_, bf16[416,1280]{1,0:T(8,128)(2,1)S(1)} %collective-permute-done.59.refs_1_, bf16[416,1280]{1,0:T(8,128)(2,1)S(1)} %collective-permute-done.62.refs_2_, ...), custom_call_target="tpu_custom_call" | custom-call | flops 350000000 | bytes 70000 | tf_op jit(solution)/shard_map/place_windows/pallas_call | solution.py:953
  357.4 7.6 %collective-permute-done.61 = f32[160,128]{1,0:T(8,128)S(1)} collective-permute-done((f32[160,128]{1,0:T(8,128)S(1)}, f32[160,128]{1,0:T(8,128)S(1)}, u32[]{:S(2)}, u32[]{:S(2)}) %collective-permute-start.61) | collective-permute-done | bytes 81952 | tf_op jit(solution)/shard_map/ppermute | solution.py:1521
  372.1 5.7 %collective-permute-done.65.refs_1_ = bf16[416,1280]{1,0:T(8,128)(2,1)S(1)} collective-permute-done((bf16[416,1280]{1,0:T(8,128)(2,1)}, bf16[416,1280]{1,0:T(8,128)(2,1)S(1)}, u32[]{:S(2)}, u32[]{:S(2)}) %collective-permute-start.65) | collective-permute-done | bytes 1064992 | tf_op jit(solution)/shard_map/ppermute | solution.py:1505
  383.0 4.6 %write_output.1 = bf16[1568,1280]{1,0:T(8,128)(2,1)} custom-call(s32[4]{0:T(128)S(1)} %pad_add_fusion.1.order, s32[8]{0:T(128)S(1)} %copy-done.95, s32[8]{0:T(128)S(1)} %copy-done.96, bf16[416,1280]{1,0:T(8,128)(2,1)} %combine.20.refs_0_, bf16[416,1280]{1,0:T(8,128)(2,1)S(1)} %collective-permute-done.65.refs_1_, ...), custom_call_target="tpu_custom_call" | custom-call | flops 350000000 | bytes 70000 | tf_op jit(solution)/shard_map/write_output/pallas_call | solution.py:988
  (437 shorter events, 106.1 us)
Async XLA Ops:
  2.9 15.6 %collective-permute-start = (bf16[160,1344]{1,0:T(8,128)(2,1)S(1)}, bf16[160,1344]{1,0:T(8,128)(2,1)}, u32[]{:S(2)}, u32[]{:S(2)}) collective-permute-start(bf16[160,1344]{1,0:T(8,128)(2,1)S(1)} %concatenate.16.refs_0_), channel_id=1, source_target_pairs={{0,8},{4,12},{8,16},{12,20},{16,24},{20,28},{24,0},{28,4},{1,9},{5... | collective-permute-start | bytes 1290248 | tf_op jit(solution)/shard_map/ppermute | solution.py:1296
  5.9 12.5 %collective-permute-start.1 = (bf16[160,1344]{1,0:T(8,128)(2,1)S(1)}, bf16[160,1344]{1,0:T(8,128)(2,1)S(1)}, u32[]{:S(2)}, u32[]{:S(2)}) collective-permute-start(bf16[160,1344]{1,0:T(8,128)(2,1)S(1)} %concatenate.16.refs_0_), channel_id=1, source_target_pairs={{0,4},{4,0},{8,12},{12,8},{16,20},{20,16},{24,28},{28,24},{1,5},{5... | collective-permute-start | bytes 1290248 | tf_op jit(solution)/shard_map/ppermute | solution.py:1296
  19.2 13.7 %collective-permute-start.2 = (bf16[160,1344]{1,0:T(8,128)(2,1)}, bf16[160,1344]{1,0:T(8,128)(2,1)}, u32[]{:S(2)}, u32[]{:S(2)}) collective-permute-start(bf16[160,1344]{1,0:T(8,128)(2,1)} %collective-permute-done.refs_2_), channel_id=1, source_target_pairs={{0,8},{4,12},{8,16},{12,20},{16,24},{20,28},{24,0},{28,4},{1,9},{5... | collective-permute-start | bytes 1290248 | tf_op jit(solution)/shard_map/ppermute | solution.py:1300
  20.1 12.8 %collective-permute-start.3 = (bf16[160,1344]{1,0:T(8,128)(2,1)}, bf16[160,1344]{1,0:T(8,128)(2,1)}, u32[]{:S(2)}, u32[]{:S(2)}) collective-permute-start(bf16[160,1344]{1,0:T(8,128)(2,1)} %collective-permute-done.refs_2_), channel_id=1, source_target_pairs={{0,4},{4,0},{8,12},{12,8},{16,20},{20,16},{24,28},{28,24},{1,5},{5... | collective-permute-start | bytes 1290248 | tf_op jit(solution)/shard_map/ppermute | solution.py:1300
  32.9 12.7 %collective-permute-start.4 = (bf16[160,1344]{1,0:T(8,128)(2,1)}, bf16[160,1344]{1,0:T(8,128)(2,1)}, u32[]{:S(2)}, u32[]{:S(2)}) collective-permute-start(bf16[160,1344]{1,0:T(8,128)(2,1)} %collective-permute-done.2.refs_4_), channel_id=1, source_target_pairs={{0,8},{4,12},{8,16},{12,20},{16,24},{20,28},{24,0},{28,4},{1,9},{5... | collective-permute-start | bytes 1290248 | tf_op jit(solution)/shard_map/ppermute | solution.py:1305
  34.5 11.1 %collective-permute-start.5 = (bf16[160,1344]{1,0:T(8,128)(2,1)}, bf16[160,1344]{1,0:T(8,128)(2,1)S(1)}, u32[]{:S(2)}, u32[]{:S(2)}) collective-permute-start(bf16[160,1344]{1,0:T(8,128)(2,1)} %collective-permute-done.2.refs_4_), channel_id=1, source_target_pairs={{0,4},{4,0},{8,12},{12,8},{16,20},{20,16},{24,28},{28,24},{1,5},{5... | collective-permute-start | bytes 1290248 | tf_op jit(solution)/shard_map/ppermute | solution.py:1305
  47.3 25.4 %collective-permute-start.6 = (bf16[160,2560]{1,0:T(8,128)(2,1)S(1)}, bf16[160,2560]{1,0:T(8,128)(2,1)}, u32[]{:S(2)}, u32[]{:S(2)}) collective-permute-start(bf16[160,2560]{1,0:T(8,128)(2,1)S(1)} %pad_maximum_fusion.refs_4_), channel_id=1, source_target_pairs={{0,8},{4,12},{8,16},{12,20},{16,24},{20,28},{24,0},{28,4},{1,9},{5... | collective-permute-start | bytes 2457608 | tf_op jit(solution)/shard_map/ppermute | solution.py:1310
  57.0 18.2 %collective-permute-start.8 = (bf16[160,2560]{1,0:T(8,128)(2,1)S(1)}, bf16[160,2560]{1,0:T(8,128)(2,1)S(1)}, u32[]{:S(2)}, u32[]{:S(2)}) collective-permute-start(bf16[160,2560]{1,0:T(8,128)(2,1)S(1)} %pad_maximum_fusion.refs_4_), channel_id=1, source_target_pairs={{0,4},{4,0},{8,12},{12,8},{16,20},{20,16},{24,28},{28,24},{1,5},{5... | collective-permute-start | bytes 2457608 | tf_op jit(solution)/shard_map/ppermute | solution.py:1315
  75.2 16.0 %collective-permute-start.10 = (bf16[160,2560]{1,0:T(8,128)(2,1)}, bf16[160,2560]{1,0:T(8,128)(2,1)S(1)}, u32[]{:S(2)}, u32[]{:S(2)}) collective-permute-start(bf16[160,2560]{1,0:T(8,128)(2,1)} %collective-permute-done.6.refs_6_), channel_id=1, source_target_pairs={{0,4},{4,0},{8,12},{12,8},{16,20},{20,16},{24,28},{28,24},{1,5},{5... | collective-permute-start | bytes 2457608 | tf_op jit(solution)/shard_map/ppermute | solution.py:1320
  76.2 15.6 %collective-permute-start.9 = (bf16[160,2560]{1,0:T(8,128)(2,1)}, bf16[160,2560]{1,0:T(8,128)(2,1)S(1)}, u32[]{:S(2)}, u32[]{:S(2)}) collective-permute-start(bf16[160,2560]{1,0:T(8,128)(2,1)} %collective-permute-done.6.refs_6_), channel_id=1, source_target_pairs={{0,8},{4,12},{8,16},{12,20},{16,24},{20,28},{24,0},{28,4},{1,9},{5... | collective-permute-start | bytes 2457608 | tf_op jit(solution)/shard_map/ppermute | solution.py:1320
  93.9 14.8 %collective-permute-start.14 = (bf16[208,1280]{1,0:T(8,128)(2,1)S(1)}, bf16[208,1280]{1,0:T(8,128)(2,1)S(1)}, u32[]{:S(2)}, u32[]{:S(2)}) collective-permute-start(bf16[208,1280]{1,0:T(8,128)(2,1)S(1)} %combine.12), channel_id=1, source_target_pairs={{0,2},{1,3},{2,0},{3,1},{4,6},{5,7},{6,4},{7,5},{8,10},{9,11},{10,... | collective-permute-start | bytes 1597448 | tf_op jit(solution)/shard_map/ppermute | solution.py:1326
  95.5 22.0 %collective-permute-start.11 = (bf16[160,2560]{1,0:T(8,128)(2,1)S(1)}, bf16[160,2560]{1,0:T(8,128)(2,1)S(1)}, u32[]{:S(2)}, u32[]{:S(2)}) collective-permute-start(bf16[160,2560]{1,0:T(8,128)(2,1)S(1)} %collective-permute-done.9.refs_8_), channel_id=1, source_target_pairs={{0,8},{4,12},{8,16},{12,20},{16,24},{20,28},{24,0},{28,4},{1,9},{5... | collective-permute-start | bytes 2457608 | tf_op jit(solution)/shard_map/ppermute | solution.py:1323
  95.6 21.8 %collective-permute-start.12 = (bf16[160,2560]{1,0:T(8,128)(2,1)S(1)}, bf16[160,2560]{1,0:T(8,128)(2,1)S(1)}, u32[]{:S(2)}, u32[]{:S(2)}) collective-permute-start(bf16[160,2560]{1,0:T(8,128)(2,1)S(1)} %collective-permute-done.9.refs_8_), channel_id=1, source_target_pairs={{0,4},{4,0},{8,12},{12,8},{16,20},{20,16},{24,28},{28,24},{1,5},{5... | collective-permute-start | bytes 2457608 | tf_op jit(solution)/shard_map/ppermute | solution.py:1323
  110.8 15.0 %collective-permute-start.21 = (bf16[208,1280]{1,0:T(8,128)(2,1)S(1)}, bf16[208,1280]{1,0:T(8,128)(2,1)S(1)}, u32[]{:S(2)}, u32[]{:S(2)}) collective-permute-start(bf16[208,1280]{1,0:T(8,128)(2,1)S(1)} %combine.13), channel_id=1, source_target_pairs={{0,2},{1,3},{2,0},{3,1},{4,6},{5,7},{6,4},{7,5},{8,10},{9,11},{10,... | collective-permute-start | bytes 1597448 | tf_op jit(solution)/shard_map/ppermute | solution.py:1331
  113.5 23.2 %collective-permute-start.20 = (bf16[208,1280]{1,0:T(8,128)(2,1)}, bf16[208,1280]{1,0:T(8,128)(2,1)}, u32[]{:S(2)}, u32[]{:S(2)}) collective-permute-start(bf16[208,1280]{1,0:T(8,128)(2,1)} %get-tuple-element.296.refs_0_), channel_id=1, source_target_pairs={{0,2},{1,3},{2,0},{3,1},{4,6},{5,7},{6,4},{7,5},{8,10},{9,11},{10,... | collective-permute-start | bytes 1597448 | tf_op jit(solution)/shard_map/ppermute | solution.py:1333
  117.5 12.5 %collective-permute-start.18 = (bf16[80,2560]{1,0:T(8,128)(2,1)S(1)}, bf16[80,2560]{1,0:T(8,128)(2,1)S(1)}, u32[]{:S(2)}, u32[]{:S(2)}) collective-permute-start(bf16[80,2560]{1,0:T(8,128)(2,1)S(1)} %get-tuple-element.467), channel_id=1, source_target_pairs={{0,4},{4,0},{8,12},{12,8},{16,20},{20,16},{24,28},{28,24},{1,5},{5... | collective-permute-start | bytes 1228808 | tf_op jit(solution)/shard_map/ppermute | solution.py:1335
  118.6 18.0 %collective-permute-start.19 = (bf16[80,2560]{1,0:T(8,128)(2,1)S(1)}, bf16[80,2560]{1,0:T(8,128)(2,1)S(1)}, u32[]{:S(2)}, u32[]{:S(2)}) collective-permute-start(bf16[80,2560]{1,0:T(8,128)(2,1)S(1)} %get-tuple-element.466), channel_id=1, source_target_pairs={{0,4},{4,0},{8,12},{12,8},{16,20},{20,16},{24,28},{28,24},{1,5},{5... | collective-permute-start | bytes 1228808 | tf_op jit(solution)/shard_map/ppermute | solution.py:1335
  137.2 22.7 %collective-permute-start.22 = (bf16[208,1280]{1,0:T(8,128)(2,1)S(1)}, bf16[208,1280]{1,0:T(8,128)(2,1)}, u32[]{:S(2)}, u32[]{:S(2)}) collective-permute-start(bf16[208,1280]{1,0:T(8,128)(2,1)S(1)} %get-tuple-element.317.refs_0_), channel_id=1, source_target_pairs={{0,2},{1,3},{2,0},{3,1},{4,6},{5,7},{6,4},{7,5},{8,10},{9,11},{10,... | collective-permute-start | bytes 1597448 | tf_op jit(solution)/shard_map/ppermute | solution.py:1341
  160.1 26.2 %collective-permute-start.27 = (bf16[416,1280]{1,0:T(8,128)(2,1)}, bf16[416,1280]{1,0:T(8,128)(2,1)S(1)}, u32[]{:S(2)}, u32[]{:S(2)}) collective-permute-start(bf16[416,1280]{1,0:T(8,128)(2,1)} %get-tuple-element.316), channel_id=1, source_target_pairs={{0,1},{1,0},{2,3},{3,2},{4,5},{5,4},{6,7},{7,6},{8,9},{9,8},{10,11... | collective-permute-start | bytes 3194888 | tf_op jit(solution)/shard_map/ppermute | solution.py:1347
  164.2 22.1 %collective-permute-start.26 = (bf16[208,1280]{1,0:T(8,128)(2,1)S(1)}, bf16[208,1280]{1,0:T(8,128)(2,1)S(1)}, u32[]{:S(2)}, u32[]{:S(2)}) collective-permute-start(bf16[208,1280]{1,0:T(8,128)(2,1)S(1)} %combine.14), channel_id=1, source_target_pairs={{0,2},{1,3},{2,0},{3,1},{4,6},{5,7},{6,4},{7,5},{8,10},{9,11},{10,... | collective-permute-start | bytes 1597448 | tf_op jit(solution)/shard_map/ppermute | solution.py:1349
  189.9 17.1 %collective-permute-start.31 = (bf16[208,1280]{1,0:T(8,128)(2,1)}, bf16[208,1280]{1,0:T(8,128)(2,1)}, u32[]{:S(2)}, u32[]{:S(2)}) collective-permute-start(bf16[208,1280]{1,0:T(8,128)(2,1)} %get-tuple-element.359.refs_0_), channel_id=1, source_target_pairs={{0,2},{1,3},{2,0},{3,1},{4,6},{5,7},{6,4},{7,5},{8,10},{9,11},{10,... | collective-permute-start | bytes 1597448 | tf_op jit(solution)/shard_map/ppermute | solution.py:1356
  207.1 22.1 %collective-permute-start.38 = (bf16[2,160,1280]{2,1,0:T(8,128)(2,1)S(1)}, bf16[2,160,1280]{2,1,0:T(8,128)(2,1)S(1)}, u32[]{:S(2)}, u32[]{:S(2)}) collective-permute-start(bf16[2,160,1280]{2,1,0:T(8,128)(2,1)S(1)} %slice_bitcast_fusion), channel_id=1, source_target_pairs={{0,8},{4,12},{8,16},{12,20},{16,24},{20,28},{24,0},{28,4},{1,9},{5... | collective-permute-start | bytes 2457608 | tf_op jit(solution)/shard_map/ppermute | solution.py:1369
  207.9 13.0 %collective-permute-start.34 = (bf16[208,1280]{1,0:T(8,128)(2,1)}, bf16[208,1280]{1,0:T(8,128)(2,1)S(1)}, u32[]{:S(2)}, u32[]{:S(2)}) collective-permute-start(bf16[208,1280]{1,0:T(8,128)(2,1)} %get-tuple-element.359.refs_0_), channel_id=1, source_target_pairs={{0,1},{1,0},{2,3},{3,2},{4,5},{5,4},{6,7},{7,6},{8,9},{9,8},{10,11... | collective-permute-start | bytes 1597448 | tf_op jit(solution)/shard_map/ppermute | solution.py:1289
  207.9 14.5 %collective-permute-start.33 = (bf16[208,1280]{1,0:T(8,128)(2,1)S(1)}, bf16[208,1280]{1,0:T(8,128)(2,1)S(1)}, u32[]{:S(2)}, u32[]{:S(2)}) collective-permute-start(bf16[208,1280]{1,0:T(8,128)(2,1)S(1)} %get-tuple-element.344), channel_id=1, source_target_pairs={{0,2},{1,3},{2,0},{3,1},{4,6},{5,7},{6,4},{7,5},{8,10},{9,11},{10,... | collective-permute-start | bytes 1597448 | tf_op jit(solution)/shard_map/ppermute | solution.py:1365
  209.0 13.5 %collective-permute-start.35 = (bf16[208,1280]{1,0:T(8,128)(2,1)}, bf16[208,1280]{1,0:T(8,128)(2,1)S(1)}, u32[]{:S(2)}, u32[]{:S(2)}) collective-permute-start(bf16[208,1280]{1,0:T(8,128)(2,1)} %collective-permute-done.31.refs_1_), channel_id=1, source_target_pairs={{0,1},{1,0},{2,3},{3,2},{4,5},{5,4},{6,7},{7,6},{8,9},{9,8},{10,11... | collective-permute-start | bytes 1597448 | tf_op jit(solution)/shard_map/ppermute | solution.py:1289
  222.5 24.2 %collective-permute-start.37 = (bf16[2,160,1280]{2,1,0:T(8,128)(2,1)S(1)}, bf16[2,160,1280]{2,1,0:T(8,128)(2,1)S(1)}, u32[]{:S(2)}, u32[]{:S(2)}) collective-permute-start(bf16[2,160,1280]{2,1,0:T(8,128)(2,1)S(1)} %get-tuple-element.356), channel_id=1, source_target_pairs={{0,4},{4,0},{8,12},{12,8},{16,20},{20,16},{24,28},{28,24},{1,5},{5... | collective-permute-start | bytes 2457608 | tf_op jit(solution)/shard_map/ppermute | solution.py:1374
  229.5 21.3 %collective-permute-start.39 = (bf16[160,2560]{1,0:T(8,128)(2,1)S(1)}, bf16[160,2560]{1,0:T(8,128)(2,1)S(1)}, u32[]{:S(2)}, u32[]{:S(2)}) collective-permute-start(bf16[160,2560]{1,0:T(8,128)(2,1)S(1)} %combine.16), channel_id=1, source_target_pairs={{0,8},{4,12},{8,16},{12,20},{16,24},{20,28},{24,0},{28,4},{1,9},{5... | collective-permute-start | bytes 2457608 | tf_op jit(solution)/shard_map/ppermute | solution.py:1392
  229.5 17.1 %collective-permute-start.36 = (bf16[208,1280]{1,0:T(8,128)(2,1)S(1)}, bf16[208,1280]{1,0:T(8,128)(2,1)S(1)}, u32[]{:S(2)}, u32[]{:S(2)}) collective-permute-start(bf16[208,1280]{1,0:T(8,128)(2,1)S(1)} %get-tuple-element.380.refs_0_), channel_id=1, source_target_pairs={{0,2},{1,3},{2,0},{3,1},{4,6},{5,7},{6,4},{7,5},{8,10},{9,11},{10,... | collective-permute-start | bytes 1597448 | tf_op jit(solution)/shard_map/ppermute | solution.py:1384
  251.3 22.9 %collective-permute-start.43 = (bf16[2,160,1280]{2,1,0:T(8,128)(2,1)S(1)}, bf16[2,160,1280]{2,1,0:T(8,128)(2,1)S(1)}, u32[]{:S(2)}, u32[]{:S(2)}) collective-permute-start(bf16[2,160,1280]{2,1,0:T(8,128)(2,1)S(1)} %get-tuple-element.377), channel_id=1, source_target_pairs={{0,4},{4,0},{8,12},{12,8},{16,20},{20,16},{24,28},{28,24},{1,5},{5... | collective-permute-start | bytes 2457608 | tf_op jit(solution)/shard_map/ppermute | solution.py:1397
  254.5 26.8 %collective-permute-start.42 = (bf16[160,2560]{1,0:T(8,128)(2,1)S(1)}, bf16[160,2560]{1,0:T(8,128)(2,1)S(1)}, u32[]{:S(2)}, u32[]{:S(2)}) collective-permute-start(bf16[160,2560]{1,0:T(8,128)(2,1)S(1)} %get-tuple-element.376), channel_id=1, source_target_pairs={{0,8},{4,12},{8,16},{12,20},{16,24},{20,28},{24,0},{28,4},{1,9},{5... | collective-permute-start | bytes 2457608 | tf_op jit(solution)/shard_map/ppermute | solution.py:1404
  254.6 20.6 %collective-permute-start.44 = (bf16[208,1280]{1,0:T(8,128)(2,1)S(1)}, bf16[208,1280]{1,0:T(8,128)(2,1)S(1)}, u32[]{:S(2)}, u32[]{:S(2)}) collective-permute-start(bf16[208,1280]{1,0:T(8,128)(2,1)S(1)} %get-tuple-element.379), channel_id=1, source_target_pairs={{0,2},{1,3},{2,0},{3,1},{4,6},{5,7},{6,4},{7,5},{8,10},{9,11},{10,... | collective-permute-start | bytes 1597448 | tf_op jit(solution)/shard_map/ppermute | solution.py:1406
  255.1 25.3 %collective-permute-start.41 = (bf16[208,1280]{1,0:T(8,128)(2,1)S(1)}, bf16[208,1280]{1,0:T(8,128)(2,1)S(1)}, u32[]{:S(2)}, u32[]{:S(2)}) collective-permute-start(bf16[208,1280]{1,0:T(8,128)(2,1)S(1)} %get-tuple-element.375), channel_id=1, source_target_pairs={{0,2},{1,3},{2,0},{3,1},{4,6},{5,7},{6,4},{7,5},{8,10},{9,11},{10,... | collective-permute-start | bytes 1597448 | tf_op jit(solution)/shard_map/ppermute | solution.py:1403
  292.6 20.1 %collective-permute-start.49 = (bf16[208,1280]{1,0:T(8,128)(2,1)S(1)}, bf16[208,1280]{1,0:T(8,128)(2,1)S(1)}, u32[]{:S(2)}, u32[]{:S(2)}) collective-permute-start(bf16[208,1280]{1,0:T(8,128)(2,1)S(1)} %get-tuple-element.405), channel_id=1, source_target_pairs={{0,2},{1,3},{2,0},{3,1},{4,6},{5,7},{6,4},{7,5},{8,10},{9,11},{10,... | collective-permute-start | bytes 1597448 | tf_op jit(solution)/shard_map/ppermute | solution.py:1430
  293.1 19.6 %collective-permute-start.50 = (bf16[160,1280]{1,0:T(8,128)(2,1)S(1)}, bf16[160,1280]{1,0:T(8,128)(2,1)S(1)}, u32[]{:S(2)}, u32[]{:S(2)}) collective-permute-start(bf16[160,1280]{1,0:T(8,128)(2,1)S(1)} %get-tuple-element.406), channel_id=1, source_target_pairs={{0,4},{4,0},{8,12},{12,8},{16,20},{20,16},{24,28},{28,24},{1,5},{5... | collective-permute-start | bytes 1228808 | tf_op jit(solution)/shard_map/ppermute | solution.py:1431
  294.2 18.5 %collective-permute-start.51 = (bf16[160,1280]{1,0:T(8,128)(2,1)S(1)}, bf16[160,1280]{1,0:T(8,128)(2,1)S(1)}, u32[]{:S(2)}, u32[]{:S(2)}) collective-permute-start(bf16[160,1280]{1,0:T(8,128)(2,1)S(1)} %get-tuple-element.407), channel_id=1, source_target_pairs={{0,8},{4,12},{8,16},{12,20},{16,24},{20,28},{24,0},{28,4},{1,9},{5... | collective-permute-start | bytes 1228808 | tf_op jit(solution)/shard_map/ppermute | solution.py:1431
  294.6 27.1 %collective-permute-start.55 = (bf16[208,1280]{1,0:T(8,128)(2,1)}, bf16[208,1280]{1,0:T(8,128)(2,1)S(1)}, u32[]{:S(2)}, u32[]{:S(2)}) collective-permute-start(bf16[208,1280]{1,0:T(8,128)(2,1)} %copy-done.97), channel_id=1, source_target_pairs={{0,2},{1,3},{2,0},{3,1},{4,6},{5,7},{6,4},{7,5},{8,10},{9,11},{10,... | collective-permute-start | bytes 1597448 | tf_op jit(solution)/shard_map/ppermute | solution.py:1433
  313.0 14.0 %collective-permute-start.54 = (bf16[160,1280]{1,0:T(8,128)(2,1)S(1)}, bf16[160,1280]{1,0:T(8,128)(2,1)S(1)}, u32[]{:S(2)}, u32[]{:S(2)}) collective-permute-start(bf16[160,1280]{1,0:T(8,128)(2,1)S(1)} %combine.19), channel_id=1, source_target_pairs={{0,8},{4,12},{8,16},{12,20},{16,24},{20,28},{24,0},{28,4},{1,9},{5... | collective-permute-start | bytes 1228808 | tf_op jit(solution)/shard_map/ppermute | solution.py:1453
  314.1 12.8 %collective-permute-start.53 = (bf16[1,160,1280]{2,1,0:T(8,128)(2,1)S(1)}, bf16[1,160,1280]{2,1,0:T(8,128)(2,1)S(1)}, u32[]{:S(2)}, u32[]{:S(2)}) collective-permute-start(bf16[1,160,1280]{2,1,0:T(8,128)(2,1)S(1)} %get-tuple-element.423), channel_id=1, source_target_pairs={{0,4},{4,0},{8,12},{12,8},{16,20},{20,16},{24,28},{28,24},{1,5},{5... | collective-permute-start | bytes 1228808 | tf_op jit(solution)/shard_map/ppermute | solution.py:1438
  320.2 27.6 %collective-permute-start.59 = (bf16[416,1280]{1,0:T(8,128)(2,1)S(1)}, bf16[416,1280]{1,0:T(8,128)(2,1)S(1)}, u32[]{:S(2)}, u32[]{:S(2)}) collective-permute-start(bf16[416,1280]{1,0:T(8,128)(2,1)S(1)} %norm_one_back.1.refs_0_), channel_id=1, source_target_pairs={{0,2},{1,3},{2,0},{3,1},{4,6},{5,7},{6,4},{7,5},{8,10},{9,11},{10,... | collective-permute-start | bytes 3194888 | tf_op jit(solution)/shard_map/ppermute | solution.py:1463
  320.6 27.2 %collective-permute-start.52 = (bf16[2,160,1280]{2,1,0:T(8,128)(2,1)S(1)}, bf16[2,160,1280]{2,1,0:T(8,128)(2,1)S(1)}, u32[]{:S(2)}, u32[]{:S(2)}) collective-permute-start(bf16[2,160,1280]{2,1,0:T(8,128)(2,1)S(1)} %get-tuple-element.422), channel_id=1, source_target_pairs={{0,4},{4,0},{8,12},{12,8},{16,20},{20,16},{24,28},{28,24},{1,5},{5... | collective-permute-start | bytes 2457608 | tf_op jit(solution)/shard_map/ppermute | solution.py:1487
  327.2 21.8 %collective-permute-start.57 = (bf16[160,2560]{1,0:T(8,128)(2,1)S(1)}, bf16[160,2560]{1,0:T(8,128)(2,1)S(1)}, u32[]{:S(2)}, u32[]{:S(2)}) collective-permute-start(bf16[160,2560]{1,0:T(8,128)(2,1)S(1)} %combine.21), channel_id=1, source_target_pairs={{0,8},{4,12},{8,16},{12,20},{16,24},{20,28},{24,0},{28,4},{1,9},{5... | collective-permute-start | bytes 2457608 | tf_op jit(solution)/shard_map/ppermute | solution.py:1503
  331.2 16.6 %collective-permute-start.58 = (f32[160,128]{1,0:T(8,128)S(1)}, f32[160,128]{1,0:T(8,128)S(1)}, u32[]{:S(2)}, u32[]{:S(2)}) collective-permute-start(f32[160,128]{1,0:T(8,128)S(1)} %add.277), channel_id=1, source_target_pairs={{0,8},{4,12},{8,0},{12,4},{16,24},{20,28},{24,16},{28,20},{1,9},{5... | collective-permute-start | bytes 245768 | tf_op jit(solution)/shard_map/ppermute | solution.py:1504
  331.7 21.1 %collective-permute-start.62 = (bf16[416,1280]{1,0:T(8,128)(2,1)S(1)}, bf16[416,1280]{1,0:T(8,128)(2,1)S(1)}, u32[]{:S(2)}, u32[]{:S(2)}) collective-permute-start(bf16[416,1280]{1,0:T(8,128)(2,1)S(1)} %norm_one_back.1.refs_0_), channel_id=1, source_target_pairs={{0,1},{1,0},{2,3},{3,2},{4,5},{5,4},{6,7},{7,6},{8,9},{9,8},{10,11... | collective-permute-start | bytes 3194888 | tf_op jit(solution)/shard_map/ppermute | solution.py:1289
  349.1 15.9 %collective-permute-start.61 = (f32[160,128]{1,0:T(8,128)S(1)}, f32[160,128]{1,0:T(8,128)S(1)}, u32[]{:S(2)}, u32[]{:S(2)}) collective-permute-start(f32[160,128]{1,0:T(8,128)S(1)} %add.278), channel_id=1, source_target_pairs={{0,16},{4,20},{8,24},{12,28},{16,0},{20,4},{24,8},{28,12},{1,17},{... | collective-permute-start | bytes 245768 | tf_op jit(solution)/shard_map/ppermute | solution.py:1521
  350.9 14.1 %collective-permute-start.60 = (bf16[160,1280]{1,0:T(8,128)(2,1)S(1)}, bf16[160,1280]{1,0:T(8,128)(2,1)S(1)}, u32[]{:S(2)}, u32[]{:S(2)}) collective-permute-start(bf16[160,1280]{1,0:T(8,128)(2,1)S(1)} %combine.22), channel_id=1, source_target_pairs={{0,8},{4,12},{8,16},{12,20},{16,24},{20,28},{24,0},{28,4},{1,9},{5... | collective-permute-start | bytes 1228808 | tf_op jit(solution)/shard_map/ppermute | solution.py:1520
  352.0 25.8 %collective-permute-start.65 = (bf16[416,1280]{1,0:T(8,128)(2,1)}, bf16[416,1280]{1,0:T(8,128)(2,1)S(1)}, u32[]{:S(2)}, u32[]{:S(2)}) collective-permute-start(bf16[416,1280]{1,0:T(8,128)(2,1)} %combine.20.refs_0_), channel_id=1, source_target_pairs={{0,2},{1,3},{2,0},{3,1},{4,6},{5,7},{6,4},{7,5},{8,10},{9,11},{10,... | collective-permute-start | bytes 3194888 | tf_op jit(solution)/shard_map/ppermute | solution.py:1505
  367.0 13.0 %collective-permute-start.69 = (bf16[160,1280]{1,0:T(8,128)(2,1)S(1)}, bf16[160,1280]{1,0:T(8,128)(2,1)S(1)}, u32[]{:S(2)}, u32[]{:S(2)}) collective-permute-start(bf16[160,1280]{1,0:T(8,128)(2,1)S(1)} %combine.23), channel_id=1, source_target_pairs={{0,8},{4,12},{8,16},{12,20},{16,24},{20,28},{24,0},{28,4},{1,9},{5... | collective-permute-start | bytes 1228808 | tf_op jit(solution)/shard_map/ppermute | solution.py:1529
  367.1 11.4 %collective-permute-start.64 = (bf16[1,160,1280]{2,1,0:T(8,128)(2,1)}, bf16[1,160,1280]{2,1,0:T(8,128)(2,1)S(1)}, u32[]{:S(2)}, u32[]{:S(2)}) collective-permute-start(bf16[1,160,1280]{2,1,0:T(8,128)(2,1)} %get-tuple-element.449), channel_id=1, source_target_pairs={{0,4},{4,0},{8,12},{12,8},{16,20},{20,16},{24,28},{28,24},{1,5},{5... | collective-permute-start | bytes 1228808 | tf_op jit(solution)/shard_map/ppermute | solution.py:1527
  (142 other events, 1025.5 us)
